TPU v7x, 32 devices: a whole 2x2x4 slice. The times are simulated.
32 devices in a mesh: state: 8 (over y, x, core), probe: 4 (over z).
Axes of the slice: x: 2, y: 2, z: 4, core: 2. Of those that a mesh axis runs over, the one named last changes fastest.
Arguments:
- sensor_field: float32 [4, 32, 64, 512], P('probe', 'state'), may hold values from -1 to 1
- courant: float32 [64], replicated, may hold values from 0.1 to 0.45
- diffusivity: float32 [64], replicated, may hold values from 0.01 to 0.085
- probe_offset: int32 [4], P('probe'), may hold values from 0 to 511
- tile_index: int32 [8, 4096], P('state'), may hold values from 0 to 1023
- actuator_panel: bfloat16 [8, 4096, 128], P('state', 'probe'), may hold values from -3 to 3
Outputs:
- projections: float32 [4, 4, 4096], P(None, 'probe')
- response: float32 [4, 32, 64, 512], P('probe', 'state')
All inputs are finite; a program needn't handle non-finite values.
Results may differ from a plain program's by a relative error of at most 0.0003.
Values may be sent and summed in bfloat16 or wider, within the bound.
No kernel may reach another device: no remote copies, remote signals or barrier semaphores. Data moves between devices by JAX's collectives and lax.ppermute only.
A program may use at most 64 MiB of HBM per device.

v0:
```python
import jax
import jax.numpy as jnp
from jax import lax
from jax.sharding import PartitionSpec as P

TILE = 128
STEPS = 4


def padded(block, sides, width):
    for axis, dim in sides:
        count = lax.axis_size(axis)
        forward = [(i, i + 1) for i in range(count - 1)]
        forward.append((count - 1, 0))
        backward = [(target, source) for source, target in forward]
        low = lax.ppermute(
            lax.slice_in_dim(block, block.shape[dim] - width, None, axis=dim), axis, forward
        )
        high = lax.ppermute(lax.slice_in_dim(block, 0, width, axis=dim), axis, backward)
        block = jnp.concatenate([low, block, high], axis=dim)
    return block


def advance(center, lower_x, upper_x, courant, diffusion, adjoint):
    advect_rate = courant[:, None]
    diff_rate = diffusion[:, None]
    upper_z = jnp.roll(center, -1, axis=-1)
    lower_z = jnp.roll(center, 1, axis=-1)
    zero_row = jnp.zeros_like(center[..., :1, :])
    upper_y = jnp.concatenate([center[..., 1:, :], zero_row], axis=-2)
    lower_y = jnp.concatenate([zero_row, center[..., :-1, :]], axis=-2)
    doubled_center = 2.0 * center
    lateral = lower_x + upper_x - doubled_center + (upper_z + lower_z - doubled_center)
    if adjoint:
        upwind = upper_x
        edge_zero = jnp.zeros((1,), diffusion.dtype)
        rate_above = jnp.concatenate([diffusion[1:], edge_zero])[:, None]
        rate_below = jnp.concatenate([edge_zero, diffusion[:-1]])[:, None]
        normal = rate_above * upper_y + rate_below * lower_y - diff_rate * doubled_center
    else:
        upwind = lower_x
        normal = diff_rate * (upper_y + lower_y - doubled_center)
    return center + advect_rate * (upwind - center) + diff_rate * lateral + normal


def shifted_sensor(sensor, offset):
    doubled = jnp.concatenate([sensor, sensor], axis=-1)
    span_z = sensor.shape[-1]
    begin_at = span_z - offset
    return lax.dynamic_slice_in_dim(doubled, begin_at, span_z, axis=doubled.ndim - 1)


def local(sensor_field, courant, diffusivity, probe_offset, tile_index, actuator_panel):
    panel_full = lax.all_gather(actuator_panel, "probe", axis=1, tiled=True)[0]
    index_row = tile_index[0]
    slab_shape = sensor_field.shape[1:]
    cells_x = slab_shape[0]
    probe_count = probe_offset.shape[0]
    tile_total = slab_shape[0] * slab_shape[1] * slab_shape[2] // TILE
    initial = jax.vmap(shifted_sensor, in_axes=(0, 0))(sensor_field, probe_offset)

    def run_phase(field_in, adjoint):
        history = []
        extended = padded(field_in, (("state", 1),), STEPS)
        for sweep_index in range(STEPS):
            extended = advance(
                extended[:, 1:-1], extended[:, :-2], extended[:, 2:], courant, diffusivity, adjoint
            )
            margin = STEPS - sweep_index - 1
            history.append(extended[:, margin : margin + cells_x])
        return history

    def project(field_in):
        tile_view = field_in.reshape(probe_count, tile_total, TILE)
        picked = jnp.take(tile_view, index_row, axis=1)
        return jnp.sum(picked * panel_full, axis=2)

    adjoint_fields = run_phase(initial, True)
    totals = [lax.psum(project(field_in), "state") for field_in in adjoint_fields]
    projections = jnp.stack(totals)
    drive_input = projections[STEPS - 1]
    contrib = drive_input[:, :, None] * panel_full[None]
    deposit = jnp.zeros((probe_count, tile_total, TILE), jnp.float32).at[:, index_row].add(contrib)
    forced = deposit.reshape((probe_count,) + slab_shape)
    response = run_phase(forced, False)[-1]
    return (projections, response)


def solution(mesh):
    return jax.shard_map(
        local,
        mesh=mesh,
        in_specs=(
            P("probe", "state", None, None),
            P(),
            P(),
            P("probe"),
            P("state", None),
            P("state", "probe", None),
        ),
        out_specs=(P(None, "probe", None), P("probe", "state", None, None)),
        check_vma=False,
    )
```

profile of v0, /device:TPU:0, one launch (start us, length us, event | category | flops | bytes accessed | tf_op | source)
XLA Modules:
  0.0 200.4 jit_solution(7591030542417106336)
XLA Ops:
  7.2 0.0 all-gather.2.cloned.1.call-start
  7.9 1.5 fusion.44
  9.4 0.5 collective-permute-start
  9.9 2.9 %collective-permute-start.1 = (f32[1,4,64,512]{3,2,1,0:T(8,128)S(1)}, f32[1,4,64,512]{3,2,1,0:T(8,128)S(1)}, u32[]{:S(2)}, u32[]{:S(2)}) collective-permute-start(f32[1,4,64,512]{3,2,1,0:T(8,128)S(1)} %fusion.44), channel_id=1, source_target_pairs={{4,0},{8,4},{12,8},{16,12},{20,16},{24,20},{28,24},{0,28},{5,1},{9... | collective-permute-start | bytes 1572872 | tf_op jit(solution)/shard_map/ppermute | solution.py:19
  12.8 0.0 all-gather.2.cloned.1.call-update
  12.8 0.0 all-reduce.20.cloned.1.call-start
  12.9 0.1 fusion.83
  13.0 0.1 pad_maximum_fusion.2
  13.1 9.5 %collective-permute-done = f32[1,4,64,512]{3,2,1,0:T(8,128)S(1)} collective-permute-done((f32[1,4,64,512]{3,2,1,0:T(8,128)S(1)}, f32[1,4,64,512]{3,2,1,0:T(8,128)S(1)}, u32[]{:S(2)}, u32[]{:S(2)}) %collective-permute-start) | collective-permute-done | bytes 524320 | tf_op jit(solution)/shard_map/ppermute | solution.py:16
  22.6 1.5 collective-permute-done.1
  24.1 0.1 pad_maximum_fusion
  24.2 0.3 fusion.62
  24.5 0.5 fusion.64
  25.0 0.0 copy-start.6
  25.0 0.2 fusion.63
  25.2 0.5 copy-done.6
  25.7 1.1 fusion.16
  26.8 0.2 fusion.68
  27.0 0.4 fusion.70
  27.4 0.1 fusion.69
  27.6 0.9 fusion.28
  28.5 0.2 fusion.74
  28.6 0.1 fusion.75
  28.8 0.3 fusion.76
  29.1 0.4 copy-done.1
  29.4 0.7 fusion.41
  30.1 0.1 fusion.81
  30.2 0.1 fusion.80
  30.3 0.2 fusion.82
  30.5 0.5 fusion.54
  31.2 14.2 %gather_fusion.3 = f32[4096,128]{1,0:T(8,128)} fusion(f32[1024,128]{1,0:T(8,128)S(1)} %reshape.646, s32[4096]{0:T(1024)S(1)} %fusion.58), kind=kCustom, calls=%fused_computation.3.clone | custom fusion | bytes 4210688 | tf_op jit(solution)/shard_map/jit(_take)/gather | solution.py:75
  45.4 14.2 %gather_fusion.2 = f32[4096,128]{1,0:T(8,128)} fusion(f32[1024,128]{1,0:T(8,128)S(1)} %reshape.642, s32[4096]{0:T(1024)S(1)} %fusion.58), kind=kCustom, calls=%fused_computation.2.clone | custom fusion | bytes 4210688 | tf_op jit(solution)/shard_map/jit(_take)/gather | solution.py:75
  59.6 0.0 slice-done.1
  59.6 0.0 slice-start
  59.6 14.2 %gather_fusion.1 = f32[4096,128]{1,0:T(8,128)} fusion(f32[1024,128]{1,0:T(8,128)S(1)} %reshape.638, s32[4096]{0:T(1024)S(1)} %fusion.58), kind=kCustom, calls=%fused_computation.1.clone | custom fusion | bytes 4210688 | tf_op jit(solution)/shard_map/jit(_take)/gather | solution.py:75
  73.9 14.2 %gather_fusion = f32[4096,128]{1,0:T(8,128)} fusion(f32[1024,128]{1,0:T(8,128)S(1)} %reshape.634, s32[4096]{0:T(1024)S(1)} %fusion.58), kind=kCustom, calls=%fused_computation.clone | custom fusion | bytes 4210688 | tf_op jit(solution)/shard_map/jit(_take)/gather | solution.py:75
  88.1 5.7 %fusion = (f32[4096]{0:T(1024)}, f32[4096]{0:T(1024)}, f32[4096]{0:T(1024)}, f32[4096]{0:T(1024)}) fusion(bf16[1,4096,128]{2,1,0:T(8,128)(2,1)} %all-gather.2.cloned.1.call-done, f32[4096,128]{1,0:T(8,128)} %gather_fusion, pred[4096]{0:T(1024)(128)(4,1)S(1)} %compare_and_fusion, f32[4096,128]{1,0:T(8,128)} %gather_fusion.1, f32[4096,128]{1,0:T(8,128)} %gather_fusion.2, ...), kind=kLoop, calls=%fused_computation.10 | loop fusion | flops 6799360 | bytes 9506816 | tf_op jit(solution)/shard_map/reduce_sum | solution.py:76
  93.8 0.0 all-reduce.20.cloned.1.call-update
  93.9 55.3 %all-reduce.20.cloned.1.call-done = (f32[1,4096]{1,0:T(1,128)}, f32[1,1,4096]{2,1,0:T(1,128)}, f32[1,1,4096]{2,1,0:T(1,128)}, f32[1,1,4096]{2,1,0:T(1,128)}) async-done(((f32[1,4096]{1,0:T(1,128)}, f32[1,1,4096]{2,1,0:T(1,128)}, f32[1,1,4096]{2,1,0:T(1,128)}, f32[1,1,4096]{2,1,0:T(1,128)}), (f32[1,4096]{1,0:T(1,128)}, f32[1,1,4096]{2,1,0:T(1,128)}, f32[1,1,4096]{2,1,0:T(1,128)}, ...) | async-done | bytes 65552 | tf_op jit(solution)/shard_map/psum | solution.py:79
  149.2 22.6 %scatter_custom_fusion = f32[1024,128]{1,0:T(8,128)S(1)} fusion(s32[4096]{0:T(1024)S(1)} %bitcast.46, bf16[1,4096,128]{2,1,0:T(8,128)(2,1)} %all-gather.2.cloned.1.call-done, f32[4096]{0:T(1024)} %bitcast.44, f32[]{:T(128)} %constant.22.clone.1), kind=kCustom, calls=%fused_computation.15 | custom fusion | flops 1572864 | bytes 1589252 | tf_op jit(solution)/shard_map/scatter-add | solution.py:83
  171.8 0.1 reshape.546
  171.9 0.1 collective-permute-start.2
  172.0 2.6 %collective-permute-start.3 = (f32[1,4,64,512]{3,2,1,0:T(8,128)S(1)}, f32[1,4,64,512]{3,2,1,0:T(8,128)S(1)}, u32[]{:S(2)}, u32[]{:S(2)}) collective-permute-start(f32[1,4,64,512]{3,2,1,0:T(8,128)S(1)} %reshape.546), channel_id=1, source_target_pairs={{4,0},{8,4},{12,8},{16,12},{20,16},{24,20},{28,24},{0,28},{5,1},{9... | collective-permute-start | bytes 1572872 | tf_op jit(solution)/shard_map/ppermute | solution.py:19
  174.6 0.0 copy-done.4
  174.6 0.0 copy-done.8
  174.6 0.7 pad_maximum_fusion.1
  175.3 11.6 %collective-permute-done.2 = f32[1,4,64,512]{3,2,1,0:T(8,128)S(1)} collective-permute-done((f32[1,4,64,512]{3,2,1,0:T(8,128)S(1)}, f32[1,4,64,512]{3,2,1,0:T(8,128)S(1)}, u32[]{:S(2)}, u32[]{:S(2)}) %collective-permute-start.2) | collective-permute-done | bytes 524320 | tf_op jit(solution)/shard_map/ppermute | solution.py:16
  187.0 0.0 collective-permute-done.3
  187.0 0.3 fusion.59
  187.3 0.5 fusion.61
  187.8 0.2 fusion.60
  188.0 1.0 fusion.11
  189.0 0.2 fusion.65
  189.3 0.4 fusion.67
  189.6 0.1 fusion.66
  189.8 0.8 fusion.23
  190.6 0.2 fusion.71
  190.8 0.3 fusion.73
  191.1 0.1 fusion.72
  191.2 0.7 fusion.36
  191.9 0.1 fusion.77
  192.0 0.2 fusion.79
  192.2 0.1 fusion.78
  192.3 1.3 fusion.49
  (29 shorter events, 0.3 us)
Async XLA Ops:
  7.2 5.7 %copy-start.5 = (f32[64]{0:T(128)S(1)}, f32[64]{0:T(128)}, u32[]{:S(2)}) copy-start(f32[64]{0:T(128)} %param.10) | copy-start | bytes 772
  7.2 5.9 %copy-start.3 = (s32[1,4096]{1,0:T(1,128)S(1)}, s32[1,4096]{1,0:T(1,128)}, u32[]{:S(2)}) copy-start(s32[1,4096]{1,0:T(1,128)} %param.12) | copy-start | bytes 49156
  7.2 80.9 %all-gather.2.cloned.1.call-start = ((), (), s32[]{:S(2)}) async-start(), calls=%async_computation | async-start | bytes 1310720 | tf_op jit(solution)/shard_map/all_gather | solution.py:54
  9.4 13.2 %collective-permute-start = (f32[1,4,64,512]{3,2,1,0:T(8,128)S(1)}, f32[1,4,64,512]{3,2,1,0:T(8,128)S(1)}, u32[]{:S(2)}, u32[]{:S(2)}) collective-permute-start(f32[1,4,64,512]{3,2,1,0:T(8,128)S(1)} %fusion.44), channel_id=1, source_target_pairs={{0,4},{4,8},{8,12},{12,16},{16,20},{20,24},{24,28},{28,0},{1,5},{5... | collective-permute-start | bytes 1572872 | tf_op jit(solution)/shard_map/ppermute | solution.py:16
  9.9 14.2 %collective-permute-start.1 = (f32[1,4,64,512]{3,2,1,0:T(8,128)S(1)}, f32[1,4,64,512]{3,2,1,0:T(8,128)S(1)}, u32[]{:S(2)}, u32[]{:S(2)}) collective-permute-start(f32[1,4,64,512]{3,2,1,0:T(8,128)S(1)} %fusion.44), channel_id=1, source_target_pairs={{4,0},{8,4},{12,8},{16,12},{20,16},{24,20},{28,24},{0,28},{5,1},{9... | collective-permute-start | bytes 1572872 | tf_op jit(solution)/shard_map/ppermute | solution.py:19
  12.8 136.4 %all-reduce.20.cloned.1.call-start = ((), (), s32[]{:S(2)}) async-start(), calls=%async_computation.1 | async-start | bytes 131072 | tf_op jit(solution)/shard_map/psum | solution.py:79
  25.0 0.7 copy-start.6
  26.8 2.0 copy-start
  28.4 1.0 copy-start.1
  45.4 14.2 %slice-start.1 = ((f32[1,8,64,512]{3,2,1,0:T(8,128)}), f32[1,4,64,512]{3,2,1,0:T(8,128)S(1)}, s32[]{:S(2)}) async-start(f32[1,8,64,512]{3,2,1,0:T(8,128)} %copy-done.1), calls=%async_computation.3 | async-start | bytes 1048576 | tf_op jit(solution)/shard_map/slice | solution.py:70
  59.6 14.2 %slice-start = ((f32[1,10,64,512]{3,2,1,0:T(8,128)}), f32[1,4,64,512]{3,2,1,0:T(8,128)S(1)}, s32[]{:S(2)}) async-start(f32[1,10,64,512]{3,2,1,0:T(8,128)} %copy-done), calls=%async_computation.2 | async-start | bytes 1048576 | tf_op jit(solution)/shard_map/slice | solution.py:70
  73.9 14.2 %copy-start.2 = (f32[4096,128]{1,0:T(8,128)S(1)}, f32[4096,128]{1,0:T(8,128)}, u32[]{:S(2)}) copy-start(f32[4096,128]{1,0:T(8,128)} %gather_fusion.3) | copy-start | bytes 6291460
  149.2 25.4 %copy-start.4 = (f32[1,4096]{1,0:T(1,128)S(1)}, f32[1,4096]{1,0:T(1,128)}, u32[]{:S(2)}) copy-start(f32[1,4096]{1,0:T(1,128)} %get-tuple-element.18) | copy-start | bytes 49156
  149.2 25.4 %copy-start.7 = (f32[1,1,4096]{2,1,0:T(1,128)S(1)}, f32[1,1,4096]{2,1,0:T(1,128)}, u32[]{:S(2)}) copy-start(f32[1,1,4096]{2,1,0:T(1,128)} %get-tuple-element.19) | copy-start | bytes 49156
  149.2 25.4 %copy-start.8 = (f32[1,1,4096]{2,1,0:T(1,128)S(1)}, f32[1,1,4096]{2,1,0:T(1,128)}, u32[]{:S(2)}) copy-start(f32[1,1,4096]{2,1,0:T(1,128)} %get-tuple-element.20) | copy-start | bytes 49156
  149.2 25.4 %copy-start.9 = (f32[1,1,4096]{2,1,0:T(1,128)S(1)}, f32[1,1,4096]{2,1,0:T(1,128)}, u32[]{:S(2)}) copy-start(f32[1,1,4096]{2,1,0:T(1,128)} %get-tuple-element.21) | copy-start | bytes 49156
  171.9 15.0 %collective-permute-start.2 = (f32[1,4,64,512]{3,2,1,0:T(8,128)S(1)}, f32[1,4,64,512]{3,2,1,0:T(8,128)S(1)}, u32[]{:S(2)}, u32[]{:S(2)}) collective-permute-start(f32[1,4,64,512]{3,2,1,0:T(8,128)S(1)} %reshape.546), channel_id=1, source_target_pairs={{0,4},{4,8},{8,12},{12,16},{16,20},{20,24},{24,28},{28,0},{1,5},{5... | collective-permute-start | bytes 1572872 | tf_op jit(solution)/shard_map/ppermute | solution.py:16
  172.0 15.0 %collective-permute-start.3 = (f32[1,4,64,512]{3,2,1,0:T(8,128)S(1)}, f32[1,4,64,512]{3,2,1,0:T(8,128)S(1)}, u32[]{:S(2)}, u32[]{:S(2)}) collective-permute-start(f32[1,4,64,512]{3,2,1,0:T(8,128)S(1)} %reshape.546), channel_id=1, source_target_pairs={{4,0},{8,4},{12,8},{16,12},{20,16},{24,20},{28,24},{0,28},{5,1},{9... | collective-permute-start | bytes 1572872 | tf_op jit(solution)/shard_map/ppermute | solution.py:19
Sparse Core Ops, SparseCore 0:
  13.0 28.9 all-gather.1
  94.0 55.1 all-reduce.19
where the time goes:
time: 201 us; the launch traced here: 200 us
  waiting for transfers between devices  78 us (39%)
  local copies, waits for them, and re-layouts  63.4 us (32%)
  other arithmetic  37.7 us (19%)
  between operations  15.1 us (8%)
  starting transfers between devices  6.22 us (3%)
    gather x4, local copies, waits for them, and re-layouts, project(): picked = jnp.take(tile_view, index_row, axis=1)  56.8 us
    psum x1, waiting for transfers between devices, local(): lax.psum(project(field_in), 'state')  55.3 us
    scatter-add x1, other arithmetic, local(): jnp.zeros((probe_count, tile_total, TILE), jnp.float32).at[:, index_row]  22.6 us
    ppermute x2, waiting for transfers between devices, padded(): lax.ppermute(lax.slice_in_dim(block, block.shape[dim] - width, None, axis...  21.1 us
    add x8, other arithmetic, advance(): center + advect_rate * (upwind - center) + diff_rate * lateral + normal  6.99 us
    reduce_sum x1, other arithmetic, project(): return jnp.sum(picked * panel_full, axis=2)  5.74 us
    ppermute x2, starting transfers between devices, padded(): lax.ppermute(lax.slice_in_dim(block, 0, width, axis=dim), axis, backward)  5.58 us
  transfers between devices with their start and end apart: 6, of which 4 were waited for; matrix products, arithmetic and copies ran while one was open for 32% of the time, Pallas kernels for 0%

commit v1 on v0

v1 whole, which is shorter than its diff:
```python
import jax
import jax.numpy as jnp
from jax import lax
from jax.experimental import pallas as pl
from jax.experimental.pallas import tpu as pltpu
from jax.sharding import PartitionSpec as P

TILE = 128
STEPS = 4
PAD = 8
GROUP = 256
VMEM_LIMIT = 48 * 1024 * 1024


def shift_pairs(count, by):
    return [(i, (i + by) % count) for i in range(count)]


def coefficients(courant, diffusivity):
    zero = jnp.zeros((1,), diffusivity.dtype)
    rows = jnp.stack(
        [
            1.0 - courant - 6.0 * diffusivity,
            courant + diffusivity,
            diffusivity,
            jnp.concatenate([diffusivity[1:], zero]),
            jnp.concatenate([zero, diffusivity[:-1]]),
        ]
    )
    return jnp.broadcast_to(rows[:, :, None], rows.shape + (TILE,))


def clear_pads(buffer):
    planes, columns, rows, lanes = buffer.shape
    edge = jnp.zeros((columns, PAD, lanes), buffer.dtype)

    def body(plane, carry):
        buffer[plane, :, :PAD, :] = edge
        buffer[plane, :, rows - PAD :, :] = edge
        return carry

    lax.fori_loop(0, planes, body, 0)


def stencil_block(source, coef, plane, row, height, adjoint):
    centre = source[plane, :, pl.ds(PAD + row, height), :]
    above = source[plane, :, pl.ds(PAD + row + 1, height), :]
    below = source[plane, :, pl.ds(PAD + row - 1, height), :]
    upper_x = source[plane + 1, :, pl.ds(PAD + row, height), :]
    lower_x = source[plane - 1, :, pl.ds(PAD + row, height), :]
    columns = centre.shape[0]
    lane = lax.broadcasted_iota(jnp.int32, (height, TILE), 1)
    left = [pltpu.roll(centre[c], TILE - 1, 1) for c in range(columns)]
    right = [pltpu.roll(centre[c], 1, 1) for c in range(columns)]
    block = pl.ds(row, height)
    w_centre, w_up, w_diff = coef[0, block, :], coef[1, block, :], coef[2, block, :]
    out = []
    for c in range(columns):
        upper_z = jnp.where(lane == TILE - 1, left[(c + 1) % columns], left[c])
        lower_z = jnp.where(lane == 0, right[(c - 1) % columns], right[c])
        if adjoint:
            total = w_centre * centre[c] + w_up * upper_x[c]
            total = total + w_diff * (lower_x[c] + (upper_z + lower_z))
            total = total + coef[3, block, :] * above[c] + coef[4, block, :] * below[c]
        else:
            total = w_centre * centre[c] + w_up * lower_x[c]
            total = total + w_diff * ((upper_x[c] + (upper_z + lower_z)) + (above[c] + below[c]))
        out.append(total)
    return out


def split(value):
    high = value.astype(jnp.bfloat16)
    low = (value - high.astype(jnp.float32)).astype(jnp.bfloat16)
    return high, low


def adjoint_kernel(offset, coef, own, low, high, tiles, first, second):
    cells, height, width = own.shape
    columns = width // TILE
    steps = tiles.shape[0]
    clear_pads(first)
    clear_pads(second)
    turn = offset[0] // TILE
    rest = offset[0] % TILE
    lane = lax.broadcasted_iota(jnp.int32, (height, TILE), 1)
    for slab, field in enumerate((low, own, high)):

        def load(plane, carry, slab=slab, field=field):
            rolled = [
                pltpu.roll(field[plane, :, pl.ds(c * TILE, TILE)], rest, 1) for c in range(columns)
            ]
            for c in range(columns):
                value = jnp.where(lane >= rest, rolled[c], rolled[c - 1])
                first[slab * cells + plane, lax.rem(c + turn, columns), pl.ds(PAD, height), :] = value
            return carry

        lax.fori_loop(0, cells, load, 0)
    buffers = (first, second)
    rows = 16
    for step in range(steps):
        source, target = buffers[step % 2], buffers[(step + 1) % 2]

        def outer(plane, carry, source=source, target=target):
            for row in range(0, height, rows):
                block = stencil_block(source, coef, plane, row, rows, True)
                for c in range(columns):
                    target[plane, c, pl.ds(PAD + row, rows), :] = block[c]
            return carry

        def inner(plane, carry, source=source, target=target, step=step):
            for row in range(0, height, rows):
                block = stencil_block(source, coef, plane, row, rows, True)
                for c in range(columns):
                    target[plane, c, pl.ds(PAD + row, rows), :] = block[c]
                    start = (plane - cells) * columns * height + c * height + row
                    where = pl.ds(pl.multiple_of(start, rows), rows)
                    head, tail = split(block[c])
                    tiles[step, where, pl.ds(0, TILE)] = head
                    tiles[step, where, pl.ds(TILE, TILE)] = tail
            return carry

        lax.fori_loop(step + 1, cells, outer, 0)
        lax.fori_loop(cells, 2 * cells, inner, 0)
        lax.fori_loop(2 * cells, 3 * cells - step - 1, outer, 0)


def forward_kernel(coef, own, low, high, out, first, second):
    cells, height, width = out.shape
    columns = width // TILE
    steps = STEPS
    clear_pads(first)
    clear_pads(second)
    for plane in range(cells):
        for c in range(columns):
            where = pl.ds(c * height, height)
            inside = pl.ds(PAD, height)
            first[cells + plane, c, inside, :] = own[plane, where, :]
            first[2 * cells + plane, c, inside, :] = high[plane, where, :].astype(jnp.float32)
            value = low[plane, where, :].astype(jnp.float32)
            if plane > 0:
                value = value + low[cells + plane - 1, where, :].astype(jnp.float32)
            first[plane, c, inside, :] = value
    buffers = (first, second)
    rows = 16
    for step in range(steps):
        source, target = buffers[step % 2], buffers[(step + 1) % 2]
        last = step == steps - 1

        def body(plane, carry, source=source, target=target, last=last):
            for row in range(0, height, rows):
                block = stencil_block(source, coef, plane, row, rows, False)
                for c in range(columns):
                    if last:
                        out[plane - cells, pl.ds(row, rows), pl.ds(c * TILE, TILE)] = block[c]
                    else:
                        target[plane, c, pl.ds(PAD + row, rows), :] = block[c]
            return carry

        lax.fori_loop(step + 1, 3 * cells - step - 1, body, 0)


def project_kernel(index, panel, tiles, out):
    groups = index.shape[0]
    steps, total = tiles.shape[0], tiles.shape[1]
    chunk = 256

    def body(group, carry):
        rows = panel[pl.ds(pl.multiple_of(group * GROUP, GROUP), GROUP), :]
        doubled = jnp.concatenate([rows, rows], axis=1)
        wanted = index[group]
        for step in range(steps):
            partial = jnp.zeros((8, GROUP), jnp.float32)
            for start in range(0, total, chunk):
                gram = lax.dot_general(
                    tiles[step, pl.ds(start, chunk), :],
                    doubled,
                    (((1,), (1,)), ((), ())),
                    preferred_element_type=jnp.float32,
                )
                number = lax.broadcasted_iota(jnp.int32, (chunk, GROUP), 0) + start
                kept = jnp.where(number == wanted, gram, 0.0)
                partial = partial + jnp.sum(kept.reshape(chunk // 8, 8, GROUP), axis=0)
            out[step, group] = jnp.sum(partial, axis=0, keepdims=True)
        return carry

    lax.fori_loop(0, groups, body, 0)


def deposit_kernel(count, index, panel, *refs):
    parts, (total, field, rightward, leftward, scaled) = refs[:count], refs[count:]
    groups = index.shape[0]
    cells, per_plane = field.shape[0], field.shape[1]
    values = [part[...] for part in parts]
    while len(values) > 1:
        values = [values[i] + values[i + 1] for i in range(0, len(values), 2)]
    total[...] = values[0]
    drive = values[0].reshape(groups, GROUP).T
    for group in range(groups):
        where = pl.ds(group * GROUP, GROUP)
        product = drive[:, group : group + 1] * panel[where, :].astype(jnp.float32)
        head, tail = split(product)
        scaled[where, pl.ds(0, TILE)] = head
        scaled[where, pl.ds(TILE, TILE)] = tail

    def body(plane, carry):
        number = lax.broadcasted_iota(jnp.int32, (per_plane, GROUP), 0) + plane * per_plane
        sums = jnp.zeros((per_plane, 2 * TILE), jnp.float32)
        for group in range(groups):
            chosen = jnp.where(number == index[group], 1.0, 0.0).astype(jnp.bfloat16)
            sums = sums + lax.dot_general(
                chosen,
                scaled[pl.ds(group * GROUP, GROUP), :],
                (((1,), (0,)), ((), ())),
                preferred_element_type=jnp.float32,
            )
        value = sums[:, :TILE] + sums[:, TILE:]
        field[plane] = value
        head, tail = split(value)
        leftward[plane] = head
        rightward[plane] = head

        @pl.when(plane > 0)
        def _():
            rightward[cells + plane - 1] = tail

        return carry

    lax.fori_loop(0, cells, body, 0)


def call(kernel, out_shape, scratch=(), smem=0, inputs=0, flops=0):
    in_specs = [pl.BlockSpec(memory_space=pltpu.SMEM)] * smem
    in_specs += [pl.BlockSpec(memory_space=pltpu.VMEM)] * (inputs - smem)
    out_specs = jax.tree.map(lambda _: pl.BlockSpec(memory_space=pltpu.VMEM), out_shape)
    return pl.pallas_call(
        kernel,
        out_shape=out_shape,
        in_specs=in_specs,
        out_specs=out_specs,
        scratch_shapes=list(scratch),
        compiler_params=pltpu.CompilerParams(vmem_limit_bytes=VMEM_LIMIT),
        cost_estimate=pl.CostEstimate(flops=flops, bytes_accessed=4 * 1024 * 1024, transcendentals=0),
    )


def gathered_panel(panel, axis):
    count = lax.axis_size(axis)
    if count == 1:
        return panel
    place = lax.axis_index(axis)
    up = [(i, i + 1) for i in range(count - 1)]
    down = [(i + 1, i) for i in range(count - 1)]
    from_below, from_above = [panel], [panel]
    for stage in range(1, count):
        from_below.append(lax.ppermute(from_below[-1], axis, up[stage - 1 :]))
        from_above.append(lax.ppermute(from_above[-1], axis, down[: count - stage]))
    pieces = [panel]
    for shift in range(1, count):
        pieces.append(jnp.where(place >= shift, from_below[shift], from_above[count - shift]))
    return jnp.concatenate(pieces, axis=0)


def summands(part, axis):
    count = lax.axis_size(axis)
    if count & (count - 1):
        return [lax.psum(part, axis)]
    done = 1
    while True:
        span = min(8, count // done)
        parts = [part]
        for mask in range(1, span):
            parts.append(lax.ppermute(part, axis, [(i, i ^ (mask * done)) for i in range(count)]))
        done *= span
        if done == count:
            return parts
        part = tree_sum(parts)


def tree_sum(parts):
    while len(parts) > 1:
        parts = [parts[i] + parts[i + 1] for i in range(0, len(parts), 2)]
    return parts[0]


def doubling_sum(part, axis):
    count = lax.axis_size(axis)
    if count & (count - 1):
        return lax.psum(part, axis)
    mask = 1
    while mask < count:
        part = part + lax.ppermute(part, axis, [(i, i ^ mask) for i in range(count)])
        mask *= 2
    return part


def local(sensor_field, courant, diffusivity, probe_offset, tile_index, actuator_panel):
    slabs, probes = lax.axis_size("state"), lax.axis_size("probe")
    place = lax.axis_index("probe")
    own = sensor_field[0]
    cells, height, width = own.shape
    columns = width // TILE
    tile_total = cells * height * columns
    actuators = tile_index.shape[1]
    groups = actuators // GROUP
    planes = 3 * cells
    f32, bf16 = jnp.float32, jnp.bfloat16

    low = lax.ppermute(own, "state", shift_pairs(slabs, 1))
    high = lax.ppermute(own, "state", shift_pairs(slabs, -1))
    panel = gathered_panel(actuator_panel[0], "probe")

    coef = coefficients(courant, diffusivity)
    order = lax.rem(place - jnp.arange(probes, dtype=jnp.int32) + probes, probes)
    tile = jnp.take(tile_index[0].reshape(probes, -1), order, axis=0)
    plane, inside = tile // (height * columns), tile % (height * columns)
    index = plane * (height * columns) + (inside % columns) * height + inside // columns
    index = index.reshape(groups, 1, GROUP)

    field_shape = pltpu.VMEM((planes, columns, height + 2 * PAD, TILE), f32)
    tiles = call(
        adjoint_kernel,
        jax.ShapeDtypeStruct((STEPS, tile_total, 2 * TILE), bf16),
        scratch=(field_shape, field_shape),
        smem=1,
        inputs=5,
        flops=28 * 16 * height * width,
    )(probe_offset, coef, own, low, high)

    def project(part):
        return call(
            project_kernel,
            jax.ShapeDtypeStruct((part.shape[0], groups, 1, GROUP), f32),
            inputs=3,
            flops=part.shape[0] * 2 * actuators * tile_total * 2 * TILE,
        )(index, panel, part)

    last = project(tiles[STEPS - 1 :])
    early = project(tiles[: STEPS - 1])
    parts = summands(last, "state")
    payload = jax.ShapeDtypeStruct((2 * cells - 1, height * columns, TILE), bf16)
    heads = jax.ShapeDtypeStruct((cells, height * columns, TILE), bf16)
    total, forced, rightward, leftward = call(
        lambda *refs: deposit_kernel(len(parts), *refs),
        (
            jax.ShapeDtypeStruct(last.shape, f32),
            jax.ShapeDtypeStruct((cells, height * columns, TILE), f32),
            payload,
            heads,
        ),
        scratch=(pltpu.VMEM((actuators, 2 * TILE), bf16),),
        inputs=2 + len(parts),
        flops=2 * actuators * tile_total * 2 * TILE,
    )(index, panel, *parts)
    from_low = lax.ppermute(rightward, "state", shift_pairs(slabs, 1))
    from_high = lax.ppermute(leftward, "state", shift_pairs(slabs, -1))
    response = call(
        forward_kernel,
        jax.ShapeDtypeStruct((cells, height, width), f32),
        scratch=(field_shape, field_shape),
        inputs=4,
        flops=28 * 16 * height * width,
    )(coef, forced, from_low, from_high)

    early = doubling_sum(early, "state")
    projections = jnp.concatenate([early, total], axis=0).reshape(STEPS, probes, -1)
    back = lax.rem(place - jnp.arange(probes, dtype=jnp.int32) + probes, probes)
    projections = jnp.take(projections, back, axis=1).reshape(STEPS, 1, actuators)
    return projections, response[None]


def solution(mesh):
    return jax.shard_map(
        local,
        mesh=mesh,
        in_specs=(
            P("probe", "state", None, None),
            P(),
            P(),
            P("probe"),
            P("state", None),
            P("state", "probe", None),
        ),
        out_specs=(P(None, "probe", None), P("probe", "state", None, None)),
        check_vma=False,
    )
```

time: 201 us -> 84.5 us (0.42)
  waiting for transfers between devices: 78 us -> 18.5 us
  local copies, waits for them, and re-layouts: 63.4 us -> 6.13 us
  other arithmetic: 37.7 us -> 3.02 us
  Pallas kernels: 0 us -> 29.7 us
  starting transfers between devices: 6.22 us -> 25.3 us
  between operations: 15.1 us -> 1.56 us
    gather x4 -> x3, local copies, waits for them, and re-layouts: 56.8 us -> 1.19 us  [the longest x2 0.6 us: local(): tile = jnp.take(tile_index[0].reshape(probes, -1), order, axis=0)]
    psum x1 -> x0, waiting for transfers between devices: 55.3 us -> none  [local(): lax.psum(project(field_in), 'state')]
    pallas_call x0 -> x5, Pallas kernels: none -> 29.7 us  [the longest x2 15.6 us: project(): call(project_kernel, jax.ShapeDtypeStruct((part.shape[0], groups, 1, GROU...]
    scatter-add x1 -> x0, other arithmetic: 22.6 us -> none  [local(): jnp.zeros((probe_count, tile_total, TILE), jnp.float32).at[:, index_row]]
    ppermute x4 -> x20, starting transfers between devices: 6.14 us -> 25.3 us  [the longest x3 6.91 us: gathered_panel(): from_below.append(lax.ppermute(from_below[-1], axis, up[stage - 1:]))]
    add x8 -> x4, other arithmetic: 6.99 us -> 0.48 us  [the longest x1 0.32 us: local(): plane * (height * columns) + inside % columns * height + inside // columns]
    reduce_sum x1 -> x0, other arithmetic: 5.74 us -> none  [project(): return jnp.sum(picked * panel_full, axis=2)]
    slice x29 -> x3, local copies, waits for them, and re-layouts: 5.44 us -> 0.94 us  [the longest x1 0.8 us: coefficients(): diffusivity[:-1]]
  transfers between devices with their start and end apart: 6 -> 20, of which waited for: 4 -> 9; matrix products, arithmetic and copies ran while one was open for 32% -> 9% of each run, Pallas kernels for 0% -> 17%
where the time goes in v1:
time: 84.5 us; the launch traced here: 84.2 us
  Pallas kernels  29.7 us (35%)
  starting transfers between devices  25.3 us (30%)
  waiting for transfers between devices  18.5 us (22%)
  local copies, waits for them, and re-layouts  6.13 us (7%)
  other arithmetic  3.02 us (4%)
  between operations  1.56 us (2%)
    pallas_call x2, Pallas kernels, project(): call(project_kernel, jax.ShapeDtypeStruct((part.shape[0], groups, 1, GROU...  15.6 us
    ppermute x3, waiting for transfers between devices, gathered_panel(): from_above.append(lax.ppermute(from_above[-1], axis, down[:count - stage]))  8.01 us
    ppermute x3, starting transfers between devices, gathered_panel(): from_below.append(lax.ppermute(from_below[-1], axis, up[stage - 1:]))  6.91 us
    ppermute x7, starting transfers between devices, summands(): lax.ppermute(part, axis, [(i, i ^ mask * done) for i in range(count)])  5.91 us
    pallas_call x1, Pallas kernels, local(): call(adjoint_kernel, jax.ShapeDtypeStruct((STEPS, tile_total, 2 * TILE),...  5.46 us
    ppermute x1, waiting for transfers between devices, local(): from_high = lax.ppermute(leftward, 'state', shift_pairs(slabs, -1))  5.1 us
    pallas_call x1, Pallas kernels, local(): call(forward_kernel, jax.ShapeDtypeStruct((cells, height, width), f32), s...  5.01 us
    ppermute x3, starting transfers between devices, gathered_panel(): from_above.append(lax.ppermute(from_above[-1], axis, down[:count - stage]))  3.85 us
  transfers between devices with their start and end apart: 20, of which 9 were waited for; matrix products, arithmetic and copies ran while one was open for 9% of the time, Pallas kernels for 17%

profile of v1, /device:TPU:0, one launch (start us, length us, event | category | flops | bytes accessed | tf_op | source)
XLA Modules:
  0.0 84.2 jit_solution(1914986335130802828)
XLA Ops:
  0.6 1.3 %collective-permute-start.1 = (bf16[1024,128]{1,0:T(8,128)(2,1)}, bf16[1024,128]{1,0:T(8,128)(2,1)S(1)}, u32[]{:S(2)}, u32[]{:S(2)}) collective-permute-start(bf16[1024,128]{1,0:T(8,128)(2,1)} %bitcast.27), channel_id=1, source_target_pairs={{1,0},{2,1},{3,2},{5,4},{6,5},{7,6},{9,8},{10,9},{11,10},{13,12},{... | collective-permute-start | bytes 786440 | tf_op jit(solution)/shard_map/ppermute | solution.py:257
  1.9 5.6 %collective-permute-start = (bf16[1024,128]{1,0:T(8,128)(2,1)}, bf16[1024,128]{1,0:T(8,128)(2,1)S(1)}, u32[]{:S(2)}, u32[]{:S(2)}) collective-permute-start(bf16[1024,128]{1,0:T(8,128)(2,1)} %bitcast.28), channel_id=1, source_target_pairs={{0,1},{1,2},{2,3},{4,5},{5,6},{6,7},{8,9},{9,10},{10,11},{12,13},{... | collective-permute-start | bytes 786440 | tf_op jit(solution)/shard_map/ppermute | solution.py:256
  7.5 0.1 collective-permute-start.6
  7.6 2.6 %collective-permute-start.7 = (f32[4,64,512]{2,1,0:T(8,128)}, f32[4,64,512]{2,1,0:T(8,128)S(1)}, u32[]{:S(2)}, u32[]{:S(2)}) collective-permute-start(f32[4,64,512]{2,1,0:T(8,128)} %bitcast.23), channel_id=1, source_target_pairs={{0,28},{4,0},{8,4},{12,8},{16,12},{20,16},{24,20},{28,24},{1,29},{... | collective-permute-start | bytes 1572872 | tf_op jit(solution)/shard_map/ppermute | solution.py:310
  10.2 0.5 broadcast.317
  10.8 1.4 %reduce.5 = s32[4096]{0:T(1024)S(1)} reduce(s32[1,4096]{1,0:T(1,128)} %param.10, s32[]{:T(128)} %broadcast.317), dimensions={0}, to_apply=%param.10.reduce_sub_computation.3 | reduce | bytes 32772 | tf_op args[4]
  12.2 0.6 gather_fusion
  12.8 0.1 broadcast_in_dim.40
  12.9 0.1 broadcast_in_dim.41
  12.9 0.3 fusion.2.index.refs_0_
  13.3 0.1 collective-permute-done
  13.4 0.7 collective-permute-start.4
  14.0 0.7 add_bitcast_fusion
  14.7 0.0 collective-permute-done.1
  14.7 1.3 %collective-permute-start.2 = (bf16[1024,128]{1,0:T(8,128)(2,1)S(1)}, bf16[1024,128]{1,0:T(8,128)(2,1)S(1)}, u32[]{:S(2)}, u32[]{:S(2)}) collective-permute-start(bf16[1024,128]{1,0:T(8,128)(2,1)S(1)} %collective-permute-done.1), channel_id=1, source_target_pairs={{1,0},{2,1},{5,4},{6,5},{9,8},{10,9},{13,12},{14,13},{17,16},{18,1... | collective-permute-start | bytes 786440 | tf_op jit(solution)/shard_map/ppermute | solution.py:257
  16.0 0.8 fusion.6
  16.8 0.0 collective-permute-done.4
  16.8 0.7 collective-permute-start.5
  17.5 0.1 maximum_bitcast_fusion
  18.2 0.7 stack.23
  18.9 7.9 %collective-permute-done.2 = bf16[1024,128]{1,0:T(8,128)(2,1)S(1)} collective-permute-done((bf16[1024,128]{1,0:T(8,128)(2,1)S(1)}, bf16[1024,128]{1,0:T(8,128)(2,1)S(1)}, u32[]{:S(2)}, u32[]{:S(2)}) %collective-permute-start.2) | collective-permute-done | bytes 262176 | tf_op jit(solution)/shard_map/ppermute | solution.py:257
  26.8 1.3 %collective-permute-start.3 = (bf16[1024,128]{1,0:T(8,128)(2,1)S(1)}, bf16[1024,128]{1,0:T(8,128)(2,1)S(1)}, u32[]{:S(2)}, u32[]{:S(2)}) collective-permute-start(bf16[1024,128]{1,0:T(8,128)(2,1)S(1)} %collective-permute-done.2), channel_id=1, source_target_pairs={{1,0},{5,4},{9,8},{13,12},{17,16},{21,20},{25,24},{29,28}} | collective-permute-start | bytes 786440 | tf_op jit(solution)/shard_map/ppermute | solution.py:257
  28.1 0.0 collective-permute-done.6.low
  28.1 0.0 collective-permute-done.7.high
  28.1 0.1 broadcast_in_dim.44.coef
  28.2 0.0 copy-start
  28.3 1.0 %copy-done = f32[1,4,64,512]{3,2,1,0:T(8,128)S(1)} copy-done((f32[1,4,64,512]{3,2,1,0:T(8,128)S(1)}, f32[1,4,64,512]{3,2,1,0:T(8,128)}, u32[]{:S(2)}) %copy-start) | copy-done | bytes 524312
  29.3 5.5 %shard_map.77 = bf16[4,1024,256]{2,1,0:T(8,128)(2,1)S(1)} custom-call(s32[1]{0:T(128)S(6)} %copy.14.offset, f32[5,64,128]{2,1,0:T(8,128)S(1)} %broadcast_in_dim.44.coef, f32[4,64,512]{2,1,0:T(8,128)S(1)} %bitcast.24, f32[4,64,512]{2,1,0:T(8,128)S(1)} %collective-permute-done.6.low, f32[4,64,512]{2,1,0:T(8,128)S(1)} %collective-permute-done.7.high), custom_call_target="tpu_custom_call" | custom-call | flops 14680064 | bytes 4194304 | tf_op jit(solution)/shard_map/pallas_call | solution.py:321
  34.8 0.0 copy-start.1
  34.8 0.1 slice.20.tiles
  34.9 0.0 collective-permute-done.5
  34.9 0.1 collective-permute-done.3
  35.1 0.6 copy-done.1
  35.7 0.1 pad_maximum_fusion.panel.refs_1_
  35.8 10.1 %shard_map.78 = f32[3,16,1,256]{3,2,1,0:T(1,128)S(1)} custom-call(s32[16,1,256]{2,1,0:T(1,128)S(1)} %fusion.2.index.refs_0_, bf16[4096,128]{1,0:T(8,128)(2,1)S(1)} %pad_maximum_fusion.panel.refs_1_, bf16[3,1024,256]{2,1,0:T(8,128)(2,1)S(1)} %slice.20.tiles), custom_call_target="tpu_custom_call" | custom-call | flops 6442450944 | bytes 4194304 | tf_op jit(solution)/shard_map/pallas_call | solution.py:331
  45.9 0.1 collective-permute-start.8
  46.0 1.2 %collective-permute-done.8 = f32[3,16,1,256]{3,2,1,0:T(1,128)S(1)} collective-permute-done((f32[3,16,1,256]{3,2,1,0:T(1,128)S(1)}, f32[3,16,1,256]{3,2,1,0:T(1,128)S(1)}, u32[]{:S(2)}, u32[]{:S(2)}) %collective-permute-start.8) | collective-permute-done | bytes 49184 | tf_op jit(solution)/shard_map/ppermute | solution.py:292
  47.2 0.1 add.113
  47.3 1.6 %collective-permute-start.9 = (f32[3,16,1,256]{3,2,1,0:T(1,128)S(1)}, f32[3,16,1,256]{3,2,1,0:T(1,128)S(1)}, u32[]{:S(2)}, u32[]{:S(2)}) collective-permute-start(f32[3,16,1,256]{3,2,1,0:T(1,128)S(1)} %add.113), channel_id=1, source_target_pairs={{0,8},{4,12},{8,0},{12,4},{16,24},{20,28},{24,16},{28,20},{1,9},{5... | collective-permute-start | bytes 147464 | tf_op jit(solution)/shard_map/ppermute | solution.py:292
  48.8 5.5 %shard_map.79.refs_2_ = f32[1,16,1,256]{3,2,1,0:T(1,128)S(1)} custom-call(s32[16,1,256]{2,1,0:T(1,128)S(1)} %fusion.2.index.refs_0_, bf16[4096,128]{1,0:T(8,128)(2,1)S(1)} %pad_maximum_fusion.panel.refs_1_, bf16[1,1024,256]{2,1,0:T(8,128)(2,1)S(1)} %slice.21.tiles), custom_call_target="tpu_custom_call" | custom-call | flops 2147483648 | bytes 4194304 | tf_op jit(solution)/shard_map/pallas_call | solution.py:331
  54.3 0.1 collective-permute-start.11
  54.4 0.6 collective-permute-start.12
  55.1 1.2 %collective-permute-start.13 = (f32[1,16,1,256]{3,2,1,0:T(1,128)S(1)}, f32[1,16,1,256]{3,2,1,0:T(1,128)S(1)}, u32[]{:S(2)}, u32[]{:S(2)}) collective-permute-start(f32[1,16,1,256]{3,2,1,0:T(1,128)S(1)} %shard_map.79.refs_2_), channel_id=1, source_target_pairs={{0,12},{4,8},{8,4},{12,0},{16,28},{20,24},{24,20},{28,16},{1,13},{... | collective-permute-start | bytes 49160 | tf_op jit(solution)/shard_map/ppermute | solution.py:273
  56.3 1.5 %collective-permute-start.14 = (f32[1,16,1,256]{3,2,1,0:T(1,128)S(1)}, f32[1,16,1,256]{3,2,1,0:T(1,128)S(1)}, u32[]{:S(2)}, u32[]{:S(2)}) collective-permute-start(f32[1,16,1,256]{3,2,1,0:T(1,128)S(1)} %shard_map.79.refs_2_), channel_id=1, source_target_pairs={{0,16},{4,20},{8,24},{12,28},{16,0},{20,4},{24,8},{28,12},{1,17},{... | collective-permute-start | bytes 49160 | tf_op jit(solution)/shard_map/ppermute | solution.py:273
  57.8 0.0 collective-permute-done.11.refs_3_
  57.8 0.2 collective-permute-start.15
  58.0 0.4 collective-permute-done.12.refs_4_
  58.4 1.4 %collective-permute-start.16 = (f32[1,16,1,256]{3,2,1,0:T(1,128)S(1)}, f32[1,16,1,256]{3,2,1,0:T(1,128)S(1)}, u32[]{:S(2)}, u32[]{:S(2)}) collective-permute-start(f32[1,16,1,256]{3,2,1,0:T(1,128)S(1)} %shard_map.79.refs_2_), channel_id=1, source_target_pairs={{0,24},{4,28},{8,16},{12,20},{16,8},{20,12},{24,0},{28,4},{1,25},{... | collective-permute-start | bytes 49160 | tf_op jit(solution)/shard_map/ppermute | solution.py:273
  59.8 0.9 %collective-permute-start.17 = (f32[1,16,1,256]{3,2,1,0:T(1,128)S(1)}, f32[1,16,1,256]{3,2,1,0:T(1,128)S(1)}, u32[]{:S(2)}, u32[]{:S(2)}) collective-permute-start(f32[1,16,1,256]{3,2,1,0:T(1,128)S(1)} %shard_map.79.refs_2_), channel_id=1, source_target_pairs={{0,28},{4,24},{8,20},{12,16},{16,12},{20,8},{24,4},{28,0},{1,29},{... | collective-permute-start | bytes 49160 | tf_op jit(solution)/shard_map/ppermute | solution.py:273
  60.7 0.1 broadcast_bitcast_fusion
  60.8 0.1 add.114
  60.8 1.6 %collective-permute-start.10 = (f32[3,16,1,256]{3,2,1,0:T(1,128)S(1)}, f32[3,16,1,256]{3,2,1,0:T(1,128)S(1)}, u32[]{:S(2)}, u32[]{:S(2)}) collective-permute-start(f32[3,16,1,256]{3,2,1,0:T(1,128)S(1)} %add.114), channel_id=1, source_target_pairs={{0,16},{4,20},{8,24},{12,28},{16,0},{20,4},{24,8},{28,12},{1,17},{... | collective-permute-start | bytes 147464 | tf_op jit(solution)/shard_map/ppermute | solution.py:292
  62.4 0.6 collective-permute-done.16.refs_8_
  63.0 0.8 %collective-permute-done.17.refs_9_ = f32[1,16,1,256]{3,2,1,0:T(1,128)S(1)} collective-permute-done((f32[1,16,1,256]{3,2,1,0:T(1,128)S(1)}, f32[1,16,1,256]{3,2,1,0:T(1,128)S(1)}, u32[]{:S(2)}, u32[]{:S(2)}) %collective-permute-start.17) | collective-permute-done | bytes 16416 | tf_op jit(solution)/shard_map/ppermute | solution.py:273
  63.9 3.6 %shard_map.80 = (f32[1,16,1,256]{3,2,1,0:T(1,128)S(1)}, f32[4,256,128]{2,1,0:T(8,128)S(1)}, bf16[7,256,128]{2,1,0:T(8,128)(2,1)S(1)}, bf16[4,256,128]{2,1,0:T(8,128)(2,1)S(1)}) custom-call(s32[16,1,256]{2,1,0:T(1,128)S(1)} %fusion.2.index.refs_0_, bf16[4096,128]{1,0:T(8,128)(2,1)S(1)} %pad_maximum_fusion.panel.refs_1_, ...), custom_call_target="tpu_custom_call" | custom-call | flops 2147483648 | bytes 4194304 | tf_op jit(solution)/shard_map/pallas_call | solution.py:343
  67.5 0.2 collective-permute-start.18
  67.7 2.5 %collective-permute-start.19 = (bf16[4,256,128]{2,1,0:T(8,128)(2,1)S(1)}, bf16[4,256,128]{2,1,0:T(8,128)(2,1)S(1)}, u32[]{:S(2)}, u32[]{:S(2)}) collective-permute-start(bf16[4,256,128]{2,1,0:T(8,128)(2,1)S(1)} %get-tuple-element.9), channel_id=1, source_target_pairs={{0,28},{4,0},{8,4},{12,8},{16,12},{20,16},{24,20},{28,24},{1,29},{... | collective-permute-start | bytes 786440 | tf_op jit(solution)/shard_map/ppermute | solution.py:356
  70.2 0.1 add.115
  70.2 0.2 maximum_reduce_fusion
  70.5 0.6 gather_fusion.1
  71.1 0.7 copy.10
  71.8 5.1 %collective-permute-done.19.high = bf16[4,256,128]{2,1,0:T(8,128)(2,1)S(1)} collective-permute-done((bf16[4,256,128]{2,1,0:T(8,128)(2,1)S(1)}, bf16[4,256,128]{2,1,0:T(8,128)(2,1)S(1)}, u32[]{:S(2)}, u32[]{:S(2)}) %collective-permute-start.19) | collective-permute-done | bytes 262176 | tf_op jit(solution)/shard_map/ppermute | solution.py:356
  76.9 2.2 %collective-permute-done.18.low = bf16[7,256,128]{2,1,0:T(8,128)(2,1)S(1)} collective-permute-done((bf16[7,256,128]{2,1,0:T(8,128)(2,1)S(1)}, bf16[7,256,128]{2,1,0:T(8,128)(2,1)S(1)}, u32[]{:S(2)}, u32[]{:S(2)}) %collective-permute-start.18) | collective-permute-done | bytes 458784 | tf_op jit(solution)/shard_map/ppermute | solution.py:355
  79.2 5.0 %shard_map.81 = f32[4,64,512]{2,1,0:T(8,128)} custom-call(f32[5,64,128]{2,1,0:T(8,128)S(1)} %broadcast_in_dim.44.coef, f32[4,256,128]{2,1,0:T(8,128)S(1)} %get-tuple-element.7.own, bf16[7,256,128]{2,1,0:T(8,128)(2,1)S(1)} %collective-permute-done.18.low, bf16[4,256,128]{2,1,0:T(8,128)(2,1)S(1)} %collective-permute-done.19.high), custom_call_target="tpu_custom_call" | custom-call | flops 14680064 | bytes 4194304 | tf_op jit(solution)/shard_map/pallas_call | solution.py:357
  (18 shorter events, 0.3 us)
Async XLA Ops:
  0.6 14.1 %collective-permute-start.1 = (bf16[1024,128]{1,0:T(8,128)(2,1)}, bf16[1024,128]{1,0:T(8,128)(2,1)S(1)}, u32[]{:S(2)}, u32[]{:S(2)}) collective-permute-start(bf16[1024,128]{1,0:T(8,128)(2,1)} %bitcast.27), channel_id=1, source_target_pairs={{1,0},{2,1},{3,2},{5,4},{6,5},{7,6},{9,8},{10,9},{11,10},{13,12},{... | collective-permute-start | bytes 786440 | tf_op jit(solution)/shard_map/ppermute | solution.py:257
  1.9 11.4 %collective-permute-start = (bf16[1024,128]{1,0:T(8,128)(2,1)}, bf16[1024,128]{1,0:T(8,128)(2,1)S(1)}, u32[]{:S(2)}, u32[]{:S(2)}) collective-permute-start(bf16[1024,128]{1,0:T(8,128)(2,1)} %bitcast.28), channel_id=1, source_target_pairs={{0,1},{1,2},{2,3},{4,5},{5,6},{6,7},{8,9},{9,10},{10,11},{12,13},{... | collective-permute-start | bytes 786440 | tf_op jit(solution)/shard_map/ppermute | solution.py:256
  7.5 20.6 %collective-permute-start.6 = (f32[4,64,512]{2,1,0:T(8,128)}, f32[4,64,512]{2,1,0:T(8,128)S(1)}, u32[]{:S(2)}, u32[]{:S(2)}) collective-permute-start(f32[4,64,512]{2,1,0:T(8,128)} %bitcast.22), channel_id=1, source_target_pairs={{0,4},{4,8},{8,12},{12,16},{16,20},{20,24},{24,28},{28,0},{1,5},{5... | collective-permute-start | bytes 1572872 | tf_op jit(solution)/shard_map/ppermute | solution.py:309
  7.6 20.6 %collective-permute-start.7 = (f32[4,64,512]{2,1,0:T(8,128)}, f32[4,64,512]{2,1,0:T(8,128)S(1)}, u32[]{:S(2)}, u32[]{:S(2)}) collective-permute-start(f32[4,64,512]{2,1,0:T(8,128)} %bitcast.23), channel_id=1, source_target_pairs={{0,28},{4,0},{8,4},{12,8},{16,12},{20,16},{24,20},{28,24},{1,29},{... | collective-permute-start | bytes 1572872 | tf_op jit(solution)/shard_map/ppermute | solution.py:310
  13.4 3.5 %collective-permute-start.4 = (bf16[1024,128]{1,0:T(8,128)(2,1)S(1)}, bf16[1024,128]{1,0:T(8,128)(2,1)S(1)}, u32[]{:S(2)}, u32[]{:S(2)}) collective-permute-start(bf16[1024,128]{1,0:T(8,128)(2,1)S(1)} %collective-permute-done), channel_id=1, source_target_pairs={{1,2},{2,3},{5,6},{6,7},{9,10},{10,11},{13,14},{14,15},{17,18},{18... | collective-permute-start | bytes 786440 | tf_op jit(solution)/shard_map/ppermute | solution.py:256
  14.7 12.1 %collective-permute-start.2 = (bf16[1024,128]{1,0:T(8,128)(2,1)S(1)}, bf16[1024,128]{1,0:T(8,128)(2,1)S(1)}, u32[]{:S(2)}, u32[]{:S(2)}) collective-permute-start(bf16[1024,128]{1,0:T(8,128)(2,1)S(1)} %collective-permute-done.1), channel_id=1, source_target_pairs={{1,0},{2,1},{5,4},{6,5},{9,8},{10,9},{13,12},{14,13},{17,16},{18,1... | collective-permute-start | bytes 786440 | tf_op jit(solution)/shard_map/ppermute | solution.py:257
  16.8 18.1 %collective-permute-start.5 = (bf16[1024,128]{1,0:T(8,128)(2,1)S(1)}, bf16[1024,128]{1,0:T(8,128)(2,1)S(1)}, u32[]{:S(2)}, u32[]{:S(2)}) collective-permute-start(bf16[1024,128]{1,0:T(8,128)(2,1)S(1)} %collective-permute-done.4), channel_id=1, source_target_pairs={{2,3},{6,7},{10,11},{14,15},{18,19},{22,23},{26,27},{30,31}} | collective-permute-start | bytes 786440 | tf_op jit(solution)/shard_map/ppermute | solution.py:256
  26.8 8.3 %collective-permute-start.3 = (bf16[1024,128]{1,0:T(8,128)(2,1)S(1)}, bf16[1024,128]{1,0:T(8,128)(2,1)S(1)}, u32[]{:S(2)}, u32[]{:S(2)}) collective-permute-start(bf16[1024,128]{1,0:T(8,128)(2,1)S(1)} %collective-permute-done.2), channel_id=1, source_target_pairs={{1,0},{5,4},{9,8},{13,12},{17,16},{21,20},{25,24},{29,28}} | collective-permute-start | bytes 786440 | tf_op jit(solution)/shard_map/ppermute | solution.py:257
  28.2 1.0 %copy-start = (f32[1,4,64,512]{3,2,1,0:T(8,128)S(1)}, f32[1,4,64,512]{3,2,1,0:T(8,128)}, u32[]{:S(2)}) copy-start(f32[1,4,64,512]{3,2,1,0:T(8,128)} %param.6) | copy-start | bytes 1572868
  34.8 1.0 %copy-start.1 = (bf16[1,1024,128]{2,1,0:T(8,128)(2,1)S(1)}, bf16[1,1024,128]{2,1,0:T(8,128)(2,1)}, u32[]{:S(2)}) copy-start(bf16[1,1024,128]{2,1,0:T(8,128)(2,1)} %param.11) | copy-start | bytes 786436
  45.9 1.3 %collective-permute-start.8 = (f32[3,16,1,256]{3,2,1,0:T(1,128)S(1)}, f32[3,16,1,256]{3,2,1,0:T(1,128)S(1)}, u32[]{:S(2)}, u32[]{:S(2)}) collective-permute-start(f32[3,16,1,256]{3,2,1,0:T(1,128)S(1)} %shard_map.78), channel_id=1, source_target_pairs={{0,4},{4,0},{8,12},{12,8},{16,20},{20,16},{24,28},{28,24},{1,5},{5... | collective-permute-start | bytes 147464 | tf_op jit(solution)/shard_map/ppermute | solution.py:292
  47.3 12.5 %collective-permute-start.9 = (f32[3,16,1,256]{3,2,1,0:T(1,128)S(1)}, f32[3,16,1,256]{3,2,1,0:T(1,128)S(1)}, u32[]{:S(2)}, u32[]{:S(2)}) collective-permute-start(f32[3,16,1,256]{3,2,1,0:T(1,128)S(1)} %add.113), channel_id=1, source_target_pairs={{0,8},{4,12},{8,0},{12,4},{16,24},{20,28},{24,16},{28,20},{1,9},{5... | collective-permute-start | bytes 147464 | tf_op jit(solution)/shard_map/ppermute | solution.py:292
  54.3 3.5 %collective-permute-start.11 = (f32[1,16,1,256]{3,2,1,0:T(1,128)S(1)}, f32[1,16,1,256]{3,2,1,0:T(1,128)S(1)}, u32[]{:S(2)}, u32[]{:S(2)}) collective-permute-start(f32[1,16,1,256]{3,2,1,0:T(1,128)S(1)} %shard_map.79.refs_2_), channel_id=1, source_target_pairs={{0,4},{4,0},{8,12},{12,8},{16,20},{20,16},{24,28},{28,24},{1,5},{5... | collective-permute-start | bytes 49160 | tf_op jit(solution)/shard_map/ppermute | solution.py:273
  54.4 4.0 %collective-permute-start.12 = (f32[1,16,1,256]{3,2,1,0:T(1,128)S(1)}, f32[1,16,1,256]{3,2,1,0:T(1,128)S(1)}, u32[]{:S(2)}, u32[]{:S(2)}) collective-permute-start(f32[1,16,1,256]{3,2,1,0:T(1,128)S(1)} %shard_map.79.refs_2_), channel_id=1, source_target_pairs={{0,8},{4,12},{8,0},{12,4},{16,24},{20,28},{24,16},{28,20},{1,9},{5... | collective-permute-start | bytes 49160 | tf_op jit(solution)/shard_map/ppermute | solution.py:273
  55.1 5.8 %collective-permute-start.13 = (f32[1,16,1,256]{3,2,1,0:T(1,128)S(1)}, f32[1,16,1,256]{3,2,1,0:T(1,128)S(1)}, u32[]{:S(2)}, u32[]{:S(2)}) collective-permute-start(f32[1,16,1,256]{3,2,1,0:T(1,128)S(1)} %shard_map.79.refs_2_), channel_id=1, source_target_pairs={{0,12},{4,8},{8,4},{12,0},{16,28},{20,24},{24,20},{28,16},{1,13},{... | collective-permute-start | bytes 49160 | tf_op jit(solution)/shard_map/ppermute | solution.py:273
  56.3 6.1 %collective-permute-start.14 = (f32[1,16,1,256]{3,2,1,0:T(1,128)S(1)}, f32[1,16,1,256]{3,2,1,0:T(1,128)S(1)}, u32[]{:S(2)}, u32[]{:S(2)}) collective-permute-start(f32[1,16,1,256]{3,2,1,0:T(1,128)S(1)} %shard_map.79.refs_2_), channel_id=1, source_target_pairs={{0,16},{4,20},{8,24},{12,28},{16,0},{20,4},{24,8},{28,12},{1,17},{... | collective-permute-start | bytes 49160 | tf_op jit(solution)/shard_map/ppermute | solution.py:273
  57.8 4.6 %collective-permute-start.15 = (f32[1,16,1,256]{3,2,1,0:T(1,128)S(1)}, f32[1,16,1,256]{3,2,1,0:T(1,128)S(1)}, u32[]{:S(2)}, u32[]{:S(2)}) collective-permute-start(f32[1,16,1,256]{3,2,1,0:T(1,128)S(1)} %shard_map.79.refs_2_), channel_id=1, source_target_pairs={{0,20},{4,16},{8,28},{12,24},{16,4},{20,0},{24,12},{28,8},{1,21},{... | collective-permute-start | bytes 49160 | tf_op jit(solution)/shard_map/ppermute | solution.py:273
  58.4 4.6 %collective-permute-start.16 = (f32[1,16,1,256]{3,2,1,0:T(1,128)S(1)}, f32[1,16,1,256]{3,2,1,0:T(1,128)S(1)}, u32[]{:S(2)}, u32[]{:S(2)}) collective-permute-start(f32[1,16,1,256]{3,2,1,0:T(1,128)S(1)} %shard_map.79.refs_2_), channel_id=1, source_target_pairs={{0,24},{4,28},{8,16},{12,20},{16,8},{20,12},{24,0},{28,4},{1,25},{... | collective-permute-start | bytes 49160 | tf_op jit(solution)/shard_map/ppermute | solution.py:273
  59.8 4.1 %collective-permute-start.17 = (f32[1,16,1,256]{3,2,1,0:T(1,128)S(1)}, f32[1,16,1,256]{3,2,1,0:T(1,128)S(1)}, u32[]{:S(2)}, u32[]{:S(2)}) collective-permute-start(f32[1,16,1,256]{3,2,1,0:T(1,128)S(1)} %shard_map.79.refs_2_), channel_id=1, source_target_pairs={{0,28},{4,24},{8,20},{12,16},{16,12},{20,8},{24,4},{28,0},{1,29},{... | collective-permute-start | bytes 49160 | tf_op jit(solution)/shard_map/ppermute | solution.py:273
  60.8 9.4 %collective-permute-start.10 = (f32[3,16,1,256]{3,2,1,0:T(1,128)S(1)}, f32[3,16,1,256]{3,2,1,0:T(1,128)S(1)}, u32[]{:S(2)}, u32[]{:S(2)}) collective-permute-start(f32[3,16,1,256]{3,2,1,0:T(1,128)S(1)} %add.114), channel_id=1, source_target_pairs={{0,16},{4,20},{8,24},{12,28},{16,0},{20,4},{24,8},{28,12},{1,17},{... | collective-permute-start | bytes 147464 | tf_op jit(solution)/shard_map/ppermute | solution.py:292
  67.5 11.7 %collective-permute-start.18 = (bf16[7,256,128]{2,1,0:T(8,128)(2,1)S(1)}, bf16[7,256,128]{2,1,0:T(8,128)(2,1)S(1)}, u32[]{:S(2)}, u32[]{:S(2)}) collective-permute-start(bf16[7,256,128]{2,1,0:T(8,128)(2,1)S(1)} %get-tuple-element.8), channel_id=1, source_target_pairs={{0,4},{4,8},{8,12},{12,16},{16,20},{20,24},{24,28},{28,0},{1,5},{5... | collective-permute-start | bytes 1376264 | tf_op jit(solution)/shard_map/ppermute | solution.py:355
  67.7 9.3 %collective-permute-start.19 = (bf16[4,256,128]{2,1,0:T(8,128)(2,1)S(1)}, bf16[4,256,128]{2,1,0:T(8,128)(2,1)S(1)}, u32[]{:S(2)}, u32[]{:S(2)}) collective-permute-start(bf16[4,256,128]{2,1,0:T(8,128)(2,1)S(1)} %get-tuple-element.9), channel_id=1, source_target_pairs={{0,28},{4,0},{8,4},{12,8},{16,12},{20,16},{24,20},{28,24},{1,29},{... | collective-permute-start | bytes 786440 | tf_op jit(solution)/shard_map/ppermute | solution.py:356

commit v2 on v1

--- a/solution.py
+++ b/solution.py
@@ -1,5 +1,6 @@
 import jax
 import jax.numpy as jnp
+import numpy as np
 from jax import lax
 from jax.experimental import pallas as pl
 from jax.experimental.pallas import tpu as pltpu
@@ -97,7 +98,7 @@
 
         lax.fori_loop(0, cells, load, 0)
     buffers = (first, second)
-    rows = 16
+    rows = 8
     for step in range(steps):
         source, target = buffers[step % 2], buffers[(step + 1) % 2]
 
@@ -109,13 +110,15 @@
             return carry
 
         def inner(plane, carry, source=source, target=target, step=step):
-            for row in range(0, height, rows):
+            for row in range(0, height, 2 * rows):
                 block = stencil_block(source, coef, plane, row, rows, True)
+                after = stencil_block(source, coef, plane, row + rows, rows, True)
                 for c in range(columns):
                     target[plane, c, pl.ds(PAD + row, rows), :] = block[c]
+                    target[plane, c, pl.ds(PAD + row + rows, rows), :] = after[c]
                     start = (plane - cells) * columns * height + c * height + row
-                    where = pl.ds(pl.multiple_of(start, rows), rows)
-                    head, tail = split(block[c])
+                    where = pl.ds(pl.multiple_of(start, 2 * rows), 2 * rows)
+                    head, tail = split(jnp.concatenate([block[c], after[c]], axis=0))
                     tiles[step, where, pl.ds(0, TILE)] = head
                     tiles[step, where, pl.ds(TILE, TILE)] = tail
             return carry
@@ -142,7 +145,7 @@
                 value = value + low[cells + plane - 1, where, :].astype(jnp.float32)
             first[plane, c, inside, :] = value
     buffers = (first, second)
-    rows = 16
+    rows = 8
     for step in range(steps):
         source, target = buffers[step % 2], buffers[(step + 1) % 2]
         last = step == steps - 1
@@ -160,58 +163,93 @@
         lax.fori_loop(step + 1, 3 * cells - step - 1, body, 0)
 
 
-def project_kernel(index, panel, tiles, out):
+def transposed(rows):
+    return rows.astype(jnp.float32).T.astype(jnp.bfloat16)
+
+
+def wanted_tile(index, group, columns, height):
+    tile = index[group]
+    inside = tile & (columns * height - 1)
+    return (tile - inside) + (inside & (columns - 1)) * height + inside // columns
+
+
+def kept_sum(tiles, step, weights, wanted):
+    chunk = 256
+    partial = jnp.zeros((8, GROUP), jnp.float32)
+    for start in range(0, tiles.shape[1], chunk):
+        gram = jnp.dot(
+            tiles[step, pl.ds(start, chunk), :], weights, preferred_element_type=jnp.float32
+        )
+        number = lax.broadcasted_iota(jnp.int32, (chunk, GROUP), 0) + start
+        kept = jnp.where(number == wanted, gram, 0.0)
+        partial = partial + jnp.sum(kept.reshape(chunk // 8, 8, GROUP), axis=0)
+    return jnp.sum(partial, axis=0, keepdims=True)
+
+
+def last_kernel(columns, height, chunks, source, index, tiles, before, *refs):
+    panels, (out, turned) = refs[: len(chunks)], refs[len(chunks) :]
+    shard = panels[0].shape[0] // GROUP
+    if before is not None:
+        out[...] = before[...]
+    for place, (chunk, panel) in enumerate(zip(chunks, panels)):
+
+        def body(group, carry, place=place, chunk=chunk, panel=panel):
+            rows = panel[pl.ds(pl.multiple_of(group * GROUP, GROUP), GROUP), :]
+            across = transposed(rows)
+            turned[place * shard + group] = across
+            number = source[chunk] * shard + group
+            weights = jnp.concatenate([across, across], axis=0)
+            wanted = wanted_tile(index, number, columns, height)
+            out[number] = kept_sum(tiles, tiles.shape[0] - 1, weights, wanted)
+            return carry
+
+        lax.fori_loop(0, shard, body, 0)
+
+
+def early_kernel(columns, height, source, index, tiles, head, tail, out):
+    shard = tail.shape[0]
+    for turned, first in ((head, 0), (tail, head.shape[0])):
+
+        def body(group, carry, turned=turned, first=first):
+            chunk = first + group
+            number = source[chunk // shard] * shard + lax.rem(chunk, shard)
+            across = turned[group]
+            weights = jnp.concatenate([across, across], axis=0)
+            wanted = wanted_tile(index, number, columns, height)
+            for step in range(out.shape[0]):
+                out[step, number] = kept_sum(tiles, step, weights, wanted)
+            return carry
+
+        lax.fori_loop(0, turned.shape[0], body, 0)
+
+
+def deposit_kernel(columns, height, source, index, parts, *refs):
+    panels, (total, field, rightward, leftward, scaled, wanted) = refs[:-6], refs[-6:]
     groups = index.shape[0]
-    steps, total = tiles.shape[0], tiles.shape[1]
-    chunk = 256
-
-    def body(group, carry):
-        rows = panel[pl.ds(pl.multiple_of(group * GROUP, GROUP), GROUP), :]
-        doubled = jnp.concatenate([rows, rows], axis=1)
-        wanted = index[group]
-        for step in range(steps):
-            partial = jnp.zeros((8, GROUP), jnp.float32)
-            for start in range(0, total, chunk):
-                gram = lax.dot_general(
-                    tiles[step, pl.ds(start, chunk), :],
-                    doubled,
-                    (((1,), (1,)), ((), ())),
-                    preferred_element_type=jnp.float32,
-                )
-                number = lax.broadcasted_iota(jnp.int32, (chunk, GROUP), 0) + start
-                kept = jnp.where(number == wanted, gram, 0.0)
-                partial = partial + jnp.sum(kept.reshape(chunk // 8, 8, GROUP), axis=0)
-            out[step, group] = jnp.sum(partial, axis=0, keepdims=True)
-        return carry
-
-    lax.fori_loop(0, groups, body, 0)
-
-
-def deposit_kernel(count, index, panel, *refs):
-    parts, (total, field, rightward, leftward, scaled) = refs[:count], refs[count:]
-    groups = index.shape[0]
+    shard = groups // len(panels)
     cells, per_plane = field.shape[0], field.shape[1]
-    values = [part[...] for part in parts]
-    while len(values) > 1:
-        values = [values[i] + values[i + 1] for i in range(0, len(values), 2)]
-    total[...] = values[0]
-    drive = values[0].reshape(groups, GROUP).T
+    summed = parts[0]
+    for part in range(1, parts.shape[0]):
+        summed = summed + parts[part]
+    total[...] = summed
+    numbers = [source[g // shard] * shard + g % shard for g in range(groups)]
+    drive = jnp.concatenate([total[number] for number in numbers], axis=0).T
     for group in range(groups):
+        rows = panels[group // shard][pl.ds((group % shard) * GROUP, GROUP), :]
+        head, tail = split(drive[:, group : group + 1] * rows.astype(jnp.float32))
         where = pl.ds(group * GROUP, GROUP)
-        product = drive[:, group : group + 1] * panel[where, :].astype(jnp.float32)
-        head, tail = split(product)
         scaled[where, pl.ds(0, TILE)] = head
         scaled[where, pl.ds(TILE, TILE)] = tail
+        wanted[group] = wanted_tile(index, numbers[group], columns, height)
 
     def body(plane, carry):
         number = lax.broadcasted_iota(jnp.int32, (per_plane, GROUP), 0) + plane * per_plane
         sums = jnp.zeros((per_plane, 2 * TILE), jnp.float32)
         for group in range(groups):
-            chosen = jnp.where(number == index[group], 1.0, 0.0).astype(jnp.bfloat16)
-            sums = sums + lax.dot_general(
+            chosen = jnp.where(number == wanted[group], 1.0, 0.0).astype(jnp.bfloat16)
+            sums = sums + jnp.dot(
                 chosen,
                 scaled[pl.ds(group * GROUP, GROUP), :],
-                (((1,), (0,)), ((), ())),
                 preferred_element_type=jnp.float32,
             )
         value = sums[:, :TILE] + sums[:, TILE:]
@@ -244,43 +282,18 @@
     )
 
 
-def gathered_panel(panel, axis):
+def ring_order(count):
+    return list(range(0, count, 2)) + [i for i in range(count - 1, 0, -1) if i % 2]
+
+
+def tied(value, *others):
+    return lax.optimization_barrier((value,) + others)[0]
+
+
+def gathered(part, axis):
     count = lax.axis_size(axis)
-    if count == 1:
-        return panel
-    place = lax.axis_index(axis)
-    up = [(i, i + 1) for i in range(count - 1)]
-    down = [(i + 1, i) for i in range(count - 1)]
-    from_below, from_above = [panel], [panel]
-    for stage in range(1, count):
-        from_below.append(lax.ppermute(from_below[-1], axis, up[stage - 1 :]))
-        from_above.append(lax.ppermute(from_above[-1], axis, down[: count - stage]))
-    pieces = [panel]
-    for shift in range(1, count):
-        pieces.append(jnp.where(place >= shift, from_below[shift], from_above[count - shift]))
-    return jnp.concatenate(pieces, axis=0)
-
-
-def summands(part, axis):
-    count = lax.axis_size(axis)
-    if count & (count - 1):
-        return [lax.psum(part, axis)]
-    done = 1
-    while True:
-        span = min(8, count // done)
-        parts = [part]
-        for mask in range(1, span):
-            parts.append(lax.ppermute(part, axis, [(i, i ^ (mask * done)) for i in range(count)]))
-        done *= span
-        if done == count:
-            return parts
-        part = tree_sum(parts)
-
-
-def tree_sum(parts):
-    while len(parts) > 1:
-        parts = [parts[i] + parts[i + 1] for i in range(0, len(parts), 2)]
-    return parts[0]
+    copies = jnp.broadcast_to(part[None], (count,) + part.shape)
+    return lax.all_to_all(copies, axis, 0, 0)
 
 
 def doubling_sum(part, axis):
@@ -296,26 +309,30 @@
 
 def local(sensor_field, courant, diffusivity, probe_offset, tile_index, actuator_panel):
     slabs, probes = lax.axis_size("state"), lax.axis_size("probe")
-    place = lax.axis_index("probe")
     own = sensor_field[0]
     cells, height, width = own.shape
     columns = width // TILE
     tile_total = cells * height * columns
     actuators = tile_index.shape[1]
     groups = actuators // GROUP
+    shard = groups // probes
     planes = 3 * cells
     f32, bf16 = jnp.float32, jnp.bfloat16
 
+    ring = ring_order(probes)
+    hops = [(ring[i], ring[(i + 1) % probes]) for i in range(probes)]
+    panels = [actuator_panel[0]]
+    for _ in range(probes - 1):
+        panels.append(lax.ppermute(panels[-1], "probe", hops))
+    origin = np.zeros((probes, probes), np.int32)
+    for spot, device in enumerate(ring):
+        origin[device] = [ring[(spot - stage) % probes] for stage in range(probes)]
+    source = jnp.asarray(origin)[lax.axis_index("probe")]
     low = lax.ppermute(own, "state", shift_pairs(slabs, 1))
     high = lax.ppermute(own, "state", shift_pairs(slabs, -1))
-    panel = gathered_panel(actuator_panel[0], "probe")
 
     coef = coefficients(courant, diffusivity)
-    order = lax.rem(place - jnp.arange(probes, dtype=jnp.int32) + probes, probes)
-    tile = jnp.take(tile_index[0].reshape(probes, -1), order, axis=0)
-    plane, inside = tile // (height * columns), tile % (height * columns)
-    index = plane * (height * columns) + (inside % columns) * height + inside // columns
-    index = index.reshape(groups, 1, GROUP)
+    index = tile_index.reshape(groups, 1, GROUP)
 
     field_shape = pltpu.VMEM((planes, columns, height + 2 * PAD, TILE), f32)
     tiles = call(
@@ -327,33 +344,52 @@
         flops=28 * 16 * height * width,
     )(probe_offset, coef, own, low, high)
 
-    def project(part):
-        return call(
-            project_kernel,
-            jax.ShapeDtypeStruct((part.shape[0], groups, 1, GROUP), f32),
-            inputs=3,
-            flops=part.shape[0] * 2 * actuators * tile_total * 2 * TILE,
-        )(index, panel, part)
-
-    last = project(tiles[STEPS - 1 :])
-    early = project(tiles[: STEPS - 1])
-    parts = summands(last, "state")
+    row_shape = jax.ShapeDtypeStruct((groups, 1, GROUP), f32)
+    step_flops = 2 * GROUP * tile_total * 2 * TILE
+    early_chunks, late_chunks = list(range(probes - 1)), [probes - 1]
+
+    def turned_shape(chunks):
+        return jax.ShapeDtypeStruct((len(chunks) * shard, TILE, GROUP), bf16)
+
+    before, head = call(
+        lambda source, index, tiles, *refs: last_kernel(
+            columns, height, early_chunks, source, index, tiles, None, *refs
+        ),
+        (row_shape, turned_shape(early_chunks)),
+        smem=1,
+        inputs=3 + len(early_chunks),
+        flops=step_flops * shard * len(early_chunks),
+    )(source, index, tiles, *panels[:-1])
+    last, tail = call(
+        lambda source, index, tiles, before, *refs: last_kernel(
+            columns, height, late_chunks, source, index, tiles, before, *refs
+        ),
+        (row_shape, turned_shape(late_chunks)),
+        smem=1,
+        inputs=4 + len(late_chunks),
+        flops=step_flops * shard,
+    )(source, index, tiles, before, *panels[-1:])
+    parts = gathered(last, "state")
     payload = jax.ShapeDtypeStruct((2 * cells - 1, height * columns, TILE), bf16)
     heads = jax.ShapeDtypeStruct((cells, height * columns, TILE), bf16)
     total, forced, rightward, leftward = call(
-        lambda *refs: deposit_kernel(len(parts), *refs),
-        (
-            jax.ShapeDtypeStruct(last.shape, f32),
-            jax.ShapeDtypeStruct((cells, height * columns, TILE), f32),
-            payload,
-            heads,
-        ),
-        scratch=(pltpu.VMEM((actuators, 2 * TILE), bf16),),
-        inputs=2 + len(parts),
-        flops=2 * actuators * tile_total * 2 * TILE,
-    )(index, panel, *parts)
+        lambda *refs: deposit_kernel(columns, height, *refs),
+        (row_shape, jax.ShapeDtypeStruct((cells, height * columns, TILE), f32), payload, heads),
+        scratch=(pltpu.VMEM((actuators, 2 * TILE), bf16), pltpu.VMEM((groups, 1, GROUP), jnp.int32)),
+        smem=1,
+        inputs=3 + probes,
+        flops=step_flops * groups,
+    )(source, index, parts, *panels)
     from_low = lax.ppermute(rightward, "state", shift_pairs(slabs, 1))
     from_high = lax.ppermute(leftward, "state", shift_pairs(slabs, -1))
+    early = call(
+        lambda *refs: early_kernel(columns, height, *refs),
+        jax.ShapeDtypeStruct((STEPS - 1, groups, 1, GROUP), f32),
+        smem=1,
+        inputs=5,
+        flops=step_flops * groups * (STEPS - 1),
+    )(source, tied(index, forced), tiles, head, tail)
+    early = doubling_sum(early, "state")
     response = call(
         forward_kernel,
         jax.ShapeDtypeStruct((cells, height, width), f32),
@@ -361,12 +397,8 @@
         inputs=4,
         flops=28 * 16 * height * width,
     )(coef, forced, from_low, from_high)
-
-    early = doubling_sum(early, "state")
-    projections = jnp.concatenate([early, total], axis=0).reshape(STEPS, probes, -1)
-    back = lax.rem(place - jnp.arange(probes, dtype=jnp.int32) + probes, probes)
-    projections = jnp.take(projections, back, axis=1).reshape(STEPS, 1, actuators)
-    return projections, response[None]
+    projections = jnp.concatenate([early, total[None]], axis=0)
+    return projections.reshape(STEPS, 1, actuators), response[None]
 
 
 def solution(mesh):

time: 84.5 us -> 83.8 us (level)
  blocking collectives: 0 us -> 9.05 us
  starting transfers between devices: 25.3 us -> 16.3 us
  Pallas kernels: 29.7 us -> 32.7 us
  local copies, waits for them, and re-layouts: 6.13 us -> 3.38 us
  other arithmetic: 3.02 us -> 1.6 us
    all_to_all x0 -> x1, blocking collectives: none -> 9.05 us  [gathered(): return lax.all_to_all(copies, axis, 0, 0)]
    ppermute x13 -> x3, starting transfers between devices: 16.7 us -> 10.7 us  [local(): panels.append(lax.ppermute(panels[-1], 'probe', hops))]
    ppermute x3, waiting for transfers between devices: 1.18 us -> 5.66 us  [doubling_sum(): lax.ppermute(part, axis, [(i, i ^ mask) for i in range(count)])]
    ppermute x13 -> x3, waiting for transfers between devices: 9.99 us -> 6.08 us  [local(): panels.append(lax.ppermute(panels[-1], 'probe', hops))]
    pallas_call x3 -> x4, Pallas kernels: 19.2 us -> 22 us  [the longest x1 10.2 us: local(): call(lambda *refs: early_kernel(columns, height, *refs), jax.ShapeDtypeSt...]
    unnamed x8 -> x7, local copies, waits for them, and re-layouts: 2.98 us -> 1.05 us
    ppermute x3, starting transfers between devices: 3.21 us -> 1.29 us  [doubling_sum(): lax.ppermute(part, axis, [(i, i ^ mask) for i in range(count)])]
    unnamed x1 -> x0, other arithmetic: 1.4 us -> none
  transfers between devices with their start and end apart: 20 -> 10, of which waited for: 9 -> 7; matrix products, arithmetic and copies ran while one was open for 9% -> 4% of each run, Pallas kernels for 17% -> 13%
where the time goes in v2:
time: 83.8 us; the launch traced here: 83.5 us
  Pallas kernels  32.7 us (39%)
  waiting for transfers between devices  19 us (23%)
  starting transfers between devices  16.3 us (19%)
  blocking collectives  9.05 us (11%)
  local copies, waits for them, and re-layouts  3.38 us (4%)
  other arithmetic  1.6 us (2%)
  between operations  1.42 us (2%)
    ppermute x3, starting transfers between devices, local(): panels.append(lax.ppermute(panels[-1], 'probe', hops))  10.7 us
    pallas_call x1, Pallas kernels, local(): call(lambda *refs: early_kernel(columns, height, *refs), jax.ShapeDtypeSt...  10.2 us
    all_to_all x1, blocking collectives, gathered(): return lax.all_to_all(copies, axis, 0, 0)  9.05 us
    ppermute x3, waiting for transfers between devices, local(): panels.append(lax.ppermute(panels[-1], 'probe', hops))  6.08 us
    ppermute x3, waiting for transfers between devices, doubling_sum(): lax.ppermute(part, axis, [(i, i ^ mask) for i in range(count)])  5.66 us
    pallas_call x1, Pallas kernels, local(): call(adjoint_kernel, jax.ShapeDtypeStruct((STEPS, tile_total, 2 * TILE),...  5.64 us
    pallas_call x1, Pallas kernels, local(): call(lambda source, index, tiles, *refs: last_kernel(columns, height, ear...  5.38 us
    pallas_call x1, Pallas kernels, local(): call(forward_kernel, jax.ShapeDtypeStruct((cells, height, width), f32), s...  5.08 us
  transfers between devices with their start and end apart: 10, of which 7 were waited for; matrix products, arithmetic and copies ran while one was open for 4% of the time, Pallas kernels for 13%

profile of v2, /device:TPU:0, one launch (start us, length us, event | category | flops | bytes accessed | tf_op | source)
XLA Modules:
  0.0 83.5 jit_solution(9129929263338057161)
XLA Ops:
  0.6 0.0 copy-start.1
  0.6 4.1 %collective-permute-start.2 = (bf16[1024,128]{1,0:T(8,128)(2,1)}, bf16[1024,128]{1,0:T(8,128)(2,1)S(1)}, u32[]{:S(2)}, u32[]{:S(2)}) collective-permute-start(bf16[1024,128]{1,0:T(8,128)(2,1)} %bitcast.28), channel_id=1, source_target_pairs={{0,2},{2,3},{3,1},{1,0},{4,6},{6,7},{7,5},{5,4},{8,10},{10,11},{11... | collective-permute-start | bytes 786440 | tf_op jit(solution)/shard_map/ppermute | solution.py:326
  4.7 1.6 %collective-permute-start.1 = (f32[4,64,512]{2,1,0:T(8,128)}, f32[4,64,512]{2,1,0:T(8,128)S(1)}, u32[]{:S(2)}, u32[]{:S(2)}) collective-permute-start(f32[4,64,512]{2,1,0:T(8,128)} %bitcast.20), channel_id=1, source_target_pairs={{0,28},{4,0},{8,4},{12,8},{16,12},{20,16},{24,20},{28,24},{1,29},{... | collective-permute-start | bytes 1572872 | tf_op jit(solution)/shard_map/ppermute | solution.py:332
  6.3 0.0 collective-permute-start
  6.3 0.8 fusion
  7.1 3.5 %collective-permute-done.2.refs_1_.refs_4_ = bf16[1024,128]{1,0:T(8,128)(2,1)S(1)} collective-permute-done((bf16[1024,128]{1,0:T(8,128)(2,1)}, bf16[1024,128]{1,0:T(8,128)(2,1)S(1)}, u32[]{:S(2)}, u32[]{:S(2)}) %collective-permute-start.2) | collective-permute-done | bytes 262176 | tf_op jit(solution)/shard_map/ppermute | solution.py:326
  10.6 3.3 %collective-permute-start.3 = (bf16[1024,128]{1,0:T(8,128)(2,1)S(1)}, bf16[1024,128]{1,0:T(8,128)(2,1)S(1)}, u32[]{:S(2)}, u32[]{:S(2)}) collective-permute-start(bf16[1024,128]{1,0:T(8,128)(2,1)S(1)} %collective-permute-done.2.refs_1_.refs_4_), channel_id=1, source_target_pairs={{0,2},{2,3},{3,1},{1,0},{4,6},{6,7},{7,5},{5,4},{8,10},{10,11},{11... | collective-permute-start | bytes 786440 | tf_op jit(solution)/shard_map/ppermute | solution.py:326
  13.9 0.1 maximum_bitcast_fusion
  14.6 0.7 add_bitcast_fusion
  15.3 0.7 stack.23
  16.0 2.6 %collective-permute-done.3.refs_2_.refs_5_ = bf16[1024,128]{1,0:T(8,128)(2,1)S(1)} collective-permute-done((bf16[1024,128]{1,0:T(8,128)(2,1)S(1)}, bf16[1024,128]{1,0:T(8,128)(2,1)S(1)}, u32[]{:S(2)}, u32[]{:S(2)}) %collective-permute-start.3) | collective-permute-done | bytes 262176 | tf_op jit(solution)/shard_map/ppermute | solution.py:326
  18.6 3.4 %collective-permute-start.4 = (bf16[1024,128]{1,0:T(8,128)(2,1)S(1)}, bf16[1024,128]{1,0:T(8,128)(2,1)S(1)}, u32[]{:S(2)}, u32[]{:S(2)}) collective-permute-start(bf16[1024,128]{1,0:T(8,128)(2,1)S(1)} %collective-permute-done.3.refs_2_.refs_5_), channel_id=1, source_target_pairs={{0,2},{2,3},{3,1},{1,0},{4,6},{6,7},{7,5},{5,4},{8,10},{10,11},{11... | collective-permute-start | bytes 786440 | tf_op jit(solution)/shard_map/ppermute | solution.py:326
  22.0 0.7 dynamic-slice_bitcast_fusion.source.refs_0_
  22.6 0.0 collective-permute-done.1.high
  22.6 0.0 collective-permute-done.low
  22.7 0.1 broadcast_in_dim.8.coef
  22.8 0.0 copy-start
  22.8 1.0 %copy-done = f32[1,4,64,512]{3,2,1,0:T(8,128)S(1)} copy-done((f32[1,4,64,512]{3,2,1,0:T(8,128)S(1)}, f32[1,4,64,512]{3,2,1,0:T(8,128)}, u32[]{:S(2)}) %copy-start) | copy-done | bytes 524312
  23.8 0.0 copy-start.2
  23.8 5.6 %shard_map.86.tiles.refs_2_ = bf16[4,1024,256]{2,1,0:T(8,128)(2,1)S(1)} custom-call(s32[1]{0:T(128)S(6)} %copy.13.offset, f32[5,64,128]{2,1,0:T(8,128)S(1)} %broadcast_in_dim.8.coef, f32[4,64,512]{2,1,0:T(8,128)S(1)} %bitcast.22, f32[4,64,512]{2,1,0:T(8,128)S(1)} %collective-permute-done.low, f32[4,64,512]{2,1,0:T(8,128)S(1)} %collective-permute-done.1.high), custom_call_target="tpu_custom_call" | custom-call | flops 14680064 | bytes 4194304 | tf_op jit(solution)/shard_map/pallas_call | solution.py:338
  29.5 0.0 copy-done.1
  29.5 0.0 copy-done.2
  29.5 5.4 %shard_map.87 = (f32[16,1,256]{2,1,0:T(1,128)S(1)}, bf16[12,128,256]{2,1,0:T(8,128)(2,1)S(1)}) custom-call(s32[4]{0:T(128)S(1)} %dynamic-slice_bitcast_fusion.source.refs_0_, s32[16,1,256]{2,1,0:T(1,128)S(1)} %bitcast.23, bf16[4,1024,256]{2,1,0:T(8,128)(2,1)S(1)} %shard_map.86.tiles.refs_2_, bf16[1024,128]{1,0:T(8,128)(2,1)S(1)} %bitcast.29, ...), custom_call_target="tpu_custom_call" | custom-call | flops 1610612736 | bytes 4194304 | tf_op jit(solution)/shard_map/pallas_call | solution.py:354
  34.9 0.0 collective-permute-done.4.refs_0_.refs_6_
  34.9 2.2 %shard_map.88 = (f32[16,1,256]{2,1,0:T(1,128)S(1)}, bf16[4,128,256]{2,1,0:T(8,128)(2,1)S(1)}) custom-call(s32[4]{0:T(128)S(1)} %dynamic-slice_bitcast_fusion.source.refs_0_, s32[16,1,256]{2,1,0:T(1,128)S(1)} %bitcast.24, bf16[4,1024,256]{2,1,0:T(8,128)(2,1)S(1)} %shard_map.86.tiles.refs_2_, f32[16,1,256]{2,1,0:T(1,128)S(1)} %get-tuple-element.11.before, ...), custom_call_target="tpu_custom_call" | custom-call | flops 536870912 | bytes 4194304 | tf_op jit(solution)/shard_map/pallas_call | solution.py:363
  37.0 0.1 broadcast_in_dim.20
  37.1 9.1 %all_to_all.5.refs_2_ = f32[8,16,1,256]{3,2,1,0:T(1,128)S(1)} all-to-all(f32[8,16,1,256]{3,2,1,0:T(1,128)S(1)} %broadcast_in_dim.20), channel_id=1, replica_groups=mesh['state'=8,'probe'=4] {'state'}, dimensions={0} | all-to-all | bytes 262144 | tf_op jit(solution)/shard_map/all_to_all | solution.py:296
  46.2 4.2 %shard_map.89 = (f32[16,1,256]{2,1,0:T(1,128)S(1)}, f32[4,256,128]{2,1,0:T(8,128)S(1)}, bf16[7,256,128]{2,1,0:T(8,128)(2,1)S(1)}, bf16[4,256,128]{2,1,0:T(8,128)(2,1)S(1)}) custom-call(s32[4]{0:T(128)S(1)} %dynamic-slice_bitcast_fusion.source.refs_0_, s32[16,1,256]{2,1,0:T(1,128)S(1)} %bitcast.25, f32[8,16,1,256]{3,2,1,0:T(1,128)S(1)} %all_to_all.5.refs_2_, ...), custom_call_target="tpu_custom_call" | custom-call | flops 2147483648 | bytes 4194304 | tf_op jit(solution)/shard_map/pallas_call | solution.py:375
  50.4 10.2 %shard_map.90 = f32[3,16,1,256]{3,2,1,0:T(1,128)S(1)} custom-call(s32[4]{0:T(128)S(1)} %dynamic-slice_bitcast_fusion.source.refs_0_, s32[16,1,256]{2,1,0:T(1,128)S(1)} %bitcast.26, bf16[4,1024,256]{2,1,0:T(8,128)(2,1)S(1)} %shard_map.86.tiles.refs_2_, bf16[12,128,256]{2,1,0:T(8,128)(2,1)S(1)} %get-tuple-element.15.refs_3_, ...), custom_call_target="tpu_custom_call" | custom-call | flops 6442450944 | bytes 4194304 | tf_op jit(solution)/shard_map/pallas_call | solution.py:385
  60.7 0.1 collective-permute-start.5
  60.7 1.2 %collective-permute-done.5 = f32[3,16,1,256]{3,2,1,0:T(1,128)S(1)} collective-permute-done((f32[3,16,1,256]{3,2,1,0:T(1,128)S(1)}, f32[3,16,1,256]{3,2,1,0:T(1,128)S(1)}, u32[]{:S(2)}, u32[]{:S(2)}) %collective-permute-start.5) | collective-permute-done | bytes 49184 | tf_op jit(solution)/shard_map/ppermute | solution.py:305
  62.0 0.1 add.17
  62.0 0.6 collective-permute-start.6
  62.6 3.5 %collective-permute-done.6 = f32[3,16,1,256]{3,2,1,0:T(1,128)S(1)} collective-permute-done((f32[3,16,1,256]{3,2,1,0:T(1,128)S(1)}, f32[3,16,1,256]{3,2,1,0:T(1,128)S(1)}, u32[]{:S(2)}, u32[]{:S(2)}) %collective-permute-start.6) | collective-permute-done | bytes 49184 | tf_op jit(solution)/shard_map/ppermute | solution.py:305
  66.2 0.1 add.18
  66.2 0.6 collective-permute-start.7
  66.8 0.0 collective-permute-start.8
  66.8 2.6 %collective-permute-start.9 = (bf16[4,256,128]{2,1,0:T(8,128)(2,1)S(1)}, bf16[4,256,128]{2,1,0:T(8,128)(2,1)S(1)}, u32[]{:S(2)}, u32[]{:S(2)}) collective-permute-start(bf16[4,256,128]{2,1,0:T(8,128)(2,1)S(1)} %get-tuple-element.19), channel_id=1, source_target_pairs={{0,28},{4,0},{8,4},{12,8},{16,12},{20,16},{24,20},{28,24},{1,29},{... | collective-permute-start | bytes 786440 | tf_op jit(solution)/shard_map/ppermute | solution.py:384
  69.5 0.9 %collective-permute-done.7 = f32[3,16,1,256]{3,2,1,0:T(1,128)S(1)} collective-permute-done((f32[3,16,1,256]{3,2,1,0:T(1,128)S(1)}, f32[3,16,1,256]{3,2,1,0:T(1,128)S(1)}, u32[]{:S(2)}, u32[]{:S(2)}) %collective-permute-start.7) | collective-permute-done | bytes 49184 | tf_op jit(solution)/shard_map/ppermute | solution.py:305
  70.4 0.1 add.19
  70.4 0.7 pad_maximum_fusion
  71.1 4.5 %collective-permute-done.9.high = bf16[4,256,128]{2,1,0:T(8,128)(2,1)S(1)} collective-permute-done((bf16[4,256,128]{2,1,0:T(8,128)(2,1)S(1)}, bf16[4,256,128]{2,1,0:T(8,128)(2,1)S(1)}, u32[]{:S(2)}, u32[]{:S(2)}) %collective-permute-start.9) | collective-permute-done | bytes 262176 | tf_op jit(solution)/shard_map/ppermute | solution.py:384
  75.6 2.8 %collective-permute-done.8.low = bf16[7,256,128]{2,1,0:T(8,128)(2,1)S(1)} collective-permute-done((bf16[7,256,128]{2,1,0:T(8,128)(2,1)S(1)}, bf16[7,256,128]{2,1,0:T(8,128)(2,1)S(1)}, u32[]{:S(2)}, u32[]{:S(2)}) %collective-permute-start.8) | collective-permute-done | bytes 458784 | tf_op jit(solution)/shard_map/ppermute | solution.py:383
  78.4 5.1 %shard_map.91 = f32[4,64,512]{2,1,0:T(8,128)} custom-call(f32[5,64,128]{2,1,0:T(8,128)S(1)} %broadcast_in_dim.8.coef, f32[4,256,128]{2,1,0:T(8,128)S(1)} %get-tuple-element.13.own, bf16[7,256,128]{2,1,0:T(8,128)(2,1)S(1)} %collective-permute-done.8.low, bf16[4,256,128]{2,1,0:T(8,128)(2,1)S(1)} %collective-permute-done.9.high), custom_call_target="tpu_custom_call" | custom-call | flops 14680064 | bytes 4194304 | tf_op jit(solution)/shard_map/pallas_call | solution.py:393
  (1 shorter events, 0.0 us)
Async XLA Ops:
  0.6 28.8 %copy-start.1 = (s32[1,4096]{1,0:T(1,128)S(1)}, s32[1,4096]{1,0:T(1,128)}, u32[]{:S(2)}) copy-start(s32[1,4096]{1,0:T(1,128)} %param.11) | copy-start | bytes 49156
  0.6 10.0 %collective-permute-start.2 = (bf16[1024,128]{1,0:T(8,128)(2,1)}, bf16[1024,128]{1,0:T(8,128)(2,1)S(1)}, u32[]{:S(2)}, u32[]{:S(2)}) collective-permute-start(bf16[1024,128]{1,0:T(8,128)(2,1)} %bitcast.28), channel_id=1, source_target_pairs={{0,2},{2,3},{3,1},{1,0},{4,6},{6,7},{7,5},{5,4},{8,10},{10,11},{11... | collective-permute-start | bytes 786440 | tf_op jit(solution)/shard_map/ppermute | solution.py:326
  4.7 17.9 %collective-permute-start.1 = (f32[4,64,512]{2,1,0:T(8,128)}, f32[4,64,512]{2,1,0:T(8,128)S(1)}, u32[]{:S(2)}, u32[]{:S(2)}) collective-permute-start(f32[4,64,512]{2,1,0:T(8,128)} %bitcast.20), channel_id=1, source_target_pairs={{0,28},{4,0},{8,4},{12,8},{16,12},{20,16},{24,20},{28,24},{1,29},{... | collective-permute-start | bytes 1572872 | tf_op jit(solution)/shard_map/ppermute | solution.py:332
  6.3 16.3 %collective-permute-start = (f32[4,64,512]{2,1,0:T(8,128)}, f32[4,64,512]{2,1,0:T(8,128)S(1)}, u32[]{:S(2)}, u32[]{:S(2)}) collective-permute-start(f32[4,64,512]{2,1,0:T(8,128)} %bitcast.21), channel_id=1, source_target_pairs={{0,4},{4,8},{8,12},{12,16},{16,20},{20,24},{24,28},{28,0},{1,5},{5... | collective-permute-start | bytes 1572872 | tf_op jit(solution)/shard_map/ppermute | solution.py:331
  10.6 8.0 %collective-permute-start.3 = (bf16[1024,128]{1,0:T(8,128)(2,1)S(1)}, bf16[1024,128]{1,0:T(8,128)(2,1)S(1)}, u32[]{:S(2)}, u32[]{:S(2)}) collective-permute-start(bf16[1024,128]{1,0:T(8,128)(2,1)S(1)} %collective-permute-done.2.refs_1_.refs_4_), channel_id=1, source_target_pairs={{0,2},{2,3},{3,1},{1,0},{4,6},{6,7},{7,5},{5,4},{8,10},{10,11},{11... | collective-permute-start | bytes 786440 | tf_op jit(solution)/shard_map/ppermute | solution.py:326
  18.6 16.3 %collective-permute-start.4 = (bf16[1024,128]{1,0:T(8,128)(2,1)S(1)}, bf16[1024,128]{1,0:T(8,128)(2,1)S(1)}, u32[]{:S(2)}, u32[]{:S(2)}) collective-permute-start(bf16[1024,128]{1,0:T(8,128)(2,1)S(1)} %collective-permute-done.3.refs_2_.refs_5_), channel_id=1, source_target_pairs={{0,2},{2,3},{3,1},{1,0},{4,6},{6,7},{7,5},{5,4},{8,10},{10,11},{11... | collective-permute-start | bytes 786440 | tf_op jit(solution)/shard_map/ppermute | solution.py:326
  22.8 1.0 %copy-start = (f32[1,4,64,512]{3,2,1,0:T(8,128)S(1)}, f32[1,4,64,512]{3,2,1,0:T(8,128)}, u32[]{:S(2)}) copy-start(f32[1,4,64,512]{3,2,1,0:T(8,128)} %param.7) | copy-start | bytes 1572868
  23.8 5.7 %copy-start.2 = (bf16[1,1024,128]{2,1,0:T(8,128)(2,1)S(1)}, bf16[1,1024,128]{2,1,0:T(8,128)(2,1)}, u32[]{:S(2)}) copy-start(bf16[1,1024,128]{2,1,0:T(8,128)(2,1)} %param.12) | copy-start | bytes 786436
  60.7 1.3 %collective-permute-start.5 = (f32[3,16,1,256]{3,2,1,0:T(1,128)S(1)}, f32[3,16,1,256]{3,2,1,0:T(1,128)S(1)}, u32[]{:S(2)}, u32[]{:S(2)}) collective-permute-start(f32[3,16,1,256]{3,2,1,0:T(1,128)S(1)} %shard_map.90), channel_id=1, source_target_pairs={{0,4},{4,0},{8,12},{12,8},{16,20},{20,16},{24,28},{28,24},{1,5},{5... | collective-permute-start | bytes 147464 | tf_op jit(solution)/shard_map/ppermute | solution.py:305
  62.0 4.2 %collective-permute-start.6 = (f32[3,16,1,256]{3,2,1,0:T(1,128)S(1)}, f32[3,16,1,256]{3,2,1,0:T(1,128)S(1)}, u32[]{:S(2)}, u32[]{:S(2)}) collective-permute-start(f32[3,16,1,256]{3,2,1,0:T(1,128)S(1)} %add.17), channel_id=1, source_target_pairs={{0,8},{4,12},{8,0},{12,4},{16,24},{20,28},{24,16},{28,20},{1,9},{5... | collective-permute-start | bytes 147464 | tf_op jit(solution)/shard_map/ppermute | solution.py:305
  66.2 4.2 %collective-permute-start.7 = (f32[3,16,1,256]{3,2,1,0:T(1,128)S(1)}, f32[3,16,1,256]{3,2,1,0:T(1,128)S(1)}, u32[]{:S(2)}, u32[]{:S(2)}) collective-permute-start(f32[3,16,1,256]{3,2,1,0:T(1,128)S(1)} %add.18), channel_id=1, source_target_pairs={{0,16},{4,20},{8,24},{12,28},{16,0},{20,4},{24,8},{28,12},{1,17},{... | collective-permute-start | bytes 147464 | tf_op jit(solution)/shard_map/ppermute | solution.py:305
  66.8 11.6 %collective-permute-start.8 = (bf16[7,256,128]{2,1,0:T(8,128)(2,1)S(1)}, bf16[7,256,128]{2,1,0:T(8,128)(2,1)S(1)}, u32[]{:S(2)}, u32[]{:S(2)}) collective-permute-start(bf16[7,256,128]{2,1,0:T(8,128)(2,1)S(1)} %get-tuple-element.18), channel_id=1, source_target_pairs={{0,4},{4,8},{8,12},{12,16},{16,20},{20,24},{24,28},{28,0},{1,5},{5... | collective-permute-start | bytes 1376264 | tf_op jit(solution)/shard_map/ppermute | solution.py:383
  66.8 8.8 %collective-permute-start.9 = (bf16[4,256,128]{2,1,0:T(8,128)(2,1)S(1)}, bf16[4,256,128]{2,1,0:T(8,128)(2,1)S(1)}, u32[]{:S(2)}, u32[]{:S(2)}) collective-permute-start(bf16[4,256,128]{2,1,0:T(8,128)(2,1)S(1)} %get-tuple-element.19), channel_id=1, source_target_pairs={{0,28},{4,0},{8,4},{12,8},{16,12},{20,16},{24,20},{28,24},{1,29},{... | collective-permute-start | bytes 786440 | tf_op jit(solution)/shard_map/ppermute | solution.py:384

commit v3 on v2

v3 whole, which is shorter than its diff:
```python
import jax
import jax.numpy as jnp
from jax import lax
from jax.experimental import pallas as pl
from jax.experimental.pallas import tpu as pltpu
from jax.sharding import PartitionSpec as P

TILE = 128
STEPS = 4
PAD = 8
GROUP = 256
VMEM_LIMIT = 48 * 1024 * 1024


def shift_pairs(count, by):
    return [(i, (i + by) % count) for i in range(count)]


def clear_pads(buffer):
    planes, columns, rows, lanes = buffer.shape
    edge = jnp.zeros((columns, PAD, lanes), buffer.dtype)

    def body(plane, carry):
        buffer[plane, :, :PAD, :] = edge
        buffer[plane, :, rows - PAD :, :] = edge
        return carry

    lax.fori_loop(0, planes, body, 0)


def stencil_block(source, coef, plane, row, height, adjoint):
    centre = source[plane, :, pl.ds(PAD + row, height), :]
    above = source[plane, :, pl.ds(PAD + row + 1, height), :]
    below = source[plane, :, pl.ds(PAD + row - 1, height), :]
    upper_x = source[plane + 1, :, pl.ds(PAD + row, height), :]
    lower_x = source[plane - 1, :, pl.ds(PAD + row, height), :]
    columns = centre.shape[0]
    lane = lax.broadcasted_iota(jnp.int32, (height, TILE), 1)
    left = [pltpu.roll(centre[c], TILE - 1, 1) for c in range(columns)]
    right = [pltpu.roll(centre[c], 1, 1) for c in range(columns)]
    block = pl.ds(row, height)
    w_centre, w_up, w_diff = coef[0, block, :], coef[1, block, :], coef[2, block, :]
    out = []
    for c in range(columns):
        upper_z = jnp.where(lane == TILE - 1, left[(c + 1) % columns], left[c])
        lower_z = jnp.where(lane == 0, right[(c - 1) % columns], right[c])
        if adjoint:
            total = w_centre * centre[c] + w_up * upper_x[c]
            total = total + w_diff * (lower_x[c] + (upper_z + lower_z))
            total = total + coef[3, block, :] * above[c] + coef[4, block, :] * below[c]
        else:
            total = w_centre * centre[c] + w_up * lower_x[c]
            total = total + w_diff * ((upper_x[c] + (upper_z + lower_z)) + (above[c] + below[c]))
        out.append(total)
    return out


def split(value):
    high = value.astype(jnp.bfloat16)
    low = (value - high.astype(jnp.float32)).astype(jnp.bfloat16)
    return high, low


def shifted_plane(field, plane, offset):
    height, width = field.shape[1:]
    columns = width // TILE
    turn, rest = offset // TILE, offset % TILE
    lane = lax.broadcasted_iota(jnp.int32, (height, TILE), 1)
    rolled = [pltpu.roll(field[plane, :, pl.ds(c * TILE, TILE)], rest, 1) for c in range(columns)]
    return [
        (lax.rem(c + turn, columns), jnp.where(lane >= rest, rolled[c], rolled[c - 1]))
        for c in range(columns)
    ]


def prelude_kernel(columns, height, offset, field, courant, diffusivity, above, below, tile, own, coef, wanted):
    def load(plane, carry):
        for column, value in shifted_plane(field, plane, offset[0]):
            own[plane, column] = value
        return carry

    lax.fori_loop(0, field.shape[0], load, 0)
    rates = (
        1.0 - courant[...] - 6.0 * diffusivity[...],
        courant[...] + diffusivity[...],
        diffusivity[...],
        above[...],
        below[...],
    )
    for place, rate in enumerate(rates):
        coef[place] = jnp.broadcast_to(rate, coef.shape[1:])
    inside = tile[...] & (columns * height - 1)
    wanted[...] = (tile[...] - inside) + (inside & (columns - 1)) * height + inside // columns


def adjoint_kernel(offset, coef, own, low, high, tiles, first, second):
    cells, columns, height = own.shape[:3]
    steps = tiles.shape[0]
    inside = pl.ds(PAD, height)
    clear_pads(first)
    clear_pads(second)

    def load(plane, carry):
        for slab, field in ((0, low), (2, high)):
            for column, value in shifted_plane(field, plane, offset[0]):
                first[slab * cells + plane, column, inside, :] = value
        first[cells + plane, :, inside, :] = own[plane]
        return carry

    lax.fori_loop(0, cells, load, 0)
    buffers = (first, second)
    rows = 8
    for step in range(steps):
        source, target = buffers[step % 2], buffers[(step + 1) % 2]

        def sweep(plane, carry, source=source, target=target, step=step, keep=False):
            blocks = [
                stencil_block(source, coef, plane, row, rows, True)
                for row in range(0, height, rows)
            ]
            for c in range(columns):
                value = jnp.concatenate([block[c] for block in blocks], axis=0)
                target[plane, c, inside, :] = value
                if keep:
                    start = (plane - cells) * columns * height + c * height
                    where = pl.ds(pl.multiple_of(start, height), height)
                    head, tail = split(value)
                    tiles[step, where, pl.ds(0, TILE)] = head
                    tiles[step, where, pl.ds(TILE, TILE)] = tail
            return carry

        def inner(plane, carry, sweep=sweep):
            return sweep(plane, carry, keep=True)

        if step < steps - 1:
            lax.fori_loop(step + 1, cells, sweep, 0)
        lax.fori_loop(cells, 2 * cells, inner, 0)
        if step < steps - 1:
            lax.fori_loop(2 * cells, 3 * cells - step - 1, sweep, 0)


def forward_kernel(coef, own, low, high, out, first, second):
    cells, height, width = out.shape
    columns = width // TILE
    steps = STEPS
    clear_pads(first)
    clear_pads(second)
    for plane in range(cells):
        for c in range(columns):
            where = pl.ds(c * height, height)
            inside = pl.ds(PAD, height)
            first[cells + plane, c, inside, :] = own[plane, where, :]
            first[2 * cells + plane, c, inside, :] = high[plane, where, :].astype(jnp.float32)
            value = low[plane, where, :].astype(jnp.float32)
            if plane > 0:
                value = value + low[cells + plane - 1, where, :].astype(jnp.float32)
            first[plane, c, inside, :] = value
    buffers = (first, second)
    rows = 8
    for step in range(steps):
        source, target = buffers[step % 2], buffers[(step + 1) % 2]
        last = step == steps - 1

        def body(plane, carry, source=source, target=target, last=last):
            blocks = [
                stencil_block(source, coef, plane, row, rows, False)
                for row in range(0, height, rows)
            ]
            for c in range(columns):
                value = jnp.concatenate([block[c] for block in blocks], axis=0)
                if last:
                    out[plane - cells, :, pl.ds(c * TILE, TILE)] = value
                else:
                    target[plane, c, pl.ds(PAD, height), :] = value
            return carry

        lax.fori_loop(step + 1, 3 * cells - step - 1, body, 0)


def kept_sum(tiles, step, weights, wanted):
    chunk = 256
    partial = jnp.zeros((8, GROUP), jnp.float32)
    for start in range(0, tiles.shape[1], chunk):
        gram = lax.dot_general(
            tiles[step, pl.ds(start, chunk), :],
            weights,
            (((1,), (1,)), ((), ())),
            preferred_element_type=jnp.float32,
        )
        number = lax.broadcasted_iota(jnp.int32, (chunk, GROUP), 0) + start
        kept = jnp.where(number == wanted, gram, 0.0)
        partial = partial + jnp.sum(kept.reshape(chunk // 8, 8, GROUP), axis=0)
    return jnp.sum(partial, axis=0, keepdims=True)


def project_kernel(steps, chunks, source, wanted, tiles, *refs):
    panels, (*before, out) = refs[: len(chunks)], refs[len(chunks) :]
    shard = panels[0].shape[0] // GROUP
    for given in before:
        out[...] = given[...]
    for chunk, panel in zip(chunks, panels):

        def body(place, carry, chunk=chunk, panel=panel):
            step = steps[0] + place if len(steps) > 1 else steps[0]
            results = []
            for group in range(shard):
                rows = panel[pl.ds(group * GROUP, GROUP), :]
                number = source[chunk] * shard + group
                weights = jnp.concatenate([rows, rows], axis=1)
                results.append((number, kept_sum(tiles, step, weights, wanted[number])))
            for number, result in results:
                if len(steps) > 1:
                    out[place, number] = result
                else:
                    out[number] = result
            return carry

        if len(steps) > 1:
            lax.fori_loop(0, len(steps), body, 0)
        else:
            body(0, 0)


def deposit_kernel(count, source, wanted, *refs):
    parts, panels, (total, field, rightward, leftward, scaled) = refs[:count], refs[count:-5], refs[-5:]
    groups = wanted.shape[0]
    shard = groups // len(panels)
    cells, per_plane = field.shape[0], field.shape[1]
    total[...] = tree_sum([part[...] for part in parts])
    numbers = [source[g // shard] * shard + g % shard for g in range(groups)]
    drive = jnp.concatenate([total[number] for number in numbers], axis=0).T
    for group in range(groups):
        rows = panels[group // shard][pl.ds((group % shard) * GROUP, GROUP), :]
        head, tail = split(drive[:, group : group + 1] * rows.astype(jnp.float32))
        where = pl.ds(group * GROUP, GROUP)
        scaled[where, pl.ds(0, TILE)] = head
        scaled[where, pl.ds(TILE, TILE)] = tail

    def body(plane, carry):
        number = lax.broadcasted_iota(jnp.int32, (per_plane, GROUP), 0) + plane * per_plane
        sums = jnp.zeros((per_plane, 2 * TILE), jnp.float32)
        for group in range(groups):
            chosen = jnp.where(number == wanted[numbers[group]], 1.0, 0.0).astype(jnp.bfloat16)
            sums = sums + jnp.dot(
                chosen,
                scaled[pl.ds(group * GROUP, GROUP), :],
                preferred_element_type=jnp.float32,
            )
        value = sums[:, :TILE] + sums[:, TILE:]
        field[plane] = value
        head, tail = split(value)
        leftward[plane] = head
        rightward[plane] = head

        @pl.when(plane > 0)
        def _():
            rightward[cells + plane - 1] = tail

        return carry

    lax.fori_loop(0, cells, body, 0)


def call(kernel, out_shape, scratch=(), smem=0, inputs=0, flops=0):
    in_specs = [pl.BlockSpec(memory_space=pltpu.SMEM)] * smem
    in_specs += [pl.BlockSpec(memory_space=pltpu.VMEM)] * (inputs - smem)
    out_specs = jax.tree.map(lambda _: pl.BlockSpec(memory_space=pltpu.VMEM), out_shape)
    return pl.pallas_call(
        kernel,
        out_shape=out_shape,
        in_specs=in_specs,
        out_specs=out_specs,
        scratch_shapes=list(scratch),
        compiler_params=pltpu.CompilerParams(vmem_limit_bytes=VMEM_LIMIT),
        cost_estimate=pl.CostEstimate(
            flops=flops, bytes_accessed=1024 * 1024 if flops else 1024, transcendentals=0
        ),
    )


def gathered_panel(panel, axis):
    count = lax.axis_size(axis)
    shards = {0: panel}
    mask = count // 2
    while mask:
        pairs = [(i, i ^ mask) for i in range(count)]
        for held in sorted(shards):
            shards[held | mask] = lax.ppermute(shards[held], axis, pairs)
        mask //= 2
    return [shards[k] for k in range(count)]


def tied(value, *others):
    return lax.optimization_barrier((value,) + others)[0]


def tree_sum(parts):
    while len(parts) > 1:
        parts = [parts[i] + parts[i + 1] for i in range(0, len(parts), 2)]
    return parts[0]


def summands(part, axis):
    count = lax.axis_size(axis)
    if count & (count - 1):
        return [lax.psum(part, axis)]
    done, parts = 1, [part]
    for span in (2, 4, 4, 4, 4):
        span = min(span, count // done)
        if span > 1:
            part = tree_sum(parts)
            pairs = [[(i, i ^ (k * done)) for i in range(count)] for k in range(1, span)]
            parts = [part] + [lax.ppermute(part, axis, pair) for pair in pairs]
            done *= span
    return parts


def doubling_sum(part, axis):
    count = lax.axis_size(axis)
    if count & (count - 1):
        return lax.psum(part, axis)
    mask = 1
    while mask < count:
        part = part + lax.ppermute(part, axis, [(i, i ^ mask) for i in range(count)])
        mask *= 2
    return part


def local(sensor_field, courant, diffusivity, probe_offset, tile_index, actuator_panel):
    slabs, probes = lax.axis_size("state"), lax.axis_size("probe")
    own = sensor_field[0]
    cells, height, width = own.shape
    columns = width // TILE
    tile_total = cells * height * columns
    actuators = tile_index.shape[1]
    groups = actuators // GROUP
    shard = groups // probes
    planes = 3 * cells
    f32, bf16 = jnp.float32, jnp.bfloat16

    panels = gathered_panel(actuator_panel[0], "probe")
    source = lax.axis_index("probe") ^ jnp.arange(probes, dtype=jnp.int32)
    low = lax.ppermute(own, "state", shift_pairs(slabs, 1))
    high = lax.ppermute(own, "state", shift_pairs(slabs, -1))

    zero = jnp.zeros((1,), f32)
    rates = [
        courant,
        diffusivity,
        jnp.concatenate([diffusivity[1:], zero]),
        jnp.concatenate([zero, diffusivity[:-1]]),
    ]
    shifted, coef, wanted = call(
        lambda *refs: prelude_kernel(columns, height, *refs),
        (
            jax.ShapeDtypeStruct((cells, columns, height, TILE), f32),
            jax.ShapeDtypeStruct((5, height, TILE), f32),
            jax.ShapeDtypeStruct((groups, 1, GROUP), jnp.int32),
        ),
        smem=1,
        inputs=7,
    )(probe_offset, own, *[rate[:, None] for rate in rates], tile_index.reshape(groups, 1, GROUP))

    field_shape = pltpu.VMEM((planes, columns, height + 2 * PAD, TILE), f32)
    tiles = call(
        adjoint_kernel,
        jax.ShapeDtypeStruct((STEPS, tile_total, 2 * TILE), bf16),
        scratch=(field_shape, field_shape),
        smem=1,
        inputs=5,
        flops=28 * 16 * height * width,
    )(probe_offset, coef, shifted, low, high)

    row_shape = jax.ShapeDtypeStruct((groups, 1, GROUP), f32)
    step_flops = 2 * GROUP * tile_total * 2 * TILE
    every = list(range(probes))
    before = call(
        lambda *refs: project_kernel([STEPS - 1], every[:-1], *refs),
        row_shape,
        smem=1,
        inputs=2 + probes,
        flops=step_flops * shard * (probes - 1),
    )(source, wanted, tiles, *panels[:-1])
    last = call(
        lambda *refs: project_kernel([STEPS - 1], every[-1:], *refs),
        row_shape,
        smem=1,
        inputs=5,
        flops=step_flops * shard,
    )(source, wanted, tiles, panels[-1], before)
    parts = summands(last, "state")
    payload = jax.ShapeDtypeStruct((2 * cells - 1, height * columns, TILE), bf16)
    heads = jax.ShapeDtypeStruct((cells, height * columns, TILE), bf16)
    total, forced, rightward, leftward = call(
        lambda *refs: deposit_kernel(len(parts), *refs),
        (row_shape, jax.ShapeDtypeStruct((cells, height * columns, TILE), f32), payload, heads),
        scratch=(pltpu.VMEM((actuators, 2 * TILE), bf16),),
        smem=1,
        inputs=2 + len(parts) + probes,
        flops=step_flops * groups,
    )(source, wanted, *parts, *panels)
    from_low = lax.ppermute(rightward, "state", shift_pairs(slabs, 1))
    from_high = lax.ppermute(leftward, "state", shift_pairs(slabs, -1))
    early = call(
        lambda *refs: project_kernel(list(range(STEPS - 1)), every, *refs),
        jax.ShapeDtypeStruct((STEPS - 1, groups, 1, GROUP), f32),
        smem=1,
        inputs=3 + probes,
    )(source, tied(wanted, forced), tiles, *panels)
    rounds = 1 + jnp.minimum(probe_offset[0], 0)
    early = lax.fori_loop(0, rounds, lambda _, part: doubling_sum(part, "state"), early)
    response = call(
        forward_kernel,
        jax.ShapeDtypeStruct((cells, height, width), f32),
        scratch=(field_shape, field_shape),
        inputs=4,
        flops=28 * 16 * height * width,
    )(coef, forced, from_low, from_high)
    projections = jnp.concatenate([early, total[None]], axis=0)
    return projections.reshape(STEPS, 1, actuators), response[None]


def solution(mesh):
    return jax.shard_map(
        local,
        mesh=mesh,
        in_specs=(
            P("probe", "state", None, None),
            P(),
            P(),
            P("probe"),
            P("state", None),
            P("state", "probe", None),
        ),
        out_specs=(P(None, "probe", None), P("probe", "state", None, None)),
        check_vma=False,
    )
```

time: 83.8 us -> 79.8 us (0.952)
  blocking collectives: 9.05 us -> 0 us
  local copies, waits for them, and re-layouts: 3.38 us -> 9.37 us
  waiting for transfers between devices: 19 us -> 16 us
  other arithmetic: 1.6 us -> 3.16 us
  starting transfers between devices: 16.3 us -> 17.6 us
  Pallas kernels: 32.7 us -> 31.6 us
    all_to_all x1 -> x0, blocking collectives: 9.05 us -> none  [gathered(): return lax.all_to_all(copies, axis, 0, 0)]
    unnamed x7 -> x18, local copies, waits for them, and re-layouts: 1.05 us -> 6.89 us
    ppermute x1, waiting for transfers between devices: 4.48 us -> 0.01 us  [local(): from_high = lax.ppermute(leftward, 'state', shift_pairs(slabs, -1))]
    ppermute x1, waiting for transfers between devices: 2.82 us -> 0.01 us  [local(): from_low = lax.ppermute(rightward, 'state', shift_pairs(slabs, 1))]
    ppermute x3 -> x7, waiting for transfers between devices: 6.08 us -> 8.59 us  [the longest x4 4.31 us: summands(): parts = [part] + [lax.ppermute(part, axis, pair) for pair in pairs]]
    ppermute x3, waiting for transfers between devices: 5.66 us -> 7.44 us  [doubling_sum(): lax.ppermute(part, axis, [(i, i ^ mask) for i in range(count)])]
    ppermute x3 -> x7, starting transfers between devices: 10.7 us -> 9.15 us  [the longest x3 5.53 us: gathered_panel(): shards[held | mask] = lax.ppermute(shards[held], axis, pairs)]
    broadcast_in_dim x2 -> x4, local copies, waits for them, and re-layouts: 0.17 us -> 1.68 us  [local(): rate[:, None]]
  transfers between devices with their start and end apart: 10 -> 14, of which waited for: 7 -> 8; matrix products, arithmetic and copies ran while one was open for 4% -> 7% of each run, Pallas kernels for 13% -> 24%
where the time goes in v3:
time: 79.8 us; the launch traced here: 79.2 us
  Pallas kernels  31.6 us (40%)
  starting transfers between devices  17.6 us (22%)
  waiting for transfers between devices  16 us (20%)
  local copies, waits for them, and re-layouts  9.37 us (12%)
  other arithmetic  3.16 us (4%)
  between operations  1.38 us (2%)
    pallas_call x1, Pallas kernels, local(): call(lambda *refs: project_kernel(list(range(STEPS - 1)), every, *refs),...  10.7 us
    ppermute x3, waiting for transfers between devices, doubling_sum(): lax.ppermute(part, axis, [(i, i ^ mask) for i in range(count)])  7.44 us
    unnamed x18, local copies, waits for them, and re-layouts  6.89 us
    pallas_call x1, Pallas kernels, local(): call(forward_kernel, jax.ShapeDtypeStruct((cells, height, width), f32), s...  5.94 us
    ppermute x3, starting transfers between devices, gathered_panel(): shards[held | mask] = lax.ppermute(shards[held], axis, pairs)  5.53 us
    pallas_call x1, Pallas kernels, local(): call(lambda *refs: deposit_kernel(len(parts), *refs), (row_shape, jax.Sha...  5.31 us
    pallas_call x1, Pallas kernels, local(): call(adjoint_kernel, jax.ShapeDtypeStruct((STEPS, tile_total, 2 * TILE),...  4.99 us
    ppermute x4, waiting for transfers between devices, summands(): parts = [part] + [lax.ppermute(part, axis, pair) for pair in pairs]  4.31 us
  transfers between devices with their start and end apart: 14, of which 8 were waited for; matrix products, arithmetic and copies ran while one was open for 7% of the time, Pallas kernels for 24%

profile of v3, /device:TPU:0, one launch (start us, length us, event | category | flops | bytes accessed | tf_op | source)
XLA Modules:
  0.0 79.2 jit_solution(17820419719808550546)
XLA Ops:
  0.6 0.5 collective-permute-start.3
  1.1 2.9 %collective-permute-start.4 = (f32[4,64,512]{2,1,0:T(8,128)}, f32[4,64,512]{2,1,0:T(8,128)S(1)}, u32[]{:S(2)}, u32[]{:S(2)}) collective-permute-start(f32[4,64,512]{2,1,0:T(8,128)} %bitcast.14), channel_id=1, source_target_pairs={{0,28},{4,0},{8,4},{12,8},{16,12},{20,16},{24,20},{28,24},{1,29},{... | collective-permute-start | bytes 1572872 | tf_op jit(solution)/shard_map/ppermute | solution.py:344
  4.1 3.3 %collective-permute-start.5 = (bf16[1024,128]{1,0:T(8,128)(2,1)}, bf16[1024,128]{1,0:T(8,128)(2,1)S(1)}, u32[]{:S(2)}, u32[]{:S(2)}) collective-permute-start(bf16[1024,128]{1,0:T(8,128)(2,1)} %bitcast.16), channel_id=1, source_target_pairs={{0,2},{1,3},{2,0},{3,1},{4,6},{5,7},{6,4},{7,5},{8,10},{9,11},{10,... | collective-permute-start | bytes 786440 | tf_op jit(solution)/shard_map/ppermute | solution.py:288
  7.4 1.6 %collective-permute-start.7 = (bf16[1024,128]{1,0:T(8,128)(2,1)}, bf16[1024,128]{1,0:T(8,128)(2,1)}, u32[]{:S(2)}, u32[]{:S(2)}) collective-permute-start(bf16[1024,128]{1,0:T(8,128)(2,1)} %bitcast.17), channel_id=1, source_target_pairs={{0,1},{1,0},{2,3},{3,2},{4,5},{5,4},{6,7},{7,6},{8,9},{9,8},{10,11... | collective-permute-start | bytes 786440 | tf_op jit(solution)/shard_map/ppermute | solution.py:288
  8.9 0.8 %fusion = (f32[63]{0:T(128)S(1)}, f32[63]{0:T(128)S(1)}) fusion(f32[64]{0:T(128)} %param.10), kind=kLoop, calls=%fused_computation.4 | loop fusion | bytes 1008 | tf_op jit(solution)/shard_map/slice | solution.py:351
  10.4 0.7 copy.8.refs_2_
  11.1 0.7 copy.9.refs_3_
  11.9 0.1 maximum_bitcast_fusion
  12.0 0.1 copy.10.refs_4_
  12.1 0.1 copy.11.refs_5_
  12.2 0.0 copy-start
  12.2 1.0 %copy-done = f32[1,4,64,512]{3,2,1,0:T(8,128)S(1)} copy-done((f32[1,4,64,512]{3,2,1,0:T(8,128)S(1)}, f32[1,4,64,512]{3,2,1,0:T(8,128)}, u32[]{:S(2)}) %copy-start) | copy-done | bytes 524312
  13.2 0.0 copy-start.7
  13.2 0.7 copy-done.7
  13.9 0.0 copy-start.3
  13.9 0.6 shard_map.77
  14.5 4.3 %collective-permute-done.5.refs_5_.refs_8_ = bf16[1024,128]{1,0:T(8,128)(2,1)S(1)} collective-permute-done((bf16[1024,128]{1,0:T(8,128)(2,1)}, bf16[1024,128]{1,0:T(8,128)(2,1)S(1)}, u32[]{:S(2)}, u32[]{:S(2)}) %collective-permute-start.5) | collective-permute-done | bytes 262176 | tf_op jit(solution)/shard_map/ppermute | solution.py:288
  18.8 0.7 collective-permute-start.6
  19.5 0.0 collective-permute-done.3.low
  19.5 0.0 collective-permute-done.4.high
  19.5 0.0 copy-start.1
  19.5 0.8 copy-done.1
  20.3 0.0 copy-start.2
  20.3 1.0 %copy-done.2 = f32[4,64,512]{2,1,0:T(8,128)S(1)} copy-done((f32[4,64,512]{2,1,0:T(8,128)S(1)}, f32[4,64,512]{2,1,0:T(8,128)}, u32[]{:S(2)}) %copy-start.2) | copy-done | bytes 524312
  21.3 5.0 %shard_map.78.refs_2_ = bf16[4,1024,256]{2,1,0:T(8,128)(2,1)S(1)} custom-call(s32[1]{0:T(128)S(6)} %copy.19.refs_0_.offset, f32[5,64,128]{2,1,0:T(8,128)S(1)} %get-tuple-element.29.coef, f32[4,4,64,128]{3,2,1,0:T(8,128)S(1)} %get-tuple-element.30.own, f32[4,64,512]{2,1,0:T(8,128)S(1)} %collective-permute-done.3.low, f32[4,64,512]{2,1,0:T(8,128)S(1)} %copy-done.2), custom_call_target="tpu_custom_call" | custom-call | flops 14680064 | bytes 1048576 | tf_op jit(solution)/shard_map/pallas_call | solution.py:365
  26.3 0.0 collective-permute-done.7.refs_4_.refs_7_
  26.3 0.0 copy-done.3
  26.3 2.8 %shard_map.79.refs_4_ = f32[16,1,256]{2,1,0:T(1,128)S(1)} custom-call(s32[4]{0:T(128)S(1)} %iota_xor_fusion.refs_0_, s32[16,1,256]{2,1,0:T(1,128)S(1)} %get-tuple-element.32.refs_1_, bf16[4,1024,256]{2,1,0:T(8,128)(2,1)S(1)} %shard_map.78.refs_2_, bf16[1024,128]{1,0:T(8,128)(2,1)S(1)} %bitcast.18, bf16[1024,128]{1,0:T(8,128)(2,1)} %collective-permute-done.7.refs_4_.refs_7_, ...), custom_call_target="tpu_custom_call" | custom-call | flops 1610612736 | bytes 1048576 | tf_op jit(solution)/shard_map/pallas_call | solution.py:377
  29.1 0.0 collective-permute-done.6.refs_3_.refs_9_.refs_6_
  29.2 1.3 %shard_map.80 = f32[16,1,256]{2,1,0:T(1,128)S(1)} custom-call(s32[4]{0:T(128)S(1)} %iota_xor_fusion.refs_0_, s32[16,1,256]{2,1,0:T(1,128)S(1)} %get-tuple-element.32.refs_1_, bf16[4,1024,256]{2,1,0:T(8,128)(2,1)S(1)} %shard_map.78.refs_2_, bf16[1024,128]{1,0:T(8,128)(2,1)S(1)} %collective-permute-done.6.refs_3_.refs_9_.refs_6_, ...), custom_call_target="tpu_custom_call" | custom-call | flops 536870912 | bytes 1048576 | tf_op jit(solution)/shard_map/pallas_call | solution.py:384
  30.5 0.1 collective-permute-start.8
  30.5 1.2 %collective-permute-done.8 = f32[16,1,256]{2,1,0:T(1,128)S(1)} collective-permute-done((f32[16,1,256]{2,1,0:T(1,128)S(1)}, f32[16,1,256]{2,1,0:T(1,128)S(1)}, u32[]{:S(2)}, u32[]{:S(2)}) %collective-permute-start.8) | collective-permute-done | bytes 16416 | tf_op jit(solution)/shard_map/ppermute | solution.py:313
  31.7 1.6 %collective-permute-start.9 = (f32[16,1,256]{2,1,0:T(1,128)S(1)}, f32[16,1,256]{2,1,0:T(1,128)S(1)}, u32[]{:S(2)}, u32[]{:S(2)}) collective-permute-start(f32[16,1,256]{2,1,0:T(1,128)S(1)} %add.21.refs_2_), channel_id=1, source_target_pairs={{0,8},{4,12},{8,0},{12,4},{16,24},{20,28},{24,16},{28,20},{1,9},{5... | collective-permute-start | bytes 49160 | tf_op jit(solution)/shard_map/ppermute | solution.py:313
  33.3 0.5 collective-permute-start.10
  33.8 1.5 %collective-permute-start.11 = (f32[16,1,256]{2,1,0:T(1,128)S(1)}, f32[16,1,256]{2,1,0:T(1,128)S(1)}, u32[]{:S(2)}, u32[]{:S(2)}) collective-permute-start(f32[16,1,256]{2,1,0:T(1,128)S(1)} %add.21.refs_2_), channel_id=1, source_target_pairs={{0,24},{4,28},{8,16},{12,20},{16,8},{20,12},{24,0},{28,4},{1,25},{... | collective-permute-start | bytes 49160 | tf_op jit(solution)/shard_map/ppermute | solution.py:313
  35.3 0.2 collective-permute-done.9.refs_3_
  35.5 1.7 %collective-permute-done.10.refs_4_ = f32[16,1,256]{2,1,0:T(1,128)S(1)} collective-permute-done((f32[16,1,256]{2,1,0:T(1,128)S(1)}, f32[16,1,256]{2,1,0:T(1,128)S(1)}, u32[]{:S(2)}, u32[]{:S(2)}) %collective-permute-start.10) | collective-permute-done | bytes 16416 | tf_op jit(solution)/shard_map/ppermute | solution.py:313
  37.2 1.2 %collective-permute-done.11.refs_5_ = f32[16,1,256]{2,1,0:T(1,128)S(1)} collective-permute-done((f32[16,1,256]{2,1,0:T(1,128)S(1)}, f32[16,1,256]{2,1,0:T(1,128)S(1)}, u32[]{:S(2)}, u32[]{:S(2)}) %collective-permute-start.11) | collective-permute-done | bytes 16416 | tf_op jit(solution)/shard_map/ppermute | solution.py:313
  38.4 5.3 %shard_map.81 = (f32[16,1,256]{2,1,0:T(1,128)S(1)}, f32[4,256,128]{2,1,0:T(8,128)S(1)}, bf16[7,256,128]{2,1,0:T(8,128)(2,1)}, bf16[4,256,128]{2,1,0:T(8,128)(2,1)S(1)}) custom-call(s32[4]{0:T(128)S(1)} %iota_xor_fusion.refs_0_, s32[16,1,256]{2,1,0:T(1,128)S(1)} %get-tuple-element.32.refs_1_, f32[16,1,256]{2,1,0:T(1,128)S(1)} %add.21.refs_2_, ...), custom_call_target="tpu_custom_call" | custom-call | flops 2147483648 | bytes 1048576 | tf_op jit(solution)/shard_map/pallas_call | solution.py:394
  43.7 0.0 copy-start.5
  43.7 0.7 copy-done.5
  44.4 0.0 copy-start.8
  44.5 0.7 copy-done.8
  45.1 0.0 collective-permute-start.12
  45.1 2.6 %collective-permute-start.13 = (bf16[4,256,128]{2,1,0:T(8,128)(2,1)}, bf16[4,256,128]{2,1,0:T(8,128)(2,1)}, u32[]{:S(2)}, u32[]{:S(2)}) collective-permute-start(bf16[4,256,128]{2,1,0:T(8,128)(2,1)} %copy-done.8), channel_id=1, source_target_pairs={{0,28},{4,0},{8,4},{12,8},{16,12},{20,16},{24,20},{28,24},{1,29},{... | collective-permute-start | bytes 786440 | tf_op jit(solution)/shard_map/ppermute | solution.py:403
  47.8 0.0 copy-start.4
  47.8 0.9 %copy-done.4 = bf16[1,1024,128]{2,1,0:T(8,128)(2,1)S(1)} copy-done((bf16[1,1024,128]{2,1,0:T(8,128)(2,1)S(1)}, bf16[1,1024,128]{2,1,0:T(8,128)(2,1)}, u32[]{:S(2)}) %copy-start.4) | copy-done | bytes 262168
  48.7 0.0 copy-start.6
  48.7 0.9 %copy-done.6 = bf16[1024,128]{1,0:T(8,128)(2,1)S(1)} copy-done((bf16[1024,128]{1,0:T(8,128)(2,1)S(1)}, bf16[1024,128]{1,0:T(8,128)(2,1)}, u32[]{:S(2)}) %copy-start.6) | copy-done | bytes 262168
  49.7 10.7 %shard_map.82 = f32[3,16,1,256]{3,2,1,0:T(1,128)} custom-call(s32[4]{0:T(128)S(1)} %iota_xor_fusion.refs_0_, s32[16,1,256]{2,1,0:T(1,128)S(1)} %get-tuple-element.32.refs_1_, bf16[4,1024,256]{2,1,0:T(8,128)(2,1)S(1)} %shard_map.78.refs_2_, bf16[1024,128]{1,0:T(8,128)(2,1)S(1)} %bitcast.20, bf16[1024,128]{1,0:T(8,128)(2,1)} %collective-permute-done.7.refs_4_.refs_7_, ...), custom_call_target="tpu_custom_call" | custom-call | bytes 1024 | tf_op jit(solution)/shard_map/pallas_call | solution.py:404
  60.4 11.3 %while.10 = (s32[]{:T(128)}, f32[3,16,1,256]{3,2,1,0:T(1,128)}, s32[]{:T(128)}, s32[]{:T(128)}) while((s32[]{:T(128)}, f32[3,16,1,256]{3,2,1,0:T(1,128)}, s32[]{:T(128)}, s32[]{:T(128)}) %tuple.26), condition=%wide.region_1.0_spmd, body=%wide.region_0.0_spmd.sunk | while | flops 36866 | bytes 1032365 | solution.py:411
  60.4 0.0 collective-permute-start
  60.4 1.4 %collective-permute-done = f32[3,16,1,256]{3,2,1,0:T(1,128)S(1)} collective-permute-done((f32[3,16,1,256]{3,2,1,0:T(1,128)}, f32[3,16,1,256]{3,2,1,0:T(1,128)S(1)}, u32[]{:S(2)}, u32[]{:S(2)}) %collective-permute-start) | collective-permute-done | bytes 49184 | tf_op jit(solution)/shard_map/while/body/ppermute | solution.py:324
  61.8 0.9 %add.29 = f32[3,16,1,256]{3,2,1,0:T(1,128)S(1)} add(f32[3,16,1,256]{3,2,1,0:T(1,128)} %get-tuple-element.72, f32[3,16,1,256]{3,2,1,0:T(1,128)S(1)} %collective-permute-done) | non-fusion elementwise | flops 12288 | bytes 147456 | tf_op jit(solution)/shard_map/while/body/add | solution.py:324
  62.7 0.7 collective-permute-start.1
  63.4 3.4 %collective-permute-done.1 = f32[3,16,1,256]{3,2,1,0:T(1,128)S(1)} collective-permute-done((f32[3,16,1,256]{3,2,1,0:T(1,128)S(1)}, f32[3,16,1,256]{3,2,1,0:T(1,128)S(1)}, u32[]{:S(2)}, u32[]{:S(2)}) %collective-permute-start.1) | collective-permute-done | bytes 49184 | tf_op jit(solution)/shard_map/while/body/ppermute | solution.py:324
  66.8 0.1 add.30
  66.9 1.6 %collective-permute-start.2 = (f32[3,16,1,256]{3,2,1,0:T(1,128)S(1)}, f32[3,16,1,256]{3,2,1,0:T(1,128)S(1)}, u32[]{:S(2)}, u32[]{:S(2)}) collective-permute-start(f32[3,16,1,256]{3,2,1,0:T(1,128)S(1)} %add.30), channel_id=1, source_target_pairs={{0,16},{4,20},{8,24},{12,28},{16,0},{20,4},{24,8},{28,12},{1,17},{... | collective-permute-start | bytes 147464 | tf_op jit(solution)/shard_map/while/body/ppermute | solution.py:324
  68.5 2.6 %collective-permute-done.2 = f32[3,16,1,256]{3,2,1,0:T(1,128)S(1)} collective-permute-done((f32[3,16,1,256]{3,2,1,0:T(1,128)S(1)}, f32[3,16,1,256]{3,2,1,0:T(1,128)S(1)}, u32[]{:S(2)}, u32[]{:S(2)}) %collective-permute-start.2) | collective-permute-done | bytes 49184 | tf_op jit(solution)/shard_map/while/body/ppermute | solution.py:324
  71.0 0.7 add.31
  71.7 1.5 %pad_maximum_fusion = f32[4,1,4096]{2,1,0:T(1,128)} fusion(f32[1,1,4096]{2,1,0:T(1,128)S(1)} %bitcast.22, f32[3,1,4096]{2,1,0:T(1,128)} %bitcast.23), kind=kLoop, calls=%fused_computation | loop fusion | flops 16384 | bytes 131072 | tf_op jit(solution)/shard_map/concatenate | solution.py:419
  73.2 0.0 collective-permute-done.13.high
  73.2 0.0 collective-permute-done.12.low
  73.2 5.9 %shard_map.83 = f32[4,64,512]{2,1,0:T(8,128)} custom-call(f32[5,64,128]{2,1,0:T(8,128)S(1)} %get-tuple-element.29.coef, f32[4,256,128]{2,1,0:T(8,128)S(1)} %get-tuple-element.31.own, bf16[7,256,128]{2,1,0:T(8,128)(2,1)S(1)} %collective-permute-done.12.low, bf16[4,256,128]{2,1,0:T(8,128)(2,1)} %collective-permute-done.13.high), custom_call_target="tpu_custom_call" | custom-call | flops 14680064 | bytes 1048576 | tf_op jit(solution)/shard_map/pallas_call | solution.py:412
  (2 shorter events, 0.0 us)
Async XLA Ops:
  0.6 18.8 %collective-permute-start.3 = (f32[4,64,512]{2,1,0:T(8,128)}, f32[4,64,512]{2,1,0:T(8,128)S(1)}, u32[]{:S(2)}, u32[]{:S(2)}) collective-permute-start(f32[4,64,512]{2,1,0:T(8,128)} %bitcast.13), channel_id=1, source_target_pairs={{0,4},{4,8},{8,12},{12,16},{16,20},{20,24},{24,28},{28,0},{1,5},{5... | collective-permute-start | bytes 1572872 | tf_op jit(solution)/shard_map/ppermute | solution.py:343
  1.1 18.3 %collective-permute-start.4 = (f32[4,64,512]{2,1,0:T(8,128)}, f32[4,64,512]{2,1,0:T(8,128)S(1)}, u32[]{:S(2)}, u32[]{:S(2)}) collective-permute-start(f32[4,64,512]{2,1,0:T(8,128)} %bitcast.14), channel_id=1, source_target_pairs={{0,28},{4,0},{8,4},{12,8},{16,12},{20,16},{24,20},{28,24},{1,29},{... | collective-permute-start | bytes 1572872 | tf_op jit(solution)/shard_map/ppermute | solution.py:344
  4.1 14.7 %collective-permute-start.5 = (bf16[1024,128]{1,0:T(8,128)(2,1)}, bf16[1024,128]{1,0:T(8,128)(2,1)S(1)}, u32[]{:S(2)}, u32[]{:S(2)}) collective-permute-start(bf16[1024,128]{1,0:T(8,128)(2,1)} %bitcast.16), channel_id=1, source_target_pairs={{0,2},{1,3},{2,0},{3,1},{4,6},{5,7},{6,4},{7,5},{8,10},{9,11},{10,... | collective-permute-start | bytes 786440 | tf_op jit(solution)/shard_map/ppermute | solution.py:288
  7.4 18.9 %collective-permute-start.7 = (bf16[1024,128]{1,0:T(8,128)(2,1)}, bf16[1024,128]{1,0:T(8,128)(2,1)}, u32[]{:S(2)}, u32[]{:S(2)}) collective-permute-start(bf16[1024,128]{1,0:T(8,128)(2,1)} %bitcast.17), channel_id=1, source_target_pairs={{0,1},{1,0},{2,3},{3,2},{4,5},{5,4},{6,7},{7,6},{8,9},{9,8},{10,11... | collective-permute-start | bytes 786440 | tf_op jit(solution)/shard_map/ppermute | solution.py:288
  12.2 1.0 %copy-start = (f32[1,4,64,512]{3,2,1,0:T(8,128)S(1)}, f32[1,4,64,512]{3,2,1,0:T(8,128)}, u32[]{:S(2)}) copy-start(f32[1,4,64,512]{3,2,1,0:T(8,128)} %param.8) | copy-start | bytes 1572868
  13.2 0.7 copy-start.7
  13.9 12.4 %copy-start.3 = (bf16[1,1024,128]{2,1,0:T(8,128)(2,1)S(1)}, bf16[1,1024,128]{2,1,0:T(8,128)(2,1)}, u32[]{:S(2)}) copy-start(bf16[1,1024,128]{2,1,0:T(8,128)(2,1)} %param.13) | copy-start | bytes 786436
  18.8 10.4 %collective-permute-start.6 = (bf16[1024,128]{1,0:T(8,128)(2,1)S(1)}, bf16[1024,128]{1,0:T(8,128)(2,1)S(1)}, u32[]{:S(2)}, u32[]{:S(2)}) collective-permute-start(bf16[1024,128]{1,0:T(8,128)(2,1)S(1)} %collective-permute-done.5.refs_5_.refs_8_), channel_id=1, source_target_pairs={{0,1},{1,0},{2,3},{3,2},{4,5},{5,4},{6,7},{7,6},{8,9},{9,8},{10,11... | collective-permute-start | bytes 786440 | tf_op jit(solution)/shard_map/ppermute | solution.py:288
  19.5 0.8 %copy-start.1 = (f32[4,64,512]{2,1,0:T(8,128)}, f32[4,64,512]{2,1,0:T(8,128)S(1)}, u32[]{:S(2)}) copy-start(f32[4,64,512]{2,1,0:T(8,128)S(1)} %collective-permute-done.4.high) | copy-start | bytes 1572868
  20.3 1.0 %copy-start.2 = (f32[4,64,512]{2,1,0:T(8,128)S(1)}, f32[4,64,512]{2,1,0:T(8,128)}, u32[]{:S(2)}) copy-start(f32[4,64,512]{2,1,0:T(8,128)} %copy-done.1) | copy-start | bytes 1572868
  30.5 1.2 %collective-permute-start.8 = (f32[16,1,256]{2,1,0:T(1,128)S(1)}, f32[16,1,256]{2,1,0:T(1,128)S(1)}, u32[]{:S(2)}, u32[]{:S(2)}) collective-permute-start(f32[16,1,256]{2,1,0:T(1,128)S(1)} %shard_map.80), channel_id=1, source_target_pairs={{0,4},{4,0},{8,12},{12,8},{16,20},{20,16},{24,28},{28,24},{1,5},{5... | collective-permute-start | bytes 49160 | tf_op jit(solution)/shard_map/ppermute | solution.py:313
  31.7 3.8 %collective-permute-start.9 = (f32[16,1,256]{2,1,0:T(1,128)S(1)}, f32[16,1,256]{2,1,0:T(1,128)S(1)}, u32[]{:S(2)}, u32[]{:S(2)}) collective-permute-start(f32[16,1,256]{2,1,0:T(1,128)S(1)} %add.21.refs_2_), channel_id=1, source_target_pairs={{0,8},{4,12},{8,0},{12,4},{16,24},{20,28},{24,16},{28,20},{1,9},{5... | collective-permute-start | bytes 49160 | tf_op jit(solution)/shard_map/ppermute | solution.py:313
  33.3 3.9 %collective-permute-start.10 = (f32[16,1,256]{2,1,0:T(1,128)S(1)}, f32[16,1,256]{2,1,0:T(1,128)S(1)}, u32[]{:S(2)}, u32[]{:S(2)}) collective-permute-start(f32[16,1,256]{2,1,0:T(1,128)S(1)} %add.21.refs_2_), channel_id=1, source_target_pairs={{0,16},{4,20},{8,24},{12,28},{16,0},{20,4},{24,8},{28,12},{1,17},{... | collective-permute-start | bytes 49160 | tf_op jit(solution)/shard_map/ppermute | solution.py:313
  33.8 4.6 %collective-permute-start.11 = (f32[16,1,256]{2,1,0:T(1,128)S(1)}, f32[16,1,256]{2,1,0:T(1,128)S(1)}, u32[]{:S(2)}, u32[]{:S(2)}) collective-permute-start(f32[16,1,256]{2,1,0:T(1,128)S(1)} %add.21.refs_2_), channel_id=1, source_target_pairs={{0,24},{4,28},{8,16},{12,20},{16,8},{20,12},{24,0},{28,4},{1,25},{... | collective-permute-start | bytes 49160 | tf_op jit(solution)/shard_map/ppermute | solution.py:313
  43.7 0.7 copy-start.5
  44.4 0.7 copy-start.8
  45.1 28.1 %collective-permute-start.12 = (bf16[7,256,128]{2,1,0:T(8,128)(2,1)}, bf16[7,256,128]{2,1,0:T(8,128)(2,1)S(1)}, u32[]{:S(2)}, u32[]{:S(2)}) collective-permute-start(bf16[7,256,128]{2,1,0:T(8,128)(2,1)} %get-tuple-element.35), channel_id=1, source_target_pairs={{0,4},{4,8},{8,12},{12,16},{16,20},{20,24},{24,28},{28,0},{1,5},{5... | collective-permute-start | bytes 1376264 | tf_op jit(solution)/shard_map/ppermute | solution.py:402
  45.1 28.1 %collective-permute-start.13 = (bf16[4,256,128]{2,1,0:T(8,128)(2,1)}, bf16[4,256,128]{2,1,0:T(8,128)(2,1)}, u32[]{:S(2)}, u32[]{:S(2)}) collective-permute-start(bf16[4,256,128]{2,1,0:T(8,128)(2,1)} %copy-done.8), channel_id=1, source_target_pairs={{0,28},{4,0},{8,4},{12,8},{16,12},{20,16},{24,20},{28,24},{1,29},{... | collective-permute-start | bytes 786440 | tf_op jit(solution)/shard_map/ppermute | solution.py:403
  47.8 0.9 %copy-start.4 = (bf16[1,1024,128]{2,1,0:T(8,128)(2,1)S(1)}, bf16[1,1024,128]{2,1,0:T(8,128)(2,1)}, u32[]{:S(2)}) copy-start(bf16[1,1024,128]{2,1,0:T(8,128)(2,1)} %param.13) | copy-start | bytes 786436
  48.7 0.9 %copy-start.6 = (bf16[1024,128]{1,0:T(8,128)(2,1)S(1)}, bf16[1024,128]{1,0:T(8,128)(2,1)}, u32[]{:S(2)}) copy-start(bf16[1024,128]{1,0:T(8,128)(2,1)} %copy-done.5) | copy-start | bytes 786436
  60.4 1.4 %collective-permute-start = (f32[3,16,1,256]{3,2,1,0:T(1,128)}, f32[3,16,1,256]{3,2,1,0:T(1,128)S(1)}, u32[]{:S(2)}, u32[]{:S(2)}) collective-permute-start(f32[3,16,1,256]{3,2,1,0:T(1,128)} %get-tuple-element.72), channel_id=1, source_target_pairs={{0,4},{4,0},{8,12},{12,8},{16,20},{20,16},{24,28},{28,24},{1,5},{5... | collective-permute-start | bytes 147464 | tf_op jit(solution)/shard_map/while/body/ppermute | solution.py:324
  62.7 4.2 %collective-permute-start.1 = (f32[3,16,1,256]{3,2,1,0:T(1,128)S(1)}, f32[3,16,1,256]{3,2,1,0:T(1,128)S(1)}, u32[]{:S(2)}, u32[]{:S(2)}) collective-permute-start(f32[3,16,1,256]{3,2,1,0:T(1,128)S(1)} %add.29), channel_id=1, source_target_pairs={{0,8},{4,12},{8,0},{12,4},{16,24},{20,28},{24,16},{28,20},{1,9},{5... | collective-permute-start | bytes 147464 | tf_op jit(solution)/shard_map/while/body/ppermute | solution.py:324
  66.9 4.2 %collective-permute-start.2 = (f32[3,16,1,256]{3,2,1,0:T(1,128)S(1)}, f32[3,16,1,256]{3,2,1,0:T(1,128)S(1)}, u32[]{:S(2)}, u32[]{:S(2)}) collective-permute-start(f32[3,16,1,256]{3,2,1,0:T(1,128)S(1)} %add.30), channel_id=1, source_target_pairs={{0,16},{4,20},{8,24},{12,28},{16,0},{20,4},{24,8},{28,12},{1,17},{... | collective-permute-start | bytes 147464 | tf_op jit(solution)/shard_map/while/body/ppermute | solution.py:324

commit v4 on v3

v4 whole, which is shorter than its diff:
```python
import jax
import jax.numpy as jnp
from jax import lax
from jax.experimental import pallas as pl
from jax.experimental.pallas import tpu as pltpu
from jax.sharding import PartitionSpec as P

TILE = 128
STEPS = 4
PAD = 8
GROUP = 256
VMEM_LIMIT = 24 * 1024 * 1024


def shift_pairs(count, by):
    return [(i, (i + by) % count) for i in range(count)]


def clear_pads(buffer):
    planes, columns, rows, lanes = buffer.shape
    edge = jnp.zeros((columns, PAD, lanes), buffer.dtype)

    def body(plane, carry):
        buffer[plane, :, :PAD, :] = edge
        buffer[plane, :, rows - PAD :, :] = edge
        return carry

    lax.fori_loop(0, planes, body, 0)


def sweep_rows(source, coef, planes, row, adjoint):
    here = pl.ds(pl.multiple_of(PAD + row, 8), 8)
    block = pl.ds(pl.multiple_of(row, 8), 8)
    columns = source.shape[1]
    lane = lax.broadcasted_iota(jnp.int32, (8, TILE), 1)
    weights = [coef[place, block, :] for place in range(5)]
    lower, centre = source[planes[0] - 1, :, here, :], source[planes[0], :, here, :]
    out = []
    for plane in planes:
        upper = source[plane + 1, :, here, :]
        above = source[plane, :, pl.ds(PAD + row + 1, 8), :]
        below = source[plane, :, pl.ds(PAD + row - 1, 8), :]
        left = [pltpu.roll(centre[c], TILE - 1, 1) for c in range(columns)]
        right = [pltpu.roll(centre[c], 1, 1) for c in range(columns)]
        results = []
        for c in range(columns):
            upper_z = jnp.where(lane == TILE - 1, left[(c + 1) % columns], left[c])
            lower_z = jnp.where(lane == 0, right[(c - 1) % columns], right[c])
            total = weights[0] * centre[c]
            if adjoint:
                total = total + weights[1] * upper[c]
                total = total + weights[2] * (lower[c] + (upper_z + lower_z))
                total = total + (weights[3] * above[c] + weights[4] * below[c])
            else:
                total = total + weights[1] * lower[c]
                total = total + weights[2] * ((upper[c] + (upper_z + lower_z)) + (above[c] + below[c]))
            results.append(total)
        out.append(results)
        lower, centre = centre, upper
    return out


def split(value):
    high = value.astype(jnp.bfloat16)
    low = (value - high.astype(jnp.float32)).astype(jnp.bfloat16)
    return high, low


def shifted_plane(field, plane, offset):
    height, width = field.shape[1:]
    columns = width // TILE
    turn, rest = offset // TILE, offset % TILE
    lane = lax.broadcasted_iota(jnp.int32, (height, TILE), 1)
    rolled = [pltpu.roll(field[plane, :, pl.ds(c * TILE, TILE)], rest, 1) for c in range(columns)]
    return [
        (lax.rem(c + turn, columns), jnp.where(lane >= rest, rolled[c], rolled[c - 1]))
        for c in range(columns)
    ]


def prelude_kernel(columns, height, offset, field, courant, diffusivity, above, below, tile, panel, own, coef, pick, chosen, kept):
    def load(plane, carry):
        for column, value in shifted_plane(field, plane, offset[0]):
            own[plane, column] = value
        return carry

    lax.fori_loop(0, field.shape[0], load, 0)
    rates = (
        1.0 - courant[...] - 6.0 * diffusivity[...],
        courant[...] + diffusivity[...],
        diffusivity[...],
        above[...],
        below[...],
    )
    for place, rate in enumerate(rates):
        coef[place] = jnp.broadcast_to(rate, coef.shape[1:])
    kept[...] = panel[...]
    numbers = tile[...]
    inside = numbers & (columns * height - 1)
    numbers = (numbers - inside) + (inside & (columns - 1)) * height + inside // columns
    upright = numbers.astype(jnp.float32).T.astype(jnp.int32)
    groups, total = numbers.shape[0], pick.shape[1]
    by_lane = lax.broadcasted_iota(jnp.int32, (GROUP, total), 1)
    by_row = lax.broadcasted_iota(jnp.int32, (total, GROUP), 0)
    for group in range(groups):
        block = pl.ds(group * GROUP, GROUP)
        found = jnp.where(upright[:, group : group + 1] == by_lane, 1.0, 0.0)
        pick[block, :] = found.astype(jnp.bfloat16)
        found = jnp.where(numbers[group : group + 1, :] == by_row, 1.0, 0.0)
        chosen[:, block] = found.astype(jnp.bfloat16)


def adjoint_kernel(offset, coef, own, low, high, tiles, first, second):
    cells, columns, height = own.shape[:3]
    steps = tiles.shape[1] // (2 * TILE)
    inside = pl.ds(PAD, height)
    clear_pads(first)
    clear_pads(second)

    def load(plane, carry):
        for slab, field in ((0, low), (2, high)):
            for column, value in shifted_plane(field, plane, offset[0]):
                first[slab * cells + plane, column, inside, :] = value
        first[cells + plane, :, inside, :] = own[plane]
        return carry

    lax.fori_loop(0, cells, load, 0)
    buffers = (first, second)
    for step in range(steps):
        source, target = buffers[step % 2], buffers[(step + 1) % 2]

        def sweep(place, carry, source=source, target=target, step=step):
            planes = range(step + 1, 3 * cells - step - 1)
            halves = []
            for half in range(2):
                row = place * 16 + half * 8
                blocks = sweep_rows(source, coef, planes, row, True)
                halves.append(blocks)
                if step < steps - 1:
                    for plane, block in zip(planes, blocks):
                        for c in range(columns):
                            where = pl.ds(pl.multiple_of(PAD + row, 8), 8)
                            target[plane, c, where, :] = block[c]
            for plane, upper, lower in zip(planes, *halves):
                if cells <= plane < 2 * cells:
                    for c in range(columns):
                        start = (plane - cells) * columns * height + c * height + place * 16
                        where = pl.ds(pl.multiple_of(start, 16), 16)
                        head, tail = split(jnp.concatenate([upper[c], lower[c]], axis=0))
                        tiles[where, pl.ds(2 * step * TILE, TILE)] = head
                        tiles[where, pl.ds((2 * step + 1) * TILE, TILE)] = tail
            return carry

        lax.fori_loop(0, height // 16, sweep, 0)


def forward_kernel(coef, own, low, high, out, first, second):
    cells, height, width = out.shape
    columns = width // TILE
    steps = STEPS
    clear_pads(first)
    clear_pads(second)
    for plane in range(cells):
        for c in range(columns):
            where = pl.ds(c * height, height)
            inside = pl.ds(PAD, height)
            first[cells + plane, c, inside, :] = own[plane, where, :]
            first[2 * cells + plane, c, inside, :] = high[plane, where, :].astype(jnp.float32)
            value = low[plane, where, :].astype(jnp.float32)
            if plane > 0:
                value = value + low[cells + plane - 1, where, :].astype(jnp.float32)
            first[plane, c, inside, :] = value
    buffers = (first, second)
    for step in range(steps):
        source, target = buffers[step % 2], buffers[(step + 1) % 2]

        def sweep(place, carry, source=source, target=target, step=step):
            planes = range(step + 1, 3 * cells - step - 1)
            row = place * 8
            for plane, block in zip(planes, sweep_rows(source, coef, planes, row, False)):
                for c in range(columns):
                    if step == steps - 1:
                        where = pl.ds(pl.multiple_of(row, 8), 8)
                        out[plane - cells, where, pl.ds(c * TILE, TILE)] = block[c]
                    else:
                        target[plane, c, pl.ds(pl.multiple_of(PAD + row, 8), 8), :] = block[c]
            return carry

        lax.fori_loop(0, height // 8, sweep, 0)


def project_kernel(first, count, chunks, source, pick, tiles, *refs):
    panels, (*before, out) = refs[: len(chunks)], refs[len(chunks) :]
    shard = panels[0].shape[0] // GROUP
    for given in before:
        out[...] = given[...]
    ones = jnp.ones((8, 2 * TILE), jnp.bfloat16)
    weights = tiles[:, pl.ds(2 * first * TILE, 2 * count * TILE)]
    for chunk, panel in zip(chunks, panels):

        def body(group, carry, chunk=chunk, panel=panel):
            number = source[chunk] * shard + group
            chosen = pick[pl.ds(pl.multiple_of(number * GROUP, GROUP), GROUP), :]
            found = jnp.dot(chosen, weights, preferred_element_type=jnp.float32)
            rows = panel[pl.ds(pl.multiple_of(group * GROUP, GROUP), GROUP), :].astype(jnp.float32)
            for step in range(count):
                start = 2 * step * TILE
                cells = found[:, start : start + TILE] + found[:, start + TILE : start + 2 * TILE]
                both = jnp.concatenate(split(cells * rows), axis=1)
                sums = lax.dot_general(
                    ones, both, (((1,), (1,)), ((), ())), preferred_element_type=jnp.float32
                )
                out[step, number] = sums[:1]
            return carry

        lax.fori_loop(0, shard, body, 0, unroll=2 if count > 1 and shard % 2 == 0 else shard)


def deposit_kernel(count, source, chosen, *refs):
    parts, panels, (total, field, rightward, leftward, scaled) = refs[:count], refs[count:-5], refs[-5:]
    groups = total.shape[1]
    shard = groups // len(panels)
    cells, per_plane = field.shape[0], field.shape[1]
    total[...] = tree_sum([part[...] for part in parts])
    numbers = [source[g // shard] * shard + g % shard for g in range(groups)]
    drive = jnp.concatenate([total[0, number] for number in numbers], axis=0).T
    for group, number in enumerate(numbers):
        rows = panels[group // shard][pl.ds((group % shard) * GROUP, GROUP), :]
        head, tail = split(drive[:, group : group + 1] * rows.astype(jnp.float32))
        where = pl.ds(pl.multiple_of(number * GROUP, GROUP), GROUP)
        scaled[where, pl.ds(0, TILE)] = head
        scaled[where, pl.ds(TILE, TILE)] = tail

    for plane in range(cells):
        sums = jnp.dot(
            chosen[pl.ds(plane * per_plane, per_plane), :],
            scaled[...],
            preferred_element_type=jnp.float32,
        )
        value = sums[:, :TILE] + sums[:, TILE:]
        field[plane] = value
        head, tail = split(value)
        leftward[plane] = head
        rightward[plane] = head
        if plane > 0:
            rightward[cells + plane - 1] = tail


def call(kernel, out_shape, scratch=(), smem=0, inputs=0):
    in_specs = [pl.BlockSpec(memory_space=pltpu.SMEM)] * smem
    in_specs += [pl.BlockSpec(memory_space=pltpu.VMEM)] * (inputs - smem)
    out_specs = jax.tree.map(lambda _: pl.BlockSpec(memory_space=pltpu.VMEM), out_shape)
    return pl.pallas_call(
        kernel,
        out_shape=out_shape,
        in_specs=in_specs,
        out_specs=out_specs,
        scratch_shapes=list(scratch),
        compiler_params=pltpu.CompilerParams(vmem_limit_bytes=VMEM_LIMIT),
        cost_estimate=pl.CostEstimate(flops=1024, bytes_accessed=1024, transcendentals=0),
    )


def gathered_panel(panel, axis, ready):
    count = lax.axis_size(axis)
    shards = {0: panel}
    mask = count // 2
    while mask:
        pairs = [(i, i ^ mask) for i in range(count)]
        for held in sorted(shards):
            operand = panel if len(shards) == 1 else tied(shards[held], ready)
            shards[held | mask] = lax.ppermute(operand, axis, pairs)
        mask //= 2
    return [shards[k] for k in range(1, count)]


def tied(value, *others):
    return lax.optimization_barrier((value,) + others)[0]


def tree_sum(parts):
    while len(parts) > 1:
        parts = [parts[i] + parts[i + 1] for i in range(0, len(parts), 2)]
    return parts[0]


def summands(part, axis):
    count = lax.axis_size(axis)
    if count & (count - 1):
        return [lax.psum(part, axis)]
    done, parts = 1, [part]
    for span in (2, 4, 4, 4, 4):
        span = min(span, count // done)
        if span > 1:
            part = tree_sum(parts)
            pairs = [[(i, i ^ (k * done)) for i in range(count)] for k in range(1, span)]
            parts = [part] + [lax.ppermute(part, axis, pair) for pair in pairs]
            done *= span
    return parts


def doubling_sum(part, axis):
    count = lax.axis_size(axis)
    if count & (count - 1):
        return lax.psum(part, axis)
    mask = 1
    while mask < count:
        part = part + lax.ppermute(part, axis, [(i, i ^ mask) for i in range(count)])
        mask *= 2
    return part


def local(sensor_field, courant, diffusivity, probe_offset, tile_index, actuator_panel):
    slabs, probes = lax.axis_size("state"), lax.axis_size("probe")
    own = sensor_field[0]
    cells, height, width = own.shape
    columns = width // TILE
    tile_total = cells * height * columns
    actuators = tile_index.shape[1]
    groups = actuators // GROUP
    shard = groups // probes
    planes = 3 * cells
    f32, bf16 = jnp.float32, jnp.bfloat16

    source = lax.axis_index("probe") ^ jnp.arange(probes, dtype=jnp.int32)
    low = lax.ppermute(own, "state", shift_pairs(slabs, 1))
    high = lax.ppermute(own, "state", shift_pairs(slabs, -1))

    zero = jnp.zeros((1,), f32)
    rates = [
        courant,
        diffusivity,
        jnp.concatenate([diffusivity[1:], zero]),
        jnp.concatenate([zero, diffusivity[:-1]]),
    ]
    shifted, coef, pick, chosen, panel = call(
        lambda *refs: prelude_kernel(columns, height, *refs),
        (
            jax.ShapeDtypeStruct((cells, columns, height, TILE), f32),
            jax.ShapeDtypeStruct((5, height, TILE), f32),
            jax.ShapeDtypeStruct((actuators, tile_total), bf16),
            jax.ShapeDtypeStruct((tile_total, actuators), bf16),
            jax.ShapeDtypeStruct(actuator_panel.shape[1:], bf16),
        ),
        smem=1,
        inputs=8,
    )(
        probe_offset,
        own,
        *[rate[:, None] for rate in rates],
        tile_index.reshape(groups, GROUP),
        actuator_panel[0],
    )
    panels = [panel] + gathered_panel(actuator_panel[0], "probe", coef)

    field_shape = pltpu.VMEM((planes, columns, height + 2 * PAD, TILE), f32)
    tiles = call(
        adjoint_kernel,
        jax.ShapeDtypeStruct((tile_total, 2 * STEPS * TILE), bf16),
        scratch=(field_shape, field_shape),
        smem=1,
        inputs=5,
    )(probe_offset, coef, shifted, low, high)

    every = list(range(probes))

    def project(first, count, chunks, *given):
        return call(
            lambda *refs: project_kernel(first, count, chunks, *refs),
            jax.ShapeDtypeStruct((count, groups, 1, GROUP), f32),
            smem=1,
            inputs=3 + len(chunks) + len(given),
        )

    before = project(STEPS - 1, 1, every[:-1])(source, pick, tiles, *panels[:-1])
    last = project(STEPS - 1, 1, every[-1:], before)(source, pick, tiles, panels[-1], before)
    parts = summands(last, "state")
    payload = jax.ShapeDtypeStruct((2 * cells - 1, height * columns, TILE), bf16)
    heads = jax.ShapeDtypeStruct((cells, height * columns, TILE), bf16)
    total, forced, rightward, leftward = call(
        lambda *refs: deposit_kernel(len(parts), *refs),
        (
            jax.ShapeDtypeStruct(last.shape, f32),
            jax.ShapeDtypeStruct((cells, height * columns, TILE), f32),
            payload,
            heads,
        ),
        scratch=(pltpu.VMEM((actuators, 2 * TILE), bf16),),
        smem=1,
        inputs=2 + len(parts) + probes,
    )(source, chosen, *parts, *panels)
    from_low = lax.ppermute(rightward, "state", shift_pairs(slabs, 1))
    from_high = lax.ppermute(leftward, "state", shift_pairs(slabs, -1))
    early = project(0, STEPS - 1, every)(tied(source, forced), pick, tiles, *panels)
    rounds = 1 + jnp.minimum(probe_offset[0], 0)
    early = lax.fori_loop(0, rounds, lambda _, part: doubling_sum(part, "state"), early)
    response = call(
        forward_kernel,
        jax.ShapeDtypeStruct((cells, height, width), f32),
        scratch=(field_shape, field_shape),
        inputs=4,
    )(coef, forced, from_low, from_high)
    projections = jnp.concatenate([early, total], axis=0)
    return projections.reshape(STEPS, 1, actuators), response[None]


def solution(mesh):
    return jax.shard_map(
        local,
        mesh=mesh,
        in_specs=(
            P("probe", "state", None, None),
            P(),
            P(),
            P("probe"),
            P("state", None),
            P("state", "probe", None),
        ),
        out_specs=(P(None, "probe", None), P("probe", "state", None, None)),
        check_vma=False,
    )
```

time: 79.8 us -> 90.6 us (1.14)
  Pallas kernels: 31.6 us -> 39.9 us
  local copies, waits for them, and re-layouts: 9.37 us -> 14.9 us
  starting transfers between devices: 17.6 us -> 16.5 us
    unnamed x18 -> x17, local copies, waits for them, and re-layouts: 6.89 us -> 12.4 us
    pallas_call x1, Pallas kernels: 0.59 us -> 5.76 us  [local(): call(lambda *refs: prelude_kernel(columns, height, *refs), (jax.ShapeDtyp...]
    pallas_call x5, Pallas kernels: 25.1 us -> 28.8 us  [the longest x1 13 us: local(): project(0, STEPS - 1, every)(tied(source, forced), pick, tiles, *panels)]
    add x3, other arithmetic: 1.57 us -> 0.16 us  [doubling_sum(): part + lax.ppermute(part, axis, [(i, i ^ mask) for i in range(count)])]
    unnamed x0 -> x2, other arithmetic: none -> 1.4 us
    ppermute x3, waiting for transfers between devices: 4.27 us -> 3.3 us  [gathered_panel(): shards[held | mask] = lax.ppermute(operand, axis, pairs)]
  transfers between devices with their start and end apart: 14 -> 14, of which waited for: 8 -> 7; matrix products, arithmetic and copies ran while one was open for 7% -> 6% of each run, Pallas kernels for 24% -> 32%
where the time goes in v4:
time: 90.6 us; the launch traced here: 90.2 us
  Pallas kernels  39.9 us (44%)
  starting transfers between devices  16.5 us (18%)
  waiting for transfers between devices  15.3 us (17%)
  local copies, waits for them, and re-layouts  14.9 us (16%)
  other arithmetic  2.35 us (3%)
  between operations  1.37 us (2%)
    pallas_call x1, Pallas kernels, local(): project(0, STEPS - 1, every)(tied(source, forced), pick, tiles, *panels)  13 us
    unnamed x17, local copies, waits for them, and re-layouts  12.4 us
    ppermute x3, waiting for transfers between devices, doubling_sum(): lax.ppermute(part, axis, [(i, i ^ mask) for i in range(count)])  8.09 us
    pallas_call x1, Pallas kernels, local(): project(STEPS - 1, 1, every[:-1])(source, pick, tiles, *panels[:-1])  5.79 us
    pallas_call x1, Pallas kernels, local(): call(lambda *refs: prelude_kernel(columns, height, *refs), (jax.ShapeDtyp...  5.76 us
    ppermute x3, starting transfers between devices, gathered_panel(): shards[held | mask] = lax.ppermute(operand, axis, pairs)  5.31 us
    pallas_call x1, Pallas kernels, local(): call(forward_kernel, jax.ShapeDtypeStruct((cells, height, width), f32), s...  5.3 us
    pallas_call x1, Pallas kernels, local(): call(adjoint_kernel, jax.ShapeDtypeStruct((tile_total, 2 * STEPS * TILE),...  4.11 us
  transfers between devices with their start and end apart: 14, of which 7 were waited for; matrix products, arithmetic and copies ran while one was open for 6% of the time, Pallas kernels for 32%

profile of v4, /device:TPU:0, one launch (start us, length us, event | category | flops | bytes accessed | tf_op | source)
XLA Modules:
  0.0 90.2 jit_solution(1522949411400217042)
XLA Ops:
  0.6 0.5 collective-permute-start.3
  1.1 2.9 %collective-permute-start.4 = (f32[4,64,512]{2,1,0:T(8,128)}, f32[4,64,512]{2,1,0:T(8,128)S(1)}, u32[]{:S(2)}, u32[]{:S(2)}) collective-permute-start(f32[4,64,512]{2,1,0:T(8,128)} %bitcast.14), channel_id=1, source_target_pairs={{0,28},{4,0},{8,4},{12,8},{16,12},{20,16},{24,20},{28,24},{1,29},{... | collective-permute-start | bytes 1572872 | tf_op jit(solution)/shard_map/ppermute | solution.py:327
  4.1 3.3 %collective-permute-start.5 = (bf16[1024,128]{1,0:T(8,128)(2,1)}, bf16[1024,128]{1,0:T(8,128)(2,1)S(1)}, u32[]{:S(2)}, u32[]{:S(2)}) collective-permute-start(bf16[1024,128]{1,0:T(8,128)(2,1)} %bitcast.16), channel_id=1, source_target_pairs={{0,2},{1,3},{2,0},{3,1},{4,6},{5,7},{6,4},{7,5},{8,10},{9,11},{10,... | collective-permute-start | bytes 786440 | tf_op jit(solution)/shard_map/ppermute | solution.py:272
  7.4 0.8 fusion
  8.2 0.1 maximum_bitcast_fusion
  8.2 0.1 copy.10.refs_4_
  8.3 0.1 copy.11.refs_5_
  9.1 0.5 broadcast.3
  9.6 1.4 %reduce.3 = s32[4096]{0:T(1024)S(1)} reduce(s32[1,4096]{1,0:T(1,128)} %param.12, s32[]{:T(128)} %broadcast.3), dimensions={0}, to_apply=%param.12.reduce_sub_computation.3 | reduce | bytes 32772 | tf_op args[4]
  11.0 0.7 copy.8.refs_2_
  11.8 0.7 copy.9.refs_3_
  12.5 0.0 copy-start.4
  12.5 1.0 %copy-done.4 = f32[1,4,64,512]{3,2,1,0:T(8,128)S(1)} copy-done((f32[1,4,64,512]{3,2,1,0:T(8,128)S(1)}, f32[1,4,64,512]{3,2,1,0:T(8,128)}, u32[]{:S(2)}) %copy-start.4) | copy-done | bytes 524312
  13.6 0.0 copy-start.5
  13.6 0.9 %copy-done.5 = bf16[1,1024,128]{2,1,0:T(8,128)(2,1)S(1)} copy-done((bf16[1,1024,128]{2,1,0:T(8,128)(2,1)S(1)}, bf16[1,1024,128]{2,1,0:T(8,128)(2,1)}, u32[]{:S(2)}) %copy-start.5) | copy-done | bytes 262168
  14.5 5.8 %shard_map.77 = (f32[4,4,64,128]{3,2,1,0:T(8,128)S(1)}, f32[5,64,128]{2,1,0:T(8,128)S(1)}, bf16[4096,1024]{1,0:T(8,128)(2,1)S(1)}, bf16[1024,4096]{1,0:T(8,128)(2,1)S(1)}, bf16[1024,128]{1,0:T(8,128)(2,1)S(1)}) custom-call(s32[1]{0:T(128)S(6)} %copy.19.refs_0_.offset, f32[4,64,512]{2,1,0:T(8,128)S(1)} %bitcast.15, f32[64,1]{1,0:T(8,128)S(1)} %copy.8.refs_2_, ...), custom_call_target="tpu_custom_call" | custom-call | flops 1024 | bytes 1024 | tf_op jit(solution)/shard_map/pallas_call | solution.py:336
  20.3 0.0 copy-start
  20.3 3.3 %copy-done = bf16[4096,1024]{1,0:T(8,128)(2,1)} copy-done((bf16[4096,1024]{1,0:T(8,128)(2,1)}, bf16[4096,1024]{1,0:T(8,128)(2,1)S(1)}, u32[]{:S(2)}) %copy-start) | copy-done | bytes 8388632
  23.6 0.0 copy-start.2
  23.6 3.2 %copy-done.2 = bf16[1024,4096]{1,0:T(8,128)(2,1)} copy-done((bf16[1024,4096]{1,0:T(8,128)(2,1)}, bf16[1024,4096]{1,0:T(8,128)(2,1)S(1)}, u32[]{:S(2)}) %copy-start.2) | copy-done | bytes 8388632
  26.8 1.6 %collective-permute-start.7 = (bf16[1024,128]{1,0:T(8,128)(2,1)}, bf16[1024,128]{1,0:T(8,128)(2,1)S(1)}, u32[]{:S(2)}, u32[]{:S(2)}) collective-permute-start(bf16[1024,128]{1,0:T(8,128)(2,1)} %bitcast.17), channel_id=1, source_target_pairs={{0,1},{1,0},{2,3},{3,2},{4,5},{5,4},{6,7},{7,6},{8,9},{9,8},{10,11... | collective-permute-start | bytes 786440 | tf_op jit(solution)/shard_map/ppermute | solution.py:272
  28.4 0.0 collective-permute-done.5.refs_5_.refs_8_
  28.4 0.5 collective-permute-start.6
  28.8 0.0 collective-permute-done.3.low
  28.8 0.0 collective-permute-done.4.high
  28.8 4.1 %shard_map.78.refs_2_ = bf16[1024,1024]{1,0:T(8,128)(2,1)S(1)} custom-call(s32[1]{0:T(128)S(6)} %copy.19.refs_0_.offset, f32[5,64,128]{2,1,0:T(8,128)S(1)} %get-tuple-element.34.coef, f32[4,4,64,128]{3,2,1,0:T(8,128)S(1)} %get-tuple-element.35.own, f32[4,64,512]{2,1,0:T(8,128)S(1)} %collective-permute-done.3.low, f32[4,64,512]{2,1,0:T(8,128)S(1)} %collective-permute-done.4.high), custom_call_target="tpu_custom_call" | custom-call | flops 1024 | bytes 1024 | tf_op jit(solution)/shard_map/pallas_call | solution.py:357
  32.9 3.3 %collective-permute-done.7.refs_4_.refs_7_ = bf16[1024,128]{1,0:T(8,128)(2,1)S(1)} collective-permute-done((bf16[1024,128]{1,0:T(8,128)(2,1)}, bf16[1024,128]{1,0:T(8,128)(2,1)S(1)}, u32[]{:S(2)}, u32[]{:S(2)}) %collective-permute-start.7) | collective-permute-done | bytes 262176 | tf_op jit(solution)/shard_map/ppermute | solution.py:272
  36.2 0.0 copy-start.1
  36.2 3.4 %copy-done.1 = bf16[4096,1024]{1,0:T(8,128)(2,1)S(1)} copy-done((bf16[4096,1024]{1,0:T(8,128)(2,1)S(1)}, bf16[4096,1024]{1,0:T(8,128)(2,1)}, u32[]{:S(2)}) %copy-start.1) | copy-done | bytes 8388632
  39.6 0.0 copy-start.3
  39.6 0.0 slice-start
  39.6 5.8 %shard_map.79.refs_4_ = f32[1,16,1,256]{3,2,1,0:T(1,128)S(1)} custom-call(s32[4]{0:T(128)S(1)} %iota_xor_fusion.refs_0_, bf16[4096,1024]{1,0:T(8,128)(2,1)S(1)} %copy-done.1, bf16[1024,1024]{1,0:T(8,128)(2,1)S(1)} %shard_map.78.refs_2_, bf16[1024,128]{1,0:T(8,128)(2,1)S(1)} %get-tuple-element.37.refs_3_.refs_6_, ...), custom_call_target="tpu_custom_call" | custom-call | flops 1024 | bytes 1024 | tf_op jit(solution)/shard_map/pallas_call | solution.py:375
  45.4 0.0 slice-start.1
  45.4 0.0 collective-permute-done.6.refs_3_.refs_9_.refs_6_
  45.4 2.4 %shard_map.80 = f32[1,16,1,256]{3,2,1,0:T(1,128)S(1)} custom-call(s32[4]{0:T(128)S(1)} %iota_xor_fusion.refs_0_, bf16[4096,1024]{1,0:T(8,128)(2,1)S(1)} %copy-done.1, bf16[1024,1024]{1,0:T(8,128)(2,1)S(1)} %shard_map.78.refs_2_, bf16[1024,128]{1,0:T(8,128)(2,1)S(1)} %collective-permute-done.6.refs_3_.refs_9_.refs_6_, f32[1,16,1,256]{3,2,1,0:T(1,128)S(1)} %shard_map.79.refs_4_), custom_call_target="tpu_custom_call" | custom-call | flops 1024 | bytes 1024 | tf_op jit(solution)/shard_map/pallas_call | solution.py:376
  47.8 0.0 collective-permute-start.8
  47.8 1.2 %collective-permute-done.8 = f32[1,16,1,256]{3,2,1,0:T(1,128)S(1)} collective-permute-done((f32[1,16,1,256]{3,2,1,0:T(1,128)S(1)}, f32[1,16,1,256]{3,2,1,0:T(1,128)S(1)}, u32[]{:S(2)}, u32[]{:S(2)}) %collective-permute-start.8) | collective-permute-done | bytes 16416 | tf_op jit(solution)/shard_map/ppermute | solution.py:297
  49.0 1.6 %collective-permute-start.10 = (f32[1,16,1,256]{3,2,1,0:T(1,128)S(1)}, f32[1,16,1,256]{3,2,1,0:T(1,128)S(1)}, u32[]{:S(2)}, u32[]{:S(2)}) collective-permute-start(f32[1,16,1,256]{3,2,1,0:T(1,128)S(1)} %add.21.refs_2_), channel_id=1, source_target_pairs={{0,16},{4,20},{8,24},{12,28},{16,0},{20,4},{24,8},{28,12},{1,17},{... | collective-permute-start | bytes 49160 | tf_op jit(solution)/shard_map/ppermute | solution.py:297
  50.6 0.5 collective-permute-start.11
  51.1 1.5 %collective-permute-start.9 = (f32[1,16,1,256]{3,2,1,0:T(1,128)S(1)}, f32[1,16,1,256]{3,2,1,0:T(1,128)S(1)}, u32[]{:S(2)}, u32[]{:S(2)}) collective-permute-start(f32[1,16,1,256]{3,2,1,0:T(1,128)S(1)} %add.21.refs_2_), channel_id=1, source_target_pairs={{0,8},{4,12},{8,0},{12,4},{16,24},{20,28},{24,16},{28,20},{1,9},{5... | collective-permute-start | bytes 49160 | tf_op jit(solution)/shard_map/ppermute | solution.py:297
  52.5 0.2 collective-permute-done.10.refs_4_
  52.8 2.4 %collective-permute-done.11.refs_5_ = f32[1,16,1,256]{3,2,1,0:T(1,128)S(1)} collective-permute-done((f32[1,16,1,256]{3,2,1,0:T(1,128)S(1)}, f32[1,16,1,256]{3,2,1,0:T(1,128)S(1)}, u32[]{:S(2)}, u32[]{:S(2)}) %collective-permute-start.11) | collective-permute-done | bytes 16416 | tf_op jit(solution)/shard_map/ppermute | solution.py:297
  55.2 0.0 collective-permute-done.9.refs_3_
  55.2 0.0 copy-done.3
  55.2 3.6 %shard_map.81 = (f32[1,16,1,256]{3,2,1,0:T(1,128)S(1)}, f32[4,256,128]{2,1,0:T(8,128)S(1)}, bf16[7,256,128]{2,1,0:T(8,128)(2,1)S(1)}, bf16[4,256,128]{2,1,0:T(8,128)(2,1)S(1)}) custom-call(s32[4]{0:T(128)S(1)} %iota_xor_fusion.refs_0_, bf16[1024,4096]{1,0:T(8,128)(2,1)S(1)} %copy-done.3, f32[1,16,1,256]{3,2,1,0:T(1,128)S(1)} %add.21.refs_2_, ...), custom_call_target="tpu_custom_call" | custom-call | flops 1024 | bytes 1024 | tf_op jit(solution)/shard_map/pallas_call | solution.py:380
  58.8 0.1 collective-permute-start.12
  58.9 2.6 %collective-permute-start.13 = (bf16[4,256,128]{2,1,0:T(8,128)(2,1)S(1)}, bf16[4,256,128]{2,1,0:T(8,128)(2,1)S(1)}, u32[]{:S(2)}, u32[]{:S(2)}) collective-permute-start(bf16[4,256,128]{2,1,0:T(8,128)(2,1)S(1)} %get-tuple-element.44), channel_id=1, source_target_pairs={{0,28},{4,0},{8,4},{12,8},{16,12},{20,16},{24,20},{28,24},{1,29},{... | collective-permute-start | bytes 786440 | tf_op jit(solution)/shard_map/ppermute | solution.py:393
  61.5 0.0 slice-done
  61.5 0.0 slice-done.1
  61.5 13.0 %shard_map.82 = f32[3,16,1,256]{3,2,1,0:T(1,128)S(1)} custom-call(s32[4]{0:T(128)S(1)} %iota_xor_fusion.refs_0_, bf16[4096,1024]{1,0:T(8,128)(2,1)S(1)} %bitcast.12, bf16[1024,1024]{1,0:T(8,128)(2,1)S(1)} %shard_map.78.refs_2_, bf16[1024,128]{1,0:T(8,128)(2,1)S(1)} %get-tuple-element.37.refs_3_.refs_6_, ...), custom_call_target="tpu_custom_call" | custom-call | flops 1024 | bytes 1024 | tf_op jit(solution)/shard_map/pallas_call | solution.py:394
  74.5 9.7 %while.10 = (s32[]{:T(128)}, f32[3,16,1,256]{3,2,1,0:T(1,128)S(1)}, s32[]{:T(128)}, s32[]{:T(128)}) while((s32[]{:T(128)}, f32[3,16,1,256]{3,2,1,0:T(1,128)S(1)}, s32[]{:T(128)}, s32[]{:T(128)}) %tuple.30), condition=%wide.region_1.0_spmd, body=%wide.region_0.0_spmd.sunk | while | flops 36866 | bytes 1032365 | solution.py:396
  74.5 0.0 collective-permute-start
  74.5 1.2 %collective-permute-done = f32[3,16,1,256]{3,2,1,0:T(1,128)S(1)} collective-permute-done((f32[3,16,1,256]{3,2,1,0:T(1,128)S(1)}, f32[3,16,1,256]{3,2,1,0:T(1,128)S(1)}, u32[]{:S(2)}, u32[]{:S(2)}) %collective-permute-start) | collective-permute-done | bytes 49184 | tf_op jit(solution)/shard_map/while/body/ppermute | solution.py:308
  75.7 0.1 add.33
  75.8 0.2 collective-permute-start.1
  76.0 3.9 %collective-permute-done.1 = f32[3,16,1,256]{3,2,1,0:T(1,128)S(1)} collective-permute-done((f32[3,16,1,256]{3,2,1,0:T(1,128)S(1)}, f32[3,16,1,256]{3,2,1,0:T(1,128)S(1)}, u32[]{:S(2)}, u32[]{:S(2)}) %collective-permute-start.1) | collective-permute-done | bytes 49184 | tf_op jit(solution)/shard_map/while/body/ppermute | solution.py:308
  80.0 0.1 add.34
  80.0 1.2 %collective-permute-start.2 = (f32[3,16,1,256]{3,2,1,0:T(1,128)S(1)}, f32[3,16,1,256]{3,2,1,0:T(1,128)S(1)}, u32[]{:S(2)}, u32[]{:S(2)}) collective-permute-start(f32[3,16,1,256]{3,2,1,0:T(1,128)S(1)} %add.34), channel_id=1, source_target_pairs={{0,16},{4,20},{8,24},{12,28},{16,0},{20,4},{24,8},{28,12},{1,17},{... | collective-permute-start | bytes 147464 | tf_op jit(solution)/shard_map/while/body/ppermute | solution.py:308
  81.2 2.9 %collective-permute-done.2 = f32[3,16,1,256]{3,2,1,0:T(1,128)S(1)} collective-permute-done((f32[3,16,1,256]{3,2,1,0:T(1,128)S(1)}, f32[3,16,1,256]{3,2,1,0:T(1,128)S(1)}, u32[]{:S(2)}, u32[]{:S(2)}) %collective-permute-start.2) | collective-permute-done | bytes 49184 | tf_op jit(solution)/shard_map/while/body/ppermute | solution.py:308
  84.2 0.1 add.35
  84.2 0.7 pad_maximum_fusion
  84.9 0.0 collective-permute-done.13.high
  84.9 0.0 collective-permute-done.12.low
  84.9 5.3 %shard_map.83 = f32[4,64,512]{2,1,0:T(8,128)} custom-call(f32[5,64,128]{2,1,0:T(8,128)S(1)} %get-tuple-element.34.coef, f32[4,256,128]{2,1,0:T(8,128)S(1)} %get-tuple-element.39.own, bf16[7,256,128]{2,1,0:T(8,128)(2,1)S(1)} %collective-permute-done.12.low, bf16[4,256,128]{2,1,0:T(8,128)(2,1)S(1)} %collective-permute-done.13.high), custom_call_target="tpu_custom_call" | custom-call | flops 1024 | bytes 1024 | tf_op jit(solution)/shard_map/pallas_call | solution.py:397
  (4 shorter events, 0.0 us)
Async XLA Ops:
  0.6 28.2 %collective-permute-start.3 = (f32[4,64,512]{2,1,0:T(8,128)}, f32[4,64,512]{2,1,0:T(8,128)S(1)}, u32[]{:S(2)}, u32[]{:S(2)}) collective-permute-start(f32[4,64,512]{2,1,0:T(8,128)} %bitcast.13), channel_id=1, source_target_pairs={{0,4},{4,8},{8,12},{12,16},{16,20},{20,24},{24,28},{28,0},{1,5},{5... | collective-permute-start | bytes 1572872 | tf_op jit(solution)/shard_map/ppermute | solution.py:326
  1.1 27.7 %collective-permute-start.4 = (f32[4,64,512]{2,1,0:T(8,128)}, f32[4,64,512]{2,1,0:T(8,128)S(1)}, u32[]{:S(2)}, u32[]{:S(2)}) collective-permute-start(f32[4,64,512]{2,1,0:T(8,128)} %bitcast.14), channel_id=1, source_target_pairs={{0,28},{4,0},{8,4},{12,8},{16,12},{20,16},{24,20},{28,24},{1,29},{... | collective-permute-start | bytes 1572872 | tf_op jit(solution)/shard_map/ppermute | solution.py:327
  4.1 24.3 %collective-permute-start.5 = (bf16[1024,128]{1,0:T(8,128)(2,1)}, bf16[1024,128]{1,0:T(8,128)(2,1)S(1)}, u32[]{:S(2)}, u32[]{:S(2)}) collective-permute-start(bf16[1024,128]{1,0:T(8,128)(2,1)} %bitcast.16), channel_id=1, source_target_pairs={{0,2},{1,3},{2,0},{3,1},{4,6},{5,7},{6,4},{7,5},{8,10},{9,11},{10,... | collective-permute-start | bytes 786440 | tf_op jit(solution)/shard_map/ppermute | solution.py:272
  12.5 1.0 %copy-start.4 = (f32[1,4,64,512]{3,2,1,0:T(8,128)S(1)}, f32[1,4,64,512]{3,2,1,0:T(8,128)}, u32[]{:S(2)}) copy-start(f32[1,4,64,512]{3,2,1,0:T(8,128)} %param.8) | copy-start | bytes 1572868
  13.6 0.9 %copy-start.5 = (bf16[1,1024,128]{2,1,0:T(8,128)(2,1)S(1)}, bf16[1,1024,128]{2,1,0:T(8,128)(2,1)}, u32[]{:S(2)}) copy-start(bf16[1,1024,128]{2,1,0:T(8,128)(2,1)} %param.13) | copy-start | bytes 786436
  20.3 3.3 %copy-start = (bf16[4096,1024]{1,0:T(8,128)(2,1)}, bf16[4096,1024]{1,0:T(8,128)(2,1)S(1)}, u32[]{:S(2)}) copy-start(bf16[4096,1024]{1,0:T(8,128)(2,1)S(1)} %get-tuple-element.33.refs_1_) | copy-start | bytes 25165828
  23.6 3.2 %copy-start.2 = (bf16[1024,4096]{1,0:T(8,128)(2,1)}, bf16[1024,4096]{1,0:T(8,128)(2,1)S(1)}, u32[]{:S(2)}) copy-start(bf16[1024,4096]{1,0:T(8,128)(2,1)S(1)} %get-tuple-element.32.refs_1_) | copy-start | bytes 25165828
  26.8 9.5 %collective-permute-start.7 = (bf16[1024,128]{1,0:T(8,128)(2,1)}, bf16[1024,128]{1,0:T(8,128)(2,1)S(1)}, u32[]{:S(2)}, u32[]{:S(2)}) collective-permute-start(bf16[1024,128]{1,0:T(8,128)(2,1)} %bitcast.17), channel_id=1, source_target_pairs={{0,1},{1,0},{2,3},{3,2},{4,5},{5,4},{6,7},{7,6},{8,9},{9,8},{10,11... | collective-permute-start | bytes 786440 | tf_op jit(solution)/shard_map/ppermute | solution.py:272
  28.4 17.1 %collective-permute-start.6 = (bf16[1024,128]{1,0:T(8,128)(2,1)S(1)}, bf16[1024,128]{1,0:T(8,128)(2,1)S(1)}, u32[]{:S(2)}, u32[]{:S(2)}) collective-permute-start(bf16[1024,128]{1,0:T(8,128)(2,1)S(1)} %collective-permute-done.5.refs_5_.refs_8_), channel_id=1, source_target_pairs={{0,1},{1,0},{2,3},{3,2},{4,5},{5,4},{6,7},{7,6},{8,9},{9,8},{10,11... | collective-permute-start | bytes 786440 | tf_op jit(solution)/shard_map/ppermute | solution.py:272
  36.2 3.4 %copy-start.1 = (bf16[4096,1024]{1,0:T(8,128)(2,1)S(1)}, bf16[4096,1024]{1,0:T(8,128)(2,1)}, u32[]{:S(2)}) copy-start(bf16[4096,1024]{1,0:T(8,128)(2,1)} %copy-done) | copy-start | bytes 25165828
  39.6 15.6 %copy-start.3 = (bf16[1024,4096]{1,0:T(8,128)(2,1)S(1)}, bf16[1024,4096]{1,0:T(8,128)(2,1)}, u32[]{:S(2)}) copy-start(bf16[1024,4096]{1,0:T(8,128)(2,1)} %copy-done.2) | copy-start | bytes 25165828
  39.6 21.9 %slice-start = ((s8[8388608]{0:T(1024)(128)(4,1)}), s8[4194304]{0:T(1024)(128)(4,1)S(1)}, s32[]{:S(2)}) async-start(s8[8388608]{0:T(1024)(128)(4,1)} %bitcast.11), calls=%async_computation | async-start | bytes 8388608
  45.4 16.1 %slice-start.1 = ((s8[8388608]{0:T(1024)(128)(4,1)}), s8[4194304]{0:T(1024)(128)(4,1)S(1)}, s32[]{:S(2)}) async-start(s8[8388608]{0:T(1024)(128)(4,1)} %bitcast.11), calls=%async_computation.1 | async-start | bytes 8388608
  47.8 1.2 %collective-permute-start.8 = (f32[1,16,1,256]{3,2,1,0:T(1,128)S(1)}, f32[1,16,1,256]{3,2,1,0:T(1,128)S(1)}, u32[]{:S(2)}, u32[]{:S(2)}) collective-permute-start(f32[1,16,1,256]{3,2,1,0:T(1,128)S(1)} %shard_map.80), channel_id=1, source_target_pairs={{0,4},{4,0},{8,12},{12,8},{16,20},{20,16},{24,28},{28,24},{1,5},{5... | collective-permute-start | bytes 49160 | tf_op jit(solution)/shard_map/ppermute | solution.py:297
  49.0 3.8 %collective-permute-start.10 = (f32[1,16,1,256]{3,2,1,0:T(1,128)S(1)}, f32[1,16,1,256]{3,2,1,0:T(1,128)S(1)}, u32[]{:S(2)}, u32[]{:S(2)}) collective-permute-start(f32[1,16,1,256]{3,2,1,0:T(1,128)S(1)} %add.21.refs_2_), channel_id=1, source_target_pairs={{0,16},{4,20},{8,24},{12,28},{16,0},{20,4},{24,8},{28,12},{1,17},{... | collective-permute-start | bytes 49160 | tf_op jit(solution)/shard_map/ppermute | solution.py:297
  50.6 4.6 %collective-permute-start.11 = (f32[1,16,1,256]{3,2,1,0:T(1,128)S(1)}, f32[1,16,1,256]{3,2,1,0:T(1,128)S(1)}, u32[]{:S(2)}, u32[]{:S(2)}) collective-permute-start(f32[1,16,1,256]{3,2,1,0:T(1,128)S(1)} %add.21.refs_2_), channel_id=1, source_target_pairs={{0,24},{4,28},{8,16},{12,20},{16,8},{20,12},{24,0},{28,4},{1,25},{... | collective-permute-start | bytes 49160 | tf_op jit(solution)/shard_map/ppermute | solution.py:297
  51.1 4.1 %collective-permute-start.9 = (f32[1,16,1,256]{3,2,1,0:T(1,128)S(1)}, f32[1,16,1,256]{3,2,1,0:T(1,128)S(1)}, u32[]{:S(2)}, u32[]{:S(2)}) collective-permute-start(f32[1,16,1,256]{3,2,1,0:T(1,128)S(1)} %add.21.refs_2_), channel_id=1, source_target_pairs={{0,8},{4,12},{8,0},{12,4},{16,24},{20,28},{24,16},{28,20},{1,9},{5... | collective-permute-start | bytes 49160 | tf_op jit(solution)/shard_map/ppermute | solution.py:297
  58.8 26.1 %collective-permute-start.12 = (bf16[7,256,128]{2,1,0:T(8,128)(2,1)S(1)}, bf16[7,256,128]{2,1,0:T(8,128)(2,1)S(1)}, u32[]{:S(2)}, u32[]{:S(2)}) collective-permute-start(bf16[7,256,128]{2,1,0:T(8,128)(2,1)S(1)} %get-tuple-element.43), channel_id=1, source_target_pairs={{0,4},{4,8},{8,12},{12,16},{16,20},{20,24},{24,28},{28,0},{1,5},{5... | collective-permute-start | bytes 1376264 | tf_op jit(solution)/shard_map/ppermute | solution.py:392
  58.9 26.0 %collective-permute-start.13 = (bf16[4,256,128]{2,1,0:T(8,128)(2,1)S(1)}, bf16[4,256,128]{2,1,0:T(8,128)(2,1)S(1)}, u32[]{:S(2)}, u32[]{:S(2)}) collective-permute-start(bf16[4,256,128]{2,1,0:T(8,128)(2,1)S(1)} %get-tuple-element.44), channel_id=1, source_target_pairs={{0,28},{4,0},{8,4},{12,8},{16,12},{20,16},{24,20},{28,24},{1,29},{... | collective-permute-start | bytes 786440 | tf_op jit(solution)/shard_map/ppermute | solution.py:393
  74.5 1.2 %collective-permute-start = (f32[3,16,1,256]{3,2,1,0:T(1,128)S(1)}, f32[3,16,1,256]{3,2,1,0:T(1,128)S(1)}, u32[]{:S(2)}, u32[]{:S(2)}) collective-permute-start(f32[3,16,1,256]{3,2,1,0:T(1,128)S(1)} %get-tuple-element.80), channel_id=1, source_target_pairs={{0,4},{4,0},{8,12},{12,8},{16,20},{20,16},{24,28},{28,24},{1,5},{5... | collective-permute-start | bytes 147464 | tf_op jit(solution)/shard_map/while/body/ppermute | solution.py:308
  75.8 4.2 %collective-permute-start.1 = (f32[3,16,1,256]{3,2,1,0:T(1,128)S(1)}, f32[3,16,1,256]{3,2,1,0:T(1,128)S(1)}, u32[]{:S(2)}, u32[]{:S(2)}) collective-permute-start(f32[3,16,1,256]{3,2,1,0:T(1,128)S(1)} %add.33), channel_id=1, source_target_pairs={{0,8},{4,12},{8,0},{12,4},{16,24},{20,28},{24,16},{28,20},{1,9},{5... | collective-permute-start | bytes 147464 | tf_op jit(solution)/shard_map/while/body/ppermute | solution.py:308
  80.0 4.2 %collective-permute-start.2 = (f32[3,16,1,256]{3,2,1,0:T(1,128)S(1)}, f32[3,16,1,256]{3,2,1,0:T(1,128)S(1)}, u32[]{:S(2)}, u32[]{:S(2)}) collective-permute-start(f32[3,16,1,256]{3,2,1,0:T(1,128)S(1)} %add.34), channel_id=1, source_target_pairs={{0,16},{4,20},{8,24},{12,28},{16,0},{20,4},{24,8},{28,12},{1,17},{... | collective-permute-start | bytes 147464 | tf_op jit(solution)/shard_map/while/body/ppermute | solution.py:308

commit v5 on v4

--- a/solution.py
+++ b/solution.py
@@ -78,7 +78,7 @@
     ]
 
 
-def prelude_kernel(columns, height, offset, field, courant, diffusivity, above, below, tile, panel, own, coef, pick, chosen, kept):
+def prelude_kernel(columns, height, offset, field, courant, diffusivity, above, below, tile, panel, own, coef, start, chosen, kept):
     def load(plane, carry):
         for column, value in shifted_plane(field, plane, offset[0]):
             own[plane, column] = value
@@ -98,21 +98,19 @@
     numbers = tile[...]
     inside = numbers & (columns * height - 1)
     numbers = (numbers - inside) + (inside & (columns - 1)) * height + inside // columns
-    upright = numbers.astype(jnp.float32).T.astype(jnp.int32)
-    groups, total = numbers.shape[0], pick.shape[1]
-    by_lane = lax.broadcasted_iota(jnp.int32, (GROUP, total), 1)
-    by_row = lax.broadcasted_iota(jnp.int32, (total, GROUP), 0)
-    for group in range(groups):
-        block = pl.ds(group * GROUP, GROUP)
-        found = jnp.where(upright[:, group : group + 1] == by_lane, 1.0, 0.0)
-        pick[block, :] = found.astype(jnp.bfloat16)
+    start[...] = numbers * STEPS
+    by_row = lax.broadcasted_iota(jnp.int32, (chosen.shape[0], GROUP), 0)
+    for group in range(numbers.shape[0]):
         found = jnp.where(numbers[group : group + 1, :] == by_row, 1.0, 0.0)
-        chosen[:, block] = found.astype(jnp.bfloat16)
+        chosen[:, pl.ds(group * GROUP, GROUP)] = found.astype(jnp.bfloat16)
 
 
 def adjoint_kernel(offset, coef, own, low, high, tiles, first, second):
     cells, columns, height = own.shape[:3]
-    steps = tiles.shape[1] // (2 * TILE)
+    steps = STEPS
+    edge = jnp.zeros((PAD, TILE), jnp.float32)
+    tiles[:PAD, :] = edge
+    tiles[tiles.shape[0] - PAD :, :] = edge
     inside = pl.ds(PAD, height)
     clear_pads(first)
     clear_pads(second)
@@ -131,27 +129,18 @@
 
         def sweep(place, carry, source=source, target=target, step=step):
             planes = range(step + 1, 3 * cells - step - 1)
-            halves = []
-            for half in range(2):
-                row = place * 16 + half * 8
-                blocks = sweep_rows(source, coef, planes, row, True)
-                halves.append(blocks)
-                if step < steps - 1:
-                    for plane, block in zip(planes, blocks):
-                        for c in range(columns):
-                            where = pl.ds(pl.multiple_of(PAD + row, 8), 8)
-                            target[plane, c, where, :] = block[c]
-            for plane, upper, lower in zip(planes, *halves):
-                if cells <= plane < 2 * cells:
-                    for c in range(columns):
-                        start = (plane - cells) * columns * height + c * height + place * 16
-                        where = pl.ds(pl.multiple_of(start, 16), 16)
-                        head, tail = split(jnp.concatenate([upper[c], lower[c]], axis=0))
-                        tiles[where, pl.ds(2 * step * TILE, TILE)] = head
-                        tiles[where, pl.ds((2 * step + 1) * TILE, TILE)] = tail
+            row = place * 8
+            for plane, block in zip(planes, sweep_rows(source, coef, planes, row, True)):
+                for c in range(columns):
+                    if step < steps - 1:
+                        where = pl.ds(pl.multiple_of(PAD + row, 8), 8)
+                        target[plane, c, where, :] = block[c]
+                    if cells <= plane < 2 * cells:
+                        number = ((plane - cells) * columns + c) * height + row
+                        tiles[pl.ds(PAD + number * steps + step, 8, stride=steps), :] = block[c]
             return carry
 
-        lax.fori_loop(0, height // 16, sweep, 0)
+        lax.fori_loop(0, height // 8, sweep, 0)
 
 
 def forward_kernel(coef, own, low, high, out, first, second):
@@ -189,47 +178,51 @@
         lax.fori_loop(0, height // 8, sweep, 0)
 
 
-def project_kernel(first, count, chunks, source, pick, tiles, *refs):
-    panels, (*before, out) = refs[: len(chunks)], refs[len(chunks) :]
+def project_kernel(chunks, source, start, tiles, *refs):
+    panels, (*before, out, wide) = refs[: len(chunks)], refs[len(chunks) :]
     shard = panels[0].shape[0] // GROUP
     for given in before:
         out[...] = given[...]
-    ones = jnp.ones((8, 2 * TILE), jnp.bfloat16)
-    weights = tiles[:, pl.ds(2 * first * TILE, 2 * count * TILE)]
+    first = lax.broadcasted_iota(jnp.int32, (8, TILE), 0) < STEPS
+    lane = lax.broadcasted_iota(jnp.int32, (8, TILE), 1)
     for chunk, panel in zip(chunks, panels):
-
-        def body(group, carry, chunk=chunk, panel=panel):
+        wide[...] = panel[...].astype(jnp.float32)
+
+        def body(group, carry, chunk=chunk):
             number = source[chunk] * shard + group
-            chosen = pick[pl.ds(pl.multiple_of(number * GROUP, GROUP), GROUP), :]
-            found = jnp.dot(chosen, weights, preferred_element_type=jnp.float32)
-            rows = panel[pl.ds(pl.multiple_of(group * GROUP, GROUP), GROUP), :].astype(jnp.float32)
-            for step in range(count):
-                start = 2 * step * TILE
-                cells = found[:, start : start + TILE] + found[:, start + TILE : start + 2 * TILE]
-                both = jnp.concatenate(split(cells * rows), axis=1)
-                sums = lax.dot_general(
-                    ones, both, (((1,), (1,)), ((), ())), preferred_element_type=jnp.float32
+            sums = jnp.zeros((8, TILE), jnp.float32)
+            for place in range(TILE):
+                left, right = start[number, place], start[number, TILE + place]
+                cells = jnp.where(
+                    first, tiles[pl.ds(PAD + left, 8), :], tiles[pl.ds(PAD - STEPS + right, 8), :]
                 )
-                out[step, number] = sums[:1]
+                row = group * GROUP + place
+                rows = jnp.where(first, wide[pl.ds(row, 1), :], wide[pl.ds(row + TILE, 1), :])
+                total = jnp.sum(cells * rows, axis=1, keepdims=True)
+                sums = jnp.where(lane == place, total, sums)
+            out[number] = sums
             return carry
 
-        lax.fori_loop(0, shard, body, 0, unroll=2 if count > 1 and shard % 2 == 0 else shard)
+        lax.fori_loop(0, shard, body, 0)
 
 
 def deposit_kernel(count, source, chosen, *refs):
     parts, panels, (total, field, rightward, leftward, scaled) = refs[:count], refs[count:-5], refs[-5:]
-    groups = total.shape[1]
+    groups = total.shape[0]
     shard = groups // len(panels)
     cells, per_plane = field.shape[0], field.shape[1]
     total[...] = tree_sum([part[...] for part in parts])
     numbers = [source[g // shard] * shard + g % shard for g in range(groups)]
-    drive = jnp.concatenate([total[0, number] for number in numbers], axis=0).T
+    last = [total[n, pl.ds(half * STEPS + STEPS - 1, 1), :] for n in numbers for half in range(2)]
+    drive = jnp.concatenate(last, axis=0).T
     for group, number in enumerate(numbers):
-        rows = panels[group // shard][pl.ds((group % shard) * GROUP, GROUP), :]
-        head, tail = split(drive[:, group : group + 1] * rows.astype(jnp.float32))
-        where = pl.ds(pl.multiple_of(number * GROUP, GROUP), GROUP)
-        scaled[where, pl.ds(0, TILE)] = head
-        scaled[where, pl.ds(TILE, TILE)] = tail
+        for half in range(2):
+            place = 2 * group + half
+            rows = panels[group // shard][pl.ds((group % shard) * GROUP + half * TILE, TILE), :]
+            head, tail = split(drive[:, place : place + 1] * rows.astype(jnp.float32))
+            where = pl.ds(pl.multiple_of(number * GROUP + half * TILE, TILE), TILE)
+            scaled[where, pl.ds(0, TILE)] = head
+            scaled[where, pl.ds(TILE, TILE)] = tail
 
     for plane in range(cells):
         sums = jnp.dot(
@@ -299,17 +292,6 @@
     return parts
 
 
-def doubling_sum(part, axis):
-    count = lax.axis_size(axis)
-    if count & (count - 1):
-        return lax.psum(part, axis)
-    mask = 1
-    while mask < count:
-        part = part + lax.ppermute(part, axis, [(i, i ^ mask) for i in range(count)])
-        mask *= 2
-    return part
-
-
 def local(sensor_field, courant, diffusivity, probe_offset, tile_index, actuator_panel):
     slabs, probes = lax.axis_size("state"), lax.axis_size("probe")
     own = sensor_field[0]
@@ -333,12 +315,12 @@
         jnp.concatenate([diffusivity[1:], zero]),
         jnp.concatenate([zero, diffusivity[:-1]]),
     ]
-    shifted, coef, pick, chosen, panel = call(
+    shifted, coef, start, chosen, panel = call(
         lambda *refs: prelude_kernel(columns, height, *refs),
         (
             jax.ShapeDtypeStruct((cells, columns, height, TILE), f32),
             jax.ShapeDtypeStruct((5, height, TILE), f32),
-            jax.ShapeDtypeStruct((actuators, tile_total), bf16),
+            jax.ShapeDtypeStruct((groups, GROUP), jnp.int32),
             jax.ShapeDtypeStruct((tile_total, actuators), bf16),
             jax.ShapeDtypeStruct(actuator_panel.shape[1:], bf16),
         ),
@@ -356,7 +338,7 @@
     field_shape = pltpu.VMEM((planes, columns, height + 2 * PAD, TILE), f32)
     tiles = call(
         adjoint_kernel,
-        jax.ShapeDtypeStruct((tile_total, 2 * STEPS * TILE), bf16),
+        jax.ShapeDtypeStruct((tile_total * STEPS + 2 * PAD, TILE), f32),
         scratch=(field_shape, field_shape),
         smem=1,
         inputs=5,
@@ -364,23 +346,23 @@
 
     every = list(range(probes))
 
-    def project(first, count, chunks, *given):
+    def project(chunks, *given):
         return call(
-            lambda *refs: project_kernel(first, count, chunks, *refs),
-            jax.ShapeDtypeStruct((count, groups, 1, GROUP), f32),
-            smem=1,
+            lambda *refs: project_kernel(chunks, *refs),
+            jax.ShapeDtypeStruct((groups, 2 * STEPS, TILE), f32),
+            scratch=(pltpu.VMEM((shard * GROUP, TILE), f32),),
+            smem=2,
             inputs=3 + len(chunks) + len(given),
-        )
-
-    before = project(STEPS - 1, 1, every[:-1])(source, pick, tiles, *panels[:-1])
-    last = project(STEPS - 1, 1, every[-1:], before)(source, pick, tiles, panels[-1], before)
-    parts = summands(last, "state")
+        )(source, start, tiles, *[panels[chunk] for chunk in chunks], *given)
+
+    before = project(every[:-1])
+    parts = summands(project(every[-1:], before), "state")
     payload = jax.ShapeDtypeStruct((2 * cells - 1, height * columns, TILE), bf16)
     heads = jax.ShapeDtypeStruct((cells, height * columns, TILE), bf16)
     total, forced, rightward, leftward = call(
         lambda *refs: deposit_kernel(len(parts), *refs),
         (
-            jax.ShapeDtypeStruct(last.shape, f32),
+            jax.ShapeDtypeStruct(before.shape, f32),
             jax.ShapeDtypeStruct((cells, height * columns, TILE), f32),
             payload,
             heads,
@@ -391,16 +373,13 @@
     )(source, chosen, *parts, *panels)
     from_low = lax.ppermute(rightward, "state", shift_pairs(slabs, 1))
     from_high = lax.ppermute(leftward, "state", shift_pairs(slabs, -1))
-    early = project(0, STEPS - 1, every)(tied(source, forced), pick, tiles, *panels)
-    rounds = 1 + jnp.minimum(probe_offset[0], 0)
-    early = lax.fori_loop(0, rounds, lambda _, part: doubling_sum(part, "state"), early)
     response = call(
         forward_kernel,
         jax.ShapeDtypeStruct((cells, height, width), f32),
         scratch=(field_shape, field_shape),
         inputs=4,
     )(coef, forced, from_low, from_high)
-    projections = jnp.concatenate([early, total], axis=0)
+    projections = total.reshape(groups, 2, STEPS, TILE).transpose(2, 0, 1, 3)
     return projections.reshape(STEPS, 1, actuators), response[None]
 
 

time: 90.6 us -> 68.3 us (0.75)
  Pallas kernels: 39.9 us -> 26.4 us
  local copies, waits for them, and re-layouts: 14.9 us -> 7.93 us
  starting transfers between devices: 16.5 us -> 15.1 us
    pallas_call x4 -> x3, Pallas kernels: 25.2 us -> 12 us  [the longest x2 6.96 us: project(): call(lambda *refs: project_kernel(chunks, *refs), jax.ShapeDtypeStruct((g...]
    ppermute x3 -> x0, waiting for transfers between devices: 8.09 us -> none  [doubling_sum(): lax.ppermute(part, axis, [(i, i ^ mask) for i in range(count)])]
    unnamed x17 -> x7, local copies, waits for them, and re-layouts: 12.4 us -> 4.77 us
    ppermute x1, waiting for transfers between devices: 0.01 us -> 6.1 us  [local(): from_high = lax.ppermute(leftward, 'state', shift_pairs(slabs, -1))]
    ppermute x1, waiting for transfers between devices: 0.01 us -> 2.21 us  [local(): from_low = lax.ppermute(rightward, 'state', shift_pairs(slabs, 1))]
    ppermute x3 -> x0, starting transfers between devices: 1.46 us -> none  [doubling_sum(): lax.ppermute(part, axis, [(i, i ^ mask) for i in range(count)])]
    ppermute x4, waiting for transfers between devices: 3.86 us -> 5.03 us  [summands(): parts = [part] + [lax.ppermute(part, axis, pair) for pair in pairs]]
    ppermute x3, waiting for transfers between devices: 3.3 us -> 2.34 us  [gathered_panel(): shards[held | mask] = lax.ppermute(operand, axis, pairs)]
  transfers between devices with their start and end apart: 14 -> 11, of which waited for: 7 -> 7; matrix products, arithmetic and copies ran while one was open for 6% -> 8% of each run, Pallas kernels for 32% -> 22%
where the time goes in v5:
time: 68.3 us; the launch traced here: 68 us
  Pallas kernels  26.4 us (39%)
  waiting for transfers between devices  15.7 us (23%)
  starting transfers between devices  15.1 us (22%)
  local copies, waits for them, and re-layouts  7.93 us (12%)
  other arithmetic  1.49 us (2%)
  between operations  1.38 us (2%)
    pallas_call x2, Pallas kernels, project(): call(lambda *refs: project_kernel(chunks, *refs), jax.ShapeDtypeStruct((g...  6.96 us
    ppermute x1, waiting for transfers between devices, local(): from_high = lax.ppermute(leftward, 'state', shift_pairs(slabs, -1))  6.1 us
    pallas_call x1, Pallas kernels, local(): call(lambda *refs: prelude_kernel(columns, height, *refs), (jax.ShapeDtyp...  5.42 us
    ppermute x3, starting transfers between devices, gathered_panel(): shards[held | mask] = lax.ppermute(operand, axis, pairs)  5.31 us
    pallas_call x1, Pallas kernels, local(): call(forward_kernel, jax.ShapeDtypeStruct((cells, height, width), f32), s...  5.29 us
    pallas_call x1, Pallas kernels, local(): call(adjoint_kernel, jax.ShapeDtypeStruct((tile_total * STEPS + 2 * PAD,...  5.06 us
    ppermute x4, waiting for transfers between devices, summands(): parts = [part] + [lax.ppermute(part, axis, pair) for pair in pairs]  5.03 us
    unnamed x7, local copies, waits for them, and re-layouts  4.77 us
  transfers between devices with their start and end apart: 11, of which 7 were waited for; matrix products, arithmetic and copies ran while one was open for 8% of the time, Pallas kernels for 22%

profile of v5, /device:TPU:0, one launch (start us, length us, event | category | flops | bytes accessed | tf_op | source)
XLA Modules:
  0.0 68.0 jit_solution(15594114694071844961)
XLA Ops:
  0.6 0.5 collective-permute-start
  1.1 2.9 %collective-permute-start.1 = (f32[4,64,512]{2,1,0:T(8,128)}, f32[4,64,512]{2,1,0:T(8,128)S(1)}, u32[]{:S(2)}, u32[]{:S(2)}) collective-permute-start(f32[4,64,512]{2,1,0:T(8,128)} %bitcast.14), channel_id=1, source_target_pairs={{0,28},{4,0},{8,4},{12,8},{16,12},{20,16},{24,20},{28,24},{1,29},{... | collective-permute-start | bytes 1572872 | tf_op jit(solution)/shard_map/ppermute | solution.py:309
  4.1 3.3 %collective-permute-start.2 = (bf16[1024,128]{1,0:T(8,128)(2,1)}, bf16[1024,128]{1,0:T(8,128)(2,1)S(1)}, u32[]{:S(2)}, u32[]{:S(2)}) collective-permute-start(bf16[1024,128]{1,0:T(8,128)(2,1)} %bitcast.5.refs_7_), channel_id=1, source_target_pairs={{0,2},{1,3},{2,0},{3,1},{4,6},{5,7},{6,4},{7,5},{8,10},{9,11},{10,... | collective-permute-start | bytes 786440 | tf_op jit(solution)/shard_map/ppermute | solution.py:265
  7.4 0.8 %fusion = (f32[63]{0:T(128)S(1)}, f32[63]{0:T(128)S(1)}) fusion(f32[64]{0:T(128)} %param.8), kind=kLoop, calls=%fused_computation.3 | loop fusion | bytes 1008 | tf_op jit(solution)/shard_map/slice | solution.py:316
  8.2 0.1 maximum_bitcast_fusion
  8.2 0.1 copy.10.refs_4_
  8.3 0.1 copy.11.refs_5_
  9.1 0.5 broadcast.3
  9.6 1.4 %reduce.3 = s32[4096]{0:T(1024)S(1)} reduce(s32[1,4096]{1,0:T(1,128)} %param.10, s32[]{:T(128)} %broadcast.3), dimensions={0}, to_apply=%param.10.reduce_sub_computation.3 | reduce | bytes 32772 | tf_op args[4]
  11.0 0.7 %copy.8.refs_2_ = f32[64,1]{1,0:T(8,128)S(1)} copy(f32[64,1]{0,1:T(1,128)} %bitcast.20) | data formatting | bytes 512 | tf_op jit(solution)/shard_map/broadcast_in_dim | solution.py:332
  11.8 0.7 %copy.9.refs_3_ = f32[64,1]{1,0:T(8,128)S(1)} copy(f32[64,1]{0,1:T(1,128)} %bitcast.19) | data formatting | bytes 512 | tf_op jit(solution)/shard_map/broadcast_in_dim | solution.py:332
  12.5 0.0 copy-start.2
  12.5 1.0 %copy-done.2 = f32[1,4,64,512]{3,2,1,0:T(8,128)S(1)} copy-done((f32[1,4,64,512]{3,2,1,0:T(8,128)S(1)}, f32[1,4,64,512]{3,2,1,0:T(8,128)}, u32[]{:S(2)}) %copy-start.2) | copy-done | bytes 524312
  13.6 5.4 %shard_map.77 = (f32[4,4,64,128]{3,2,1,0:T(8,128)S(1)}, f32[5,64,128]{2,1,0:T(8,128)S(1)}, s32[16,256]{1,0:T(8,128)S(1)}, bf16[1024,4096]{1,0:T(8,128)(2,1)S(1)}, bf16[1024,128]{1,0:T(8,128)(2,1)S(1)}) custom-call(s32[1]{0:T(128)S(6)} %copy.13.refs_0_.offset, f32[4,64,512]{2,1,0:T(8,128)S(1)} %bitcast.15, f32[64,1]{1,0:T(8,128)S(1)} %copy.8.refs_2_, ...), custom_call_target="tpu_custom_call" | custom-call | flops 1024 | bytes 1024 | tf_op jit(solution)/shard_map/pallas_call | solution.py:318
  19.0 0.0 copy-start
  19.0 3.2 %copy-done = bf16[1024,4096]{1,0:T(8,128)(2,1)} copy-done((bf16[1024,4096]{1,0:T(8,128)(2,1)}, bf16[1024,4096]{1,0:T(8,128)(2,1)S(1)}, u32[]{:S(2)}) %copy-start) | copy-done | bytes 8388632
  22.2 1.6 %collective-permute-start.4 = (bf16[1024,128]{1,0:T(8,128)(2,1)}, bf16[1024,128]{1,0:T(8,128)(2,1)S(1)}, u32[]{:S(2)}, u32[]{:S(2)}) collective-permute-start(bf16[1024,128]{1,0:T(8,128)(2,1)} %bitcast.5.refs_7_), channel_id=1, source_target_pairs={{0,1},{1,0},{2,3},{3,2},{4,5},{5,4},{6,7},{7,6},{8,9},{9,8},{10,11... | collective-permute-start | bytes 786440 | tf_op jit(solution)/shard_map/ppermute | solution.py:265
  23.8 0.0 collective-permute-done.2.refs_5_.refs_8_
  23.8 0.5 collective-permute-start.3
  24.2 0.0 copy-start.1
  24.2 0.0 collective-permute-done.low
  24.2 0.0 collective-permute-done.1.high
  24.3 5.1 %shard_map.78.refs_2_ = f32[4112,128]{1,0:T(8,128)S(1)} custom-call(s32[1]{0:T(128)S(6)} %copy.13.refs_0_.offset, f32[5,64,128]{2,1,0:T(8,128)S(1)} %get-tuple-element.15.coef, f32[4,4,64,128]{3,2,1,0:T(8,128)S(1)} %get-tuple-element.16.own, f32[4,64,512]{2,1,0:T(8,128)S(1)} %collective-permute-done.low, f32[4,64,512]{2,1,0:T(8,128)S(1)} %collective-permute-done.1.high), custom_call_target="tpu_custom_call" | custom-call | flops 1024 | bytes 1024 | tf_op jit(solution)/shard_map/pallas_call | solution.py:339
  29.3 2.3 %collective-permute-done.4.refs_4_.refs_7_ = bf16[1024,128]{1,0:T(8,128)(2,1)S(1)} collective-permute-done((bf16[1024,128]{1,0:T(8,128)(2,1)}, bf16[1024,128]{1,0:T(8,128)(2,1)S(1)}, u32[]{:S(2)}, u32[]{:S(2)}) %collective-permute-start.4) | collective-permute-done | bytes 262176 | tf_op jit(solution)/shard_map/ppermute | solution.py:265
  31.7 4.8 %shard_map.79.refs_4_ = f32[16,8,128]{2,1,0:T(8,128)S(1)} custom-call(s32[4]{0:T(128)S(1)} %iota_xor_fusion.refs_0_, s32[16,256]{1,0:T(8,128)S(1)} %get-tuple-element.14.refs_1_, f32[4112,128]{1,0:T(8,128)S(1)} %shard_map.78.refs_2_, bf16[1024,128]{1,0:T(8,128)(2,1)S(1)} %get-tuple-element.18.refs_3_.refs_6_, ...), custom_call_target="tpu_custom_call" | custom-call | flops 1024 | bytes 1024 | tf_op jit(solution)/shard_map/pallas_call | solution.py:350
  36.5 0.0 collective-permute-done.3.refs_3_.refs_9_
  36.5 2.2 %shard_map.80 = f32[16,8,128]{2,1,0:T(8,128)S(1)} custom-call(s32[4]{0:T(128)S(1)} %iota_xor_fusion.refs_0_, s32[16,256]{1,0:T(8,128)S(1)} %get-tuple-element.14.refs_1_, f32[4112,128]{1,0:T(8,128)S(1)} %shard_map.78.refs_2_, bf16[1024,128]{1,0:T(8,128)(2,1)S(1)} %collective-permute-done.3.refs_3_.refs_9_, f32[16,8,128]{2,1,0:T(8,128)S(1)} %shard_map.79.refs_4_), custom_call_target="tpu_custom_call" | custom-call | flops 1024 | bytes 1024 | tf_op jit(solution)/shard_map/pallas_call | solution.py:350
  38.6 0.1 collective-permute-start.5
  38.7 1.2 %collective-permute-done.5 = f32[16,8,128]{2,1,0:T(8,128)S(1)} collective-permute-done((f32[16,8,128]{2,1,0:T(8,128)S(1)}, f32[16,8,128]{2,1,0:T(8,128)S(1)}, u32[]{:S(2)}, u32[]{:S(2)}) %collective-permute-start.5) | collective-permute-done | bytes 65568 | tf_op jit(solution)/shard_map/ppermute | solution.py:290
  40.0 0.6 collective-permute-start.6
  40.6 1.6 %collective-permute-start.7 = (f32[16,8,128]{2,1,0:T(8,128)S(1)}, f32[16,8,128]{2,1,0:T(8,128)S(1)}, u32[]{:S(2)}, u32[]{:S(2)}) collective-permute-start(f32[16,8,128]{2,1,0:T(8,128)S(1)} %add.3.refs_2_), channel_id=1, source_target_pairs={{0,16},{4,20},{8,24},{12,28},{16,0},{20,4},{24,8},{28,12},{1,17},{... | collective-permute-start | bytes 196616 | tf_op jit(solution)/shard_map/ppermute | solution.py:290
  42.1 1.4 %collective-permute-start.8 = (f32[16,8,128]{2,1,0:T(8,128)S(1)}, f32[16,8,128]{2,1,0:T(8,128)S(1)}, u32[]{:S(2)}, u32[]{:S(2)}) collective-permute-start(f32[16,8,128]{2,1,0:T(8,128)S(1)} %add.3.refs_2_), channel_id=1, source_target_pairs={{0,24},{4,28},{8,16},{12,20},{16,8},{20,12},{24,0},{28,4},{1,25},{... | collective-permute-start | bytes 196616 | tf_op jit(solution)/shard_map/ppermute | solution.py:290
  43.5 0.9 %collective-permute-done.6.refs_3_ = f32[16,8,128]{2,1,0:T(8,128)S(1)} collective-permute-done((f32[16,8,128]{2,1,0:T(8,128)S(1)}, f32[16,8,128]{2,1,0:T(8,128)S(1)}, u32[]{:S(2)}, u32[]{:S(2)}) %collective-permute-start.6) | collective-permute-done | bytes 65568 | tf_op jit(solution)/shard_map/ppermute | solution.py:290
  44.4 0.5 collective-permute-done.7.refs_4_
  44.9 2.5 %collective-permute-done.8.refs_5_ = f32[16,8,128]{2,1,0:T(8,128)S(1)} collective-permute-done((f32[16,8,128]{2,1,0:T(8,128)S(1)}, f32[16,8,128]{2,1,0:T(8,128)S(1)}, u32[]{:S(2)}, u32[]{:S(2)}) %collective-permute-start.8) | collective-permute-done | bytes 65568 | tf_op jit(solution)/shard_map/ppermute | solution.py:290
  47.3 0.0 copy-done.1
  47.3 3.7 %shard_map.81 = (f32[16,8,128]{2,1,0:T(8,128)S(1)}, f32[4,256,128]{2,1,0:T(8,128)S(1)}, bf16[7,256,128]{2,1,0:T(8,128)(2,1)S(1)}, bf16[4,256,128]{2,1,0:T(8,128)(2,1)S(1)}) custom-call(s32[4]{0:T(128)S(1)} %iota_xor_fusion.refs_0_, bf16[1024,4096]{1,0:T(8,128)(2,1)S(1)} %copy-done.1, f32[16,8,128]{2,1,0:T(8,128)S(1)} %add.3.refs_2_, ...), custom_call_target="tpu_custom_call" | custom-call | flops 1024 | bytes 1024 | tf_op jit(solution)/shard_map/pallas_call | solution.py:362
  51.0 0.1 collective-permute-start.9
  51.1 2.6 %collective-permute-start.10 = (bf16[4,256,128]{2,1,0:T(8,128)(2,1)S(1)}, bf16[4,256,128]{2,1,0:T(8,128)(2,1)S(1)}, u32[]{:S(2)}, u32[]{:S(2)}) collective-permute-start(bf16[4,256,128]{2,1,0:T(8,128)(2,1)S(1)} %get-tuple-element.23), channel_id=1, source_target_pairs={{0,28},{4,0},{8,4},{12,8},{16,12},{20,16},{24,20},{28,24},{1,29},{... | collective-permute-start | bytes 786440 | tf_op jit(solution)/shard_map/ppermute | solution.py:375
  53.7 0.7 copy.12
  54.4 6.1 %collective-permute-done.10.high = bf16[4,256,128]{2,1,0:T(8,128)(2,1)S(1)} collective-permute-done((bf16[4,256,128]{2,1,0:T(8,128)(2,1)S(1)}, bf16[4,256,128]{2,1,0:T(8,128)(2,1)S(1)}, u32[]{:S(2)}, u32[]{:S(2)}) %collective-permute-start.10) | collective-permute-done | bytes 262176 | tf_op jit(solution)/shard_map/ppermute | solution.py:375
  60.5 2.2 %collective-permute-done.9.low = bf16[7,256,128]{2,1,0:T(8,128)(2,1)S(1)} collective-permute-done((bf16[7,256,128]{2,1,0:T(8,128)(2,1)S(1)}, bf16[7,256,128]{2,1,0:T(8,128)(2,1)S(1)}, u32[]{:S(2)}, u32[]{:S(2)}) %collective-permute-start.9) | collective-permute-done | bytes 458784 | tf_op jit(solution)/shard_map/ppermute | solution.py:374
  62.7 5.3 %shard_map.82 = f32[4,64,512]{2,1,0:T(8,128)} custom-call(f32[5,64,128]{2,1,0:T(8,128)S(1)} %get-tuple-element.15.coef, f32[4,256,128]{2,1,0:T(8,128)S(1)} %get-tuple-element.21.own, bf16[7,256,128]{2,1,0:T(8,128)(2,1)S(1)} %collective-permute-done.9.low, bf16[4,256,128]{2,1,0:T(8,128)(2,1)S(1)} %collective-permute-done.10.high), custom_call_target="tpu_custom_call" | custom-call | flops 1024 | bytes 1024 | tf_op jit(solution)/shard_map/pallas_call | solution.py:376
  (3 shorter events, 0.0 us)
Async XLA Ops:
  0.6 23.6 %collective-permute-start = (f32[4,64,512]{2,1,0:T(8,128)}, f32[4,64,512]{2,1,0:T(8,128)S(1)}, u32[]{:S(2)}, u32[]{:S(2)}) collective-permute-start(f32[4,64,512]{2,1,0:T(8,128)} %bitcast.13), channel_id=1, source_target_pairs={{0,4},{4,8},{8,12},{12,16},{16,20},{20,24},{24,28},{28,0},{1,5},{5... | collective-permute-start | bytes 1572872 | tf_op jit(solution)/shard_map/ppermute | solution.py:308
  1.1 23.1 %collective-permute-start.1 = (f32[4,64,512]{2,1,0:T(8,128)}, f32[4,64,512]{2,1,0:T(8,128)S(1)}, u32[]{:S(2)}, u32[]{:S(2)}) collective-permute-start(f32[4,64,512]{2,1,0:T(8,128)} %bitcast.14), channel_id=1, source_target_pairs={{0,28},{4,0},{8,4},{12,8},{16,12},{20,16},{24,20},{28,24},{1,29},{... | collective-permute-start | bytes 1572872 | tf_op jit(solution)/shard_map/ppermute | solution.py:309
  4.1 19.7 %collective-permute-start.2 = (bf16[1024,128]{1,0:T(8,128)(2,1)}, bf16[1024,128]{1,0:T(8,128)(2,1)S(1)}, u32[]{:S(2)}, u32[]{:S(2)}) collective-permute-start(bf16[1024,128]{1,0:T(8,128)(2,1)} %bitcast.5.refs_7_), channel_id=1, source_target_pairs={{0,2},{1,3},{2,0},{3,1},{4,6},{5,7},{6,4},{7,5},{8,10},{9,11},{10,... | collective-permute-start | bytes 786440 | tf_op jit(solution)/shard_map/ppermute | solution.py:265
  12.5 1.0 %copy-start.2 = (f32[1,4,64,512]{3,2,1,0:T(8,128)S(1)}, f32[1,4,64,512]{3,2,1,0:T(8,128)}, u32[]{:S(2)}) copy-start(f32[1,4,64,512]{3,2,1,0:T(8,128)} %param.6) | copy-start | bytes 1572868
  19.0 3.2 %copy-start = (bf16[1024,4096]{1,0:T(8,128)(2,1)}, bf16[1024,4096]{1,0:T(8,128)(2,1)S(1)}, u32[]{:S(2)}) copy-start(bf16[1024,4096]{1,0:T(8,128)(2,1)S(1)} %get-tuple-element.13.refs_1_) | copy-start | bytes 25165828
  22.2 9.5 %collective-permute-start.4 = (bf16[1024,128]{1,0:T(8,128)(2,1)}, bf16[1024,128]{1,0:T(8,128)(2,1)S(1)}, u32[]{:S(2)}, u32[]{:S(2)}) collective-permute-start(bf16[1024,128]{1,0:T(8,128)(2,1)} %bitcast.5.refs_7_), channel_id=1, source_target_pairs={{0,1},{1,0},{2,3},{3,2},{4,5},{5,4},{6,7},{7,6},{8,9},{9,8},{10,11... | collective-permute-start | bytes 786440 | tf_op jit(solution)/shard_map/ppermute | solution.py:265
  23.8 12.7 %collective-permute-start.3 = (bf16[1024,128]{1,0:T(8,128)(2,1)S(1)}, bf16[1024,128]{1,0:T(8,128)(2,1)S(1)}, u32[]{:S(2)}, u32[]{:S(2)}) collective-permute-start(bf16[1024,128]{1,0:T(8,128)(2,1)S(1)} %collective-permute-done.2.refs_5_.refs_8_), channel_id=1, source_target_pairs={{0,1},{1,0},{2,3},{3,2},{4,5},{5,4},{6,7},{7,6},{8,9},{9,8},{10,11... | collective-permute-start | bytes 786440 | tf_op jit(solution)/shard_map/ppermute | solution.py:265
  24.2 23.1 %copy-start.1 = (bf16[1024,4096]{1,0:T(8,128)(2,1)S(1)}, bf16[1024,4096]{1,0:T(8,128)(2,1)}, u32[]{:S(2)}) copy-start(bf16[1024,4096]{1,0:T(8,128)(2,1)} %copy-done) | copy-start | bytes 25165828
  38.6 1.3 %collective-permute-start.5 = (f32[16,8,128]{2,1,0:T(8,128)S(1)}, f32[16,8,128]{2,1,0:T(8,128)S(1)}, u32[]{:S(2)}, u32[]{:S(2)}) collective-permute-start(f32[16,8,128]{2,1,0:T(8,128)S(1)} %shard_map.80), channel_id=1, source_target_pairs={{0,4},{4,0},{8,12},{12,8},{16,20},{20,16},{24,28},{28,24},{1,5},{5... | collective-permute-start | bytes 196616 | tf_op jit(solution)/shard_map/ppermute | solution.py:290
  40.0 4.4 %collective-permute-start.6 = (f32[16,8,128]{2,1,0:T(8,128)S(1)}, f32[16,8,128]{2,1,0:T(8,128)S(1)}, u32[]{:S(2)}, u32[]{:S(2)}) collective-permute-start(f32[16,8,128]{2,1,0:T(8,128)S(1)} %add.3.refs_2_), channel_id=1, source_target_pairs={{0,8},{4,12},{8,0},{12,4},{16,24},{20,28},{24,16},{28,20},{1,9},{5... | collective-permute-start | bytes 196616 | tf_op jit(solution)/shard_map/ppermute | solution.py:290
  40.6 4.3 %collective-permute-start.7 = (f32[16,8,128]{2,1,0:T(8,128)S(1)}, f32[16,8,128]{2,1,0:T(8,128)S(1)}, u32[]{:S(2)}, u32[]{:S(2)}) collective-permute-start(f32[16,8,128]{2,1,0:T(8,128)S(1)} %add.3.refs_2_), channel_id=1, source_target_pairs={{0,16},{4,20},{8,24},{12,28},{16,0},{20,4},{24,8},{28,12},{1,17},{... | collective-permute-start | bytes 196616 | tf_op jit(solution)/shard_map/ppermute | solution.py:290
  42.1 5.2 %collective-permute-start.8 = (f32[16,8,128]{2,1,0:T(8,128)S(1)}, f32[16,8,128]{2,1,0:T(8,128)S(1)}, u32[]{:S(2)}, u32[]{:S(2)}) collective-permute-start(f32[16,8,128]{2,1,0:T(8,128)S(1)} %add.3.refs_2_), channel_id=1, source_target_pairs={{0,24},{4,28},{8,16},{12,20},{16,8},{20,12},{24,0},{28,4},{1,25},{... | collective-permute-start | bytes 196616 | tf_op jit(solution)/shard_map/ppermute | solution.py:290
  51.0 11.7 %collective-permute-start.9 = (bf16[7,256,128]{2,1,0:T(8,128)(2,1)S(1)}, bf16[7,256,128]{2,1,0:T(8,128)(2,1)S(1)}, u32[]{:S(2)}, u32[]{:S(2)}) collective-permute-start(bf16[7,256,128]{2,1,0:T(8,128)(2,1)S(1)} %get-tuple-element.22), channel_id=1, source_target_pairs={{0,4},{4,8},{8,12},{12,16},{16,20},{20,24},{24,28},{28,0},{1,5},{5... | collective-permute-start | bytes 1376264 | tf_op jit(solution)/shard_map/ppermute | solution.py:374
  51.1 9.4 %collective-permute-start.10 = (bf16[4,256,128]{2,1,0:T(8,128)(2,1)S(1)}, bf16[4,256,128]{2,1,0:T(8,128)(2,1)S(1)}, u32[]{:S(2)}, u32[]{:S(2)}) collective-permute-start(bf16[4,256,128]{2,1,0:T(8,128)(2,1)S(1)} %get-tuple-element.23), channel_id=1, source_target_pairs={{0,28},{4,0},{8,4},{12,8},{16,12},{20,16},{24,20},{28,24},{1,29},{... | collective-permute-start | bytes 786440 | tf_op jit(solution)/shard_map/ppermute | solution.py:375

commit v6 on v5

--- a/solution.py
+++ b/solution.py
@@ -9,7 +9,6 @@
 STEPS = 4
 PAD = 8
 GROUP = 256
-VMEM_LIMIT = 24 * 1024 * 1024
 
 
 def shift_pairs(count, by):
@@ -78,31 +77,41 @@
     ]
 
 
-def prelude_kernel(columns, height, offset, field, courant, diffusivity, above, below, tile, panel, own, coef, start, chosen, kept):
+def prelude_kernel(offset, field, courant, diffusivity, tile, panel, own, coef, start, chosen, kept):
+    columns, height = own.shape[1:3]
+
     def load(plane, carry):
         for column, value in shifted_plane(field, plane, offset[0]):
             own[plane, column] = value
         return carry
 
     lax.fori_loop(0, field.shape[0], load, 0)
-    rates = (
-        1.0 - courant[...] - 6.0 * diffusivity[...],
-        courant[...] + diffusivity[...],
-        diffusivity[...],
-        above[...],
-        below[...],
-    )
-    for place, rate in enumerate(rates):
-        coef[place] = jnp.broadcast_to(rate, coef.shape[1:])
     kept[...] = panel[...]
+    padding = jnp.zeros((6, height), jnp.float32)
+    upright = jnp.concatenate([courant[...], diffusivity[...], padding], axis=0).T
+    speed = jnp.broadcast_to(upright[:, 0:1], (height, TILE))
+    rate = jnp.broadcast_to(upright[:, 1:2], (height, TILE))
+    edge = jnp.zeros((1, TILE), jnp.float32)
+    coef[0] = 1.0 - speed - 6.0 * rate
+    coef[1] = speed + rate
+    coef[2] = rate
+    coef[3] = jnp.concatenate([rate[1:], edge], axis=0)
+    coef[4] = jnp.concatenate([edge, rate[:-1]], axis=0)
     numbers = tile[...]
     inside = numbers & (columns * height - 1)
     numbers = (numbers - inside) + (inside & (columns - 1)) * height + inside // columns
     start[...] = numbers * STEPS
-    by_row = lax.broadcasted_iota(jnp.int32, (chosen.shape[0], GROUP), 0)
-    for group in range(numbers.shape[0]):
-        found = jnp.where(numbers[group : group + 1, :] == by_row, 1.0, 0.0)
-        chosen[:, pl.ds(group * GROUP, GROUP)] = found.astype(jnp.bfloat16)
+    rows = 64
+
+    def choose(place, carry):
+        by_row = lax.broadcasted_iota(jnp.int32, (rows, TILE), 0) + place * rows
+        where = pl.ds(pl.multiple_of(place * rows, rows), rows)
+        for left in range(0, chosen.shape[1], TILE):
+            found = jnp.where(numbers[:, left : left + TILE] == by_row, 1.0, 0.0)
+            chosen[where, pl.ds(left, TILE)] = found.astype(jnp.bfloat16)
+        return carry
+
+    lax.fori_loop(0, chosen.shape[0] // rows, choose, 0)
 
 
 def adjoint_kernel(offset, coef, own, low, high, tiles, first, second):
@@ -192,7 +201,8 @@
             number = source[chunk] * shard + group
             sums = jnp.zeros((8, TILE), jnp.float32)
             for place in range(TILE):
-                left, right = start[number, place], start[number, TILE + place]
+                left = start[0, number * GROUP + place]
+                right = start[0, number * GROUP + TILE + place]
                 cells = jnp.where(
                     first, tiles[pl.ds(PAD + left, 8), :], tiles[pl.ds(PAD - STEPS + right, 8), :]
                 )
@@ -239,7 +249,7 @@
             rightward[cells + plane - 1] = tail
 
 
-def call(kernel, out_shape, scratch=(), smem=0, inputs=0):
+def call(kernel, out_shape, vmem, scratch=(), smem=0, inputs=0):
     in_specs = [pl.BlockSpec(memory_space=pltpu.SMEM)] * smem
     in_specs += [pl.BlockSpec(memory_space=pltpu.VMEM)] * (inputs - smem)
     out_specs = jax.tree.map(lambda _: pl.BlockSpec(memory_space=pltpu.VMEM), out_shape)
@@ -249,19 +259,18 @@
         in_specs=in_specs,
         out_specs=out_specs,
         scratch_shapes=list(scratch),
-        compiler_params=pltpu.CompilerParams(vmem_limit_bytes=VMEM_LIMIT),
+        compiler_params=pltpu.CompilerParams(vmem_limit_bytes=vmem * 1024 * 1024),
         cost_estimate=pl.CostEstimate(flops=1024, bytes_accessed=1024, transcendentals=0),
     )
 
 
 def gathered_panel(panel, axis, ready):
     count = lax.axis_size(axis)
-    shards = {0: panel}
-    mask = count // 2
+    shards, mask = {0: panel}, count // 2
     while mask:
         pairs = [(i, i ^ mask) for i in range(count)]
         for held in sorted(shards):
-            operand = panel if len(shards) == 1 else tied(shards[held], ready)
+            operand = tied(shards[held], ready) if held else panel
             shards[held | mask] = lax.ppermute(operand, axis, pairs)
         mask //= 2
     return [shards[k] for k in range(1, count)]
@@ -308,48 +317,38 @@
     low = lax.ppermute(own, "state", shift_pairs(slabs, 1))
     high = lax.ppermute(own, "state", shift_pairs(slabs, -1))
 
-    zero = jnp.zeros((1,), f32)
-    rates = [
-        courant,
-        diffusivity,
-        jnp.concatenate([diffusivity[1:], zero]),
-        jnp.concatenate([zero, diffusivity[:-1]]),
-    ]
     shifted, coef, start, chosen, panel = call(
-        lambda *refs: prelude_kernel(columns, height, *refs),
+        prelude_kernel,
         (
             jax.ShapeDtypeStruct((cells, columns, height, TILE), f32),
             jax.ShapeDtypeStruct((5, height, TILE), f32),
-            jax.ShapeDtypeStruct((groups, GROUP), jnp.int32),
+            jax.ShapeDtypeStruct(tile_index.shape, jnp.int32),
             jax.ShapeDtypeStruct((tile_total, actuators), bf16),
             jax.ShapeDtypeStruct(actuator_panel.shape[1:], bf16),
         ),
+        vmem=14,
         smem=1,
-        inputs=8,
-    )(
-        probe_offset,
-        own,
-        *[rate[:, None] for rate in rates],
-        tile_index.reshape(groups, GROUP),
-        actuator_panel[0],
-    )
-    panels = [panel] + gathered_panel(actuator_panel[0], "probe", coef)
+        inputs=6,
+    )(probe_offset, own, courant[None], diffusivity[None], tile_index, actuator_panel[0])
 
     field_shape = pltpu.VMEM((planes, columns, height + 2 * PAD, TILE), f32)
     tiles = call(
         adjoint_kernel,
         jax.ShapeDtypeStruct((tile_total * STEPS + 2 * PAD, TILE), f32),
+        vmem=10,
         scratch=(field_shape, field_shape),
         smem=1,
         inputs=5,
     )(probe_offset, coef, shifted, low, high)
 
+    panels = [panel] + gathered_panel(actuator_panel[0], "probe", tiles)
     every = list(range(probes))
 
     def project(chunks, *given):
         return call(
             lambda *refs: project_kernel(chunks, *refs),
             jax.ShapeDtypeStruct((groups, 2 * STEPS, TILE), f32),
+            vmem=6,
             scratch=(pltpu.VMEM((shard * GROUP, TILE), f32),),
             smem=2,
             inputs=3 + len(chunks) + len(given),
@@ -367,6 +366,7 @@
             payload,
             heads,
         ),
+        vmem=18,
         scratch=(pltpu.VMEM((actuators, 2 * TILE), bf16),),
         smem=1,
         inputs=2 + len(parts) + probes,
@@ -376,6 +376,7 @@
     response = call(
         forward_kernel,
         jax.ShapeDtypeStruct((cells, height, width), f32),
+        vmem=10,
         scratch=(field_shape, field_shape),
         inputs=4,
     )(coef, forced, from_low, from_high)

time: 68.3 us -> 66.1 us (0.968)
  local copies, waits for them, and re-layouts: 7.93 us -> 11.3 us
  Pallas kernels: 26.4 us -> 23.1 us
  other arithmetic: 1.49 us -> 0.01 us
  waiting for transfers between devices: 15.7 us -> 15 us
    unnamed x7 -> x14, local copies, waits for them, and re-layouts: 4.77 us -> 10.6 us
    pallas_call x2, Pallas kernels: 10.7 us -> 7.88 us  [the longest x1 5.3 us: local(): call(forward_kernel, jax.ShapeDtypeStruct((cells, height, width), f32), v...]
    broadcast_in_dim x4 -> x0, local copies, waits for them, and re-layouts: 1.68 us -> none  [local(): rate[:, None]]
    unnamed x1 -> x0, other arithmetic: 1.4 us -> none
    slice x1 -> x0, local copies, waits for them, and re-layouts: 0.8 us -> none  [local(): diffusivity[:-1]]
  transfers between devices with their start and end apart: 11 -> 11, of which waited for: 7 -> 7; matrix products, arithmetic and copies ran while one was open for 8% -> 1% of each run, Pallas kernels for 22% -> 18%
where the time goes in v6:
time: 66.1 us; the launch traced here: 65.8 us
  Pallas kernels  23.1 us (35%)
  starting transfers between devices  15.1 us (23%)
  waiting for transfers between devices  15 us (23%)
  local copies, waits for them, and re-layouts  11.3 us (17%)
  between operations  1.37 us (2%)
    unnamed x14, local copies, waits for them, and re-layouts  10.6 us
    pallas_call x2, Pallas kernels, project(): call(lambda *refs: project_kernel(chunks, *refs), jax.ShapeDtypeStruct((g...  6.45 us
    ppermute x1, waiting for transfers between devices, local(): from_high = lax.ppermute(leftward, 'state', shift_pairs(slabs, -1))  6.1 us
    ppermute x3, starting transfers between devices, gathered_panel(): shards[held | mask] = lax.ppermute(operand, axis, pairs)  5.37 us
    pallas_call x1, Pallas kernels, local(): call(forward_kernel, jax.ShapeDtypeStruct((cells, height, width), f32), v...  5.3 us
    pallas_call x1, Pallas kernels, local(): call(adjoint_kernel, jax.ShapeDtypeStruct((tile_total * STEPS + 2 * PAD,...  5.06 us
    ppermute x4, waiting for transfers between devices, summands(): parts = [part] + [lax.ppermute(part, axis, pair) for pair in pairs]  4.92 us
    pallas_call x1, Pallas kernels, local(): call(lambda *refs: deposit_kernel(len(parts), *refs), (jax.ShapeDtypeStru...  3.68 us
  transfers between devices with their start and end apart: 11, of which 7 were waited for; matrix products, arithmetic and copies ran while one was open for 1% of the time, Pallas kernels for 18%

profile of v6, /device:TPU:0, one launch (start us, length us, event | category | flops | bytes accessed | tf_op | source)
XLA Modules:
  0.0 65.8 jit_solution(16315576434559113688)
XLA Ops:
  0.6 0.5 collective-permute-start
  1.1 2.9 %collective-permute-start.1 = (f32[4,64,512]{2,1,0:T(8,128)}, f32[4,64,512]{2,1,0:T(8,128)S(1)}, u32[]{:S(2)}, u32[]{:S(2)}) collective-permute-start(f32[4,64,512]{2,1,0:T(8,128)} %bitcast.10), channel_id=1, source_target_pairs={{0,28},{4,0},{8,4},{12,8},{16,12},{20,16},{24,20},{28,24},{1,29},{... | collective-permute-start | bytes 1572872 | tf_op jit(solution)/shard_map/ppermute | solution.py:318
  4.1 3.3 %collective-permute-start.2 = (bf16[1024,128]{1,0:T(8,128)(2,1)}, bf16[1024,128]{1,0:T(8,128)(2,1)S(1)}, u32[]{:S(2)}, u32[]{:S(2)}) collective-permute-start(bf16[1024,128]{1,0:T(8,128)(2,1)} %bitcast.12), channel_id=1, source_target_pairs={{0,2},{1,3},{2,0},{3,1},{4,6},{5,7},{6,4},{7,5},{8,10},{9,11},{10,... | collective-permute-start | bytes 786440 | tf_op jit(solution)/shard_map/ppermute | solution.py:274
  7.4 1.6 %collective-permute-start.4 = (bf16[1024,128]{1,0:T(8,128)(2,1)}, bf16[1024,128]{1,0:T(8,128)(2,1)S(1)}, u32[]{:S(2)}, u32[]{:S(2)}) collective-permute-start(bf16[1024,128]{1,0:T(8,128)(2,1)} %bitcast.13), channel_id=1, source_target_pairs={{0,1},{1,0},{2,3},{3,2},{4,5},{5,4},{6,7},{7,6},{8,9},{9,8},{10,11... | collective-permute-start | bytes 786440 | tf_op jit(solution)/shard_map/ppermute | solution.py:274
  9.6 0.0 copy-start.2
  9.6 1.0 %copy-done.2 = f32[1,4,64,512]{3,2,1,0:T(8,128)S(1)} copy-done((f32[1,4,64,512]{3,2,1,0:T(8,128)S(1)}, f32[1,4,64,512]{3,2,1,0:T(8,128)}, u32[]{:S(2)}) %copy-start.2) | copy-done | bytes 524312
  10.6 0.0 copy-start.3
  10.6 0.9 %copy-done.3 = bf16[1,1024,128]{2,1,0:T(8,128)(2,1)S(1)} copy-done((bf16[1,1024,128]{2,1,0:T(8,128)(2,1)S(1)}, bf16[1,1024,128]{2,1,0:T(8,128)(2,1)}, u32[]{:S(2)}) %copy-start.3) | copy-done | bytes 262168
  11.6 0.0 copy-start.4
  11.6 0.7 %copy-done.4 = s32[1,4096]{1,0:T(1,128)S(1)} copy-done((s32[1,4096]{1,0:T(1,128)S(1)}, s32[1,4096]{1,0:T(1,128)}, u32[]{:S(2)}) %copy-start.4) | copy-done | bytes 16408
  12.3 0.0 copy-start.5
  12.3 0.7 copy-done.5
  13.0 0.0 copy-start.6
  13.0 0.7 copy-done.6
  13.6 2.6 %shard_map.77 = (f32[4,4,64,128]{3,2,1,0:T(8,128)S(1)}, f32[5,64,128]{2,1,0:T(8,128)S(1)}, s32[1,4096]{1,0:T(1,128)S(1)}, bf16[1024,4096]{1,0:T(8,128)(2,1)S(1)}, bf16[1024,128]{1,0:T(8,128)(2,1)S(1)}) custom-call(s32[1]{0:T(128)S(6)} %copy.9.offset, f32[4,64,512]{2,1,0:T(8,128)S(1)} %bitcast.11, f32[1,64]{1,0:T(1,128)S(1)} %bitcast.16, ...), custom_call_target="tpu_custom_call" | custom-call | flops 1024 | bytes 1024 | tf_op jit(solution)/shard_map/pallas_call | solution.py:320
  16.2 0.0 copy-start
  16.2 3.2 %copy-done = bf16[1024,4096]{1,0:T(8,128)(2,1)} copy-done((bf16[1024,4096]{1,0:T(8,128)(2,1)}, bf16[1024,4096]{1,0:T(8,128)(2,1)S(1)}, u32[]{:S(2)}) %copy-start) | copy-done | bytes 8388632
  19.4 0.0 collective-permute-done.low
  19.4 0.0 collective-permute-done.1.high
  19.4 5.1 %shard_map.78.refs_2_ = f32[4112,128]{1,0:T(8,128)S(1)} custom-call(s32[1]{0:T(128)S(6)} %copy.9.offset, f32[5,64,128]{2,1,0:T(8,128)S(1)} %get-tuple-element.14.coef, f32[4,4,64,128]{3,2,1,0:T(8,128)S(1)} %get-tuple-element.15.own, f32[4,64,512]{2,1,0:T(8,128)S(1)} %collective-permute-done.low, f32[4,64,512]{2,1,0:T(8,128)S(1)} %collective-permute-done.1.high), custom_call_target="tpu_custom_call" | custom-call | flops 1024 | bytes 1024 | tf_op jit(solution)/shard_map/pallas_call | solution.py:335
  24.5 0.0 collective-permute-done.2.refs_5_.refs_8_
  24.5 0.5 collective-permute-start.3
  25.0 0.0 collective-permute-done.4.refs_4_.refs_7_
  25.0 4.4 %shard_map.79.refs_4_ = f32[16,8,128]{2,1,0:T(8,128)S(1)} custom-call(s32[4]{0:T(128)S(1)} %iota_xor_fusion.refs_0_, s32[1,4096]{1,0:T(1,128)S(1)} %get-tuple-element.13.refs_1_, f32[4112,128]{1,0:T(8,128)S(1)} %shard_map.78.refs_2_, bf16[1024,128]{1,0:T(8,128)(2,1)S(1)} %get-tuple-element.17.refs_3_.refs_6_, ...), custom_call_target="tpu_custom_call" | custom-call | flops 1024 | bytes 1024 | tf_op jit(solution)/shard_map/pallas_call | solution.py:348
  29.5 1.7 %collective-permute-done.3.refs_3_.refs_9_ = bf16[1024,128]{1,0:T(8,128)(2,1)S(1)} collective-permute-done((bf16[1024,128]{1,0:T(8,128)(2,1)S(1)}, bf16[1024,128]{1,0:T(8,128)(2,1)S(1)}, u32[]{:S(2)}, u32[]{:S(2)}) %collective-permute-start.3) | collective-permute-done | bytes 262176 | tf_op jit(solution)/shard_map/ppermute | solution.py:274
  31.2 2.0 %shard_map.80 = f32[16,8,128]{2,1,0:T(8,128)S(1)} custom-call(s32[4]{0:T(128)S(1)} %iota_xor_fusion.refs_0_, s32[1,4096]{1,0:T(1,128)S(1)} %get-tuple-element.13.refs_1_, f32[4112,128]{1,0:T(8,128)S(1)} %shard_map.78.refs_2_, bf16[1024,128]{1,0:T(8,128)(2,1)S(1)} %collective-permute-done.3.refs_3_.refs_9_, f32[16,8,128]{2,1,0:T(8,128)S(1)} %shard_map.79.refs_4_), custom_call_target="tpu_custom_call" | custom-call | flops 1024 | bytes 1024 | tf_op jit(solution)/shard_map/pallas_call | solution.py:348
  33.2 0.1 collective-permute-start.5
  33.3 1.2 %collective-permute-done.5 = f32[16,8,128]{2,1,0:T(8,128)S(1)} collective-permute-done((f32[16,8,128]{2,1,0:T(8,128)S(1)}, f32[16,8,128]{2,1,0:T(8,128)S(1)}, u32[]{:S(2)}, u32[]{:S(2)}) %collective-permute-start.5) | collective-permute-done | bytes 65568 | tf_op jit(solution)/shard_map/ppermute | solution.py:299
  34.6 1.6 %collective-permute-start.6 = (f32[16,8,128]{2,1,0:T(8,128)S(1)}, f32[16,8,128]{2,1,0:T(8,128)S(1)}, u32[]{:S(2)}, u32[]{:S(2)}) collective-permute-start(f32[16,8,128]{2,1,0:T(8,128)S(1)} %add.3.refs_2_), channel_id=1, source_target_pairs={{0,8},{4,12},{8,0},{12,4},{16,24},{20,28},{24,16},{28,20},{1,9},{5... | collective-permute-start | bytes 196616 | tf_op jit(solution)/shard_map/ppermute | solution.py:299
  36.1 0.5 collective-permute-start.7
  36.6 1.5 %collective-permute-start.8 = (f32[16,8,128]{2,1,0:T(8,128)S(1)}, f32[16,8,128]{2,1,0:T(8,128)S(1)}, u32[]{:S(2)}, u32[]{:S(2)}) collective-permute-start(f32[16,8,128]{2,1,0:T(8,128)S(1)} %add.3.refs_2_), channel_id=1, source_target_pairs={{0,24},{4,28},{8,16},{12,20},{16,8},{20,12},{24,0},{28,4},{1,25},{... | collective-permute-start | bytes 196616 | tf_op jit(solution)/shard_map/ppermute | solution.py:299
  38.1 0.8 %collective-permute-done.6.refs_3_ = f32[16,8,128]{2,1,0:T(8,128)S(1)} collective-permute-done((f32[16,8,128]{2,1,0:T(8,128)S(1)}, f32[16,8,128]{2,1,0:T(8,128)S(1)}, u32[]{:S(2)}, u32[]{:S(2)}) %collective-permute-start.6) | collective-permute-done | bytes 65568 | tf_op jit(solution)/shard_map/ppermute | solution.py:299
  38.9 2.2 %collective-permute-done.7.refs_4_ = f32[16,8,128]{2,1,0:T(8,128)S(1)} collective-permute-done((f32[16,8,128]{2,1,0:T(8,128)S(1)}, f32[16,8,128]{2,1,0:T(8,128)S(1)}, u32[]{:S(2)}, u32[]{:S(2)}) %collective-permute-start.7) | collective-permute-done | bytes 65568 | tf_op jit(solution)/shard_map/ppermute | solution.py:299
  41.1 0.7 %collective-permute-done.8.refs_5_ = f32[16,8,128]{2,1,0:T(8,128)S(1)} collective-permute-done((f32[16,8,128]{2,1,0:T(8,128)S(1)}, f32[16,8,128]{2,1,0:T(8,128)S(1)}, u32[]{:S(2)}, u32[]{:S(2)}) %collective-permute-start.8) | collective-permute-done | bytes 65568 | tf_op jit(solution)/shard_map/ppermute | solution.py:299
  41.8 0.0 copy-start.1
  41.8 3.4 %copy-done.1 = bf16[1024,4096]{1,0:T(8,128)(2,1)S(1)} copy-done((bf16[1024,4096]{1,0:T(8,128)(2,1)S(1)}, bf16[1024,4096]{1,0:T(8,128)(2,1)}, u32[]{:S(2)}) %copy-start.1) | copy-done | bytes 8388632
  45.2 3.7 %shard_map.81 = (f32[16,8,128]{2,1,0:T(8,128)S(1)}, f32[4,256,128]{2,1,0:T(8,128)S(1)}, bf16[7,256,128]{2,1,0:T(8,128)(2,1)S(1)}, bf16[4,256,128]{2,1,0:T(8,128)(2,1)S(1)}) custom-call(s32[4]{0:T(128)S(1)} %iota_xor_fusion.refs_0_, bf16[1024,4096]{1,0:T(8,128)(2,1)S(1)} %copy-done.1, f32[16,8,128]{2,1,0:T(8,128)S(1)} %add.3.refs_2_, ...), custom_call_target="tpu_custom_call" | custom-call | flops 1024 | bytes 1024 | tf_op jit(solution)/shard_map/pallas_call | solution.py:361
  48.9 0.1 collective-permute-start.9
  48.9 2.6 %collective-permute-start.10 = (bf16[4,256,128]{2,1,0:T(8,128)(2,1)S(1)}, bf16[4,256,128]{2,1,0:T(8,128)(2,1)S(1)}, u32[]{:S(2)}, u32[]{:S(2)}) collective-permute-start(bf16[4,256,128]{2,1,0:T(8,128)(2,1)S(1)} %get-tuple-element.21), channel_id=1, source_target_pairs={{0,28},{4,0},{8,4},{12,8},{16,12},{20,16},{24,20},{28,24},{1,29},{... | collective-permute-start | bytes 786440 | tf_op jit(solution)/shard_map/ppermute | solution.py:375
  51.6 0.7 %copy.8 = f32[4,16,2,128]{3,2,1,0:T(2,128)} copy(f32[4,16,2,128]{3,0,2,1:T(4,128)S(1)} %bitcast.15) | data formatting | bytes 131072 | tf_op jit(solution)/shard_map/transpose | solution.py:383
  52.2 6.1 %collective-permute-done.10.high = bf16[4,256,128]{2,1,0:T(8,128)(2,1)S(1)} collective-permute-done((bf16[4,256,128]{2,1,0:T(8,128)(2,1)S(1)}, bf16[4,256,128]{2,1,0:T(8,128)(2,1)S(1)}, u32[]{:S(2)}, u32[]{:S(2)}) %collective-permute-start.10) | collective-permute-done | bytes 262176 | tf_op jit(solution)/shard_map/ppermute | solution.py:375
  58.3 2.2 %collective-permute-done.9.low = bf16[7,256,128]{2,1,0:T(8,128)(2,1)S(1)} collective-permute-done((bf16[7,256,128]{2,1,0:T(8,128)(2,1)S(1)}, bf16[7,256,128]{2,1,0:T(8,128)(2,1)S(1)}, u32[]{:S(2)}, u32[]{:S(2)}) %collective-permute-start.9) | collective-permute-done | bytes 458784 | tf_op jit(solution)/shard_map/ppermute | solution.py:374
  60.5 5.3 %shard_map.82 = f32[4,64,512]{2,1,0:T(8,128)} custom-call(f32[5,64,128]{2,1,0:T(8,128)S(1)} %get-tuple-element.14.coef, f32[4,256,128]{2,1,0:T(8,128)S(1)} %get-tuple-element.19.own, bf16[7,256,128]{2,1,0:T(8,128)(2,1)S(1)} %collective-permute-done.9.low, bf16[4,256,128]{2,1,0:T(8,128)(2,1)S(1)} %collective-permute-done.10.high), custom_call_target="tpu_custom_call" | custom-call | flops 1024 | bytes 1024 | tf_op jit(solution)/shard_map/pallas_call | solution.py:376
  (2 shorter events, 0.0 us)
Async XLA Ops:
  0.6 18.8 %collective-permute-start = (f32[4,64,512]{2,1,0:T(8,128)}, f32[4,64,512]{2,1,0:T(8,128)S(1)}, u32[]{:S(2)}, u32[]{:S(2)}) collective-permute-start(f32[4,64,512]{2,1,0:T(8,128)} %bitcast.9), channel_id=1, source_target_pairs={{0,4},{4,8},{8,12},{12,16},{16,20},{20,24},{24,28},{28,0},{1,5},{5... | collective-permute-start | bytes 1572872 | tf_op jit(solution)/shard_map/ppermute | solution.py:317
  1.1 18.3 %collective-permute-start.1 = (f32[4,64,512]{2,1,0:T(8,128)}, f32[4,64,512]{2,1,0:T(8,128)S(1)}, u32[]{:S(2)}, u32[]{:S(2)}) collective-permute-start(f32[4,64,512]{2,1,0:T(8,128)} %bitcast.10), channel_id=1, source_target_pairs={{0,28},{4,0},{8,4},{12,8},{16,12},{20,16},{24,20},{28,24},{1,29},{... | collective-permute-start | bytes 1572872 | tf_op jit(solution)/shard_map/ppermute | solution.py:318
  4.1 20.4 %collective-permute-start.2 = (bf16[1024,128]{1,0:T(8,128)(2,1)}, bf16[1024,128]{1,0:T(8,128)(2,1)S(1)}, u32[]{:S(2)}, u32[]{:S(2)}) collective-permute-start(bf16[1024,128]{1,0:T(8,128)(2,1)} %bitcast.12), channel_id=1, source_target_pairs={{0,2},{1,3},{2,0},{3,1},{4,6},{5,7},{6,4},{7,5},{8,10},{9,11},{10,... | collective-permute-start | bytes 786440 | tf_op jit(solution)/shard_map/ppermute | solution.py:274
  7.4 17.7 %collective-permute-start.4 = (bf16[1024,128]{1,0:T(8,128)(2,1)}, bf16[1024,128]{1,0:T(8,128)(2,1)S(1)}, u32[]{:S(2)}, u32[]{:S(2)}) collective-permute-start(bf16[1024,128]{1,0:T(8,128)(2,1)} %bitcast.13), channel_id=1, source_target_pairs={{0,1},{1,0},{2,3},{3,2},{4,5},{5,4},{6,7},{7,6},{8,9},{9,8},{10,11... | collective-permute-start | bytes 786440 | tf_op jit(solution)/shard_map/ppermute | solution.py:274
  9.6 1.0 %copy-start.2 = (f32[1,4,64,512]{3,2,1,0:T(8,128)S(1)}, f32[1,4,64,512]{3,2,1,0:T(8,128)}, u32[]{:S(2)}) copy-start(f32[1,4,64,512]{3,2,1,0:T(8,128)} %param.6) | copy-start | bytes 1572868
  10.6 0.9 %copy-start.3 = (bf16[1,1024,128]{2,1,0:T(8,128)(2,1)S(1)}, bf16[1,1024,128]{2,1,0:T(8,128)(2,1)}, u32[]{:S(2)}) copy-start(bf16[1,1024,128]{2,1,0:T(8,128)(2,1)} %param.11) | copy-start | bytes 786436
  11.6 0.7 %copy-start.4 = (s32[1,4096]{1,0:T(1,128)S(1)}, s32[1,4096]{1,0:T(1,128)}, u32[]{:S(2)}) copy-start(s32[1,4096]{1,0:T(1,128)} %tile.1) | copy-start | bytes 49156
  12.3 0.7 copy-start.5
  13.0 0.7 copy-start.6
  16.2 3.2 %copy-start = (bf16[1024,4096]{1,0:T(8,128)(2,1)}, bf16[1024,4096]{1,0:T(8,128)(2,1)S(1)}, u32[]{:S(2)}) copy-start(bf16[1024,4096]{1,0:T(8,128)(2,1)S(1)} %get-tuple-element.12.refs_1_) | copy-start | bytes 25165828
  24.5 6.7 %collective-permute-start.3 = (bf16[1024,128]{1,0:T(8,128)(2,1)S(1)}, bf16[1024,128]{1,0:T(8,128)(2,1)S(1)}, u32[]{:S(2)}, u32[]{:S(2)}) collective-permute-start(bf16[1024,128]{1,0:T(8,128)(2,1)S(1)} %collective-permute-done.2.refs_5_.refs_8_), channel_id=1, source_target_pairs={{0,1},{1,0},{2,3},{3,2},{4,5},{5,4},{6,7},{7,6},{8,9},{9,8},{10,11... | collective-permute-start | bytes 786440 | tf_op jit(solution)/shard_map/ppermute | solution.py:274
  33.2 1.3 %collective-permute-start.5 = (f32[16,8,128]{2,1,0:T(8,128)S(1)}, f32[16,8,128]{2,1,0:T(8,128)S(1)}, u32[]{:S(2)}, u32[]{:S(2)}) collective-permute-start(f32[16,8,128]{2,1,0:T(8,128)S(1)} %shard_map.80), channel_id=1, source_target_pairs={{0,4},{4,0},{8,12},{12,8},{16,20},{20,16},{24,28},{28,24},{1,5},{5... | collective-permute-start | bytes 196616 | tf_op jit(solution)/shard_map/ppermute | solution.py:299
  34.6 4.3 %collective-permute-start.6 = (f32[16,8,128]{2,1,0:T(8,128)S(1)}, f32[16,8,128]{2,1,0:T(8,128)S(1)}, u32[]{:S(2)}, u32[]{:S(2)}) collective-permute-start(f32[16,8,128]{2,1,0:T(8,128)S(1)} %add.3.refs_2_), channel_id=1, source_target_pairs={{0,8},{4,12},{8,0},{12,4},{16,24},{20,28},{24,16},{28,20},{1,9},{5... | collective-permute-start | bytes 196616 | tf_op jit(solution)/shard_map/ppermute | solution.py:299
  36.1 5.0 %collective-permute-start.7 = (f32[16,8,128]{2,1,0:T(8,128)S(1)}, f32[16,8,128]{2,1,0:T(8,128)S(1)}, u32[]{:S(2)}, u32[]{:S(2)}) collective-permute-start(f32[16,8,128]{2,1,0:T(8,128)S(1)} %add.3.refs_2_), channel_id=1, source_target_pairs={{0,16},{4,20},{8,24},{12,28},{16,0},{20,4},{24,8},{28,12},{1,17},{... | collective-permute-start | bytes 196616 | tf_op jit(solution)/shard_map/ppermute | solution.py:299
  36.6 5.2 %collective-permute-start.8 = (f32[16,8,128]{2,1,0:T(8,128)S(1)}, f32[16,8,128]{2,1,0:T(8,128)S(1)}, u32[]{:S(2)}, u32[]{:S(2)}) collective-permute-start(f32[16,8,128]{2,1,0:T(8,128)S(1)} %add.3.refs_2_), channel_id=1, source_target_pairs={{0,24},{4,28},{8,16},{12,20},{16,8},{20,12},{24,0},{28,4},{1,25},{... | collective-permute-start | bytes 196616 | tf_op jit(solution)/shard_map/ppermute | solution.py:299
  41.8 3.4 %copy-start.1 = (bf16[1024,4096]{1,0:T(8,128)(2,1)S(1)}, bf16[1024,4096]{1,0:T(8,128)(2,1)}, u32[]{:S(2)}) copy-start(bf16[1024,4096]{1,0:T(8,128)(2,1)} %copy-done) | copy-start | bytes 25165828
  48.9 11.7 %collective-permute-start.9 = (bf16[7,256,128]{2,1,0:T(8,128)(2,1)S(1)}, bf16[7,256,128]{2,1,0:T(8,128)(2,1)S(1)}, u32[]{:S(2)}, u32[]{:S(2)}) collective-permute-start(bf16[7,256,128]{2,1,0:T(8,128)(2,1)S(1)} %get-tuple-element.20), channel_id=1, source_target_pairs={{0,4},{4,8},{8,12},{12,16},{16,20},{20,24},{24,28},{28,0},{1,5},{5... | collective-permute-start | bytes 1376264 | tf_op jit(solution)/shard_map/ppermute | solution.py:374
  48.9 9.4 %collective-permute-start.10 = (bf16[4,256,128]{2,1,0:T(8,128)(2,1)S(1)}, bf16[4,256,128]{2,1,0:T(8,128)(2,1)S(1)}, u32[]{:S(2)}, u32[]{:S(2)}) collective-permute-start(bf16[4,256,128]{2,1,0:T(8,128)(2,1)S(1)} %get-tuple-element.21), channel_id=1, source_target_pairs={{0,28},{4,0},{8,4},{12,8},{16,12},{20,16},{24,20},{28,24},{1,29},{... | collective-permute-start | bytes 786440 | tf_op jit(solution)/shard_map/ppermute | solution.py:375

commit v7 on v6

--- a/solution.py
+++ b/solution.py
@@ -70,14 +70,15 @@
     columns = width // TILE
     turn, rest = offset // TILE, offset % TILE
     lane = lax.broadcasted_iota(jnp.int32, (height, TILE), 1)
-    rolled = [pltpu.roll(field[plane, :, pl.ds(c * TILE, TILE)], rest, 1) for c in range(columns)]
+    parts = [field[plane, :, pl.ds(c * TILE, TILE)].astype(jnp.float32) for c in range(columns)]
+    rolled = [pltpu.roll(part, rest, 1) for part in parts]
     return [
         (lax.rem(c + turn, columns), jnp.where(lane >= rest, rolled[c], rolled[c - 1]))
         for c in range(columns)
     ]
 
 
-def prelude_kernel(offset, field, courant, diffusivity, tile, panel, own, coef, start, chosen, kept):
+def prelude_kernel(offset, field, courant, diffusivity, tile, panel, own, coef, start, kept, chosen, built, sems):
     columns, height = own.shape[1:3]
 
     def load(plane, carry):
@@ -101,17 +102,27 @@
     inside = numbers & (columns * height - 1)
     numbers = (numbers - inside) + (inside & (columns - 1)) * height + inside // columns
     start[...] = numbers * STEPS
-    rows = 64
+    rows = built.shape[0] // sems.shape[0]
+
+    def block(place):
+        where = pl.ds(pl.multiple_of(place * rows, rows), rows)
+        return pltpu.make_async_copy(built.at[where], chosen.at[where], sems.at[place])
 
     def choose(place, carry):
         by_row = lax.broadcasted_iota(jnp.int32, (rows, TILE), 0) + place * rows
         where = pl.ds(pl.multiple_of(place * rows, rows), rows)
-        for left in range(0, chosen.shape[1], TILE):
+        for left in range(0, built.shape[1], TILE):
             found = jnp.where(numbers[:, left : left + TILE] == by_row, 1.0, 0.0)
-            chosen[where, pl.ds(left, TILE)] = found.astype(jnp.bfloat16)
+            built[where, pl.ds(left, TILE)] = found.astype(jnp.bfloat16)
+        block(place).start()
         return carry
 
-    lax.fori_loop(0, chosen.shape[0] // rows, choose, 0)
+    def finish(place, carry):
+        block(place).wait()
+        return carry
+
+    lax.fori_loop(0, sems.shape[0], choose, 0)
+    lax.fori_loop(0, sems.shape[0], finish, 0)
 
 
 def adjoint_kernel(offset, coef, own, low, high, tiles, first, second):
@@ -188,10 +199,12 @@
 
 
 def project_kernel(chunks, source, start, tiles, *refs):
-    panels, (*before, out, wide) = refs[: len(chunks)], refs[len(chunks) :]
+    count = len(chunks)
+    panels, (*before, early, last, wide) = refs[:count], refs[count:]
     shard = panels[0].shape[0] // GROUP
-    for given in before:
-        out[...] = given[...]
+    if before:
+        early[...] = before[0][...]
+        last[...] = before[1][...]
     first = lax.broadcasted_iota(jnp.int32, (8, TILE), 0) < STEPS
     lane = lax.broadcasted_iota(jnp.int32, (8, TILE), 1)
     for chunk, panel in zip(chunks, panels):
@@ -210,20 +223,33 @@
                 rows = jnp.where(first, wide[pl.ds(row, 1), :], wide[pl.ds(row + TILE, 1), :])
                 total = jnp.sum(cells * rows, axis=1, keepdims=True)
                 sums = jnp.where(lane == place, total, sums)
-            out[number] = sums
+            for half in range(2):
+                row = 2 * number + half
+                for step in range(STEPS):
+                    value = sums[half * STEPS + step : half * STEPS + step + 1]
+                    if step < STEPS - 1:
+                        early[step, pl.ds(row, 1), :] = value
+                    else:
+                        last[pl.ds(row, 1), :] = value
             return carry
 
         lax.fori_loop(0, shard, body, 0)
 
 
 def deposit_kernel(count, source, chosen, *refs):
-    parts, panels, (total, field, rightward, leftward, scaled) = refs[:count], refs[count:-5], refs[-5:]
-    groups = total.shape[0]
+    parts, panels = refs[:count], refs[count:-7]
+    total, field, rightward, leftward, scaled, held, sems = refs[-7:]
+    groups = total.shape[0] // 2
     shard = groups // len(panels)
     cells, per_plane = field.shape[0], field.shape[1]
+    copies = []
+    for plane in range(cells):
+        where = pl.ds(plane * per_plane, per_plane)
+        copies.append(pltpu.make_async_copy(chosen.at[where], held.at[where], sems.at[plane]))
+        copies[plane].start()
     total[...] = tree_sum([part[...] for part in parts])
     numbers = [source[g // shard] * shard + g % shard for g in range(groups)]
-    last = [total[n, pl.ds(half * STEPS + STEPS - 1, 1), :] for n in numbers for half in range(2)]
+    last = [total[pl.ds(2 * number + half, 1), :] for number in numbers for half in range(2)]
     drive = jnp.concatenate(last, axis=0).T
     for group, number in enumerate(numbers):
         for half in range(2):
@@ -235,8 +261,9 @@
             scaled[where, pl.ds(TILE, TILE)] = tail
 
     for plane in range(cells):
+        copies[plane].wait()
         sums = jnp.dot(
-            chosen[pl.ds(plane * per_plane, per_plane), :],
+            held[pl.ds(plane * per_plane, per_plane), :],
             scaled[...],
             preferred_element_type=jnp.float32,
         )
@@ -249,10 +276,17 @@
             rightward[cells + plane - 1] = tail
 
 
-def call(kernel, out_shape, vmem, scratch=(), smem=0, inputs=0):
+def call(kernel, out_shape, vmem, scratch=(), smem=0, inputs=0, hbm_in=(), hbm_out=()):
     in_specs = [pl.BlockSpec(memory_space=pltpu.SMEM)] * smem
     in_specs += [pl.BlockSpec(memory_space=pltpu.VMEM)] * (inputs - smem)
+    for place in hbm_in:
+        in_specs[place] = pl.BlockSpec(memory_space=pltpu.HBM)
     out_specs = jax.tree.map(lambda _: pl.BlockSpec(memory_space=pltpu.VMEM), out_shape)
+    if hbm_out:
+        out_specs = list(out_specs)
+        for place in hbm_out:
+            out_specs[place] = pl.BlockSpec(memory_space=pltpu.HBM)
+        out_specs = tuple(out_specs)
     return pl.pallas_call(
         kernel,
         out_shape=out_shape,
@@ -314,19 +348,21 @@
     f32, bf16 = jnp.float32, jnp.bfloat16
 
     source = lax.axis_index("probe") ^ jnp.arange(probes, dtype=jnp.int32)
-    low = lax.ppermute(own, "state", shift_pairs(slabs, 1))
+    low = lax.ppermute(own.astype(bf16), "state", shift_pairs(slabs, 1))
     high = lax.ppermute(own, "state", shift_pairs(slabs, -1))
 
-    shifted, coef, start, chosen, panel = call(
+    shifted, coef, start, panel, chosen = call(
         prelude_kernel,
         (
             jax.ShapeDtypeStruct((cells, columns, height, TILE), f32),
             jax.ShapeDtypeStruct((5, height, TILE), f32),
             jax.ShapeDtypeStruct(tile_index.shape, jnp.int32),
+            jax.ShapeDtypeStruct(actuator_panel.shape[1:], bf16),
             jax.ShapeDtypeStruct((tile_total, actuators), bf16),
-            jax.ShapeDtypeStruct(actuator_panel.shape[1:], bf16),
         ),
         vmem=14,
+        scratch=(pltpu.VMEM((tile_total, actuators), bf16), pltpu.SemaphoreType.DMA((16,))),
+        hbm_out=(4,),
         smem=1,
         inputs=6,
     )(probe_offset, own, courant[None], diffusivity[None], tile_index, actuator_panel[0])
@@ -347,28 +383,36 @@
     def project(chunks, *given):
         return call(
             lambda *refs: project_kernel(chunks, *refs),
-            jax.ShapeDtypeStruct((groups, 2 * STEPS, TILE), f32),
+            (
+                jax.ShapeDtypeStruct((STEPS - 1, 2 * groups, TILE), f32),
+                jax.ShapeDtypeStruct((2 * groups, TILE), f32),
+            ),
             vmem=6,
             scratch=(pltpu.VMEM((shard * GROUP, TILE), f32),),
             smem=2,
             inputs=3 + len(chunks) + len(given),
         )(source, start, tiles, *[panels[chunk] for chunk in chunks], *given)
 
-    before = project(every[:-1])
-    parts = summands(project(every[-1:], before), "state")
+    early, last = project(every[-1:], *project(every[:-1]))
+    parts = summands(last, "state")
     payload = jax.ShapeDtypeStruct((2 * cells - 1, height * columns, TILE), bf16)
     heads = jax.ShapeDtypeStruct((cells, height * columns, TILE), bf16)
     total, forced, rightward, leftward = call(
         lambda *refs: deposit_kernel(len(parts), *refs),
         (
-            jax.ShapeDtypeStruct(before.shape, f32),
+            jax.ShapeDtypeStruct(last.shape, f32),
             jax.ShapeDtypeStruct((cells, height * columns, TILE), f32),
             payload,
             heads,
         ),
-        vmem=18,
-        scratch=(pltpu.VMEM((actuators, 2 * TILE), bf16),),
+        vmem=16,
+        scratch=(
+            pltpu.VMEM((actuators, 2 * TILE), bf16),
+            pltpu.VMEM((tile_total, actuators), bf16),
+            pltpu.SemaphoreType.DMA((cells,)),
+        ),
         smem=1,
+        hbm_in=(1,),
         inputs=2 + len(parts) + probes,
     )(source, chosen, *parts, *panels)
     from_low = lax.ppermute(rightward, "state", shift_pairs(slabs, 1))
@@ -380,7 +424,9 @@
         scratch=(field_shape, field_shape),
         inputs=4,
     )(coef, forced, from_low, from_high)
-    projections = total.reshape(groups, 2, STEPS, TILE).transpose(2, 0, 1, 3)
+    rounds = 1 + jnp.minimum(probe_offset[0], 0)
+    early = lax.fori_loop(0, rounds, lambda _, part: tree_sum(summands(part, "state")), early)
+    projections = jnp.concatenate([early, total[None]], axis=0)
     return projections.reshape(STEPS, 1, actuators), response[None]
 
 

time: 66.1 us -> 73.4 us (1.11); the launches traced: 65.8 us -> 72.4 us
  Pallas kernels: 23.1 us -> 27.2 us
  starting transfers between devices: 15.1 us -> 18 us
  other arithmetic: 0.01 us -> 1.83 us
  waiting for transfers between devices: 15 us -> 13.3 us
    ppermute x1, waiting for transfers between devices: 6.1 us -> 0.01 us  [local(): from_high = lax.ppermute(leftward, 'state', shift_pairs(slabs, -1))]
    ppermute x4 -> x8, waiting for transfers between devices: 4.92 us -> 10.6 us  [summands(): parts = [part] + [lax.ppermute(part, axis, pair) for pair in pairs]]
    ppermute x4 -> x8, starting transfers between devices: 3.62 us -> 7.12 us  [summands(): parts = [part] + [lax.ppermute(part, axis, pair) for pair in pairs]]
    pallas_call x1, Pallas kernels: 3.68 us -> 6.87 us  [local(): call(lambda *refs: deposit_kernel(len(parts), *refs), (jax.ShapeDtypeStru...]
    ppermute x1, waiting for transfers between devices: 2.21 us -> 0.3 us  [local(): from_low = lax.ppermute(rightward, 'state', shift_pairs(slabs, 1))]
    convert_element_type x0 -> x1, other arithmetic: none -> 1.11 us  [local(): low = lax.ppermute(own.astype(bf16), 'state', shift_pairs(slabs, 1))]
    pallas_call x1, Pallas kernels: 2.58 us -> 3.5 us  [local(): call(prelude_kernel, (jax.ShapeDtypeStruct((cells, columns, height, TILE)...]
  transfers between devices with their start and end apart: 11 -> 15, of which waited for: 7 -> 10; matrix products, arithmetic and copies ran while one was open for 1% -> 3% of each run, Pallas kernels for 18% -> 18%
where the time goes in v7:
time: 73.4 us; the launch traced here: 72.4 us
  Pallas kernels  27.2 us (37%)
  starting transfers between devices  18 us (25%)
  waiting for transfers between devices  13.3 us (18%)
  local copies, waits for them, and re-layouts  10.7 us (15%)
  other arithmetic  1.83 us (2%)
  between operations  1.38 us (2%)
    unnamed x14, local copies, waits for them, and re-layouts  10.7 us
    ppermute x8, waiting for transfers between devices, summands(): parts = [part] + [lax.ppermute(part, axis, pair) for pair in pairs]  10.6 us
    ppermute x8, starting transfers between devices, summands(): parts = [part] + [lax.ppermute(part, axis, pair) for pair in pairs]  7.12 us
    pallas_call x1, Pallas kernels, local(): call(lambda *refs: deposit_kernel(len(parts), *refs), (jax.ShapeDtypeStru...  6.87 us
    pallas_call x2, Pallas kernels, project(): call(lambda *refs: project_kernel(chunks, *refs), (jax.ShapeDtypeStruct((...  6.49 us
    pallas_call x1, Pallas kernels, local(): call(forward_kernel, jax.ShapeDtypeStruct((cells, height, width), f32), v...  5.3 us
    pallas_call x1, Pallas kernels, local(): call(adjoint_kernel, jax.ShapeDtypeStruct((tile_total * STEPS + 2 * PAD,...  4.99 us
    ppermute x3, starting transfers between devices, gathered_panel(): shards[held | mask] = lax.ppermute(operand, axis, pairs)  4.75 us
  transfers between devices with their start and end apart: 15, of which 10 were waited for; matrix products, arithmetic and copies ran while one was open for 3% of the time, Pallas kernels for 18%

profile of v7, /device:TPU:0, one launch (start us, length us, event | category | flops | bytes accessed | tf_op | source)
XLA Modules:
  0.0 72.4 jit_solution(2478205470405987993)
XLA Ops:
  0.6 3.4 %collective-permute-start.5 = (f32[4,64,512]{2,1,0:T(8,128)}, f32[4,64,512]{2,1,0:T(8,128)S(1)}, u32[]{:S(2)}, u32[]{:S(2)}) collective-permute-start(f32[4,64,512]{2,1,0:T(8,128)} %bitcast.9), channel_id=1, source_target_pairs={{0,28},{4,0},{8,4},{12,8},{16,12},{20,16},{24,20},{28,24},{1,29},{... | collective-permute-start | bytes 1572872 | tf_op jit(solution)/shard_map/ppermute | solution.py:352
  4.0 1.1 %bitcast_convert_fusion = bf16[4,64,512]{2,1,0:T(8,128)(2,1)S(1)} fusion(f32[1,4,64,512]{3,2,1,0:T(8,128)} %param.8), kind=kLoop, calls=%fused_computation.3 | loop fusion | flops 131072 | bytes 786432 | tf_op jit(solution)/shard_map/convert_element_type | solution.py:351
  5.1 0.1 collective-permute-start.4
  5.2 2.7 %collective-permute-start.6 = (bf16[1024,128]{1,0:T(8,128)(2,1)}, bf16[1024,128]{1,0:T(8,128)(2,1)S(1)}, u32[]{:S(2)}, u32[]{:S(2)}) collective-permute-start(bf16[1024,128]{1,0:T(8,128)(2,1)} %bitcast.11), channel_id=1, source_target_pairs={{0,2},{1,3},{2,0},{3,1},{4,6},{5,7},{6,4},{7,5},{8,10},{9,11},{10,... | collective-permute-start | bytes 786440 | tf_op jit(solution)/shard_map/ppermute | solution.py:308
  7.8 1.6 %collective-permute-start.8 = (bf16[1024,128]{1,0:T(8,128)(2,1)}, bf16[1024,128]{1,0:T(8,128)(2,1)S(1)}, u32[]{:S(2)}, u32[]{:S(2)}) collective-permute-start(bf16[1024,128]{1,0:T(8,128)(2,1)} %bitcast.12), channel_id=1, source_target_pairs={{0,1},{1,0},{2,3},{3,2},{4,5},{5,4},{6,7},{7,6},{8,9},{9,8},{10,11... | collective-permute-start | bytes 786440 | tf_op jit(solution)/shard_map/ppermute | solution.py:308
  10.1 0.0 copy-start.2
  10.1 1.0 %copy-done.2 = f32[1,4,64,512]{3,2,1,0:T(8,128)S(1)} copy-done((f32[1,4,64,512]{3,2,1,0:T(8,128)S(1)}, f32[1,4,64,512]{3,2,1,0:T(8,128)}, u32[]{:S(2)}) %copy-start.2) | copy-done | bytes 524312
  11.1 0.0 copy-start.3
  11.1 0.9 %copy-done.3 = bf16[1,1024,128]{2,1,0:T(8,128)(2,1)S(1)} copy-done((bf16[1,1024,128]{2,1,0:T(8,128)(2,1)S(1)}, bf16[1,1024,128]{2,1,0:T(8,128)(2,1)}, u32[]{:S(2)}) %copy-start.3) | copy-done | bytes 262168
  12.1 0.0 copy-start.4
  12.1 0.7 copy-done.4
  12.8 0.0 copy-start.5
  12.8 0.7 copy-done.5
  13.4 0.0 copy-start.6
  13.4 0.7 copy-done.6
  14.1 3.5 %shard_map.77 = (f32[4,4,64,128]{3,2,1,0:T(8,128)S(1)}, f32[5,64,128]{2,1,0:T(8,128)S(1)}, s32[1,4096]{1,0:T(1,128)S(1)}, bf16[1024,128]{1,0:T(8,128)(2,1)S(1)}, bf16[1024,4096]{1,0:T(8,128)(2,1)S(1)}) custom-call(s32[1]{0:T(128)S(6)} %copy.15.offset, f32[4,64,512]{2,1,0:T(8,128)S(1)} %bitcast.10, f32[1,64]{1,0:T(1,128)S(1)} %bitcast.15, ...), custom_call_target="tpu_custom_call" | custom-call | flops 1024 | bytes 1024 | tf_op jit(solution)/shard_map/pallas_call | solution.py:354
  17.6 0.0 copy-start
  17.6 3.3 %copy-done = bf16[1024,4096]{1,0:T(8,128)(2,1)} copy-done((bf16[1024,4096]{1,0:T(8,128)(2,1)}, bf16[1024,4096]{1,0:T(8,128)(2,1)S(1)}, u32[]{:S(2)}) %copy-start) | copy-done | bytes 8388632
  20.9 0.0 collective-permute-done.4.low
  20.9 0.0 collective-permute-done.5.high
  20.9 5.0 %shard_map.78.refs_2_ = f32[4112,128]{1,0:T(8,128)S(1)} custom-call(s32[1]{0:T(128)S(6)} %copy.15.offset, f32[5,64,128]{2,1,0:T(8,128)S(1)} %get-tuple-element.35.coef, f32[4,4,64,128]{3,2,1,0:T(8,128)S(1)} %get-tuple-element.36.own, bf16[4,64,512]{2,1,0:T(8,128)(2,1)S(1)} %collective-permute-done.4.low, f32[4,64,512]{2,1,0:T(8,128)S(1)} %collective-permute-done.5.high), custom_call_target="tpu_custom_call" | custom-call | flops 1024 | bytes 1024 | tf_op jit(solution)/shard_map/pallas_call | solution.py:371
  25.9 0.0 collective-permute-done.6.refs_5_.refs_8_
  25.9 0.5 collective-permute-start.7
  26.4 0.0 collective-permute-done.8.refs_4_.refs_7_
  26.4 4.4 %shard_map.79 = (f32[3,32,128]{2,1,0:T(8,128)S(1)}, f32[32,128]{1,0:T(8,128)S(1)}) custom-call(s32[4]{0:T(128)S(1)} %iota_xor_fusion.refs_0_, s32[1,4096]{1,0:T(1,128)S(1)} %get-tuple-element.34.refs_1_, f32[4112,128]{1,0:T(8,128)S(1)} %shard_map.78.refs_2_, bf16[1024,128]{1,0:T(8,128)(2,1)S(1)} %get-tuple-element.38.refs_3_.refs_6_, ...), custom_call_target="tpu_custom_call" | custom-call | flops 1024 | bytes 1024 | tf_op jit(solution)/shard_map/pallas_call | solution.py:384
  30.9 2.4 %collective-permute-done.7.refs_3_.refs_9_ = bf16[1024,128]{1,0:T(8,128)(2,1)S(1)} collective-permute-done((bf16[1024,128]{1,0:T(8,128)(2,1)S(1)}, bf16[1024,128]{1,0:T(8,128)(2,1)S(1)}, u32[]{:S(2)}, u32[]{:S(2)}) %collective-permute-start.7) | collective-permute-done | bytes 262176 | tf_op jit(solution)/shard_map/ppermute | solution.py:308
  33.3 2.0 %shard_map.80 = (f32[3,32,128]{2,1,0:T(8,128)S(1)}, f32[32,128]{1,0:T(8,128)S(1)}) custom-call(s32[4]{0:T(128)S(1)} %iota_xor_fusion.refs_0_, s32[1,4096]{1,0:T(1,128)S(1)} %get-tuple-element.34.refs_1_, f32[4112,128]{1,0:T(8,128)S(1)} %shard_map.78.refs_2_, bf16[1024,128]{1,0:T(8,128)(2,1)S(1)} %collective-permute-done.7.refs_3_.refs_9_, ...), custom_call_target="tpu_custom_call" | custom-call | flops 1024 | bytes 1024 | tf_op jit(solution)/shard_map/pallas_call | solution.py:384
  35.3 0.1 collective-permute-start.9
  35.4 1.2 %collective-permute-done.9 = f32[32,128]{1,0:T(8,128)S(1)} collective-permute-done((f32[32,128]{1,0:T(8,128)S(1)}, f32[32,128]{1,0:T(8,128)S(1)}, u32[]{:S(2)}, u32[]{:S(2)}) %collective-permute-start.9) | collective-permute-done | bytes 16416 | tf_op jit(solution)/shard_map/ppermute | solution.py:333
  36.6 1.5 %collective-permute-start.10 = (f32[32,128]{1,0:T(8,128)S(1)}, f32[32,128]{1,0:T(8,128)S(1)}, u32[]{:S(2)}, u32[]{:S(2)}) collective-permute-start(f32[32,128]{1,0:T(8,128)S(1)} %add.26.refs_2_), channel_id=1, source_target_pairs={{0,8},{4,12},{8,0},{12,4},{16,24},{20,28},{24,16},{28,20},{1,9},{5... | collective-permute-start | bytes 49160 | tf_op jit(solution)/shard_map/ppermute | solution.py:333
  38.0 1.5 %collective-permute-start.11 = (f32[32,128]{1,0:T(8,128)S(1)}, f32[32,128]{1,0:T(8,128)S(1)}, u32[]{:S(2)}, u32[]{:S(2)}) collective-permute-start(f32[32,128]{1,0:T(8,128)S(1)} %add.26.refs_2_), channel_id=1, source_target_pairs={{0,16},{4,20},{8,24},{12,28},{16,0},{20,4},{24,8},{28,12},{1,17},{... | collective-permute-start | bytes 49160 | tf_op jit(solution)/shard_map/ppermute | solution.py:333
  39.6 0.5 collective-permute-start.12
  40.1 0.2 collective-permute-done.10.refs_3_
  40.3 1.5 %collective-permute-done.11.refs_4_ = f32[32,128]{1,0:T(8,128)S(1)} collective-permute-done((f32[32,128]{1,0:T(8,128)S(1)}, f32[32,128]{1,0:T(8,128)S(1)}, u32[]{:S(2)}, u32[]{:S(2)}) %collective-permute-start.11) | collective-permute-done | bytes 16416 | tf_op jit(solution)/shard_map/ppermute | solution.py:333
  41.8 2.4 %collective-permute-done.12.refs_5_ = f32[32,128]{1,0:T(8,128)S(1)} collective-permute-done((f32[32,128]{1,0:T(8,128)S(1)}, f32[32,128]{1,0:T(8,128)S(1)}, u32[]{:S(2)}, u32[]{:S(2)}) %collective-permute-start.12) | collective-permute-done | bytes 16416 | tf_op jit(solution)/shard_map/ppermute | solution.py:333
  44.2 0.0 copy-start.1
  44.2 3.4 %copy-done.1 = bf16[1024,4096]{1,0:T(8,128)(2,1)S(1)} copy-done((bf16[1024,4096]{1,0:T(8,128)(2,1)S(1)}, bf16[1024,4096]{1,0:T(8,128)(2,1)}, u32[]{:S(2)}) %copy-start.1) | copy-done | bytes 8388632
  47.6 6.9 %shard_map.81 = (f32[32,128]{1,0:T(8,128)S(1)}, f32[4,256,128]{2,1,0:T(8,128)S(1)}, bf16[7,256,128]{2,1,0:T(8,128)(2,1)S(1)}, bf16[4,256,128]{2,1,0:T(8,128)(2,1)S(1)}) custom-call(s32[4]{0:T(128)S(1)} %iota_xor_fusion.refs_0_, bf16[1024,4096]{1,0:T(8,128)(2,1)S(1)} %copy-done.1, f32[32,128]{1,0:T(8,128)S(1)} %add.26.refs_2_, ...), custom_call_target="tpu_custom_call" | custom-call | flops 1024 | bytes 1024 | tf_op jit(solution)/shard_map/pallas_call | solution.py:400
  54.5 0.1 collective-permute-start.13
  54.5 2.6 %collective-permute-start.14 = (bf16[4,256,128]{2,1,0:T(8,128)(2,1)S(1)}, bf16[4,256,128]{2,1,0:T(8,128)(2,1)S(1)}, u32[]{:S(2)}, u32[]{:S(2)}) collective-permute-start(bf16[4,256,128]{2,1,0:T(8,128)(2,1)S(1)} %get-tuple-element.48), channel_id=1, source_target_pairs={{0,28},{4,0},{8,4},{12,8},{16,12},{20,16},{24,20},{28,24},{1,29},{... | collective-permute-start | bytes 786440 | tf_op jit(solution)/shard_map/ppermute | solution.py:419
  57.2 8.9 %while.10 = (s32[]{:T(128)}, f32[3,32,128]{2,1,0:T(8,128)S(1)}, s32[]{:T(128)}, s32[]{:T(128)}) while((s32[]{:T(128)}, f32[3,32,128]{2,1,0:T(8,128)S(1)}, s32[]{:T(128)}, s32[]{:T(128)}) %tuple.24), condition=%wide.region_1.0_spmd, body=%wide.region_0.0_spmd.sunk | while | flops 49154 | bytes 1179861 | solution.py:428
  57.2 0.0 collective-permute-start
  57.2 1.2 %collective-permute-done = f32[3,32,128]{2,1,0:T(8,128)S(1)} collective-permute-done((f32[3,32,128]{2,1,0:T(8,128)S(1)}, f32[3,32,128]{2,1,0:T(8,128)S(1)}, u32[]{:S(2)}, u32[]{:S(2)}) %collective-permute-start) | collective-permute-done | bytes 49184 | tf_op jit(solution)/shard_map/while/body/ppermute | solution.py:333
  58.4 0.6 collective-permute-start.1
  59.0 0.6 collective-permute-start.2
  59.6 2.4 %collective-permute-start.3 = (f32[3,32,128]{2,1,0:T(8,128)S(1)}, f32[3,32,128]{2,1,0:T(8,128)S(1)}, u32[]{:S(2)}, u32[]{:S(2)}) collective-permute-start(f32[3,32,128]{2,1,0:T(8,128)S(1)} %add.39), channel_id=1, source_target_pairs={{0,8},{4,12},{8,0},{12,4},{16,24},{20,28},{24,16},{28,20},{1,9},{5... | collective-permute-start | bytes 147464 | tf_op jit(solution)/shard_map/while/body/ppermute | solution.py:333
  62.0 1.4 %collective-permute-done.1 = f32[3,32,128]{2,1,0:T(8,128)S(1)} collective-permute-done((f32[3,32,128]{2,1,0:T(8,128)S(1)}, f32[3,32,128]{2,1,0:T(8,128)S(1)}, u32[]{:S(2)}, u32[]{:S(2)}) %collective-permute-start.1) | collective-permute-done | bytes 49184 | tf_op jit(solution)/shard_map/while/body/ppermute | solution.py:333
  63.3 1.6 %collective-permute-done.2 = f32[3,32,128]{2,1,0:T(8,128)S(1)} collective-permute-done((f32[3,32,128]{2,1,0:T(8,128)S(1)}, f32[3,32,128]{2,1,0:T(8,128)S(1)}, u32[]{:S(2)}, u32[]{:S(2)}) %collective-permute-start.2) | collective-permute-done | bytes 49184 | tf_op jit(solution)/shard_map/while/body/ppermute | solution.py:333
  64.9 1.2 %collective-permute-done.3 = f32[3,32,128]{2,1,0:T(8,128)S(1)} collective-permute-done((f32[3,32,128]{2,1,0:T(8,128)S(1)}, f32[3,32,128]{2,1,0:T(8,128)S(1)}, u32[]{:S(2)}, u32[]{:S(2)}) %collective-permute-start.3) | collective-permute-done | bytes 49184 | tf_op jit(solution)/shard_map/while/body/ppermute | solution.py:333
  66.1 0.7 pad_maximum_fusion
  66.8 0.0 collective-permute-done.14.high
  66.8 0.3 collective-permute-done.13.low
  67.1 5.3 %shard_map.82 = f32[4,64,512]{2,1,0:T(8,128)} custom-call(f32[5,64,128]{2,1,0:T(8,128)S(1)} %get-tuple-element.35.coef, f32[4,256,128]{2,1,0:T(8,128)S(1)} %get-tuple-element.46.own, bf16[7,256,128]{2,1,0:T(8,128)(2,1)S(1)} %collective-permute-done.13.low, bf16[4,256,128]{2,1,0:T(8,128)(2,1)S(1)} %collective-permute-done.14.high), custom_call_target="tpu_custom_call" | custom-call | flops 1024 | bytes 1024 | tf_op jit(solution)/shard_map/pallas_call | solution.py:420
  (4 shorter events, 0.0 us)
Async XLA Ops:
  0.6 20.3 %collective-permute-start.5 = (f32[4,64,512]{2,1,0:T(8,128)}, f32[4,64,512]{2,1,0:T(8,128)S(1)}, u32[]{:S(2)}, u32[]{:S(2)}) collective-permute-start(f32[4,64,512]{2,1,0:T(8,128)} %bitcast.9), channel_id=1, source_target_pairs={{0,28},{4,0},{8,4},{12,8},{16,12},{20,16},{24,20},{28,24},{1,29},{... | collective-permute-start | bytes 1572872 | tf_op jit(solution)/shard_map/ppermute | solution.py:352
  5.1 15.8 %collective-permute-start.4 = (bf16[4,64,512]{2,1,0:T(8,128)(2,1)S(1)}, bf16[4,64,512]{2,1,0:T(8,128)(2,1)S(1)}, u32[]{:S(2)}, u32[]{:S(2)}) collective-permute-start(bf16[4,64,512]{2,1,0:T(8,128)(2,1)S(1)} %bitcast_convert_fusion), channel_id=1, source_target_pairs={{0,4},{4,8},{8,12},{12,16},{16,20},{20,24},{24,28},{28,0},{1,5},{5... | collective-permute-start | bytes 786440 | tf_op jit(solution)/shard_map/ppermute | solution.py:351
  5.2 20.7 %collective-permute-start.6 = (bf16[1024,128]{1,0:T(8,128)(2,1)}, bf16[1024,128]{1,0:T(8,128)(2,1)S(1)}, u32[]{:S(2)}, u32[]{:S(2)}) collective-permute-start(bf16[1024,128]{1,0:T(8,128)(2,1)} %bitcast.11), channel_id=1, source_target_pairs={{0,2},{1,3},{2,0},{3,1},{4,6},{5,7},{6,4},{7,5},{8,10},{9,11},{10,... | collective-permute-start | bytes 786440 | tf_op jit(solution)/shard_map/ppermute | solution.py:308
  7.8 18.6 %collective-permute-start.8 = (bf16[1024,128]{1,0:T(8,128)(2,1)}, bf16[1024,128]{1,0:T(8,128)(2,1)S(1)}, u32[]{:S(2)}, u32[]{:S(2)}) collective-permute-start(bf16[1024,128]{1,0:T(8,128)(2,1)} %bitcast.12), channel_id=1, source_target_pairs={{0,1},{1,0},{2,3},{3,2},{4,5},{5,4},{6,7},{7,6},{8,9},{9,8},{10,11... | collective-permute-start | bytes 786440 | tf_op jit(solution)/shard_map/ppermute | solution.py:308
  10.1 1.0 %copy-start.2 = (f32[1,4,64,512]{3,2,1,0:T(8,128)S(1)}, f32[1,4,64,512]{3,2,1,0:T(8,128)}, u32[]{:S(2)}) copy-start(f32[1,4,64,512]{3,2,1,0:T(8,128)} %param.8) | copy-start | bytes 1572868
  11.1 0.9 %copy-start.3 = (bf16[1,1024,128]{2,1,0:T(8,128)(2,1)S(1)}, bf16[1,1024,128]{2,1,0:T(8,128)(2,1)}, u32[]{:S(2)}) copy-start(bf16[1,1024,128]{2,1,0:T(8,128)(2,1)} %param.13) | copy-start | bytes 786436
  12.1 0.7 copy-start.4
  12.8 0.7 copy-start.5
  13.4 0.7 copy-start.6
  17.6 3.3 %copy-start = (bf16[1024,4096]{1,0:T(8,128)(2,1)}, bf16[1024,4096]{1,0:T(8,128)(2,1)S(1)}, u32[]{:S(2)}) copy-start(bf16[1024,4096]{1,0:T(8,128)(2,1)S(1)} %get-tuple-element.43.refs_1_) | copy-start | bytes 25165828
  25.9 7.4 %collective-permute-start.7 = (bf16[1024,128]{1,0:T(8,128)(2,1)S(1)}, bf16[1024,128]{1,0:T(8,128)(2,1)S(1)}, u32[]{:S(2)}, u32[]{:S(2)}) collective-permute-start(bf16[1024,128]{1,0:T(8,128)(2,1)S(1)} %collective-permute-done.6.refs_5_.refs_8_), channel_id=1, source_target_pairs={{0,1},{1,0},{2,3},{3,2},{4,5},{5,4},{6,7},{7,6},{8,9},{9,8},{10,11... | collective-permute-start | bytes 786440 | tf_op jit(solution)/shard_map/ppermute | solution.py:308
  35.3 1.2 %collective-permute-start.9 = (f32[32,128]{1,0:T(8,128)S(1)}, f32[32,128]{1,0:T(8,128)S(1)}, u32[]{:S(2)}, u32[]{:S(2)}) collective-permute-start(f32[32,128]{1,0:T(8,128)S(1)} %get-tuple-element.44), channel_id=1, source_target_pairs={{0,4},{4,0},{8,12},{12,8},{16,20},{20,16},{24,28},{28,24},{1,5},{5... | collective-permute-start | bytes 49160 | tf_op jit(solution)/shard_map/ppermute | solution.py:333
  36.6 3.7 %collective-permute-start.10 = (f32[32,128]{1,0:T(8,128)S(1)}, f32[32,128]{1,0:T(8,128)S(1)}, u32[]{:S(2)}, u32[]{:S(2)}) collective-permute-start(f32[32,128]{1,0:T(8,128)S(1)} %add.26.refs_2_), channel_id=1, source_target_pairs={{0,8},{4,12},{8,0},{12,4},{16,24},{20,28},{24,16},{28,20},{1,9},{5... | collective-permute-start | bytes 49160 | tf_op jit(solution)/shard_map/ppermute | solution.py:333
  38.0 3.7 %collective-permute-start.11 = (f32[32,128]{1,0:T(8,128)S(1)}, f32[32,128]{1,0:T(8,128)S(1)}, u32[]{:S(2)}, u32[]{:S(2)}) collective-permute-start(f32[32,128]{1,0:T(8,128)S(1)} %add.26.refs_2_), channel_id=1, source_target_pairs={{0,16},{4,20},{8,24},{12,28},{16,0},{20,4},{24,8},{28,12},{1,17},{... | collective-permute-start | bytes 49160 | tf_op jit(solution)/shard_map/ppermute | solution.py:333
  39.6 4.6 %collective-permute-start.12 = (f32[32,128]{1,0:T(8,128)S(1)}, f32[32,128]{1,0:T(8,128)S(1)}, u32[]{:S(2)}, u32[]{:S(2)}) collective-permute-start(f32[32,128]{1,0:T(8,128)S(1)} %add.26.refs_2_), channel_id=1, source_target_pairs={{0,24},{4,28},{8,16},{12,20},{16,8},{20,12},{24,0},{28,4},{1,25},{... | collective-permute-start | bytes 49160 | tf_op jit(solution)/shard_map/ppermute | solution.py:333
  44.2 3.4 %copy-start.1 = (bf16[1024,4096]{1,0:T(8,128)(2,1)S(1)}, bf16[1024,4096]{1,0:T(8,128)(2,1)}, u32[]{:S(2)}) copy-start(bf16[1024,4096]{1,0:T(8,128)(2,1)} %copy-done) | copy-start | bytes 25165828
  54.5 12.6 %collective-permute-start.13 = (bf16[7,256,128]{2,1,0:T(8,128)(2,1)S(1)}, bf16[7,256,128]{2,1,0:T(8,128)(2,1)S(1)}, u32[]{:S(2)}, u32[]{:S(2)}) collective-permute-start(bf16[7,256,128]{2,1,0:T(8,128)(2,1)S(1)} %get-tuple-element.47), channel_id=1, source_target_pairs={{0,4},{4,8},{8,12},{12,16},{16,20},{20,24},{24,28},{28,0},{1,5},{5... | collective-permute-start | bytes 1376264 | tf_op jit(solution)/shard_map/ppermute | solution.py:418
  54.5 12.3 %collective-permute-start.14 = (bf16[4,256,128]{2,1,0:T(8,128)(2,1)S(1)}, bf16[4,256,128]{2,1,0:T(8,128)(2,1)S(1)}, u32[]{:S(2)}, u32[]{:S(2)}) collective-permute-start(bf16[4,256,128]{2,1,0:T(8,128)(2,1)S(1)} %get-tuple-element.48), channel_id=1, source_target_pairs={{0,28},{4,0},{8,4},{12,8},{16,12},{20,16},{24,20},{28,24},{1,29},{... | collective-permute-start | bytes 786440 | tf_op jit(solution)/shard_map/ppermute | solution.py:419
  57.2 1.2 %collective-permute-start = (f32[3,32,128]{2,1,0:T(8,128)S(1)}, f32[3,32,128]{2,1,0:T(8,128)S(1)}, u32[]{:S(2)}, u32[]{:S(2)}) collective-permute-start(f32[3,32,128]{2,1,0:T(8,128)S(1)} %get-tuple-element.80), channel_id=1, source_target_pairs={{0,4},{4,0},{8,12},{12,8},{16,20},{20,16},{24,28},{28,24},{1,5},{5... | collective-permute-start | bytes 147464 | tf_op jit(solution)/shard_map/while/body/ppermute | solution.py:333
  58.4 4.9 %collective-permute-start.1 = (f32[3,32,128]{2,1,0:T(8,128)S(1)}, f32[3,32,128]{2,1,0:T(8,128)S(1)}, u32[]{:S(2)}, u32[]{:S(2)}) collective-permute-start(f32[3,32,128]{2,1,0:T(8,128)S(1)} %add.39), channel_id=1, source_target_pairs={{0,16},{4,20},{8,24},{12,28},{16,0},{20,4},{24,8},{28,12},{1,17},{... | collective-permute-start | bytes 147464 | tf_op jit(solution)/shard_map/while/body/ppermute | solution.py:333
  59.0 5.9 %collective-permute-start.2 = (f32[3,32,128]{2,1,0:T(8,128)S(1)}, f32[3,32,128]{2,1,0:T(8,128)S(1)}, u32[]{:S(2)}, u32[]{:S(2)}) collective-permute-start(f32[3,32,128]{2,1,0:T(8,128)S(1)} %add.39), channel_id=1, source_target_pairs={{0,24},{4,28},{8,16},{12,20},{16,8},{20,12},{24,0},{28,4},{1,25},{... | collective-permute-start | bytes 147464 | tf_op jit(solution)/shard_map/while/body/ppermute | solution.py:333
  59.6 6.5 %collective-permute-start.3 = (f32[3,32,128]{2,1,0:T(8,128)S(1)}, f32[3,32,128]{2,1,0:T(8,128)S(1)}, u32[]{:S(2)}, u32[]{:S(2)}) collective-permute-start(f32[3,32,128]{2,1,0:T(8,128)S(1)} %add.39), channel_id=1, source_target_pairs={{0,8},{4,12},{8,0},{12,4},{16,24},{20,28},{24,16},{28,20},{1,9},{5... | collective-permute-start | bytes 147464 | tf_op jit(solution)/shard_map/while/body/ppermute | solution.py:333

commit v8 on v7

--- a/solution.py
+++ b/solution.py
@@ -9,6 +9,7 @@
 STEPS = 4
 PAD = 8
 GROUP = 256
+ROOM = 6
 
 
 def shift_pairs(count, by):
@@ -106,7 +107,7 @@
 
     def block(place):
         where = pl.ds(pl.multiple_of(place * rows, rows), rows)
-        return pltpu.make_async_copy(built.at[where], chosen.at[where], sems.at[place])
+        return pltpu.make_async_copy(built.at[where], chosen.at[0, where], sems.at[place])
 
     def choose(place, carry):
         by_row = lax.broadcasted_iota(jnp.int32, (rows, TILE), 0) + place * rows
@@ -199,12 +200,10 @@
 
 
 def project_kernel(chunks, source, start, tiles, *refs):
-    count = len(chunks)
-    panels, (*before, early, last, wide) = refs[:count], refs[count:]
+    panels, (*before, out, wide) = refs[: len(chunks)], refs[len(chunks) :]
     shard = panels[0].shape[0] // GROUP
-    if before:
-        early[...] = before[0][...]
-        last[...] = before[1][...]
+    for given in before:
+        out[...] = given[...]
     first = lax.broadcasted_iota(jnp.int32, (8, TILE), 0) < STEPS
     lane = lax.broadcasted_iota(jnp.int32, (8, TILE), 1)
     for chunk, panel in zip(chunks, panels):
@@ -223,14 +222,7 @@
                 rows = jnp.where(first, wide[pl.ds(row, 1), :], wide[pl.ds(row + TILE, 1), :])
                 total = jnp.sum(cells * rows, axis=1, keepdims=True)
                 sums = jnp.where(lane == place, total, sums)
-            for half in range(2):
-                row = 2 * number + half
-                for step in range(STEPS):
-                    value = sums[half * STEPS + step : half * STEPS + step + 1]
-                    if step < STEPS - 1:
-                        early[step, pl.ds(row, 1), :] = value
-                    else:
-                        last[pl.ds(row, 1), :] = value
+            out[number] = sums
             return carry
 
         lax.fori_loop(0, shard, body, 0)
@@ -239,17 +231,17 @@
 def deposit_kernel(count, source, chosen, *refs):
     parts, panels = refs[:count], refs[count:-7]
     total, field, rightward, leftward, scaled, held, sems = refs[-7:]
-    groups = total.shape[0] // 2
+    groups = total.shape[0]
     shard = groups // len(panels)
     cells, per_plane = field.shape[0], field.shape[1]
     copies = []
     for plane in range(cells):
         where = pl.ds(plane * per_plane, per_plane)
-        copies.append(pltpu.make_async_copy(chosen.at[where], held.at[where], sems.at[plane]))
+        copies.append(pltpu.make_async_copy(chosen.at[0, where], held.at[where], sems.at[plane]))
         copies[plane].start()
     total[...] = tree_sum([part[...] for part in parts])
     numbers = [source[g // shard] * shard + g % shard for g in range(groups)]
-    last = [total[pl.ds(2 * number + half, 1), :] for number in numbers for half in range(2)]
+    last = [total[n, pl.ds(half * STEPS + STEPS - 1, 1), :] for n in numbers for half in range(2)]
     drive = jnp.concatenate(last, axis=0).T
     for group, number in enumerate(numbers):
         for half in range(2):
@@ -348,8 +340,9 @@
     f32, bf16 = jnp.float32, jnp.bfloat16
 
     source = lax.axis_index("probe") ^ jnp.arange(probes, dtype=jnp.int32)
-    low = lax.ppermute(own.astype(bf16), "state", shift_pairs(slabs, 1))
-    high = lax.ppermute(own, "state", shift_pairs(slabs, -1))
+    rounded = own.astype(bf16)
+    low = lax.ppermute(rounded, "state", shift_pairs(slabs, 1))
+    high = lax.ppermute(tied(own, rounded), "state", shift_pairs(slabs, -1))
 
     shifted, coef, start, panel, chosen = call(
         prelude_kernel,
@@ -358,9 +351,9 @@
             jax.ShapeDtypeStruct((5, height, TILE), f32),
             jax.ShapeDtypeStruct(tile_index.shape, jnp.int32),
             jax.ShapeDtypeStruct(actuator_panel.shape[1:], bf16),
-            jax.ShapeDtypeStruct((tile_total, actuators), bf16),
+            jax.ShapeDtypeStruct((ROOM, tile_total, actuators), bf16),
         ),
-        vmem=14,
+        vmem=16,
         scratch=(pltpu.VMEM((tile_total, actuators), bf16), pltpu.SemaphoreType.DMA((16,))),
         hbm_out=(4,),
         smem=1,
@@ -377,30 +370,27 @@
         inputs=5,
     )(probe_offset, coef, shifted, low, high)
 
-    panels = [panel] + gathered_panel(actuator_panel[0], "probe", tiles)
+    panels = [panel] + gathered_panel(actuator_panel[0], "probe", coef)
     every = list(range(probes))
 
     def project(chunks, *given):
         return call(
             lambda *refs: project_kernel(chunks, *refs),
-            (
-                jax.ShapeDtypeStruct((STEPS - 1, 2 * groups, TILE), f32),
-                jax.ShapeDtypeStruct((2 * groups, TILE), f32),
-            ),
+            jax.ShapeDtypeStruct((groups, 2 * STEPS, TILE), f32),
             vmem=6,
             scratch=(pltpu.VMEM((shard * GROUP, TILE), f32),),
             smem=2,
             inputs=3 + len(chunks) + len(given),
         )(source, start, tiles, *[panels[chunk] for chunk in chunks], *given)
 
-    early, last = project(every[-1:], *project(every[:-1]))
-    parts = summands(last, "state")
+    before = project(every[:-1])
+    parts = summands(project(every[-1:], before), "state")
     payload = jax.ShapeDtypeStruct((2 * cells - 1, height * columns, TILE), bf16)
     heads = jax.ShapeDtypeStruct((cells, height * columns, TILE), bf16)
     total, forced, rightward, leftward = call(
         lambda *refs: deposit_kernel(len(parts), *refs),
         (
-            jax.ShapeDtypeStruct(last.shape, f32),
+            jax.ShapeDtypeStruct(before.shape, f32),
             jax.ShapeDtypeStruct((cells, height * columns, TILE), f32),
             payload,
             heads,
@@ -424,9 +414,7 @@
         scratch=(field_shape, field_shape),
         inputs=4,
     )(coef, forced, from_low, from_high)
-    rounds = 1 + jnp.minimum(probe_offset[0], 0)
-    early = lax.fori_loop(0, rounds, lambda _, part: tree_sum(summands(part, "state")), early)
-    projections = jnp.concatenate([early, total[None]], axis=0)
+    projections = total.reshape(groups, 2, STEPS, TILE).transpose(2, 0, 1, 3)
     return projections.reshape(STEPS, 1, actuators), response[None]
 
 

time: 73.4 us -> 65.5 us (0.89)
  local copies, waits for them, and re-layouts: 10.7 us -> 4.68 us
  starting transfers between devices: 18 us -> 14.6 us
  waiting for transfers between devices: 13.3 us -> 14.8 us
  Pallas kernels: 27.2 us -> 28.6 us
  other arithmetic: 1.83 us -> 1.09 us
    unnamed x14 -> x10, local copies, waits for them, and re-layouts: 10.7 us -> 4.01 us
    ppermute x1, waiting for transfers between devices: 0.01 us -> 5.45 us  [local(): from_high = lax.ppermute(leftward, 'state', shift_pairs(slabs, -1))]
    ppermute x8 -> x4, waiting for transfers between devices: 10.6 us -> 5.93 us  [summands(): parts = [part] + [lax.ppermute(part, axis, pair) for pair in pairs]]
    ppermute x8 -> x4, starting transfers between devices: 7.12 us -> 3.62 us  [summands(): parts = [part] + [lax.ppermute(part, axis, pair) for pair in pairs]]
    ppermute x1, waiting for transfers between devices: 0.3 us -> 2.73 us  [local(): from_low = lax.ppermute(rightward, 'state', shift_pairs(slabs, 1))]
    ppermute x3, waiting for transfers between devices: 2.4 us -> 0.67 us  [gathered_panel(): shards[held | mask] = lax.ppermute(operand, axis, pairs)]
    pallas_call x1, Pallas kernels: 6.87 us -> 7.76 us  [local(): call(lambda *refs: deposit_kernel(len(parts), *refs), (jax.ShapeDtypeStru...]
  transfers between devices with their start and end apart: 15 -> 11, of which waited for: 10 -> 7; matrix products, arithmetic and copies ran while one was open for 3% -> 1% of each run, Pallas kernels for 18% -> 21%
where the time goes in v8:
time: 65.5 us; the launch traced here: 65.2 us
  Pallas kernels  28.6 us (44%)
  waiting for transfers between devices  14.8 us (23%)
  starting transfers between devices  14.6 us (22%)
  local copies, waits for them, and re-layouts  4.68 us (7%)
  between operations  1.37 us (2%)
  other arithmetic  1.09 us (2%)
    pallas_call x1, Pallas kernels, local(): call(lambda *refs: deposit_kernel(len(parts), *refs), (jax.ShapeDtypeStru...  7.76 us
    pallas_call x2, Pallas kernels, project(): call(lambda *refs: project_kernel(chunks, *refs), jax.ShapeDtypeStruct((g...  6.46 us
    ppermute x4, waiting for transfers between devices, summands(): parts = [part] + [lax.ppermute(part, axis, pair) for pair in pairs]  5.93 us
    ppermute x1, waiting for transfers between devices, local(): from_high = lax.ppermute(leftward, 'state', shift_pairs(slabs, -1))  5.45 us
    pallas_call x1, Pallas kernels, local(): call(forward_kernel, jax.ShapeDtypeStruct((cells, height, width), f32), v...  5.3 us
    pallas_call x1, Pallas kernels, local(): call(adjoint_kernel, jax.ShapeDtypeStruct((tile_total * STEPS + 2 * PAD,...  4.99 us
    ppermute x3, starting transfers between devices, gathered_panel(): shards[held | mask] = lax.ppermute(operand, axis, pairs)  4.94 us
    pallas_call x1, Pallas kernels, local(): call(prelude_kernel, (jax.ShapeDtypeStruct((cells, columns, height, TILE)...  4.1 us
  transfers between devices with their start and end apart: 11, of which 7 were waited for; matrix products, arithmetic and copies ran while one was open for 1% of the time, Pallas kernels for 21%

profile of v8, /device:TPU:0, one launch (start us, length us, event | category | flops | bytes accessed | tf_op | source)
XLA Modules:
  0.0 65.2 jit_solution(3543573440425268)
XLA Ops:
  0.6 1.1 %bitcast_convert_fusion = bf16[4,64,512]{2,1,0:T(8,128)(2,1)S(1)} fusion(f32[1,4,64,512]{3,2,1,0:T(8,128)} %param.6), kind=kLoop, calls=%fused_computation.1 | loop fusion | flops 131072 | bytes 786432 | tf_op jit(solution)/shard_map/convert_element_type | solution.py:343
  1.7 3.4 %collective-permute-start.1 = (f32[4,64,512]{2,1,0:T(8,128)}, f32[4,64,512]{2,1,0:T(8,128)S(1)}, u32[]{:S(2)}, u32[]{:S(2)}) collective-permute-start(f32[4,64,512]{2,1,0:T(8,128)} %bitcast.10), channel_id=1, source_target_pairs={{0,28},{4,0},{8,4},{12,8},{16,12},{20,16},{24,20},{28,24},{1,29},{... | collective-permute-start | bytes 1572872 | tf_op jit(solution)/shard_map/ppermute | solution.py:345
  5.1 2.6 %collective-permute-start.2 = (bf16[1024,128]{1,0:T(8,128)(2,1)}, bf16[1024,128]{1,0:T(8,128)(2,1)S(1)}, u32[]{:S(2)}, u32[]{:S(2)}) collective-permute-start(bf16[1024,128]{1,0:T(8,128)(2,1)} %bitcast.12), channel_id=1, source_target_pairs={{0,2},{1,3},{2,0},{3,1},{4,6},{5,7},{6,4},{7,5},{8,10},{9,11},{10,... | collective-permute-start | bytes 786440 | tf_op jit(solution)/shard_map/ppermute | solution.py:300
  7.7 0.0 collective-permute-start
  7.7 1.6 %collective-permute-start.4 = (bf16[1024,128]{1,0:T(8,128)(2,1)}, bf16[1024,128]{1,0:T(8,128)(2,1)S(1)}, u32[]{:S(2)}, u32[]{:S(2)}) collective-permute-start(bf16[1024,128]{1,0:T(8,128)(2,1)} %bitcast.13), channel_id=1, source_target_pairs={{0,1},{1,0},{2,3},{3,2},{4,5},{5,4},{6,7},{7,6},{8,9},{9,8},{10,11... | collective-permute-start | bytes 786440 | tf_op jit(solution)/shard_map/ppermute | solution.py:300
  9.9 0.0 copy-start
  9.9 1.0 %copy-done = f32[1,4,64,512]{3,2,1,0:T(8,128)S(1)} copy-done((f32[1,4,64,512]{3,2,1,0:T(8,128)S(1)}, f32[1,4,64,512]{3,2,1,0:T(8,128)}, u32[]{:S(2)}) %copy-start) | copy-done | bytes 524312
  11.0 0.0 copy-start.1
  11.0 0.9 %copy-done.1 = bf16[1,1024,128]{2,1,0:T(8,128)(2,1)S(1)} copy-done((bf16[1,1024,128]{2,1,0:T(8,128)(2,1)S(1)}, bf16[1,1024,128]{2,1,0:T(8,128)(2,1)}, u32[]{:S(2)}) %copy-start.1) | copy-done | bytes 262168
  11.9 0.0 copy-start.2
  11.9 0.7 %copy-done.2 = s32[1,4096]{1,0:T(1,128)S(1)} copy-done((s32[1,4096]{1,0:T(1,128)S(1)}, s32[1,4096]{1,0:T(1,128)}, u32[]{:S(2)}) %copy-start.2) | copy-done | bytes 16408
  12.6 0.0 copy-start.3
  12.6 0.7 %copy-done.3 = f32[64]{0:T(128)S(1)} copy-done((f32[64]{0:T(128)S(1)}, f32[64]{0:T(128)}, u32[]{:S(2)}) %copy-start.3) | copy-done | bytes 280
  13.3 0.0 copy-start.4
  13.3 0.7 %copy-done.4 = f32[64]{0:T(128)S(1)} copy-done((f32[64]{0:T(128)S(1)}, f32[64]{0:T(128)}, u32[]{:S(2)}) %copy-start.4) | copy-done | bytes 280
  13.9 4.1 %shard_map.77 = (f32[4,4,64,128]{3,2,1,0:T(8,128)S(1)}, f32[5,64,128]{2,1,0:T(8,128)S(1)}, s32[1,4096]{1,0:T(1,128)S(1)}, bf16[1024,128]{1,0:T(8,128)(2,1)S(1)}, bf16[6,1024,4096]{2,1,0:T(8,128)(2,1)}) custom-call(s32[1]{0:T(128)S(6)} %copy.9.offset, f32[4,64,512]{2,1,0:T(8,128)S(1)} %bitcast.11, f32[1,64]{1,0:T(1,128)S(1)} %bitcast.16, ...), custom_call_target="tpu_custom_call" | custom-call | flops 1024 | bytes 1024 | tf_op jit(solution)/shard_map/pallas_call | solution.py:347
  18.0 0.7 %collective-permute-done.2.refs_5_.refs_8_ = bf16[1024,128]{1,0:T(8,128)(2,1)S(1)} collective-permute-done((bf16[1024,128]{1,0:T(8,128)(2,1)}, bf16[1024,128]{1,0:T(8,128)(2,1)S(1)}, u32[]{:S(2)}, u32[]{:S(2)}) %collective-permute-start.2) | collective-permute-done | bytes 262176 | tf_op jit(solution)/shard_map/ppermute | solution.py:300
  18.7 0.8 %collective-permute-start.3 = (bf16[1024,128]{1,0:T(8,128)(2,1)S(1)}, bf16[1024,128]{1,0:T(8,128)(2,1)S(1)}, u32[]{:S(2)}, u32[]{:S(2)}) collective-permute-start(bf16[1024,128]{1,0:T(8,128)(2,1)S(1)} %collective-permute-done.2.refs_5_.refs_8_), channel_id=1, source_target_pairs={{0,1},{1,0},{2,3},{3,2},{4,5},{5,4},{6,7},{7,6},{8,9},{9,8},{10,11... | collective-permute-start | bytes 786440 | tf_op jit(solution)/shard_map/ppermute | solution.py:300
  19.5 0.0 collective-permute-done.low
  19.5 0.0 collective-permute-done.1.high
  19.5 5.0 %shard_map.78.refs_2_ = f32[4112,128]{1,0:T(8,128)S(1)} custom-call(s32[1]{0:T(128)S(6)} %copy.9.offset, f32[5,64,128]{2,1,0:T(8,128)S(1)} %get-tuple-element.15.coef, f32[4,4,64,128]{3,2,1,0:T(8,128)S(1)} %get-tuple-element.16.own, bf16[4,64,512]{2,1,0:T(8,128)(2,1)S(1)} %collective-permute-done.low, f32[4,64,512]{2,1,0:T(8,128)S(1)} %collective-permute-done.1.high), custom_call_target="tpu_custom_call" | custom-call | flops 1024 | bytes 1024 | tf_op jit(solution)/shard_map/pallas_call | solution.py:364
  24.5 0.0 collective-permute-done.4.refs_4_.refs_7_
  24.5 4.4 %shard_map.79.refs_4_ = f32[16,8,128]{2,1,0:T(8,128)S(1)} custom-call(s32[4]{0:T(128)S(1)} %iota_xor_fusion.refs_0_, s32[1,4096]{1,0:T(1,128)S(1)} %get-tuple-element.14.refs_1_, f32[4112,128]{1,0:T(8,128)S(1)} %shard_map.78.refs_2_, bf16[1024,128]{1,0:T(8,128)(2,1)S(1)} %get-tuple-element.19.refs_3_.refs_6_, ...), custom_call_target="tpu_custom_call" | custom-call | flops 1024 | bytes 1024 | tf_op jit(solution)/shard_map/pallas_call | solution.py:377
  28.9 0.0 collective-permute-done.3.refs_3_.refs_9_
  28.9 2.0 %shard_map.80 = f32[16,8,128]{2,1,0:T(8,128)S(1)} custom-call(s32[4]{0:T(128)S(1)} %iota_xor_fusion.refs_0_, s32[1,4096]{1,0:T(1,128)S(1)} %get-tuple-element.14.refs_1_, f32[4112,128]{1,0:T(8,128)S(1)} %shard_map.78.refs_2_, bf16[1024,128]{1,0:T(8,128)(2,1)S(1)} %collective-permute-done.3.refs_3_.refs_9_, f32[16,8,128]{2,1,0:T(8,128)S(1)} %shard_map.79.refs_4_), custom_call_target="tpu_custom_call" | custom-call | flops 1024 | bytes 1024 | tf_op jit(solution)/shard_map/pallas_call | solution.py:377
  31.0 0.1 collective-permute-start.5
  31.1 1.2 %collective-permute-done.5 = f32[16,8,128]{2,1,0:T(8,128)S(1)} collective-permute-done((f32[16,8,128]{2,1,0:T(8,128)S(1)}, f32[16,8,128]{2,1,0:T(8,128)S(1)}, u32[]{:S(2)}, u32[]{:S(2)}) %collective-permute-start.5) | collective-permute-done | bytes 65568 | tf_op jit(solution)/shard_map/ppermute | solution.py:325
  32.3 1.6 %collective-permute-start.6 = (f32[16,8,128]{2,1,0:T(8,128)S(1)}, f32[16,8,128]{2,1,0:T(8,128)S(1)}, u32[]{:S(2)}, u32[]{:S(2)}) collective-permute-start(f32[16,8,128]{2,1,0:T(8,128)S(1)} %add.3.refs_2_), channel_id=1, source_target_pairs={{0,8},{4,12},{8,0},{12,4},{16,24},{20,28},{24,16},{28,20},{1,9},{5... | collective-permute-start | bytes 196616 | tf_op jit(solution)/shard_map/ppermute | solution.py:325
  33.9 1.5 %collective-permute-start.7 = (f32[16,8,128]{2,1,0:T(8,128)S(1)}, f32[16,8,128]{2,1,0:T(8,128)S(1)}, u32[]{:S(2)}, u32[]{:S(2)}) collective-permute-start(f32[16,8,128]{2,1,0:T(8,128)S(1)} %add.3.refs_2_), channel_id=1, source_target_pairs={{0,16},{4,20},{8,24},{12,28},{16,0},{20,4},{24,8},{28,12},{1,17},{... | collective-permute-start | bytes 196616 | tf_op jit(solution)/shard_map/ppermute | solution.py:325
  35.4 0.5 collective-permute-start.8
  35.9 0.8 %collective-permute-done.6.refs_3_ = f32[16,8,128]{2,1,0:T(8,128)S(1)} collective-permute-done((f32[16,8,128]{2,1,0:T(8,128)S(1)}, f32[16,8,128]{2,1,0:T(8,128)S(1)}, u32[]{:S(2)}, u32[]{:S(2)}) %collective-permute-start.6) | collective-permute-done | bytes 65568 | tf_op jit(solution)/shard_map/ppermute | solution.py:325
  36.6 1.5 %collective-permute-done.7.refs_4_ = f32[16,8,128]{2,1,0:T(8,128)S(1)} collective-permute-done((f32[16,8,128]{2,1,0:T(8,128)S(1)}, f32[16,8,128]{2,1,0:T(8,128)S(1)}, u32[]{:S(2)}, u32[]{:S(2)}) %collective-permute-start.7) | collective-permute-done | bytes 65568 | tf_op jit(solution)/shard_map/ppermute | solution.py:325
  38.1 2.4 %collective-permute-done.8.refs_5_ = f32[16,8,128]{2,1,0:T(8,128)S(1)} collective-permute-done((f32[16,8,128]{2,1,0:T(8,128)S(1)}, f32[16,8,128]{2,1,0:T(8,128)S(1)}, u32[]{:S(2)}, u32[]{:S(2)}) %collective-permute-start.8) | collective-permute-done | bytes 65568 | tf_op jit(solution)/shard_map/ppermute | solution.py:325
  40.5 7.8 %shard_map.81 = (f32[16,8,128]{2,1,0:T(8,128)S(1)}, f32[4,256,128]{2,1,0:T(8,128)S(1)}, bf16[7,256,128]{2,1,0:T(8,128)(2,1)S(1)}, bf16[4,256,128]{2,1,0:T(8,128)(2,1)S(1)}) custom-call(s32[4]{0:T(128)S(1)} %iota_xor_fusion.refs_0_, bf16[6,1024,4096]{2,1,0:T(8,128)(2,1)} %get-tuple-element.13.refs_1_, f32[16,8,128]{2,1,0:T(8,128)S(1)} %add.3.refs_2_, ...), custom_call_target="tpu_custom_call" | custom-call | flops 1024 | bytes 1024 | tf_op jit(solution)/shard_map/pallas_call | solution.py:390
  48.3 0.1 collective-permute-start.9
  48.4 2.6 %collective-permute-start.10 = (bf16[4,256,128]{2,1,0:T(8,128)(2,1)S(1)}, bf16[4,256,128]{2,1,0:T(8,128)(2,1)S(1)}, u32[]{:S(2)}, u32[]{:S(2)}) collective-permute-start(bf16[4,256,128]{2,1,0:T(8,128)(2,1)S(1)} %get-tuple-element.23), channel_id=1, source_target_pairs={{0,28},{4,0},{8,4},{12,8},{16,12},{20,16},{24,20},{28,24},{1,29},{... | collective-permute-start | bytes 786440 | tf_op jit(solution)/shard_map/ppermute | solution.py:409
  51.0 0.7 %copy.8 = f32[4,16,2,128]{3,2,1,0:T(2,128)} copy(f32[4,16,2,128]{3,0,2,1:T(4,128)S(1)} %bitcast.15) | data formatting | bytes 131072 | tf_op jit(solution)/shard_map/transpose | solution.py:417
  51.7 5.4 %collective-permute-done.10.high = bf16[4,256,128]{2,1,0:T(8,128)(2,1)S(1)} collective-permute-done((bf16[4,256,128]{2,1,0:T(8,128)(2,1)S(1)}, bf16[4,256,128]{2,1,0:T(8,128)(2,1)S(1)}, u32[]{:S(2)}, u32[]{:S(2)}) %collective-permute-start.10) | collective-permute-done | bytes 262176 | tf_op jit(solution)/shard_map/ppermute | solution.py:409
  57.1 2.7 %collective-permute-done.9.low = bf16[7,256,128]{2,1,0:T(8,128)(2,1)S(1)} collective-permute-done((bf16[7,256,128]{2,1,0:T(8,128)(2,1)S(1)}, bf16[7,256,128]{2,1,0:T(8,128)(2,1)S(1)}, u32[]{:S(2)}, u32[]{:S(2)}) %collective-permute-start.9) | collective-permute-done | bytes 458784 | tf_op jit(solution)/shard_map/ppermute | solution.py:408
  59.9 5.3 %shard_map.82 = f32[4,64,512]{2,1,0:T(8,128)} custom-call(f32[5,64,128]{2,1,0:T(8,128)S(1)} %get-tuple-element.15.coef, f32[4,256,128]{2,1,0:T(8,128)S(1)} %get-tuple-element.21.own, bf16[7,256,128]{2,1,0:T(8,128)(2,1)S(1)} %collective-permute-done.9.low, bf16[4,256,128]{2,1,0:T(8,128)(2,1)S(1)} %collective-permute-done.10.high), custom_call_target="tpu_custom_call" | custom-call | flops 1024 | bytes 1024 | tf_op jit(solution)/shard_map/pallas_call | solution.py:410
  (2 shorter events, 0.0 us)
Async XLA Ops:
  1.7 17.8 %collective-permute-start.1 = (f32[4,64,512]{2,1,0:T(8,128)}, f32[4,64,512]{2,1,0:T(8,128)S(1)}, u32[]{:S(2)}, u32[]{:S(2)}) collective-permute-start(f32[4,64,512]{2,1,0:T(8,128)} %bitcast.10), channel_id=1, source_target_pairs={{0,28},{4,0},{8,4},{12,8},{16,12},{20,16},{24,20},{28,24},{1,29},{... | collective-permute-start | bytes 1572872 | tf_op jit(solution)/shard_map/ppermute | solution.py:345
  5.1 13.6 %collective-permute-start.2 = (bf16[1024,128]{1,0:T(8,128)(2,1)}, bf16[1024,128]{1,0:T(8,128)(2,1)S(1)}, u32[]{:S(2)}, u32[]{:S(2)}) collective-permute-start(bf16[1024,128]{1,0:T(8,128)(2,1)} %bitcast.12), channel_id=1, source_target_pairs={{0,2},{1,3},{2,0},{3,1},{4,6},{5,7},{6,4},{7,5},{8,10},{9,11},{10,... | collective-permute-start | bytes 786440 | tf_op jit(solution)/shard_map/ppermute | solution.py:300
  7.7 11.8 %collective-permute-start = (bf16[4,64,512]{2,1,0:T(8,128)(2,1)S(1)}, bf16[4,64,512]{2,1,0:T(8,128)(2,1)S(1)}, u32[]{:S(2)}, u32[]{:S(2)}) collective-permute-start(bf16[4,64,512]{2,1,0:T(8,128)(2,1)S(1)} %bitcast_convert_fusion), channel_id=1, source_target_pairs={{0,4},{4,8},{8,12},{12,16},{16,20},{20,24},{24,28},{28,0},{1,5},{5... | collective-permute-start | bytes 786440 | tf_op jit(solution)/shard_map/ppermute | solution.py:344
  7.7 16.8 %collective-permute-start.4 = (bf16[1024,128]{1,0:T(8,128)(2,1)}, bf16[1024,128]{1,0:T(8,128)(2,1)S(1)}, u32[]{:S(2)}, u32[]{:S(2)}) collective-permute-start(bf16[1024,128]{1,0:T(8,128)(2,1)} %bitcast.13), channel_id=1, source_target_pairs={{0,1},{1,0},{2,3},{3,2},{4,5},{5,4},{6,7},{7,6},{8,9},{9,8},{10,11... | collective-permute-start | bytes 786440 | tf_op jit(solution)/shard_map/ppermute | solution.py:300
  9.9 1.0 %copy-start = (f32[1,4,64,512]{3,2,1,0:T(8,128)S(1)}, f32[1,4,64,512]{3,2,1,0:T(8,128)}, u32[]{:S(2)}) copy-start(f32[1,4,64,512]{3,2,1,0:T(8,128)} %param.6) | copy-start | bytes 1572868
  11.0 0.9 %copy-start.1 = (bf16[1,1024,128]{2,1,0:T(8,128)(2,1)S(1)}, bf16[1,1024,128]{2,1,0:T(8,128)(2,1)}, u32[]{:S(2)}) copy-start(bf16[1,1024,128]{2,1,0:T(8,128)(2,1)} %param.11) | copy-start | bytes 786436
  11.9 0.7 %copy-start.2 = (s32[1,4096]{1,0:T(1,128)S(1)}, s32[1,4096]{1,0:T(1,128)}, u32[]{:S(2)}) copy-start(s32[1,4096]{1,0:T(1,128)} %tile.1) | copy-start | bytes 49156
  12.6 0.7 %copy-start.3 = (f32[64]{0:T(128)S(1)}, f32[64]{0:T(128)}, u32[]{:S(2)}) copy-start(f32[64]{0:T(128)} %param.7) | copy-start | bytes 772
  13.3 0.7 %copy-start.4 = (f32[64]{0:T(128)S(1)}, f32[64]{0:T(128)}, u32[]{:S(2)}) copy-start(f32[64]{0:T(128)} %param.8) | copy-start | bytes 772
  18.7 10.2 %collective-permute-start.3 = (bf16[1024,128]{1,0:T(8,128)(2,1)S(1)}, bf16[1024,128]{1,0:T(8,128)(2,1)S(1)}, u32[]{:S(2)}, u32[]{:S(2)}) collective-permute-start(bf16[1024,128]{1,0:T(8,128)(2,1)S(1)} %collective-permute-done.2.refs_5_.refs_8_), channel_id=1, source_target_pairs={{0,1},{1,0},{2,3},{3,2},{4,5},{5,4},{6,7},{7,6},{8,9},{9,8},{10,11... | collective-permute-start | bytes 786440 | tf_op jit(solution)/shard_map/ppermute | solution.py:300
  31.0 1.3 %collective-permute-start.5 = (f32[16,8,128]{2,1,0:T(8,128)S(1)}, f32[16,8,128]{2,1,0:T(8,128)S(1)}, u32[]{:S(2)}, u32[]{:S(2)}) collective-permute-start(f32[16,8,128]{2,1,0:T(8,128)S(1)} %shard_map.80), channel_id=1, source_target_pairs={{0,4},{4,0},{8,12},{12,8},{16,20},{20,16},{24,28},{28,24},{1,5},{5... | collective-permute-start | bytes 196616 | tf_op jit(solution)/shard_map/ppermute | solution.py:325
  32.3 4.3 %collective-permute-start.6 = (f32[16,8,128]{2,1,0:T(8,128)S(1)}, f32[16,8,128]{2,1,0:T(8,128)S(1)}, u32[]{:S(2)}, u32[]{:S(2)}) collective-permute-start(f32[16,8,128]{2,1,0:T(8,128)S(1)} %add.3.refs_2_), channel_id=1, source_target_pairs={{0,8},{4,12},{8,0},{12,4},{16,24},{20,28},{24,16},{28,20},{1,9},{5... | collective-permute-start | bytes 196616 | tf_op jit(solution)/shard_map/ppermute | solution.py:325
  33.9 4.3 %collective-permute-start.7 = (f32[16,8,128]{2,1,0:T(8,128)S(1)}, f32[16,8,128]{2,1,0:T(8,128)S(1)}, u32[]{:S(2)}, u32[]{:S(2)}) collective-permute-start(f32[16,8,128]{2,1,0:T(8,128)S(1)} %add.3.refs_2_), channel_id=1, source_target_pairs={{0,16},{4,20},{8,24},{12,28},{16,0},{20,4},{24,8},{28,12},{1,17},{... | collective-permute-start | bytes 196616 | tf_op jit(solution)/shard_map/ppermute | solution.py:325
  35.4 5.2 %collective-permute-start.8 = (f32[16,8,128]{2,1,0:T(8,128)S(1)}, f32[16,8,128]{2,1,0:T(8,128)S(1)}, u32[]{:S(2)}, u32[]{:S(2)}) collective-permute-start(f32[16,8,128]{2,1,0:T(8,128)S(1)} %add.3.refs_2_), channel_id=1, source_target_pairs={{0,24},{4,28},{8,16},{12,20},{16,8},{20,12},{24,0},{28,4},{1,25},{... | collective-permute-start | bytes 196616 | tf_op jit(solution)/shard_map/ppermute | solution.py:325
  48.3 11.5 %collective-permute-start.9 = (bf16[7,256,128]{2,1,0:T(8,128)(2,1)S(1)}, bf16[7,256,128]{2,1,0:T(8,128)(2,1)S(1)}, u32[]{:S(2)}, u32[]{:S(2)}) collective-permute-start(bf16[7,256,128]{2,1,0:T(8,128)(2,1)S(1)} %get-tuple-element.22), channel_id=1, source_target_pairs={{0,4},{4,8},{8,12},{12,16},{16,20},{20,24},{24,28},{28,0},{1,5},{5... | collective-permute-start | bytes 1376264 | tf_op jit(solution)/shard_map/ppermute | solution.py:408
  48.4 8.7 %collective-permute-start.10 = (bf16[4,256,128]{2,1,0:T(8,128)(2,1)S(1)}, bf16[4,256,128]{2,1,0:T(8,128)(2,1)S(1)}, u32[]{:S(2)}, u32[]{:S(2)}) collective-permute-start(bf16[4,256,128]{2,1,0:T(8,128)(2,1)S(1)} %get-tuple-element.23), channel_id=1, source_target_pairs={{0,28},{4,0},{8,4},{12,8},{16,12},{20,16},{24,20},{28,24},{1,29},{... | collective-permute-start | bytes 786440 | tf_op jit(solution)/shard_map/ppermute | solution.py:409

commit v9 on v6

--- a/solution.py
+++ b/solution.py
@@ -65,19 +65,25 @@
     return high, low
 
 
-def shifted_plane(field, plane, offset):
+def shifted_plane(field, plane, offset, tail=None):
     height, width = field.shape[1:]
     columns = width // TILE
     turn, rest = offset // TILE, offset % TILE
     lane = lax.broadcasted_iota(jnp.int32, (height, TILE), 1)
-    rolled = [pltpu.roll(field[plane, :, pl.ds(c * TILE, TILE)], rest, 1) for c in range(columns)]
+    parts = [field[plane, :, pl.ds(c * TILE, TILE)].astype(jnp.float32) for c in range(columns)]
+    if tail is not None:
+        parts = [
+            part + field[tail, :, pl.ds(c * TILE, TILE)].astype(jnp.float32)
+            for c, part in enumerate(parts)
+        ]
+    rolled = [pltpu.roll(part, rest, 1) for part in parts]
     return [
         (lax.rem(c + turn, columns), jnp.where(lane >= rest, rolled[c], rolled[c - 1]))
         for c in range(columns)
     ]
 
 
-def prelude_kernel(offset, field, courant, diffusivity, tile, panel, own, coef, start, chosen, kept):
+def prelude_kernel(offset, field, courant, diffusivity, tile, panel, own, coef, start, kept):
     columns, height = own.shape[1:3]
 
     def load(plane, carry):
@@ -101,17 +107,6 @@
     inside = numbers & (columns * height - 1)
     numbers = (numbers - inside) + (inside & (columns - 1)) * height + inside // columns
     start[...] = numbers * STEPS
-    rows = 64
-
-    def choose(place, carry):
-        by_row = lax.broadcasted_iota(jnp.int32, (rows, TILE), 0) + place * rows
-        where = pl.ds(pl.multiple_of(place * rows, rows), rows)
-        for left in range(0, chosen.shape[1], TILE):
-            found = jnp.where(numbers[:, left : left + TILE] == by_row, 1.0, 0.0)
-            chosen[where, pl.ds(left, TILE)] = found.astype(jnp.bfloat16)
-        return carry
-
-    lax.fori_loop(0, chosen.shape[0] // rows, choose, 0)
 
 
 def adjoint_kernel(offset, coef, own, low, high, tiles, first, second):
@@ -124,14 +119,13 @@
     clear_pads(first)
     clear_pads(second)
 
-    def load(plane, carry):
-        for slab, field in ((0, low), (2, high)):
-            for column, value in shifted_plane(field, plane, offset[0]):
-                first[slab * cells + plane, column, inside, :] = value
+    for plane in range(cells):
+        for column, value in shifted_plane(low, plane, offset[0]):
+            first[plane, column, inside, :] = value
+        near = cells + plane if plane < cells - 1 else None
+        for column, value in shifted_plane(high, plane, offset[0], near):
+            first[2 * cells + plane, column, inside, :] = value
         first[cells + plane, :, inside, :] = own[plane]
-        return carry
-
-    lax.fori_loop(0, cells, load, 0)
     buffers = (first, second)
     for step in range(steps):
         source, target = buffers[step % 2], buffers[(step + 1) % 2]
@@ -216,11 +210,25 @@
         lax.fori_loop(0, shard, body, 0)
 
 
-def deposit_kernel(count, source, chosen, *refs):
-    parts, panels, (total, field, rightward, leftward, scaled) = refs[:count], refs[count:-5], refs[-5:]
+def deposit_kernel(count, source, start, *refs):
+    parts, panels = refs[:count], refs[count:-7]
+    total, field, rightward, leftward, scaled, *chosen = refs[-7:]
     groups = total.shape[0]
     shard = groups // len(panels)
     cells, per_plane = field.shape[0], field.shape[1]
+    tile = start[...]
+
+    def choose(plane):
+        target = chosen[plane % 2]
+        rows = 64
+        for top in range(0, per_plane, rows):
+            first = (plane * per_plane + top) * STEPS
+            by_row = lax.broadcasted_iota(jnp.int32, (rows, TILE), 0) * STEPS + first
+            for left in range(0, tile.shape[1], TILE):
+                found = jnp.where(tile[:, left : left + TILE] == by_row, 1.0, 0.0)
+                target[pl.ds(top, rows), pl.ds(left, TILE)] = found.astype(jnp.bfloat16)
+
+    choose(0)
     total[...] = tree_sum([part[...] for part in parts])
     numbers = [source[g // shard] * shard + g % shard for g in range(groups)]
     last = [total[n, pl.ds(half * STEPS + STEPS - 1, 1), :] for n in numbers for half in range(2)]
@@ -235,11 +243,9 @@
             scaled[where, pl.ds(TILE, TILE)] = tail
 
     for plane in range(cells):
-        sums = jnp.dot(
-            chosen[pl.ds(plane * per_plane, per_plane), :],
-            scaled[...],
-            preferred_element_type=jnp.float32,
-        )
+        if plane < cells - 1:
+            choose(plane + 1)
+        sums = jnp.dot(chosen[plane % 2][...], scaled[...], preferred_element_type=jnp.float32)
         value = sums[:, :TILE] + sums[:, TILE:]
         field[plane] = value
         head, tail = split(value)
@@ -314,19 +320,21 @@
     f32, bf16 = jnp.float32, jnp.bfloat16
 
     source = lax.axis_index("probe") ^ jnp.arange(probes, dtype=jnp.int32)
-    low = lax.ppermute(own, "state", shift_pairs(slabs, 1))
-    high = lax.ppermute(own, "state", shift_pairs(slabs, -1))
-
-    shifted, coef, start, chosen, panel = call(
+    head = own.astype(bf16)
+    tail = (own - head.astype(f32)).astype(bf16)[: cells - 1]
+    low = lax.ppermute(head, "state", shift_pairs(slabs, 1))
+    both = jnp.concatenate([head, tail], axis=0)
+    high = lax.ppermute(both, "state", shift_pairs(slabs, -1))
+
+    shifted, coef, start, panel = call(
         prelude_kernel,
         (
             jax.ShapeDtypeStruct((cells, columns, height, TILE), f32),
             jax.ShapeDtypeStruct((5, height, TILE), f32),
             jax.ShapeDtypeStruct(tile_index.shape, jnp.int32),
-            jax.ShapeDtypeStruct((tile_total, actuators), bf16),
             jax.ShapeDtypeStruct(actuator_panel.shape[1:], bf16),
         ),
-        vmem=14,
+        vmem=8,
         smem=1,
         inputs=6,
     )(probe_offset, own, courant[None], diffusivity[None], tile_index, actuator_panel[0])
@@ -341,7 +349,7 @@
         inputs=5,
     )(probe_offset, coef, shifted, low, high)
 
-    panels = [panel] + gathered_panel(actuator_panel[0], "probe", tiles)
+    panels = [panel] + gathered_panel(actuator_panel[0], "probe", coef)
     every = list(range(probes))
 
     def project(chunks, *given):
@@ -366,11 +374,15 @@
             payload,
             heads,
         ),
-        vmem=18,
-        scratch=(pltpu.VMEM((actuators, 2 * TILE), bf16),),
+        vmem=16,
+        scratch=(
+            pltpu.VMEM((actuators, 2 * TILE), bf16),
+            pltpu.VMEM((height * columns, actuators), bf16),
+            pltpu.VMEM((height * columns, actuators), bf16),
+        ),
         smem=1,
         inputs=2 + len(parts) + probes,
-    )(source, chosen, *parts, *panels)
+    )(source, start, *parts, *panels)
     from_low = lax.ppermute(rightward, "state", shift_pairs(slabs, 1))
     from_high = lax.ppermute(leftward, "state", shift_pairs(slabs, -1))
     response = call(

time: 66.1 us -> 61.3 us (0.927)
  local copies, waits for them, and re-layouts: 11.3 us -> 0.69 us
  waiting for transfers between devices: 15 us -> 19.8 us
  other arithmetic: 0.01 us -> 2.17 us
  starting transfers between devices: 15.1 us -> 14.4 us
    unnamed x14 -> x10, local copies, waits for them, and re-layouts: 10.6 us -> 0.02 us
    ppermute x3, waiting for transfers between devices: 1.75 us -> 5.54 us  [gathered_panel(): shards[held | mask] = lax.ppermute(operand, axis, pairs)]
    convert_element_type x0 -> x2, other arithmetic: none -> 2.11 us  [the longest x1 1.07 us: local(): head = own.astype(bf16)]
    pallas_call x1, Pallas kernels: 2.58 us -> 0.6 us  [local(): call(prelude_kernel, (jax.ShapeDtypeStruct((cells, columns, height, TILE)...]
    pallas_call x1, Pallas kernels: 3.68 us -> 5.5 us  [local(): call(lambda *refs: deposit_kernel(len(parts), *refs), (jax.ShapeDtypeStru...]
    ppermute x2, starting transfers between devices: 3.45 us -> 1.66 us  [the longest x1 1.66 us: local(): high = lax.ppermute(both, 'state', shift_pairs(slabs, -1))]
    ppermute x3, starting transfers between devices: 5.37 us -> 6.44 us  [gathered_panel(): shards[held | mask] = lax.ppermute(operand, axis, pairs)]
  transfers between devices with their start and end apart: 11 -> 11, of which waited for: 7 -> 8; matrix products, arithmetic and copies ran while one was open for 1% -> 5% of each run, Pallas kernels for 18% -> 16%
where the time goes in v9:
time: 61.3 us; the launch traced here: 61 us
  Pallas kernels  22.6 us (37%)
  waiting for transfers between devices  19.8 us (32%)
  starting transfers between devices  14.4 us (23%)
  other arithmetic  2.17 us (4%)
  between operations  1.43 us (2%)
  local copies, waits for them, and re-layouts  0.69 us (1%)
    pallas_call x2, Pallas kernels, project(): call(lambda *refs: project_kernel(chunks, *refs), jax.ShapeDtypeStruct((g...  6.46 us
    ppermute x3, starting transfers between devices, gathered_panel(): shards[held | mask] = lax.ppermute(operand, axis, pairs)  6.44 us
    ppermute x4, waiting for transfers between devices, summands(): parts = [part] + [lax.ppermute(part, axis, pair) for pair in pairs]  5.55 us
    ppermute x3, waiting for transfers between devices, gathered_panel(): shards[held | mask] = lax.ppermute(operand, axis, pairs)  5.54 us
    pallas_call x1, Pallas kernels, local(): call(lambda *refs: deposit_kernel(len(parts), *refs), (jax.ShapeDtypeStru...  5.5 us
    ppermute x1, waiting for transfers between devices, local(): from_high = lax.ppermute(leftward, 'state', shift_pairs(slabs, -1))  5.47 us
    pallas_call x1, Pallas kernels, local(): call(forward_kernel, jax.ShapeDtypeStruct((cells, height, width), f32), v...  5.3 us
    pallas_call x1, Pallas kernels, local(): call(adjoint_kernel, jax.ShapeDtypeStruct((tile_total * STEPS + 2 * PAD,...  4.7 us
  transfers between devices with their start and end apart: 11, of which 8 were waited for; matrix products, arithmetic and copies ran while one was open for 5% of the time, Pallas kernels for 16%

profile of v9, /device:TPU:0, one launch (start us, length us, event | category | flops | bytes accessed | tf_op | source)
XLA Modules:
  0.0 61.0 jit_solution(10304205594486281830)
XLA Ops:
  0.6 0.0 copy-start.1
  0.6 0.0 copy-start
  0.7 0.0 copy-start.3
  0.7 0.0 copy-start.4
  0.7 0.0 copy-start.2
  0.7 4.1 %collective-permute-start.2 = (bf16[1024,128]{1,0:T(8,128)(2,1)}, bf16[1024,128]{1,0:T(8,128)(2,1)S(1)}, u32[]{:S(2)}, u32[]{:S(2)}) collective-permute-start(bf16[1024,128]{1,0:T(8,128)(2,1)} %bitcast.12), channel_id=1, source_target_pairs={{0,2},{1,3},{2,0},{3,1},{4,6},{5,7},{6,4},{7,5},{8,10},{9,11},{10,... | collective-permute-start | bytes 786440 | tf_op jit(solution)/shard_map/ppermute | solution.py:280
  4.8 1.1 %bitcast_convert_fusion = bf16[4,64,512]{2,1,0:T(8,128)(2,1)S(1)} fusion(f32[1,4,64,512]{3,2,1,0:T(8,128)} %param.6), kind=kLoop, calls=%fused_computation.4 | loop fusion | flops 131072 | bytes 786432 | tf_op jit(solution)/shard_map/convert_element_type | solution.py:323
  5.9 1.0 %fusion = bf16[3,64,512]{2,1,0:T(8,128)(2,1)S(1)} fusion(f32[4,64,512]{2,1,0:T(8,128)} %bitcast.10, bf16[4,64,512]{2,1,0:T(8,128)(2,1)S(1)} %bitcast_convert_fusion), kind=kLoop, calls=%fused_computation.2 | loop fusion | flops 294912 | bytes 786432 | tf_op jit(solution)/shard_map/convert_element_type | solution.py:324
  7.0 1.7 %collective-permute-start.1 = (bf16[7,64,512]{2,1,0:T(8,128)(2,1)S(1)}, bf16[7,64,512]{2,1,0:T(8,128)(2,1)S(1)}, u32[]{:S(2)}, u32[]{:S(2)}) collective-permute-start(bf16[7,64,512]{2,1,0:T(8,128)(2,1)S(1)} %pad_maximum_fusion), channel_id=1, source_target_pairs={{0,28},{4,0},{8,4},{12,8},{16,12},{20,16},{24,20},{28,24},{1,29},{... | collective-permute-start | bytes 1376264 | tf_op jit(solution)/shard_map/ppermute | solution.py:327
  8.6 0.0 collective-permute-start
  8.6 0.0 copy-done.1
  8.6 1.6 %collective-permute-start.4 = (bf16[1024,128]{1,0:T(8,128)(2,1)S(1)}, bf16[1024,128]{1,0:T(8,128)(2,1)S(1)}, u32[]{:S(2)}, u32[]{:S(2)}) collective-permute-start(bf16[1024,128]{1,0:T(8,128)(2,1)S(1)} %bitcast.13), channel_id=1, source_target_pairs={{0,1},{1,0},{2,3},{3,2},{4,5},{5,4},{6,7},{7,6},{8,9},{9,8},{10,11... | collective-permute-start | bytes 786440 | tf_op jit(solution)/shard_map/ppermute | solution.py:280
  10.8 0.0 copy-done
  10.9 0.0 copy-done.3
  10.9 0.0 copy-done.4
  10.9 0.0 copy-done.2
  10.9 0.6 shard_map.77
  11.5 5.5 %collective-permute-done.2.refs_5_.refs_8_ = bf16[1024,128]{1,0:T(8,128)(2,1)S(1)} collective-permute-done((bf16[1024,128]{1,0:T(8,128)(2,1)}, bf16[1024,128]{1,0:T(8,128)(2,1)S(1)}, u32[]{:S(2)}, u32[]{:S(2)}) %collective-permute-start.2) | collective-permute-done | bytes 262176 | tf_op jit(solution)/shard_map/ppermute | solution.py:280
  17.0 0.8 %collective-permute-start.3 = (bf16[1024,128]{1,0:T(8,128)(2,1)S(1)}, bf16[1024,128]{1,0:T(8,128)(2,1)S(1)}, u32[]{:S(2)}, u32[]{:S(2)}) collective-permute-start(bf16[1024,128]{1,0:T(8,128)(2,1)S(1)} %collective-permute-done.2.refs_5_.refs_8_), channel_id=1, source_target_pairs={{0,1},{1,0},{2,3},{3,2},{4,5},{5,4},{6,7},{7,6},{8,9},{9,8},{10,11... | collective-permute-start | bytes 786440 | tf_op jit(solution)/shard_map/ppermute | solution.py:280
  17.8 0.4 collective-permute-done.low
  18.2 0.0 collective-permute-done.1.high
  18.2 4.7 %shard_map.78.refs_2_ = f32[4112,128]{1,0:T(8,128)S(1)} custom-call(s32[1]{0:T(128)S(6)} %copy.9.offset, f32[5,64,128]{2,1,0:T(8,128)S(1)} %get-tuple-element.12.coef, f32[4,4,64,128]{3,2,1,0:T(8,128)S(1)} %get-tuple-element.13.own, bf16[4,64,512]{2,1,0:T(8,128)(2,1)S(1)} %collective-permute-done.low, bf16[7,64,512]{2,1,0:T(8,128)(2,1)S(1)} %collective-permute-done.1.high), custom_call_target="tpu_custom_call" | custom-call | flops 1024 | bytes 1024 | tf_op jit(solution)/shard_map/pallas_call | solution.py:343
  22.9 0.0 collective-permute-done.4.refs_4_.refs_7_
  22.9 4.4 %shard_map.79.refs_4_ = f32[16,8,128]{2,1,0:T(8,128)S(1)} custom-call(s32[4]{0:T(128)S(1)} %iota_xor_fusion.refs_0_, s32[1,4096]{1,0:T(1,128)S(1)} %get-tuple-element.11.refs_1_, f32[4112,128]{1,0:T(8,128)S(1)} %shard_map.78.refs_2_, bf16[1024,128]{1,0:T(8,128)(2,1)S(1)} %get-tuple-element.15.refs_3_.refs_6_, ...), custom_call_target="tpu_custom_call" | custom-call | flops 1024 | bytes 1024 | tf_op jit(solution)/shard_map/pallas_call | solution.py:356
  27.3 0.0 collective-permute-done.3.refs_3_.refs_9_
  27.3 2.0 %shard_map.80 = f32[16,8,128]{2,1,0:T(8,128)S(1)} custom-call(s32[4]{0:T(128)S(1)} %iota_xor_fusion.refs_0_, s32[1,4096]{1,0:T(1,128)S(1)} %get-tuple-element.11.refs_1_, f32[4112,128]{1,0:T(8,128)S(1)} %shard_map.78.refs_2_, bf16[1024,128]{1,0:T(8,128)(2,1)S(1)} %collective-permute-done.3.refs_3_.refs_9_, f32[16,8,128]{2,1,0:T(8,128)S(1)} %shard_map.79.refs_4_), custom_call_target="tpu_custom_call" | custom-call | flops 1024 | bytes 1024 | tf_op jit(solution)/shard_map/pallas_call | solution.py:356
  29.4 0.1 collective-permute-start.5
  29.5 1.2 %collective-permute-done.5 = f32[16,8,128]{2,1,0:T(8,128)S(1)} collective-permute-done((f32[16,8,128]{2,1,0:T(8,128)S(1)}, f32[16,8,128]{2,1,0:T(8,128)S(1)}, u32[]{:S(2)}, u32[]{:S(2)}) %collective-permute-start.5) | collective-permute-done | bytes 65568 | tf_op jit(solution)/shard_map/ppermute | solution.py:305
  30.7 1.2 %collective-permute-start.6 = (f32[16,8,128]{2,1,0:T(8,128)S(1)}, f32[16,8,128]{2,1,0:T(8,128)S(1)}, u32[]{:S(2)}, u32[]{:S(2)}) collective-permute-start(f32[16,8,128]{2,1,0:T(8,128)S(1)} %add.3.refs_2_), channel_id=1, source_target_pairs={{0,8},{4,12},{8,0},{12,4},{16,24},{20,28},{24,16},{28,20},{1,9},{5... | collective-permute-start | bytes 196616 | tf_op jit(solution)/shard_map/ppermute | solution.py:305
  31.9 1.5 %collective-permute-start.7 = (f32[16,8,128]{2,1,0:T(8,128)S(1)}, f32[16,8,128]{2,1,0:T(8,128)S(1)}, u32[]{:S(2)}, u32[]{:S(2)}) collective-permute-start(f32[16,8,128]{2,1,0:T(8,128)S(1)} %add.3.refs_2_), channel_id=1, source_target_pairs={{0,16},{4,20},{8,24},{12,28},{16,0},{20,4},{24,8},{28,12},{1,17},{... | collective-permute-start | bytes 196616 | tf_op jit(solution)/shard_map/ppermute | solution.py:305
  33.4 0.9 %collective-permute-start.8 = (f32[16,8,128]{2,1,0:T(8,128)S(1)}, f32[16,8,128]{2,1,0:T(8,128)S(1)}, u32[]{:S(2)}, u32[]{:S(2)}) collective-permute-start(f32[16,8,128]{2,1,0:T(8,128)S(1)} %add.3.refs_2_), channel_id=1, source_target_pairs={{0,24},{4,28},{8,16},{12,20},{16,8},{20,12},{24,0},{28,4},{1,25},{... | collective-permute-start | bytes 196616 | tf_op jit(solution)/shard_map/ppermute | solution.py:305
  34.3 0.8 %collective-permute-done.6.refs_3_ = f32[16,8,128]{2,1,0:T(8,128)S(1)} collective-permute-done((f32[16,8,128]{2,1,0:T(8,128)S(1)}, f32[16,8,128]{2,1,0:T(8,128)S(1)}, u32[]{:S(2)}, u32[]{:S(2)}) %collective-permute-start.6) | collective-permute-done | bytes 65568 | tf_op jit(solution)/shard_map/ppermute | solution.py:305
  35.0 1.1 %collective-permute-done.7.refs_4_ = f32[16,8,128]{2,1,0:T(8,128)S(1)} collective-permute-done((f32[16,8,128]{2,1,0:T(8,128)S(1)}, f32[16,8,128]{2,1,0:T(8,128)S(1)}, u32[]{:S(2)}, u32[]{:S(2)}) %collective-permute-start.7) | collective-permute-done | bytes 65568 | tf_op jit(solution)/shard_map/ppermute | solution.py:305
  36.2 2.4 %collective-permute-done.8.refs_5_ = f32[16,8,128]{2,1,0:T(8,128)S(1)} collective-permute-done((f32[16,8,128]{2,1,0:T(8,128)S(1)}, f32[16,8,128]{2,1,0:T(8,128)S(1)}, u32[]{:S(2)}, u32[]{:S(2)}) %collective-permute-start.8) | collective-permute-done | bytes 65568 | tf_op jit(solution)/shard_map/ppermute | solution.py:305
  38.6 5.5 %shard_map.81 = (f32[16,8,128]{2,1,0:T(8,128)S(1)}, f32[4,256,128]{2,1,0:T(8,128)S(1)}, bf16[7,256,128]{2,1,0:T(8,128)(2,1)S(1)}, bf16[4,256,128]{2,1,0:T(8,128)(2,1)S(1)}) custom-call(s32[4]{0:T(128)S(1)} %iota_xor_fusion.refs_0_, s32[1,4096]{1,0:T(1,128)S(1)} %get-tuple-element.11.refs_1_, f32[16,8,128]{2,1,0:T(8,128)S(1)} %add.3.refs_2_, ...), custom_call_target="tpu_custom_call" | custom-call | flops 1024 | bytes 1024 | tf_op jit(solution)/shard_map/pallas_call | solution.py:369
  44.1 0.1 collective-permute-start.9
  44.1 2.6 %collective-permute-start.10 = (bf16[4,256,128]{2,1,0:T(8,128)(2,1)S(1)}, bf16[4,256,128]{2,1,0:T(8,128)(2,1)S(1)}, u32[]{:S(2)}, u32[]{:S(2)}) collective-permute-start(bf16[4,256,128]{2,1,0:T(8,128)(2,1)S(1)} %get-tuple-element.19), channel_id=1, source_target_pairs={{0,28},{4,0},{8,4},{12,8},{16,12},{20,16},{24,20},{28,24},{1,29},{... | collective-permute-start | bytes 786440 | tf_op jit(solution)/shard_map/ppermute | solution.py:387
  46.8 0.7 %copy.8 = f32[4,16,2,128]{3,2,1,0:T(2,128)} copy(f32[4,16,2,128]{3,0,2,1:T(4,128)S(1)} %bitcast.15) | data formatting | bytes 131072 | tf_op jit(solution)/shard_map/transpose | solution.py:395
  47.4 5.5 %collective-permute-done.10.high = bf16[4,256,128]{2,1,0:T(8,128)(2,1)S(1)} collective-permute-done((bf16[4,256,128]{2,1,0:T(8,128)(2,1)S(1)}, bf16[4,256,128]{2,1,0:T(8,128)(2,1)S(1)}, u32[]{:S(2)}, u32[]{:S(2)}) %collective-permute-start.10) | collective-permute-done | bytes 262176 | tf_op jit(solution)/shard_map/ppermute | solution.py:387
  52.9 2.8 %collective-permute-done.9.low = bf16[7,256,128]{2,1,0:T(8,128)(2,1)S(1)} collective-permute-done((bf16[7,256,128]{2,1,0:T(8,128)(2,1)S(1)}, bf16[7,256,128]{2,1,0:T(8,128)(2,1)S(1)}, u32[]{:S(2)}, u32[]{:S(2)}) %collective-permute-start.9) | collective-permute-done | bytes 458784 | tf_op jit(solution)/shard_map/ppermute | solution.py:386
  55.7 5.3 %shard_map.82 = f32[4,64,512]{2,1,0:T(8,128)} custom-call(f32[5,64,128]{2,1,0:T(8,128)S(1)} %get-tuple-element.12.coef, f32[4,256,128]{2,1,0:T(8,128)S(1)} %get-tuple-element.17.own, bf16[7,256,128]{2,1,0:T(8,128)(2,1)S(1)} %collective-permute-done.9.low, bf16[4,256,128]{2,1,0:T(8,128)(2,1)S(1)} %collective-permute-done.10.high), custom_call_target="tpu_custom_call" | custom-call | flops 1024 | bytes 1024 | tf_op jit(solution)/shard_map/pallas_call | solution.py:388
  (3 shorter events, 0.1 us)
Async XLA Ops:
  0.6 8.0 %copy-start.1 = (bf16[1,1024,128]{2,1,0:T(8,128)(2,1)S(1)}, bf16[1,1024,128]{2,1,0:T(8,128)(2,1)}, u32[]{:S(2)}) copy-start(bf16[1,1024,128]{2,1,0:T(8,128)(2,1)} %param.11) | copy-start | bytes 786436
  0.6 10.2 %copy-start = (f32[1,4,64,512]{3,2,1,0:T(8,128)S(1)}, f32[1,4,64,512]{3,2,1,0:T(8,128)}, u32[]{:S(2)}) copy-start(f32[1,4,64,512]{3,2,1,0:T(8,128)} %param.6) | copy-start | bytes 1572868
  0.7 10.2 %copy-start.3 = (f32[64]{0:T(128)S(1)}, f32[64]{0:T(128)}, u32[]{:S(2)}) copy-start(f32[64]{0:T(128)} %param.7) | copy-start | bytes 772
  0.7 10.2 %copy-start.4 = (f32[64]{0:T(128)S(1)}, f32[64]{0:T(128)}, u32[]{:S(2)}) copy-start(f32[64]{0:T(128)} %param.8) | copy-start | bytes 772
  0.7 10.2 %copy-start.2 = (s32[1,4096]{1,0:T(1,128)S(1)}, s32[1,4096]{1,0:T(1,128)}, u32[]{:S(2)}) copy-start(s32[1,4096]{1,0:T(1,128)} %tile.1) | copy-start | bytes 49156
  0.7 16.3 %collective-permute-start.2 = (bf16[1024,128]{1,0:T(8,128)(2,1)}, bf16[1024,128]{1,0:T(8,128)(2,1)S(1)}, u32[]{:S(2)}, u32[]{:S(2)}) collective-permute-start(bf16[1024,128]{1,0:T(8,128)(2,1)} %bitcast.12), channel_id=1, source_target_pairs={{0,2},{1,3},{2,0},{3,1},{4,6},{5,7},{6,4},{7,5},{8,10},{9,11},{10,... | collective-permute-start | bytes 786440 | tf_op jit(solution)/shard_map/ppermute | solution.py:280
  7.0 11.2 %collective-permute-start.1 = (bf16[7,64,512]{2,1,0:T(8,128)(2,1)S(1)}, bf16[7,64,512]{2,1,0:T(8,128)(2,1)S(1)}, u32[]{:S(2)}, u32[]{:S(2)}) collective-permute-start(bf16[7,64,512]{2,1,0:T(8,128)(2,1)S(1)} %pad_maximum_fusion), channel_id=1, source_target_pairs={{0,28},{4,0},{8,4},{12,8},{16,12},{20,16},{24,20},{28,24},{1,29},{... | collective-permute-start | bytes 1376264 | tf_op jit(solution)/shard_map/ppermute | solution.py:327
  8.6 9.6 %collective-permute-start = (bf16[4,64,512]{2,1,0:T(8,128)(2,1)S(1)}, bf16[4,64,512]{2,1,0:T(8,128)(2,1)S(1)}, u32[]{:S(2)}, u32[]{:S(2)}) collective-permute-start(bf16[4,64,512]{2,1,0:T(8,128)(2,1)S(1)} %bitcast_convert_fusion), channel_id=1, source_target_pairs={{0,4},{4,8},{8,12},{12,16},{16,20},{20,24},{24,28},{28,0},{1,5},{5... | collective-permute-start | bytes 786440 | tf_op jit(solution)/shard_map/ppermute | solution.py:325
  8.6 14.3 %collective-permute-start.4 = (bf16[1024,128]{1,0:T(8,128)(2,1)S(1)}, bf16[1024,128]{1,0:T(8,128)(2,1)S(1)}, u32[]{:S(2)}, u32[]{:S(2)}) collective-permute-start(bf16[1024,128]{1,0:T(8,128)(2,1)S(1)} %bitcast.13), channel_id=1, source_target_pairs={{0,1},{1,0},{2,3},{3,2},{4,5},{5,4},{6,7},{7,6},{8,9},{9,8},{10,11... | collective-permute-start | bytes 786440 | tf_op jit(solution)/shard_map/ppermute | solution.py:280
  17.0 10.3 %collective-permute-start.3 = (bf16[1024,128]{1,0:T(8,128)(2,1)S(1)}, bf16[1024,128]{1,0:T(8,128)(2,1)S(1)}, u32[]{:S(2)}, u32[]{:S(2)}) collective-permute-start(bf16[1024,128]{1,0:T(8,128)(2,1)S(1)} %collective-permute-done.2.refs_5_.refs_8_), channel_id=1, source_target_pairs={{0,1},{1,0},{2,3},{3,2},{4,5},{5,4},{6,7},{7,6},{8,9},{9,8},{10,11... | collective-permute-start | bytes 786440 | tf_op jit(solution)/shard_map/ppermute | solution.py:280
  29.4 1.3 %collective-permute-start.5 = (f32[16,8,128]{2,1,0:T(8,128)S(1)}, f32[16,8,128]{2,1,0:T(8,128)S(1)}, u32[]{:S(2)}, u32[]{:S(2)}) collective-permute-start(f32[16,8,128]{2,1,0:T(8,128)S(1)} %shard_map.80), channel_id=1, source_target_pairs={{0,4},{4,0},{8,12},{12,8},{16,20},{20,16},{24,28},{28,24},{1,5},{5... | collective-permute-start | bytes 196616 | tf_op jit(solution)/shard_map/ppermute | solution.py:305
  30.7 4.3 %collective-permute-start.6 = (f32[16,8,128]{2,1,0:T(8,128)S(1)}, f32[16,8,128]{2,1,0:T(8,128)S(1)}, u32[]{:S(2)}, u32[]{:S(2)}) collective-permute-start(f32[16,8,128]{2,1,0:T(8,128)S(1)} %add.3.refs_2_), channel_id=1, source_target_pairs={{0,8},{4,12},{8,0},{12,4},{16,24},{20,28},{24,16},{28,20},{1,9},{5... | collective-permute-start | bytes 196616 | tf_op jit(solution)/shard_map/ppermute | solution.py:305
  31.9 4.3 %collective-permute-start.7 = (f32[16,8,128]{2,1,0:T(8,128)S(1)}, f32[16,8,128]{2,1,0:T(8,128)S(1)}, u32[]{:S(2)}, u32[]{:S(2)}) collective-permute-start(f32[16,8,128]{2,1,0:T(8,128)S(1)} %add.3.refs_2_), channel_id=1, source_target_pairs={{0,16},{4,20},{8,24},{12,28},{16,0},{20,4},{24,8},{28,12},{1,17},{... | collective-permute-start | bytes 196616 | tf_op jit(solution)/shard_map/ppermute | solution.py:305
  33.4 5.2 %collective-permute-start.8 = (f32[16,8,128]{2,1,0:T(8,128)S(1)}, f32[16,8,128]{2,1,0:T(8,128)S(1)}, u32[]{:S(2)}, u32[]{:S(2)}) collective-permute-start(f32[16,8,128]{2,1,0:T(8,128)S(1)} %add.3.refs_2_), channel_id=1, source_target_pairs={{0,24},{4,28},{8,16},{12,20},{16,8},{20,12},{24,0},{28,4},{1,25},{... | collective-permute-start | bytes 196616 | tf_op jit(solution)/shard_map/ppermute | solution.py:305
  44.1 11.7 %collective-permute-start.9 = (bf16[7,256,128]{2,1,0:T(8,128)(2,1)S(1)}, bf16[7,256,128]{2,1,0:T(8,128)(2,1)S(1)}, u32[]{:S(2)}, u32[]{:S(2)}) collective-permute-start(bf16[7,256,128]{2,1,0:T(8,128)(2,1)S(1)} %get-tuple-element.18), channel_id=1, source_target_pairs={{0,4},{4,8},{8,12},{12,16},{16,20},{20,24},{24,28},{28,0},{1,5},{5... | collective-permute-start | bytes 1376264 | tf_op jit(solution)/shard_map/ppermute | solution.py:386
  44.1 8.8 %collective-permute-start.10 = (bf16[4,256,128]{2,1,0:T(8,128)(2,1)S(1)}, bf16[4,256,128]{2,1,0:T(8,128)(2,1)S(1)}, u32[]{:S(2)}, u32[]{:S(2)}) collective-permute-start(bf16[4,256,128]{2,1,0:T(8,128)(2,1)S(1)} %get-tuple-element.19), channel_id=1, source_target_pairs={{0,28},{4,0},{8,4},{12,8},{16,12},{20,16},{24,20},{28,24},{1,29},{... | collective-permute-start | bytes 786440 | tf_op jit(solution)/shard_map/ppermute | solution.py:387

commit v10 on v9

--- a/solution.py
+++ b/solution.py
@@ -65,17 +65,12 @@
     return high, low
 
 
-def shifted_plane(field, plane, offset, tail=None):
+def shifted_plane(field, plane, offset):
     height, width = field.shape[1:]
     columns = width // TILE
     turn, rest = offset // TILE, offset % TILE
     lane = lax.broadcasted_iota(jnp.int32, (height, TILE), 1)
     parts = [field[plane, :, pl.ds(c * TILE, TILE)].astype(jnp.float32) for c in range(columns)]
-    if tail is not None:
-        parts = [
-            part + field[tail, :, pl.ds(c * TILE, TILE)].astype(jnp.float32)
-            for c, part in enumerate(parts)
-        ]
     rolled = [pltpu.roll(part, rest, 1) for part in parts]
     return [
         (lax.rem(c + turn, columns), jnp.where(lane >= rest, rolled[c], rolled[c - 1]))
@@ -119,13 +114,14 @@
     clear_pads(first)
     clear_pads(second)
 
-    for plane in range(cells):
-        for column, value in shifted_plane(low, plane, offset[0]):
-            first[plane, column, inside, :] = value
-        near = cells + plane if plane < cells - 1 else None
-        for column, value in shifted_plane(high, plane, offset[0], near):
-            first[2 * cells + plane, column, inside, :] = value
+    def load(plane, carry):
+        for slab, field in ((0, low), (2, high)):
+            for column, value in shifted_plane(field, plane, offset[0]):
+                first[slab * cells + plane, column, inside, :] = value
         first[cells + plane, :, inside, :] = own[plane]
+        return carry
+
+    lax.fori_loop(0, cells, load, 0)
     buffers = (first, second)
     for step in range(steps):
         source, target = buffers[step % 2], buffers[(step + 1) % 2]
@@ -143,7 +139,7 @@
                         tiles[pl.ds(PAD + number * steps + step, 8, stride=steps), :] = block[c]
             return carry
 
-        lax.fori_loop(0, height // 8, sweep, 0)
+        lax.fori_loop(0, height // 8, sweep, 0, unroll=4)
 
 
 def forward_kernel(coef, own, low, high, out, first, second):
@@ -178,7 +174,7 @@
                         target[plane, c, pl.ds(pl.multiple_of(PAD + row, 8), 8), :] = block[c]
             return carry
 
-        lax.fori_loop(0, height // 8, sweep, 0)
+        lax.fori_loop(0, height // 8, sweep, 0, unroll=4)
 
 
 def project_kernel(chunks, source, start, tiles, *refs):
@@ -216,7 +212,8 @@
     groups = total.shape[0]
     shard = groups // len(panels)
     cells, per_plane = field.shape[0], field.shape[1]
-    tile = start[...]
+    tile = start[...].astype(jnp.int16)
+    one, none = jnp.ones((), jnp.bfloat16), jnp.zeros((), jnp.bfloat16)
 
     def choose(plane):
         target = chosen[plane % 2]
@@ -224,9 +221,10 @@
         for top in range(0, per_plane, rows):
             first = (plane * per_plane + top) * STEPS
             by_row = lax.broadcasted_iota(jnp.int32, (rows, TILE), 0) * STEPS + first
+            by_row = by_row.astype(jnp.int16)
             for left in range(0, tile.shape[1], TILE):
-                found = jnp.where(tile[:, left : left + TILE] == by_row, 1.0, 0.0)
-                target[pl.ds(top, rows), pl.ds(left, TILE)] = found.astype(jnp.bfloat16)
+                found = jnp.where(tile[:, left : left + TILE] == by_row, one, none)
+                target[pl.ds(top, rows), pl.ds(left, TILE)] = found
 
     choose(0)
     total[...] = tree_sum([part[...] for part in parts])
@@ -297,7 +295,7 @@
     if count & (count - 1):
         return [lax.psum(part, axis)]
     done, parts = 1, [part]
-    for span in (2, 4, 4, 4, 4):
+    for span in [2] * count.bit_length():
         span = min(span, count // done)
         if span > 1:
             part = tree_sum(parts)
@@ -320,11 +318,8 @@
     f32, bf16 = jnp.float32, jnp.bfloat16
 
     source = lax.axis_index("probe") ^ jnp.arange(probes, dtype=jnp.int32)
-    head = own.astype(bf16)
-    tail = (own - head.astype(f32)).astype(bf16)[: cells - 1]
-    low = lax.ppermute(head, "state", shift_pairs(slabs, 1))
-    both = jnp.concatenate([head, tail], axis=0)
-    high = lax.ppermute(both, "state", shift_pairs(slabs, -1))
+    high = lax.ppermute(own, "state", shift_pairs(slabs, -1))
+    low = lax.ppermute(own.astype(bf16), "state", shift_pairs(slabs, 1))
 
     shifted, coef, start, panel = call(
         prelude_kernel,
@@ -349,7 +344,7 @@
         inputs=5,
     )(probe_offset, coef, shifted, low, high)
 
-    panels = [panel] + gathered_panel(actuator_panel[0], "probe", coef)
+    panels = [panel] + gathered_panel(actuator_panel[0], "probe", tiles)
     every = list(range(probes))
 
     def project(chunks, *given):

time: 61.3 us -> 59.5 us (0.971)
  Pallas kernels: 22.6 us -> 18.4 us
  local copies, waits for them, and re-layouts: 0.69 us -> 4.68 us
  waiting for transfers between devices: 19.8 us -> 18.2 us
  other arithmetic: 2.17 us -> 1.13 us
  starting transfers between devices: 14.4 us -> 15.4 us
    unnamed x10, local copies, waits for them, and re-layouts: 0.02 us -> 4.01 us
    pallas_call x1, Pallas kernels: 5.3 us -> 3.51 us  [local(): call(forward_kernel, jax.ShapeDtypeStruct((cells, height, width), f32), v...]
    ppermute x2, starting transfers between devices: 1.66 us -> 3.44 us  [the longest x1 3.39 us: local(): high = lax.ppermute(own, 'state', shift_pairs(slabs, -1))]
    ppermute x3, starting transfers between devices: 6.44 us -> 4.9 us  [gathered_panel(): shards[held | mask] = lax.ppermute(operand, axis, pairs)]
    pallas_call x1, Pallas kernels: 4.7 us -> 3.17 us  [local(): call(adjoint_kernel, jax.ShapeDtypeStruct((tile_total * STEPS + 2 * PAD,...]
    ppermute x3, waiting for transfers between devices: 5.54 us -> 4.07 us  [gathered_panel(): shards[held | mask] = lax.ppermute(operand, axis, pairs)]
    convert_element_type x2 -> x1, other arithmetic: 2.11 us -> 1.11 us  [local(): low = lax.ppermute(own.astype(bf16), 'state', shift_pairs(slabs, 1))]
    pallas_call x1, Pallas kernels: 5.5 us -> 4.64 us  [local(): call(lambda *refs: deposit_kernel(len(parts), *refs), (jax.ShapeDtypeStru...]
  transfers between devices with their start and end apart: 11 -> 10, of which waited for: 8 -> 7; matrix products, arithmetic and copies ran while one was open for 5% -> 3% of each run, Pallas kernels for 16% -> 14%
where the time goes in v10:
time: 59.5 us; the launch traced here: 59.1 us
  Pallas kernels  18.4 us (31%)
  waiting for transfers between devices  18.2 us (31%)
  starting transfers between devices  15.4 us (26%)
  local copies, waits for them, and re-layouts  4.68 us (8%)
  between operations  1.36 us (2%)
  other arithmetic  1.13 us (2%)
    pallas_call x2, Pallas kernels, project(): call(lambda *refs: project_kernel(chunks, *refs), jax.ShapeDtypeStruct((g...  6.45 us
    ppermute x1, waiting for transfers between devices, local(): from_high = lax.ppermute(leftward, 'state', shift_pairs(slabs, -1))  6.08 us
    ppermute x3, waiting for transfers between devices, summands(): parts = [part] + [lax.ppermute(part, axis, pair) for pair in pairs]  5.95 us
    ppermute x3, starting transfers between devices, gathered_panel(): shards[held | mask] = lax.ppermute(operand, axis, pairs)  4.9 us
    pallas_call x1, Pallas kernels, local(): call(lambda *refs: deposit_kernel(len(parts), *refs), (jax.ShapeDtypeStru...  4.64 us
    ppermute x3, starting transfers between devices, summands(): parts = [part] + [lax.ppermute(part, axis, pair) for pair in pairs]  4.38 us
    ppermute x3, waiting for transfers between devices, gathered_panel(): shards[held | mask] = lax.ppermute(operand, axis, pairs)  4.07 us
    unnamed x10, local copies, waits for them, and re-layouts  4.01 us
  transfers between devices with their start and end apart: 10, of which 7 were waited for; matrix products, arithmetic and copies ran while one was open for 3% of the time, Pallas kernels for 14%

profile of v10, /device:TPU:0, one launch (start us, length us, event | category | flops | bytes accessed | tf_op | source)
XLA Modules:
  0.0 59.1 jit_solution(15377750744122871785)
XLA Ops:
  0.6 3.4 %collective-permute-start.1 = (f32[4,64,512]{2,1,0:T(8,128)}, f32[4,64,512]{2,1,0:T(8,128)S(1)}, u32[]{:S(2)}, u32[]{:S(2)}) collective-permute-start(f32[4,64,512]{2,1,0:T(8,128)} %bitcast.10), channel_id=1, source_target_pairs={{0,28},{4,0},{8,4},{12,8},{16,12},{20,16},{24,20},{28,24},{1,29},{... | collective-permute-start | bytes 1572872 | tf_op jit(solution)/shard_map/ppermute | solution.py:321
  4.0 1.1 %bitcast_convert_fusion = bf16[4,64,512]{2,1,0:T(8,128)(2,1)S(1)} fusion(f32[1,4,64,512]{3,2,1,0:T(8,128)} %param.6), kind=kLoop, calls=%fused_computation.1 | loop fusion | flops 131072 | bytes 786432 | tf_op jit(solution)/shard_map/convert_element_type | solution.py:322
  5.1 0.1 collective-permute-start
  5.2 2.7 %collective-permute-start.2 = (bf16[1024,128]{1,0:T(8,128)(2,1)}, bf16[1024,128]{1,0:T(8,128)(2,1)S(1)}, u32[]{:S(2)}, u32[]{:S(2)}) collective-permute-start(bf16[1024,128]{1,0:T(8,128)(2,1)} %bitcast.12), channel_id=1, source_target_pairs={{0,2},{1,3},{2,0},{3,1},{4,6},{5,7},{6,4},{7,5},{8,10},{9,11},{10,... | collective-permute-start | bytes 786440 | tf_op jit(solution)/shard_map/ppermute | solution.py:278
  7.8 1.6 %collective-permute-start.4 = (bf16[1024,128]{1,0:T(8,128)(2,1)}, bf16[1024,128]{1,0:T(8,128)(2,1)S(1)}, u32[]{:S(2)}, u32[]{:S(2)}) collective-permute-start(bf16[1024,128]{1,0:T(8,128)(2,1)} %bitcast.13), channel_id=1, source_target_pairs={{0,1},{1,0},{2,3},{3,2},{4,5},{5,4},{6,7},{7,6},{8,9},{9,8},{10,11... | collective-permute-start | bytes 786440 | tf_op jit(solution)/shard_map/ppermute | solution.py:278
  10.1 0.0 copy-start
  10.1 1.0 %copy-done = f32[1,4,64,512]{3,2,1,0:T(8,128)S(1)} copy-done((f32[1,4,64,512]{3,2,1,0:T(8,128)S(1)}, f32[1,4,64,512]{3,2,1,0:T(8,128)}, u32[]{:S(2)}) %copy-start) | copy-done | bytes 524312
  11.1 0.0 copy-start.1
  11.1 0.9 %copy-done.1 = bf16[1,1024,128]{2,1,0:T(8,128)(2,1)S(1)} copy-done((bf16[1,1024,128]{2,1,0:T(8,128)(2,1)S(1)}, bf16[1,1024,128]{2,1,0:T(8,128)(2,1)}, u32[]{:S(2)}) %copy-start.1) | copy-done | bytes 262168
  12.1 0.0 copy-start.2
  12.1 0.7 %copy-done.2 = s32[1,4096]{1,0:T(1,128)S(1)} copy-done((s32[1,4096]{1,0:T(1,128)S(1)}, s32[1,4096]{1,0:T(1,128)}, u32[]{:S(2)}) %copy-start.2) | copy-done | bytes 16408
  12.8 0.0 copy-start.3
  12.8 0.7 %copy-done.3 = f32[64]{0:T(128)S(1)} copy-done((f32[64]{0:T(128)S(1)}, f32[64]{0:T(128)}, u32[]{:S(2)}) %copy-start.3) | copy-done | bytes 280
  13.4 0.0 copy-start.4
  13.4 0.7 %copy-done.4 = f32[64]{0:T(128)S(1)} copy-done((f32[64]{0:T(128)S(1)}, f32[64]{0:T(128)}, u32[]{:S(2)}) %copy-start.4) | copy-done | bytes 280
  14.1 0.6 %shard_map.77 = (f32[4,4,64,128]{3,2,1,0:T(8,128)S(1)}, f32[5,64,128]{2,1,0:T(8,128)S(1)}, s32[1,4096]{1,0:T(1,128)S(1)}, bf16[1024,128]{1,0:T(8,128)(2,1)S(1)}) custom-call(s32[1]{0:T(128)S(6)} %copy.9.offset, f32[4,64,512]{2,1,0:T(8,128)S(1)} %bitcast.11, f32[1,64]{1,0:T(1,128)S(1)} %bitcast.16, f32[1,64]{1,0:T(1,128)S(1)} %bitcast.17, ...), custom_call_target="tpu_custom_call" | custom-call | flops 1024 | bytes 1024 | tf_op jit(solution)/shard_map/pallas_call | solution.py:324
  14.7 0.0 collective-permute-done.low
  14.7 0.0 collective-permute-done.1.high
  14.8 3.2 %shard_map.78.refs_2_ = f32[4112,128]{1,0:T(8,128)S(1)} custom-call(s32[1]{0:T(128)S(6)} %copy.9.offset, f32[5,64,128]{2,1,0:T(8,128)S(1)} %get-tuple-element.12.coef, f32[4,4,64,128]{3,2,1,0:T(8,128)S(1)} %get-tuple-element.13.own, bf16[4,64,512]{2,1,0:T(8,128)(2,1)S(1)} %collective-permute-done.low, f32[4,64,512]{2,1,0:T(8,128)S(1)} %collective-permute-done.1.high), custom_call_target="tpu_custom_call" | custom-call | flops 1024 | bytes 1024 | tf_op jit(solution)/shard_map/pallas_call | solution.py:338
  17.9 2.0 %collective-permute-done.2.refs_5_.refs_6_ = bf16[1024,128]{1,0:T(8,128)(2,1)S(1)} collective-permute-done((bf16[1024,128]{1,0:T(8,128)(2,1)}, bf16[1024,128]{1,0:T(8,128)(2,1)S(1)}, u32[]{:S(2)}, u32[]{:S(2)}) %collective-permute-start.2) | collective-permute-done | bytes 262176 | tf_op jit(solution)/shard_map/ppermute | solution.py:278
  19.9 0.7 %collective-permute-start.3 = (bf16[1024,128]{1,0:T(8,128)(2,1)S(1)}, bf16[1024,128]{1,0:T(8,128)(2,1)S(1)}, u32[]{:S(2)}, u32[]{:S(2)}) collective-permute-start(bf16[1024,128]{1,0:T(8,128)(2,1)S(1)} %collective-permute-done.2.refs_5_.refs_6_), channel_id=1, source_target_pairs={{0,1},{1,0},{2,3},{3,2},{4,5},{5,4},{6,7},{7,6},{8,9},{9,8},{10,11... | collective-permute-start | bytes 786440 | tf_op jit(solution)/shard_map/ppermute | solution.py:278
  20.6 0.0 collective-permute-done.4.refs_4_.refs_5_
  20.6 4.4 %shard_map.79.refs_4_ = f32[16,8,128]{2,1,0:T(8,128)S(1)} custom-call(s32[4]{0:T(128)S(1)} %iota_xor_fusion.refs_0_, s32[1,4096]{1,0:T(1,128)S(1)} %get-tuple-element.11.refs_1_, f32[4112,128]{1,0:T(8,128)S(1)} %shard_map.78.refs_2_, bf16[1024,128]{1,0:T(8,128)(2,1)S(1)} %get-tuple-element.15.refs_3_.refs_4_, ...), custom_call_target="tpu_custom_call" | custom-call | flops 1024 | bytes 1024 | tf_op jit(solution)/shard_map/pallas_call | solution.py:351
  25.1 2.0 %collective-permute-done.3.refs_3_.refs_7_ = bf16[1024,128]{1,0:T(8,128)(2,1)S(1)} collective-permute-done((bf16[1024,128]{1,0:T(8,128)(2,1)S(1)}, bf16[1024,128]{1,0:T(8,128)(2,1)S(1)}, u32[]{:S(2)}, u32[]{:S(2)}) %collective-permute-start.3) | collective-permute-done | bytes 262176 | tf_op jit(solution)/shard_map/ppermute | solution.py:278
  27.1 2.0 %shard_map.80 = f32[16,8,128]{2,1,0:T(8,128)S(1)} custom-call(s32[4]{0:T(128)S(1)} %iota_xor_fusion.refs_0_, s32[1,4096]{1,0:T(1,128)S(1)} %get-tuple-element.11.refs_1_, f32[4112,128]{1,0:T(8,128)S(1)} %shard_map.78.refs_2_, bf16[1024,128]{1,0:T(8,128)(2,1)S(1)} %collective-permute-done.3.refs_3_.refs_7_, f32[16,8,128]{2,1,0:T(8,128)S(1)} %shard_map.79.refs_4_), custom_call_target="tpu_custom_call" | custom-call | flops 1024 | bytes 1024 | tf_op jit(solution)/shard_map/pallas_call | solution.py:351
  29.1 0.1 collective-permute-start.5
  29.2 1.2 %collective-permute-done.5 = f32[16,8,128]{2,1,0:T(8,128)S(1)} collective-permute-done((f32[16,8,128]{2,1,0:T(8,128)S(1)}, f32[16,8,128]{2,1,0:T(8,128)S(1)}, u32[]{:S(2)}, u32[]{:S(2)}) %collective-permute-start.5) | collective-permute-done | bytes 65568 | tf_op jit(solution)/shard_map/ppermute | solution.py:303
  30.5 2.3 %collective-permute-start.6 = (f32[16,8,128]{2,1,0:T(8,128)S(1)}, f32[16,8,128]{2,1,0:T(8,128)S(1)}, u32[]{:S(2)}, u32[]{:S(2)}) collective-permute-start(f32[16,8,128]{2,1,0:T(8,128)S(1)} %add.6), channel_id=1, source_target_pairs={{0,8},{4,12},{8,0},{12,4},{16,24},{20,28},{24,16},{28,20},{1,9},{5... | collective-permute-start | bytes 196616 | tf_op jit(solution)/shard_map/ppermute | solution.py:303
  32.7 2.4 %collective-permute-done.6 = f32[16,8,128]{2,1,0:T(8,128)S(1)} collective-permute-done((f32[16,8,128]{2,1,0:T(8,128)S(1)}, f32[16,8,128]{2,1,0:T(8,128)S(1)}, u32[]{:S(2)}, u32[]{:S(2)}) %collective-permute-start.6) | collective-permute-done | bytes 65568 | tf_op jit(solution)/shard_map/ppermute | solution.py:303
  35.2 2.0 %collective-permute-start.7 = (f32[16,8,128]{2,1,0:T(8,128)S(1)}, f32[16,8,128]{2,1,0:T(8,128)S(1)}, u32[]{:S(2)}, u32[]{:S(2)}) collective-permute-start(f32[16,8,128]{2,1,0:T(8,128)S(1)} %add.7.refs_2_), channel_id=1, source_target_pairs={{0,16},{4,20},{8,24},{12,28},{16,0},{20,4},{24,8},{28,12},{1,17},{... | collective-permute-start | bytes 196616 | tf_op jit(solution)/shard_map/ppermute | solution.py:303
  37.2 2.3 %collective-permute-done.7.refs_3_ = f32[16,8,128]{2,1,0:T(8,128)S(1)} collective-permute-done((f32[16,8,128]{2,1,0:T(8,128)S(1)}, f32[16,8,128]{2,1,0:T(8,128)S(1)}, u32[]{:S(2)}, u32[]{:S(2)}) %collective-permute-start.7) | collective-permute-done | bytes 65568 | tf_op jit(solution)/shard_map/ppermute | solution.py:303
  39.5 4.6 %shard_map.81 = (f32[16,8,128]{2,1,0:T(8,128)S(1)}, f32[4,256,128]{2,1,0:T(8,128)S(1)}, bf16[7,256,128]{2,1,0:T(8,128)(2,1)S(1)}, bf16[4,256,128]{2,1,0:T(8,128)(2,1)S(1)}) custom-call(s32[4]{0:T(128)S(1)} %iota_xor_fusion.refs_0_, s32[1,4096]{1,0:T(1,128)S(1)} %get-tuple-element.11.refs_1_, f32[16,8,128]{2,1,0:T(8,128)S(1)} %add.7.refs_2_, ...), custom_call_target="tpu_custom_call" | custom-call | flops 1024 | bytes 1024 | tf_op jit(solution)/shard_map/pallas_call | solution.py:364
  44.1 0.1 collective-permute-start.8
  44.2 2.6 %collective-permute-start.9 = (bf16[4,256,128]{2,1,0:T(8,128)(2,1)S(1)}, bf16[4,256,128]{2,1,0:T(8,128)(2,1)S(1)}, u32[]{:S(2)}, u32[]{:S(2)}) collective-permute-start(bf16[4,256,128]{2,1,0:T(8,128)(2,1)S(1)} %get-tuple-element.19), channel_id=1, source_target_pairs={{0,28},{4,0},{8,4},{12,8},{16,12},{20,16},{24,20},{28,24},{1,29},{... | collective-permute-start | bytes 786440 | tf_op jit(solution)/shard_map/ppermute | solution.py:382
  46.8 0.7 %copy.8 = f32[4,16,2,128]{3,2,1,0:T(2,128)} copy(f32[4,16,2,128]{3,0,2,1:T(4,128)S(1)} %bitcast.15) | data formatting | bytes 131072 | tf_op jit(solution)/shard_map/transpose | solution.py:390
  47.5 6.1 %collective-permute-done.9.high = bf16[4,256,128]{2,1,0:T(8,128)(2,1)S(1)} collective-permute-done((bf16[4,256,128]{2,1,0:T(8,128)(2,1)S(1)}, bf16[4,256,128]{2,1,0:T(8,128)(2,1)S(1)}, u32[]{:S(2)}, u32[]{:S(2)}) %collective-permute-start.9) | collective-permute-done | bytes 262176 | tf_op jit(solution)/shard_map/ppermute | solution.py:382
  53.6 2.1 %collective-permute-done.8.low = bf16[7,256,128]{2,1,0:T(8,128)(2,1)S(1)} collective-permute-done((bf16[7,256,128]{2,1,0:T(8,128)(2,1)S(1)}, bf16[7,256,128]{2,1,0:T(8,128)(2,1)S(1)}, u32[]{:S(2)}, u32[]{:S(2)}) %collective-permute-start.8) | collective-permute-done | bytes 458784 | tf_op jit(solution)/shard_map/ppermute | solution.py:381
  55.6 3.5 %shard_map.82 = f32[4,64,512]{2,1,0:T(8,128)} custom-call(f32[5,64,128]{2,1,0:T(8,128)S(1)} %get-tuple-element.12.coef, f32[4,256,128]{2,1,0:T(8,128)S(1)} %get-tuple-element.17.own, bf16[7,256,128]{2,1,0:T(8,128)(2,1)S(1)} %collective-permute-done.8.low, bf16[4,256,128]{2,1,0:T(8,128)(2,1)S(1)} %collective-permute-done.9.high), custom_call_target="tpu_custom_call" | custom-call | flops 1024 | bytes 1024 | tf_op jit(solution)/shard_map/pallas_call | solution.py:383
  (3 shorter events, 0.0 us)
Async XLA Ops:
  0.6 14.1 %collective-permute-start.1 = (f32[4,64,512]{2,1,0:T(8,128)}, f32[4,64,512]{2,1,0:T(8,128)S(1)}, u32[]{:S(2)}, u32[]{:S(2)}) collective-permute-start(f32[4,64,512]{2,1,0:T(8,128)} %bitcast.10), channel_id=1, source_target_pairs={{0,28},{4,0},{8,4},{12,8},{16,12},{20,16},{24,20},{28,24},{1,29},{... | collective-permute-start | bytes 1572872 | tf_op jit(solution)/shard_map/ppermute | solution.py:321
  5.1 9.6 %collective-permute-start = (bf16[4,64,512]{2,1,0:T(8,128)(2,1)S(1)}, bf16[4,64,512]{2,1,0:T(8,128)(2,1)S(1)}, u32[]{:S(2)}, u32[]{:S(2)}) collective-permute-start(bf16[4,64,512]{2,1,0:T(8,128)(2,1)S(1)} %bitcast_convert_fusion), channel_id=1, source_target_pairs={{0,4},{4,8},{8,12},{12,16},{16,20},{20,24},{24,28},{28,0},{1,5},{5... | collective-permute-start | bytes 786440 | tf_op jit(solution)/shard_map/ppermute | solution.py:322
  5.2 14.8 %collective-permute-start.2 = (bf16[1024,128]{1,0:T(8,128)(2,1)}, bf16[1024,128]{1,0:T(8,128)(2,1)S(1)}, u32[]{:S(2)}, u32[]{:S(2)}) collective-permute-start(bf16[1024,128]{1,0:T(8,128)(2,1)} %bitcast.12), channel_id=1, source_target_pairs={{0,2},{1,3},{2,0},{3,1},{4,6},{5,7},{6,4},{7,5},{8,10},{9,11},{10,... | collective-permute-start | bytes 786440 | tf_op jit(solution)/shard_map/ppermute | solution.py:278
  7.8 12.8 %collective-permute-start.4 = (bf16[1024,128]{1,0:T(8,128)(2,1)}, bf16[1024,128]{1,0:T(8,128)(2,1)S(1)}, u32[]{:S(2)}, u32[]{:S(2)}) collective-permute-start(bf16[1024,128]{1,0:T(8,128)(2,1)} %bitcast.13), channel_id=1, source_target_pairs={{0,1},{1,0},{2,3},{3,2},{4,5},{5,4},{6,7},{7,6},{8,9},{9,8},{10,11... | collective-permute-start | bytes 786440 | tf_op jit(solution)/shard_map/ppermute | solution.py:278
  10.1 1.0 %copy-start = (f32[1,4,64,512]{3,2,1,0:T(8,128)S(1)}, f32[1,4,64,512]{3,2,1,0:T(8,128)}, u32[]{:S(2)}) copy-start(f32[1,4,64,512]{3,2,1,0:T(8,128)} %param.6) | copy-start | bytes 1572868
  11.1 0.9 %copy-start.1 = (bf16[1,1024,128]{2,1,0:T(8,128)(2,1)S(1)}, bf16[1,1024,128]{2,1,0:T(8,128)(2,1)}, u32[]{:S(2)}) copy-start(bf16[1,1024,128]{2,1,0:T(8,128)(2,1)} %param.11) | copy-start | bytes 786436
  12.1 0.7 %copy-start.2 = (s32[1,4096]{1,0:T(1,128)S(1)}, s32[1,4096]{1,0:T(1,128)}, u32[]{:S(2)}) copy-start(s32[1,4096]{1,0:T(1,128)} %tile.1) | copy-start | bytes 49156
  12.8 0.7 %copy-start.3 = (f32[64]{0:T(128)S(1)}, f32[64]{0:T(128)}, u32[]{:S(2)}) copy-start(f32[64]{0:T(128)} %param.7) | copy-start | bytes 772
  13.4 0.7 %copy-start.4 = (f32[64]{0:T(128)S(1)}, f32[64]{0:T(128)}, u32[]{:S(2)}) copy-start(f32[64]{0:T(128)} %param.8) | copy-start | bytes 772
  19.9 7.2 %collective-permute-start.3 = (bf16[1024,128]{1,0:T(8,128)(2,1)S(1)}, bf16[1024,128]{1,0:T(8,128)(2,1)S(1)}, u32[]{:S(2)}, u32[]{:S(2)}) collective-permute-start(bf16[1024,128]{1,0:T(8,128)(2,1)S(1)} %collective-permute-done.2.refs_5_.refs_6_), channel_id=1, source_target_pairs={{0,1},{1,0},{2,3},{3,2},{4,5},{5,4},{6,7},{7,6},{8,9},{9,8},{10,11... | collective-permute-start | bytes 786440 | tf_op jit(solution)/shard_map/ppermute | solution.py:278
  29.1 1.3 %collective-permute-start.5 = (f32[16,8,128]{2,1,0:T(8,128)S(1)}, f32[16,8,128]{2,1,0:T(8,128)S(1)}, u32[]{:S(2)}, u32[]{:S(2)}) collective-permute-start(f32[16,8,128]{2,1,0:T(8,128)S(1)} %shard_map.80), channel_id=1, source_target_pairs={{0,4},{4,0},{8,12},{12,8},{16,20},{20,16},{24,28},{28,24},{1,5},{5... | collective-permute-start | bytes 196616 | tf_op jit(solution)/shard_map/ppermute | solution.py:303
  30.5 4.7 %collective-permute-start.6 = (f32[16,8,128]{2,1,0:T(8,128)S(1)}, f32[16,8,128]{2,1,0:T(8,128)S(1)}, u32[]{:S(2)}, u32[]{:S(2)}) collective-permute-start(f32[16,8,128]{2,1,0:T(8,128)S(1)} %add.6), channel_id=1, source_target_pairs={{0,8},{4,12},{8,0},{12,4},{16,24},{20,28},{24,16},{28,20},{1,9},{5... | collective-permute-start | bytes 196616 | tf_op jit(solution)/shard_map/ppermute | solution.py:303
  35.2 4.3 %collective-permute-start.7 = (f32[16,8,128]{2,1,0:T(8,128)S(1)}, f32[16,8,128]{2,1,0:T(8,128)S(1)}, u32[]{:S(2)}, u32[]{:S(2)}) collective-permute-start(f32[16,8,128]{2,1,0:T(8,128)S(1)} %add.7.refs_2_), channel_id=1, source_target_pairs={{0,16},{4,20},{8,24},{12,28},{16,0},{20,4},{24,8},{28,12},{1,17},{... | collective-permute-start | bytes 196616 | tf_op jit(solution)/shard_map/ppermute | solution.py:303
  44.1 11.5 %collective-permute-start.8 = (bf16[7,256,128]{2,1,0:T(8,128)(2,1)S(1)}, bf16[7,256,128]{2,1,0:T(8,128)(2,1)S(1)}, u32[]{:S(2)}, u32[]{:S(2)}) collective-permute-start(bf16[7,256,128]{2,1,0:T(8,128)(2,1)S(1)} %get-tuple-element.18), channel_id=1, source_target_pairs={{0,4},{4,8},{8,12},{12,16},{16,20},{20,24},{24,28},{28,0},{1,5},{5... | collective-permute-start | bytes 1376264 | tf_op jit(solution)/shard_map/ppermute | solution.py:381
  44.2 9.4 %collective-permute-start.9 = (bf16[4,256,128]{2,1,0:T(8,128)(2,1)S(1)}, bf16[4,256,128]{2,1,0:T(8,128)(2,1)S(1)}, u32[]{:S(2)}, u32[]{:S(2)}) collective-permute-start(bf16[4,256,128]{2,1,0:T(8,128)(2,1)S(1)} %get-tuple-element.19), channel_id=1, source_target_pairs={{0,28},{4,0},{8,4},{12,8},{16,12},{20,16},{24,20},{28,24},{1,29},{... | collective-permute-start | bytes 786440 | tf_op jit(solution)/shard_map/ppermute | solution.py:382

commit v11 on v10

--- a/solution.py
+++ b/solution.py
@@ -139,7 +139,7 @@
                         tiles[pl.ds(PAD + number * steps + step, 8, stride=steps), :] = block[c]
             return carry
 
-        lax.fori_loop(0, height // 8, sweep, 0, unroll=4)
+        lax.fori_loop(0, height // 8, sweep, 0, unroll=8)
 
 
 def forward_kernel(coef, own, low, high, out, first, second):
@@ -174,21 +174,20 @@
                         target[plane, c, pl.ds(pl.multiple_of(PAD + row, 8), 8), :] = block[c]
             return carry
 
-        lax.fori_loop(0, height // 8, sweep, 0, unroll=4)
-
-
-def project_kernel(chunks, source, start, tiles, *refs):
-    panels, (*before, out, wide) = refs[: len(chunks)], refs[len(chunks) :]
-    shard = panels[0].shape[0] // GROUP
+        lax.fori_loop(0, height // 8, sweep, 0, unroll=8)
+
+
+def project_kernel(places, shard, source, start, tiles, *refs):
+    panels, (*before, out, wide) = refs[: len(places)], refs[len(places) :]
     for given in before:
         out[...] = given[...]
     first = lax.broadcasted_iota(jnp.int32, (8, TILE), 0) < STEPS
     lane = lax.broadcasted_iota(jnp.int32, (8, TILE), 1)
-    for chunk, panel in zip(chunks, panels):
-        wide[...] = panel[...].astype(jnp.float32)
-
-        def body(group, carry, chunk=chunk):
-            number = source[chunk] * shard + group
+    for (chunk, offset), panel in zip(places, panels):
+        wide[: panel.shape[0], :] = panel[...].astype(jnp.float32)
+
+        def body(group, carry, chunk=chunk, offset=offset):
+            number = source[chunk] * shard + offset + group
             sums = jnp.zeros((8, TILE), jnp.float32)
             for place in range(TILE):
                 left = start[0, number * GROUP + place]
@@ -203,14 +202,12 @@
             out[number] = sums
             return carry
 
-        lax.fori_loop(0, shard, body, 0)
-
-
-def deposit_kernel(count, source, start, *refs):
+        lax.fori_loop(0, panel.shape[0] // GROUP, body, 0)
+
+
+def deposit_kernel(count, places, shard, source, start, *refs):
     parts, panels = refs[:count], refs[count:-7]
     total, field, rightward, leftward, scaled, *chosen = refs[-7:]
-    groups = total.shape[0]
-    shard = groups // len(panels)
     cells, per_plane = field.shape[0], field.shape[1]
     tile = start[...].astype(jnp.int16)
     one, none = jnp.ones((), jnp.bfloat16), jnp.zeros((), jnp.bfloat16)
@@ -228,17 +225,19 @@
 
     choose(0)
     total[...] = tree_sum([part[...] for part in parts])
-    numbers = [source[g // shard] * shard + g % shard for g in range(groups)]
-    last = [total[n, pl.ds(half * STEPS + STEPS - 1, 1), :] for n in numbers for half in range(2)]
+    blocks = []
+    for (chunk, offset), panel in zip(places, panels):
+        for group in range(panel.shape[0] // GROUP):
+            number = source[chunk] * shard + offset + group
+            blocks += [(number, half, panel, group * GROUP + half * TILE) for half in range(2)]
+    last = [total[number, pl.ds(half * STEPS + STEPS - 1, 1), :] for number, half, _, _ in blocks]
     drive = jnp.concatenate(last, axis=0).T
-    for group, number in enumerate(numbers):
-        for half in range(2):
-            place = 2 * group + half
-            rows = panels[group // shard][pl.ds((group % shard) * GROUP + half * TILE, TILE), :]
-            head, tail = split(drive[:, place : place + 1] * rows.astype(jnp.float32))
-            where = pl.ds(pl.multiple_of(number * GROUP + half * TILE, TILE), TILE)
-            scaled[where, pl.ds(0, TILE)] = head
-            scaled[where, pl.ds(TILE, TILE)] = tail
+    for place, (number, half, panel, row) in enumerate(blocks):
+        rows = panel[pl.ds(row, TILE), :].astype(jnp.float32)
+        head, tail = split(drive[:, place : place + 1] * rows)
+        where = pl.ds(pl.multiple_of(number * GROUP + half * TILE, TILE), TILE)
+        scaled[where, pl.ds(0, TILE)] = head
+        scaled[where, pl.ds(TILE, TILE)] = tail
 
     for plane in range(cells):
         if plane < cells - 1:
@@ -268,16 +267,31 @@
     )
 
 
-def gathered_panel(panel, axis, ready):
-    count = lax.axis_size(axis)
-    shards, mask = {0: panel}, count // 2
+def gathered_panel(panel, axis, soon, late):
+    count, rows = lax.axis_size(axis), panel.shape[0]
+    shards, mask = {0: [panel]}, count // 2
     while mask:
         pairs = [(i, i ^ mask) for i in range(count)]
         for held in sorted(shards):
-            operand = tied(shards[held], ready) if held else panel
-            shards[held | mask] = lax.ppermute(operand, axis, pairs)
+            pieces = shards[held]
+            if held:
+                ready = (soon, late) if len(pieces) > 1 else (late,)
+                pieces = [tied(piece, after) for piece, after in zip(pieces, ready)]
+            elif len(shards) == 1 and rows >= 2 * GROUP:
+                pieces = [panel[: rows // 2], panel[rows // 2 :]]
+            shards[held | mask] = [lax.ppermute(piece, axis, pairs) for piece in pieces]
         mask //= 2
     return [shards[k] for k in range(1, count)]
+
+
+def layout(panels):
+    places = []
+    for chunk, pieces in panels:
+        first = 0
+        for piece in pieces:
+            places.append((chunk, first))
+            first += piece.shape[0] // GROUP
+    return places
 
 
 def tied(value, *others):
@@ -295,7 +309,7 @@
     if count & (count - 1):
         return [lax.psum(part, axis)]
     done, parts = 1, [part]
-    for span in [2] * count.bit_length():
+    for span in (2, 4, 4, 4, 4):
         span = min(span, count // done)
         if span > 1:
             part = tree_sum(parts)
@@ -344,25 +358,26 @@
         inputs=5,
     )(probe_offset, coef, shifted, low, high)
 
-    panels = [panel] + gathered_panel(actuator_panel[0], "probe", tiles)
-    every = list(range(probes))
-
-    def project(chunks, *given):
+    panels = list(enumerate([[panel]] + gathered_panel(actuator_panel[0], "probe", coef, tiles)))
+
+    def project(shards, *given):
+        pieces = [piece for _, pieces in shards for piece in pieces]
         return call(
-            lambda *refs: project_kernel(chunks, *refs),
+            lambda *refs: project_kernel(layout(shards), shard, *refs),
             jax.ShapeDtypeStruct((groups, 2 * STEPS, TILE), f32),
             vmem=6,
             scratch=(pltpu.VMEM((shard * GROUP, TILE), f32),),
             smem=2,
-            inputs=3 + len(chunks) + len(given),
-        )(source, start, tiles, *[panels[chunk] for chunk in chunks], *given)
-
-    before = project(every[:-1])
-    parts = summands(project(every[-1:], before), "state")
+            inputs=3 + len(pieces) + len(given),
+        )(source, start, tiles, *pieces, *given)
+
+    before = project(panels[:-1])
+    parts = summands(project(panels[-1:], before), "state")
+    pieces = [piece for _, pieces in panels for piece in pieces]
     payload = jax.ShapeDtypeStruct((2 * cells - 1, height * columns, TILE), bf16)
     heads = jax.ShapeDtypeStruct((cells, height * columns, TILE), bf16)
     total, forced, rightward, leftward = call(
-        lambda *refs: deposit_kernel(len(parts), *refs),
+        lambda *refs: deposit_kernel(len(parts), layout(panels), shard, *refs),
         (
             jax.ShapeDtypeStruct(before.shape, f32),
             jax.ShapeDtypeStruct((cells, height * columns, TILE), f32),
@@ -376,8 +391,8 @@
             pltpu.VMEM((height * columns, actuators), bf16),
         ),
         smem=1,
-        inputs=2 + len(parts) + probes,
-    )(source, start, *parts, *panels)
+        inputs=2 + len(parts) + len(pieces),
+    )(source, start, *parts, *pieces)
     from_low = lax.ppermute(rightward, "state", shift_pairs(slabs, 1))
     from_high = lax.ppermute(leftward, "state", shift_pairs(slabs, -1))
     response = call(

time: 59.5 us -> 57.4 us (0.965)
  waiting for transfers between devices: 18.2 us -> 14.7 us
  starting transfers between devices: 15.4 us -> 16.9 us
  Pallas kernels: 18.4 us -> 17.2 us
  local copies, waits for them, and re-layouts: 4.68 us -> 5.67 us
    ppermute x3 -> x5, starting transfers between devices: 4.9 us -> 7.17 us  [gathered_panel(): shards[held | mask] = [lax.ppermute(piece, axis, pairs) for piece in pieces]]
    ppermute x3 -> x5, waiting for transfers between devices: 4.07 us -> 2.22 us  [gathered_panel(): shards[held | mask] = [lax.ppermute(piece, axis, pairs) for piece in pieces]]
    ppermute x3 -> x4, waiting for transfers between devices: 5.95 us -> 4.21 us  [summands(): parts = [part] + [lax.ppermute(part, axis, pair) for pair in pairs]]
    slice x0 -> x1, local copies, waits for them, and re-layouts: none -> 0.99 us  [gathered_panel(): pieces = [panel[:rows // 2], panel[rows // 2:]]]
    ppermute x3 -> x4, starting transfers between devices: 4.38 us -> 3.62 us  [summands(): parts = [part] + [lax.ppermute(part, axis, pair) for pair in pairs]]
    pallas_call x1, Pallas kernels: 3.51 us -> 2.87 us  [local(): call(forward_kernel, jax.ShapeDtypeStruct((cells, height, width), f32), v...]
  transfers between devices with their start and end apart: 10 -> 13, of which waited for: 7 -> 7; matrix products, arithmetic and copies ran while one was open for 3% -> 5% of each run, Pallas kernels for 14% -> 13%
where the time goes in v11:
time: 57.4 us; the launch traced here: 57.1 us
  Pallas kernels  17.2 us (30%)
  starting transfers between devices  16.9 us (29%)
  waiting for transfers between devices  14.7 us (26%)
  local copies, waits for them, and re-layouts  5.67 us (10%)
  between operations  1.38 us (2%)
  other arithmetic  1.12 us (2%)
    ppermute x5, starting transfers between devices, gathered_panel(): shards[held | mask] = [lax.ppermute(piece, axis, pairs) for piece in pieces]  7.17 us
    pallas_call x2, Pallas kernels, project(): call(lambda *refs: project_kernel(layout(shards), shard, *refs), jax.Shap...  6.44 us
    ppermute x1, waiting for transfers between devices, local(): from_high = lax.ppermute(leftward, 'state', shift_pairs(slabs, -1))  5.96 us
    pallas_call x1, Pallas kernels, local(): call(lambda *refs: deposit_kernel(len(parts), layout(panels), shard, *ref...  4.65 us
    ppermute x4, waiting for transfers between devices, summands(): parts = [part] + [lax.ppermute(part, axis, pair) for pair in pairs]  4.21 us
    unnamed x10, local copies, waits for them, and re-layouts  4.01 us
    ppermute x4, starting transfers between devices, summands(): parts = [part] + [lax.ppermute(part, axis, pair) for pair in pairs]  3.62 us
    ppermute x1, starting transfers between devices, local(): high = lax.ppermute(own, 'state', shift_pairs(slabs, -1))  3.39 us
  transfers between devices with their start and end apart: 13, of which 7 were waited for; matrix products, arithmetic and copies ran while one was open for 5% of the time, Pallas kernels for 13%

profile of v11, /device:TPU:0, one launch (start us, length us, event | category | flops | bytes accessed | tf_op | source)
XLA Modules:
  0.0 57.1 jit_solution(15684446185363806414)
XLA Ops:
  0.6 3.4 %collective-permute-start.1 = (f32[4,64,512]{2,1,0:T(8,128)}, f32[4,64,512]{2,1,0:T(8,128)S(1)}, u32[]{:S(2)}, u32[]{:S(2)}) collective-permute-start(f32[4,64,512]{2,1,0:T(8,128)} %bitcast.14), channel_id=1, source_target_pairs={{0,28},{4,0},{8,4},{12,8},{16,12},{20,16},{24,20},{28,24},{1,29},{... | collective-permute-start | bytes 1572872 | tf_op jit(solution)/shard_map/ppermute | solution.py:335
  4.0 1.1 %bitcast_convert_fusion = bf16[4,64,512]{2,1,0:T(8,128)(2,1)S(1)} fusion(f32[1,4,64,512]{3,2,1,0:T(8,128)} %param.6), kind=kLoop, calls=%fused_computation.3 | loop fusion | flops 131072 | bytes 786432 | tf_op jit(solution)/shard_map/convert_element_type | solution.py:336
  5.1 0.1 collective-permute-start
  5.2 1.0 %slice_bitcast_fusion = (bf16[512,128]{1,0:T(8,128)(2,1)S(1)}, bf16[512,128]{1,0:T(8,128)(2,1)S(1)}) fusion(bf16[1,1024,128]{2,1,0:T(8,128)(2,1)} %param.11), kind=kLoop, calls=%fused_computation | loop fusion | bytes 524288 | tf_op jit(solution)/shard_map/slice | solution.py:281
  6.2 2.7 %collective-permute-start.2 = (bf16[512,128]{1,0:T(8,128)(2,1)S(1)}, bf16[512,128]{1,0:T(8,128)(2,1)S(1)}, u32[]{:S(2)}, u32[]{:S(2)}) collective-permute-start(bf16[512,128]{1,0:T(8,128)(2,1)S(1)} %get-tuple-element.23), channel_id=1, source_target_pairs={{0,2},{1,3},{2,0},{3,1},{4,6},{5,7},{6,4},{7,5},{8,10},{9,11},{10,... | collective-permute-start | bytes 393224 | tf_op jit(solution)/shard_map/ppermute | solution.py:282
  8.8 1.6 %collective-permute-start.6 = (bf16[1024,128]{1,0:T(8,128)(2,1)}, bf16[1024,128]{1,0:T(8,128)(2,1)S(1)}, u32[]{:S(2)}, u32[]{:S(2)}) collective-permute-start(bf16[1024,128]{1,0:T(8,128)(2,1)} %bitcast.16), channel_id=1, source_target_pairs={{0,1},{1,0},{2,3},{3,2},{4,5},{5,4},{6,7},{7,6},{8,9},{9,8},{10,11... | collective-permute-start | bytes 786440 | tf_op jit(solution)/shard_map/ppermute | solution.py:282
  10.4 0.3 collective-permute-start.4
  11.4 0.0 copy-start
  11.4 1.0 %copy-done = f32[1,4,64,512]{3,2,1,0:T(8,128)S(1)} copy-done((f32[1,4,64,512]{3,2,1,0:T(8,128)S(1)}, f32[1,4,64,512]{3,2,1,0:T(8,128)}, u32[]{:S(2)}) %copy-start) | copy-done | bytes 524312
  12.4 0.0 copy-start.1
  12.5 0.9 %copy-done.1 = bf16[1,1024,128]{2,1,0:T(8,128)(2,1)S(1)} copy-done((bf16[1,1024,128]{2,1,0:T(8,128)(2,1)S(1)}, bf16[1,1024,128]{2,1,0:T(8,128)(2,1)}, u32[]{:S(2)}) %copy-start.1) | copy-done | bytes 262168
  13.4 0.0 copy-start.2
  13.4 0.7 %copy-done.2 = s32[1,4096]{1,0:T(1,128)S(1)} copy-done((s32[1,4096]{1,0:T(1,128)S(1)}, s32[1,4096]{1,0:T(1,128)}, u32[]{:S(2)}) %copy-start.2) | copy-done | bytes 16408
  14.1 0.0 copy-start.3
  14.1 0.7 %copy-done.3 = f32[64]{0:T(128)S(1)} copy-done((f32[64]{0:T(128)S(1)}, f32[64]{0:T(128)}, u32[]{:S(2)}) %copy-start.3) | copy-done | bytes 280
  14.8 0.0 copy-start.4
  14.8 0.7 %copy-done.4 = f32[64]{0:T(128)S(1)} copy-done((f32[64]{0:T(128)S(1)}, f32[64]{0:T(128)}, u32[]{:S(2)}) %copy-start.4) | copy-done | bytes 280
  15.4 0.6 %shard_map.77 = (f32[4,4,64,128]{3,2,1,0:T(8,128)S(1)}, f32[5,64,128]{2,1,0:T(8,128)S(1)}, s32[1,4096]{1,0:T(1,128)S(1)}, bf16[1024,128]{1,0:T(8,128)(2,1)S(1)}) custom-call(s32[1]{0:T(128)S(6)} %copy.9.offset, f32[4,64,512]{2,1,0:T(8,128)S(1)} %bitcast.15, f32[1,64]{1,0:T(1,128)S(1)} %bitcast.19, f32[1,64]{1,0:T(1,128)S(1)} %bitcast.20, ...), custom_call_target="tpu_custom_call" | custom-call | flops 1024 | bytes 1024 | tf_op jit(solution)/shard_map/pallas_call | solution.py:338
  16.0 0.3 collective-permute-done.2.refs_5_.refs_8_
  16.3 0.2 collective-permute-start.3
  16.6 0.0 collective-permute-done.low
  16.6 0.0 collective-permute-done.1.high
  16.6 2.7 %shard_map.78.refs_2_ = f32[4112,128]{1,0:T(8,128)S(1)} custom-call(s32[1]{0:T(128)S(6)} %copy.9.offset, f32[5,64,128]{2,1,0:T(8,128)S(1)} %get-tuple-element.13.coef, f32[4,4,64,128]{3,2,1,0:T(8,128)S(1)} %get-tuple-element.14.own, bf16[4,64,512]{2,1,0:T(8,128)(2,1)S(1)} %collective-permute-done.low, f32[4,64,512]{2,1,0:T(8,128)S(1)} %collective-permute-done.1.high), custom_call_target="tpu_custom_call" | custom-call | flops 1024 | bytes 1024 | tf_op jit(solution)/shard_map/pallas_call | solution.py:352
  19.3 1.9 %collective-permute-done.4.refs_6_.refs_9_ = bf16[512,128]{1,0:T(8,128)(2,1)S(1)} collective-permute-done((bf16[512,128]{1,0:T(8,128)(2,1)S(1)}, bf16[512,128]{1,0:T(8,128)(2,1)S(1)}, u32[]{:S(2)}, u32[]{:S(2)}) %collective-permute-start.4) | collective-permute-done | bytes 131104 | tf_op jit(solution)/shard_map/ppermute | solution.py:282
  21.2 2.4 %collective-permute-start.5 = (bf16[512,128]{1,0:T(8,128)(2,1)S(1)}, bf16[512,128]{1,0:T(8,128)(2,1)S(1)}, u32[]{:S(2)}, u32[]{:S(2)}) collective-permute-start(bf16[512,128]{1,0:T(8,128)(2,1)S(1)} %collective-permute-done.4.refs_6_.refs_9_), channel_id=1, source_target_pairs={{0,1},{1,0},{2,3},{3,2},{4,5},{5,4},{6,7},{7,6},{8,9},{9,8},{10,11... | collective-permute-start | bytes 393224 | tf_op jit(solution)/shard_map/ppermute | solution.py:282
  23.6 0.0 collective-permute-done.6.refs_4_.refs_7_
  23.6 4.4 %shard_map.79.refs_5_ = f32[16,8,128]{2,1,0:T(8,128)S(1)} custom-call(s32[4]{0:T(128)S(1)} %iota_xor_fusion.refs_0_, s32[1,4096]{1,0:T(1,128)S(1)} %get-tuple-element.12.refs_1_, f32[4112,128]{1,0:T(8,128)S(1)} %shard_map.78.refs_2_, bf16[1024,128]{1,0:T(8,128)(2,1)S(1)} %get-tuple-element.17.refs_3_.refs_6_, ...), custom_call_target="tpu_custom_call" | custom-call | flops 1024 | bytes 1024 | tf_op jit(solution)/shard_map/pallas_call | solution.py:365
  28.0 0.0 collective-permute-done.3.refs_3_.refs_10_
  28.0 0.0 collective-permute-done.5.refs_4_.refs_11_
  28.0 2.0 %shard_map.80 = f32[16,8,128]{2,1,0:T(8,128)S(1)} custom-call(s32[4]{0:T(128)S(1)} %iota_xor_fusion.refs_0_, s32[1,4096]{1,0:T(1,128)S(1)} %get-tuple-element.12.refs_1_, f32[4112,128]{1,0:T(8,128)S(1)} %shard_map.78.refs_2_, bf16[512,128]{1,0:T(8,128)(2,1)S(1)} %collective-permute-done.3.refs_3_.refs_10_, ...), custom_call_target="tpu_custom_call" | custom-call | flops 1024 | bytes 1024 | tf_op jit(solution)/shard_map/pallas_call | solution.py:365
  30.0 0.1 collective-permute-start.7
  30.1 1.2 %collective-permute-done.7 = f32[16,8,128]{2,1,0:T(8,128)S(1)} collective-permute-done((f32[16,8,128]{2,1,0:T(8,128)S(1)}, f32[16,8,128]{2,1,0:T(8,128)S(1)}, u32[]{:S(2)}, u32[]{:S(2)}) %collective-permute-start.7) | collective-permute-done | bytes 65568 | tf_op jit(solution)/shard_map/ppermute | solution.py:317
  31.4 1.3 %collective-permute-start.10 = (f32[16,8,128]{2,1,0:T(8,128)S(1)}, f32[16,8,128]{2,1,0:T(8,128)S(1)}, u32[]{:S(2)}, u32[]{:S(2)}) collective-permute-start(f32[16,8,128]{2,1,0:T(8,128)S(1)} %add.3.refs_2_), channel_id=1, source_target_pairs={{0,24},{4,28},{8,16},{12,20},{16,8},{20,12},{24,0},{28,4},{1,25},{... | collective-permute-start | bytes 196616 | tf_op jit(solution)/shard_map/ppermute | solution.py:317
  32.6 0.8 %collective-permute-start.8 = (f32[16,8,128]{2,1,0:T(8,128)S(1)}, f32[16,8,128]{2,1,0:T(8,128)S(1)}, u32[]{:S(2)}, u32[]{:S(2)}) collective-permute-start(f32[16,8,128]{2,1,0:T(8,128)S(1)} %add.3.refs_2_), channel_id=1, source_target_pairs={{0,8},{4,12},{8,0},{12,4},{16,24},{20,28},{24,16},{28,20},{1,9},{5... | collective-permute-start | bytes 196616 | tf_op jit(solution)/shard_map/ppermute | solution.py:317
  33.4 1.5 %collective-permute-start.9 = (f32[16,8,128]{2,1,0:T(8,128)S(1)}, f32[16,8,128]{2,1,0:T(8,128)S(1)}, u32[]{:S(2)}, u32[]{:S(2)}) collective-permute-start(f32[16,8,128]{2,1,0:T(8,128)S(1)} %add.3.refs_2_), channel_id=1, source_target_pairs={{0,16},{4,20},{8,24},{12,28},{16,0},{20,4},{24,8},{28,12},{1,17},{... | collective-permute-start | bytes 196616 | tf_op jit(solution)/shard_map/ppermute | solution.py:317
  34.9 2.3 %collective-permute-done.10.refs_5_ = f32[16,8,128]{2,1,0:T(8,128)S(1)} collective-permute-done((f32[16,8,128]{2,1,0:T(8,128)S(1)}, f32[16,8,128]{2,1,0:T(8,128)S(1)}, u32[]{:S(2)}, u32[]{:S(2)}) %collective-permute-start.10) | collective-permute-done | bytes 65568 | tf_op jit(solution)/shard_map/ppermute | solution.py:317
  37.2 0.0 collective-permute-done.8.refs_3_
  37.2 0.7 %collective-permute-done.9.refs_4_ = f32[16,8,128]{2,1,0:T(8,128)S(1)} collective-permute-done((f32[16,8,128]{2,1,0:T(8,128)S(1)}, f32[16,8,128]{2,1,0:T(8,128)S(1)}, u32[]{:S(2)}, u32[]{:S(2)}) %collective-permute-start.9) | collective-permute-done | bytes 65568 | tf_op jit(solution)/shard_map/ppermute | solution.py:317
  37.9 4.6 %shard_map.81 = (f32[16,8,128]{2,1,0:T(8,128)S(1)}, f32[4,256,128]{2,1,0:T(8,128)S(1)}, bf16[7,256,128]{2,1,0:T(8,128)(2,1)S(1)}, bf16[4,256,128]{2,1,0:T(8,128)(2,1)S(1)}) custom-call(s32[4]{0:T(128)S(1)} %iota_xor_fusion.refs_0_, s32[1,4096]{1,0:T(1,128)S(1)} %get-tuple-element.12.refs_1_, f32[16,8,128]{2,1,0:T(8,128)S(1)} %add.3.refs_2_, ...), custom_call_target="tpu_custom_call" | custom-call | flops 1024 | bytes 1024 | tf_op jit(solution)/shard_map/pallas_call | solution.py:379
  42.5 0.1 collective-permute-start.11
  42.6 2.6 %collective-permute-start.12 = (bf16[4,256,128]{2,1,0:T(8,128)(2,1)S(1)}, bf16[4,256,128]{2,1,0:T(8,128)(2,1)S(1)}, u32[]{:S(2)}, u32[]{:S(2)}) collective-permute-start(bf16[4,256,128]{2,1,0:T(8,128)(2,1)S(1)} %get-tuple-element.21), channel_id=1, source_target_pairs={{0,28},{4,0},{8,4},{12,8},{16,12},{20,16},{24,20},{28,24},{1,29},{... | collective-permute-start | bytes 786440 | tf_op jit(solution)/shard_map/ppermute | solution.py:397
  45.2 0.7 %copy.8 = f32[4,16,2,128]{3,2,1,0:T(2,128)} copy(f32[4,16,2,128]{3,0,2,1:T(4,128)S(1)} %bitcast.18) | data formatting | bytes 131072 | tf_op jit(solution)/shard_map/transpose | solution.py:405
  45.9 6.0 %collective-permute-done.12.high = bf16[4,256,128]{2,1,0:T(8,128)(2,1)S(1)} collective-permute-done((bf16[4,256,128]{2,1,0:T(8,128)(2,1)S(1)}, bf16[4,256,128]{2,1,0:T(8,128)(2,1)S(1)}, u32[]{:S(2)}, u32[]{:S(2)}) %collective-permute-start.12) | collective-permute-done | bytes 262176 | tf_op jit(solution)/shard_map/ppermute | solution.py:397
  51.9 2.3 %collective-permute-done.11.low = bf16[7,256,128]{2,1,0:T(8,128)(2,1)S(1)} collective-permute-done((bf16[7,256,128]{2,1,0:T(8,128)(2,1)S(1)}, bf16[7,256,128]{2,1,0:T(8,128)(2,1)S(1)}, u32[]{:S(2)}, u32[]{:S(2)}) %collective-permute-start.11) | collective-permute-done | bytes 458784 | tf_op jit(solution)/shard_map/ppermute | solution.py:396
  54.2 2.9 %shard_map.82 = f32[4,64,512]{2,1,0:T(8,128)} custom-call(f32[5,64,128]{2,1,0:T(8,128)S(1)} %get-tuple-element.13.coef, f32[4,256,128]{2,1,0:T(8,128)S(1)} %get-tuple-element.19.own, bf16[7,256,128]{2,1,0:T(8,128)(2,1)S(1)} %collective-permute-done.11.low, bf16[4,256,128]{2,1,0:T(8,128)(2,1)S(1)} %collective-permute-done.12.high), custom_call_target="tpu_custom_call" | custom-call | flops 1024 | bytes 1024 | tf_op jit(solution)/shard_map/pallas_call | solution.py:398
  (2 shorter events, 0.0 us)
Async XLA Ops:
  0.6 15.9 %collective-permute-start.1 = (f32[4,64,512]{2,1,0:T(8,128)}, f32[4,64,512]{2,1,0:T(8,128)S(1)}, u32[]{:S(2)}, u32[]{:S(2)}) collective-permute-start(f32[4,64,512]{2,1,0:T(8,128)} %bitcast.14), channel_id=1, source_target_pairs={{0,28},{4,0},{8,4},{12,8},{16,12},{20,16},{24,20},{28,24},{1,29},{... | collective-permute-start | bytes 1572872 | tf_op jit(solution)/shard_map/ppermute | solution.py:335
  5.1 11.4 %collective-permute-start = (bf16[4,64,512]{2,1,0:T(8,128)(2,1)S(1)}, bf16[4,64,512]{2,1,0:T(8,128)(2,1)S(1)}, u32[]{:S(2)}, u32[]{:S(2)}) collective-permute-start(bf16[4,64,512]{2,1,0:T(8,128)(2,1)S(1)} %bitcast_convert_fusion), channel_id=1, source_target_pairs={{0,4},{4,8},{8,12},{12,16},{16,20},{20,24},{24,28},{28,0},{1,5},{5... | collective-permute-start | bytes 786440 | tf_op jit(solution)/shard_map/ppermute | solution.py:336
  6.2 10.1 %collective-permute-start.2 = (bf16[512,128]{1,0:T(8,128)(2,1)S(1)}, bf16[512,128]{1,0:T(8,128)(2,1)S(1)}, u32[]{:S(2)}, u32[]{:S(2)}) collective-permute-start(bf16[512,128]{1,0:T(8,128)(2,1)S(1)} %get-tuple-element.23), channel_id=1, source_target_pairs={{0,2},{1,3},{2,0},{3,1},{4,6},{5,7},{6,4},{7,5},{8,10},{9,11},{10,... | collective-permute-start | bytes 393224 | tf_op jit(solution)/shard_map/ppermute | solution.py:282
  8.8 14.7 %collective-permute-start.6 = (bf16[1024,128]{1,0:T(8,128)(2,1)}, bf16[1024,128]{1,0:T(8,128)(2,1)S(1)}, u32[]{:S(2)}, u32[]{:S(2)}) collective-permute-start(bf16[1024,128]{1,0:T(8,128)(2,1)} %bitcast.16), channel_id=1, source_target_pairs={{0,1},{1,0},{2,3},{3,2},{4,5},{5,4},{6,7},{7,6},{8,9},{9,8},{10,11... | collective-permute-start | bytes 786440 | tf_op jit(solution)/shard_map/ppermute | solution.py:282
  10.4 10.8 %collective-permute-start.4 = (bf16[512,128]{1,0:T(8,128)(2,1)S(1)}, bf16[512,128]{1,0:T(8,128)(2,1)S(1)}, u32[]{:S(2)}, u32[]{:S(2)}) collective-permute-start(bf16[512,128]{1,0:T(8,128)(2,1)S(1)} %get-tuple-element.22), channel_id=1, source_target_pairs={{0,2},{1,3},{2,0},{3,1},{4,6},{5,7},{6,4},{7,5},{8,10},{9,11},{10,... | collective-permute-start | bytes 393224 | tf_op jit(solution)/shard_map/ppermute | solution.py:282
  11.4 1.0 %copy-start = (f32[1,4,64,512]{3,2,1,0:T(8,128)S(1)}, f32[1,4,64,512]{3,2,1,0:T(8,128)}, u32[]{:S(2)}) copy-start(f32[1,4,64,512]{3,2,1,0:T(8,128)} %param.6) | copy-start | bytes 1572868
  12.4 0.9 %copy-start.1 = (bf16[1,1024,128]{2,1,0:T(8,128)(2,1)S(1)}, bf16[1,1024,128]{2,1,0:T(8,128)(2,1)}, u32[]{:S(2)}) copy-start(bf16[1,1024,128]{2,1,0:T(8,128)(2,1)} %param.11) | copy-start | bytes 786436
  13.4 0.7 %copy-start.2 = (s32[1,4096]{1,0:T(1,128)S(1)}, s32[1,4096]{1,0:T(1,128)}, u32[]{:S(2)}) copy-start(s32[1,4096]{1,0:T(1,128)} %tile.1) | copy-start | bytes 49156
  14.1 0.7 %copy-start.3 = (f32[64]{0:T(128)S(1)}, f32[64]{0:T(128)}, u32[]{:S(2)}) copy-start(f32[64]{0:T(128)} %param.7) | copy-start | bytes 772
  14.8 0.7 %copy-start.4 = (f32[64]{0:T(128)S(1)}, f32[64]{0:T(128)}, u32[]{:S(2)}) copy-start(f32[64]{0:T(128)} %param.8) | copy-start | bytes 772
  16.3 11.7 %collective-permute-start.3 = (bf16[512,128]{1,0:T(8,128)(2,1)S(1)}, bf16[512,128]{1,0:T(8,128)(2,1)S(1)}, u32[]{:S(2)}, u32[]{:S(2)}) collective-permute-start(bf16[512,128]{1,0:T(8,128)(2,1)S(1)} %collective-permute-done.2.refs_5_.refs_8_), channel_id=1, source_target_pairs={{0,1},{1,0},{2,3},{3,2},{4,5},{5,4},{6,7},{7,6},{8,9},{9,8},{10,11... | collective-permute-start | bytes 393224 | tf_op jit(solution)/shard_map/ppermute | solution.py:282
  21.2 6.8 %collective-permute-start.5 = (bf16[512,128]{1,0:T(8,128)(2,1)S(1)}, bf16[512,128]{1,0:T(8,128)(2,1)S(1)}, u32[]{:S(2)}, u32[]{:S(2)}) collective-permute-start(bf16[512,128]{1,0:T(8,128)(2,1)S(1)} %collective-permute-done.4.refs_6_.refs_9_), channel_id=1, source_target_pairs={{0,1},{1,0},{2,3},{3,2},{4,5},{5,4},{6,7},{7,6},{8,9},{9,8},{10,11... | collective-permute-start | bytes 393224 | tf_op jit(solution)/shard_map/ppermute | solution.py:282
  30.0 1.3 %collective-permute-start.7 = (f32[16,8,128]{2,1,0:T(8,128)S(1)}, f32[16,8,128]{2,1,0:T(8,128)S(1)}, u32[]{:S(2)}, u32[]{:S(2)}) collective-permute-start(f32[16,8,128]{2,1,0:T(8,128)S(1)} %shard_map.80), channel_id=1, source_target_pairs={{0,4},{4,0},{8,12},{12,8},{16,20},{20,16},{24,28},{28,24},{1,5},{5... | collective-permute-start | bytes 196616 | tf_op jit(solution)/shard_map/ppermute | solution.py:317
  31.4 5.8 %collective-permute-start.10 = (f32[16,8,128]{2,1,0:T(8,128)S(1)}, f32[16,8,128]{2,1,0:T(8,128)S(1)}, u32[]{:S(2)}, u32[]{:S(2)}) collective-permute-start(f32[16,8,128]{2,1,0:T(8,128)S(1)} %add.3.refs_2_), channel_id=1, source_target_pairs={{0,24},{4,28},{8,16},{12,20},{16,8},{20,12},{24,0},{28,4},{1,25},{... | collective-permute-start | bytes 196616 | tf_op jit(solution)/shard_map/ppermute | solution.py:317
  32.6 4.6 %collective-permute-start.8 = (f32[16,8,128]{2,1,0:T(8,128)S(1)}, f32[16,8,128]{2,1,0:T(8,128)S(1)}, u32[]{:S(2)}, u32[]{:S(2)}) collective-permute-start(f32[16,8,128]{2,1,0:T(8,128)S(1)} %add.3.refs_2_), channel_id=1, source_target_pairs={{0,8},{4,12},{8,0},{12,4},{16,24},{20,28},{24,16},{28,20},{1,9},{5... | collective-permute-start | bytes 196616 | tf_op jit(solution)/shard_map/ppermute | solution.py:317
  33.4 4.5 %collective-permute-start.9 = (f32[16,8,128]{2,1,0:T(8,128)S(1)}, f32[16,8,128]{2,1,0:T(8,128)S(1)}, u32[]{:S(2)}, u32[]{:S(2)}) collective-permute-start(f32[16,8,128]{2,1,0:T(8,128)S(1)} %add.3.refs_2_), channel_id=1, source_target_pairs={{0,16},{4,20},{8,24},{12,28},{16,0},{20,4},{24,8},{28,12},{1,17},{... | collective-permute-start | bytes 196616 | tf_op jit(solution)/shard_map/ppermute | solution.py:317
  42.5 11.7 %collective-permute-start.11 = (bf16[7,256,128]{2,1,0:T(8,128)(2,1)S(1)}, bf16[7,256,128]{2,1,0:T(8,128)(2,1)S(1)}, u32[]{:S(2)}, u32[]{:S(2)}) collective-permute-start(bf16[7,256,128]{2,1,0:T(8,128)(2,1)S(1)} %get-tuple-element.20), channel_id=1, source_target_pairs={{0,4},{4,8},{8,12},{12,16},{16,20},{20,24},{24,28},{28,0},{1,5},{5... | collective-permute-start | bytes 1376264 | tf_op jit(solution)/shard_map/ppermute | solution.py:396
  42.6 9.3 %collective-permute-start.12 = (bf16[4,256,128]{2,1,0:T(8,128)(2,1)S(1)}, bf16[4,256,128]{2,1,0:T(8,128)(2,1)S(1)}, u32[]{:S(2)}, u32[]{:S(2)}) collective-permute-start(bf16[4,256,128]{2,1,0:T(8,128)(2,1)S(1)} %get-tuple-element.21), channel_id=1, source_target_pairs={{0,28},{4,0},{8,4},{12,8},{16,12},{20,16},{24,20},{28,24},{1,29},{... | collective-permute-start | bytes 786440 | tf_op jit(solution)/shard_map/ppermute | solution.py:397

commit v12 on v11

--- a/solution.py
+++ b/solution.py
@@ -267,18 +267,18 @@
     )
 
 
-def gathered_panel(panel, axis, soon, late):
-    count, rows = lax.axis_size(axis), panel.shape[0]
+def gathered_panel(panel, axis, late, first):
+    count = lax.axis_size(axis)
     shards, mask = {0: [panel]}, count // 2
     while mask:
         pairs = [(i, i ^ mask) for i in range(count)]
         for held in sorted(shards):
             pieces = shards[held]
             if held:
-                ready = (soon, late) if len(pieces) > 1 else (late,)
-                pieces = [tied(piece, after) for piece, after in zip(pieces, ready)]
-            elif len(shards) == 1 and rows >= 2 * GROUP:
-                pieces = [panel[: rows // 2], panel[rows // 2 :]]
+                pieces = [tied(piece, late) for piece in pieces]
+            if len(shards) == 1:
+                shards[mask] = [first]
+                continue
             shards[held | mask] = [lax.ppermute(piece, axis, pairs) for piece in pieces]
         mask //= 2
     return [shards[k] for k in range(1, count)]
@@ -348,6 +348,9 @@
         inputs=6,
     )(probe_offset, own, courant[None], diffusivity[None], tile_index, actuator_panel[0])
 
+    half = probes // 2
+    far = lax.ppermute(actuator_panel[0], "probe", [(i, i ^ half) for i in range(probes)])
+    coef = tied(coef, far)
     field_shape = pltpu.VMEM((planes, columns, height + 2 * PAD, TILE), f32)
     tiles = call(
         adjoint_kernel,
@@ -358,7 +361,7 @@
         inputs=5,
     )(probe_offset, coef, shifted, low, high)
 
-    panels = list(enumerate([[panel]] + gathered_panel(actuator_panel[0], "probe", coef, tiles)))
+    panels = list(enumerate([[panel]] + gathered_panel(actuator_panel[0], "probe", coef, far)))
 
     def project(shards, *given):
         pieces = [piece for _, pieces in shards for piece in pieces]

time: 57.4 us -> 55.8 us (0.972)
  starting transfers between devices: 16.9 us -> 14.4 us
  waiting for transfers between devices: 14.7 us -> 16.8 us
  local copies, waits for them, and re-layouts: 5.67 us -> 4.68 us
    ppermute x5 -> x2, starting transfers between devices: 7.17 us -> 2.34 us  [gathered_panel(): shards[held | mask] = [lax.ppermute(piece, axis, pairs) for piece in pieces]]
    ppermute x0 -> x1, starting transfers between devices: none -> 4.1 us  [local(): lax.ppermute(actuator_panel[0], 'probe', [(i, i ^ half) for i in range(pr...]
    ppermute x0 -> x1, waiting for transfers between devices: none -> 2.64 us  [local(): lax.ppermute(actuator_panel[0], 'probe', [(i, i ^ half) for i in range(pr...]
    ppermute x5 -> x2, waiting for transfers between devices: 2.22 us -> 0.01 us  [gathered_panel(): shards[held | mask] = [lax.ppermute(piece, axis, pairs) for piece in pieces]]
    ppermute x1, starting transfers between devices: 3.39 us -> 1.61 us  [local(): high = lax.ppermute(own, 'state', shift_pairs(slabs, -1))]
    ppermute x4, waiting for transfers between devices: 4.21 us -> 5.92 us  [summands(): parts = [part] + [lax.ppermute(part, axis, pair) for pair in pairs]]
    slice x1 -> x0, local copies, waits for them, and re-layouts: 0.99 us -> none  [gathered_panel(): pieces = [panel[:rows // 2], panel[rows // 2:]]]
  transfers between devices with their start and end apart: 13 -> 11, of which waited for: 7 -> 7; matrix products, arithmetic and copies ran while one was open for 5% -> 3% of each run, Pallas kernels for 13% -> 14%
where the time goes in v12:
time: 55.8 us; the launch traced here: 55.5 us
  Pallas kernels  17.2 us (31%)
  waiting for transfers between devices  16.8 us (30%)
  starting transfers between devices  14.4 us (26%)
  local copies, waits for them, and re-layouts  4.68 us (8%)
  between operations  1.37 us (2%)
  other arithmetic  1.09 us (2%)
    pallas_call x2, Pallas kernels, project(): call(lambda *refs: project_kernel(layout(shards), shard, *refs), jax.Shap...  6.46 us
    ppermute x4, waiting for transfers between devices, summands(): parts = [part] + [lax.ppermute(part, axis, pair) for pair in pairs]  5.92 us
    ppermute x1, waiting for transfers between devices, local(): from_high = lax.ppermute(leftward, 'state', shift_pairs(slabs, -1))  5.47 us
    pallas_call x1, Pallas kernels, local(): call(lambda *refs: deposit_kernel(len(parts), layout(panels), shard, *ref...  4.64 us
    ppermute x1, starting transfers between devices, local(): lax.ppermute(actuator_panel[0], 'probe', [(i, i ^ half) for i in range(pr...  4.1 us
    unnamed x10, local copies, waits for them, and re-layouts  4.01 us
    ppermute x4, starting transfers between devices, summands(): parts = [part] + [lax.ppermute(part, axis, pair) for pair in pairs]  3.62 us
    pallas_call x1, Pallas kernels, local(): call(forward_kernel, jax.ShapeDtypeStruct((cells, height, width), f32), v...  2.83 us
  transfers between devices with their start and end apart: 11, of which 7 were waited for; matrix products, arithmetic and copies ran while one was open for 3% of the time, Pallas kernels for 14%

profile of v12, /device:TPU:0, one launch (start us, length us, event | category | flops | bytes accessed | tf_op | source)
XLA Modules:
  0.0 55.5 jit_solution(15395999125332906576)
XLA Ops:
  0.6 4.1 %collective-permute-start = (bf16[1024,128]{1,0:T(8,128)(2,1)}, bf16[1024,128]{1,0:T(8,128)(2,1)S(1)}, u32[]{:S(2)}, u32[]{:S(2)}) collective-permute-start(bf16[1024,128]{1,0:T(8,128)(2,1)} %bitcast.12), channel_id=1, source_target_pairs={{0,2},{1,3},{2,0},{3,1},{4,6},{5,7},{6,4},{7,5},{8,10},{9,11},{10,... | collective-permute-start | bytes 786440 | tf_op jit(solution)/shard_map/ppermute | solution.py:352
  4.7 1.6 %collective-permute-start.2 = (f32[4,64,512]{2,1,0:T(8,128)}, f32[4,64,512]{2,1,0:T(8,128)S(1)}, u32[]{:S(2)}, u32[]{:S(2)}) collective-permute-start(f32[4,64,512]{2,1,0:T(8,128)} %bitcast.10), channel_id=1, source_target_pairs={{0,28},{4,0},{8,4},{12,8},{16,12},{20,16},{24,20},{28,24},{1,29},{... | collective-permute-start | bytes 1572872 | tf_op jit(solution)/shard_map/ppermute | solution.py:335
  6.3 1.6 %collective-permute-start.4 = (bf16[1024,128]{1,0:T(8,128)(2,1)}, bf16[1024,128]{1,0:T(8,128)(2,1)S(1)}, u32[]{:S(2)}, u32[]{:S(2)}) collective-permute-start(bf16[1024,128]{1,0:T(8,128)(2,1)} %bitcast.13), channel_id=1, source_target_pairs={{0,1},{1,0},{2,3},{3,2},{4,5},{5,4},{6,7},{7,6},{8,9},{9,8},{10,11... | collective-permute-start | bytes 786440 | tf_op jit(solution)/shard_map/ppermute | solution.py:282
  7.9 1.1 %bitcast_convert_fusion = bf16[4,64,512]{2,1,0:T(8,128)(2,1)S(1)} fusion(f32[1,4,64,512]{3,2,1,0:T(8,128)} %param.6), kind=kLoop, calls=%fused_computation.1 | loop fusion | flops 131072 | bytes 786432 | tf_op jit(solution)/shard_map/convert_element_type | solution.py:336
  9.0 0.1 collective-permute-start.1
  9.7 0.0 copy-start
  9.7 1.0 %copy-done = f32[1,4,64,512]{3,2,1,0:T(8,128)S(1)} copy-done((f32[1,4,64,512]{3,2,1,0:T(8,128)S(1)}, f32[1,4,64,512]{3,2,1,0:T(8,128)}, u32[]{:S(2)}) %copy-start) | copy-done | bytes 524312
  10.7 0.0 copy-start.1
  10.8 0.9 %copy-done.1 = bf16[1,1024,128]{2,1,0:T(8,128)(2,1)S(1)} copy-done((bf16[1,1024,128]{2,1,0:T(8,128)(2,1)S(1)}, bf16[1,1024,128]{2,1,0:T(8,128)(2,1)}, u32[]{:S(2)}) %copy-start.1) | copy-done | bytes 262168
  11.7 0.0 copy-start.2
  11.7 0.7 %copy-done.2 = s32[1,4096]{1,0:T(1,128)S(1)} copy-done((s32[1,4096]{1,0:T(1,128)S(1)}, s32[1,4096]{1,0:T(1,128)}, u32[]{:S(2)}) %copy-start.2) | copy-done | bytes 16408
  12.4 0.0 copy-start.3
  12.4 0.7 %copy-done.3 = f32[64]{0:T(128)S(1)} copy-done((f32[64]{0:T(128)S(1)}, f32[64]{0:T(128)}, u32[]{:S(2)}) %copy-start.3) | copy-done | bytes 280
  13.1 0.0 copy-start.4
  13.1 0.7 %copy-done.4 = f32[64]{0:T(128)S(1)} copy-done((f32[64]{0:T(128)S(1)}, f32[64]{0:T(128)}, u32[]{:S(2)}) %copy-start.4) | copy-done | bytes 280
  13.7 0.6 %shard_map.77 = (f32[4,4,64,128]{3,2,1,0:T(8,128)S(1)}, f32[5,64,128]{2,1,0:T(8,128)S(1)}, s32[1,4096]{1,0:T(1,128)S(1)}, bf16[1024,128]{1,0:T(8,128)(2,1)S(1)}) custom-call(s32[1]{0:T(128)S(6)} %copy.9.offset, f32[4,64,512]{2,1,0:T(8,128)S(1)} %bitcast.11, f32[1,64]{1,0:T(1,128)S(1)} %bitcast.16, f32[1,64]{1,0:T(1,128)S(1)} %bitcast.17, ...), custom_call_target="tpu_custom_call" | custom-call | flops 1024 | bytes 1024 | tf_op jit(solution)/shard_map/pallas_call | solution.py:338
  14.3 2.6 %collective-permute-done.refs_5_.refs_8_ = bf16[1024,128]{1,0:T(8,128)(2,1)S(1)} collective-permute-done((bf16[1024,128]{1,0:T(8,128)(2,1)}, bf16[1024,128]{1,0:T(8,128)(2,1)S(1)}, u32[]{:S(2)}, u32[]{:S(2)}) %collective-permute-start) | collective-permute-done | bytes 262176 | tf_op jit(solution)/shard_map/ppermute | solution.py:352
  17.0 0.8 %collective-permute-start.3 = (bf16[1024,128]{1,0:T(8,128)(2,1)S(1)}, bf16[1024,128]{1,0:T(8,128)(2,1)S(1)}, u32[]{:S(2)}, u32[]{:S(2)}) collective-permute-start(bf16[1024,128]{1,0:T(8,128)(2,1)S(1)} %collective-permute-done.refs_5_.refs_8_), channel_id=1, source_target_pairs={{0,1},{1,0},{2,3},{3,2},{4,5},{5,4},{6,7},{7,6},{8,9},{9,8},{10,11... | collective-permute-start | bytes 786440 | tf_op jit(solution)/shard_map/ppermute | solution.py:282
  17.7 0.0 collective-permute-done.1.low
  17.7 0.0 collective-permute-done.2.high
  17.7 2.6 %shard_map.78.refs_2_ = f32[4112,128]{1,0:T(8,128)S(1)} custom-call(s32[1]{0:T(128)S(6)} %copy.9.offset, f32[5,64,128]{2,1,0:T(8,128)S(1)} %get-tuple-element.14.coef, f32[4,4,64,128]{3,2,1,0:T(8,128)S(1)} %get-tuple-element.15.own, bf16[4,64,512]{2,1,0:T(8,128)(2,1)S(1)} %collective-permute-done.1.low, f32[4,64,512]{2,1,0:T(8,128)S(1)} %collective-permute-done.2.high), custom_call_target="tpu_custom_call" | custom-call | flops 1024 | bytes 1024 | tf_op jit(solution)/shard_map/pallas_call | solution.py:355
  20.4 0.0 collective-permute-done.4.refs_4_.refs_7_
  20.4 4.4 %shard_map.79.refs_4_ = f32[16,8,128]{2,1,0:T(8,128)S(1)} custom-call(s32[4]{0:T(128)S(1)} %iota_xor_fusion.refs_0_, s32[1,4096]{1,0:T(1,128)S(1)} %get-tuple-element.12.refs_1_, f32[4112,128]{1,0:T(8,128)S(1)} %shard_map.78.refs_2_, bf16[1024,128]{1,0:T(8,128)(2,1)S(1)} %get-tuple-element.17.refs_3_.refs_6_, ...), custom_call_target="tpu_custom_call" | custom-call | flops 1024 | bytes 1024 | tf_op jit(solution)/shard_map/pallas_call | solution.py:368
  24.8 0.0 collective-permute-done.3.refs_3_.refs_9_
  24.8 2.0 %shard_map.80 = f32[16,8,128]{2,1,0:T(8,128)S(1)} custom-call(s32[4]{0:T(128)S(1)} %iota_xor_fusion.refs_0_, s32[1,4096]{1,0:T(1,128)S(1)} %get-tuple-element.12.refs_1_, f32[4112,128]{1,0:T(8,128)S(1)} %shard_map.78.refs_2_, bf16[1024,128]{1,0:T(8,128)(2,1)S(1)} %collective-permute-done.3.refs_3_.refs_9_, f32[16,8,128]{2,1,0:T(8,128)S(1)} %shard_map.79.refs_4_), custom_call_target="tpu_custom_call" | custom-call | flops 1024 | bytes 1024 | tf_op jit(solution)/shard_map/pallas_call | solution.py:368
  26.9 0.1 collective-permute-start.5
  27.0 1.2 %collective-permute-done.5 = f32[16,8,128]{2,1,0:T(8,128)S(1)} collective-permute-done((f32[16,8,128]{2,1,0:T(8,128)S(1)}, f32[16,8,128]{2,1,0:T(8,128)S(1)}, u32[]{:S(2)}, u32[]{:S(2)}) %collective-permute-start.5) | collective-permute-done | bytes 65568 | tf_op jit(solution)/shard_map/ppermute | solution.py:317
  28.2 1.6 %collective-permute-start.6 = (f32[16,8,128]{2,1,0:T(8,128)S(1)}, f32[16,8,128]{2,1,0:T(8,128)S(1)}, u32[]{:S(2)}, u32[]{:S(2)}) collective-permute-start(f32[16,8,128]{2,1,0:T(8,128)S(1)} %add.3.refs_2_), channel_id=1, source_target_pairs={{0,8},{4,12},{8,0},{12,4},{16,24},{20,28},{24,16},{28,20},{1,9},{5... | collective-permute-start | bytes 196616 | tf_op jit(solution)/shard_map/ppermute | solution.py:317
  29.8 1.5 %collective-permute-start.7 = (f32[16,8,128]{2,1,0:T(8,128)S(1)}, f32[16,8,128]{2,1,0:T(8,128)S(1)}, u32[]{:S(2)}, u32[]{:S(2)}) collective-permute-start(f32[16,8,128]{2,1,0:T(8,128)S(1)} %add.3.refs_2_), channel_id=1, source_target_pairs={{0,16},{4,20},{8,24},{12,28},{16,0},{20,4},{24,8},{28,12},{1,17},{... | collective-permute-start | bytes 196616 | tf_op jit(solution)/shard_map/ppermute | solution.py:317
  31.3 0.5 collective-permute-start.8
  31.8 0.8 %collective-permute-done.6.refs_3_ = f32[16,8,128]{2,1,0:T(8,128)S(1)} collective-permute-done((f32[16,8,128]{2,1,0:T(8,128)S(1)}, f32[16,8,128]{2,1,0:T(8,128)S(1)}, u32[]{:S(2)}, u32[]{:S(2)}) %collective-permute-start.6) | collective-permute-done | bytes 65568 | tf_op jit(solution)/shard_map/ppermute | solution.py:317
  32.5 1.5 %collective-permute-done.7.refs_4_ = f32[16,8,128]{2,1,0:T(8,128)S(1)} collective-permute-done((f32[16,8,128]{2,1,0:T(8,128)S(1)}, f32[16,8,128]{2,1,0:T(8,128)S(1)}, u32[]{:S(2)}, u32[]{:S(2)}) %collective-permute-start.7) | collective-permute-done | bytes 65568 | tf_op jit(solution)/shard_map/ppermute | solution.py:317
  34.0 2.4 %collective-permute-done.8.refs_5_ = f32[16,8,128]{2,1,0:T(8,128)S(1)} collective-permute-done((f32[16,8,128]{2,1,0:T(8,128)S(1)}, f32[16,8,128]{2,1,0:T(8,128)S(1)}, u32[]{:S(2)}, u32[]{:S(2)}) %collective-permute-start.8) | collective-permute-done | bytes 65568 | tf_op jit(solution)/shard_map/ppermute | solution.py:317
  36.4 4.6 %shard_map.81 = (f32[16,8,128]{2,1,0:T(8,128)S(1)}, f32[4,256,128]{2,1,0:T(8,128)S(1)}, bf16[7,256,128]{2,1,0:T(8,128)(2,1)S(1)}, bf16[4,256,128]{2,1,0:T(8,128)(2,1)S(1)}) custom-call(s32[4]{0:T(128)S(1)} %iota_xor_fusion.refs_0_, s32[1,4096]{1,0:T(1,128)S(1)} %get-tuple-element.12.refs_1_, f32[16,8,128]{2,1,0:T(8,128)S(1)} %add.3.refs_2_, ...), custom_call_target="tpu_custom_call" | custom-call | flops 1024 | bytes 1024 | tf_op jit(solution)/shard_map/pallas_call | solution.py:382
  41.1 0.1 collective-permute-start.9
  41.2 2.6 %collective-permute-start.10 = (bf16[4,256,128]{2,1,0:T(8,128)(2,1)S(1)}, bf16[4,256,128]{2,1,0:T(8,128)(2,1)S(1)}, u32[]{:S(2)}, u32[]{:S(2)}) collective-permute-start(bf16[4,256,128]{2,1,0:T(8,128)(2,1)S(1)} %get-tuple-element.21), channel_id=1, source_target_pairs={{0,28},{4,0},{8,4},{12,8},{16,12},{20,16},{24,20},{28,24},{1,29},{... | collective-permute-start | bytes 786440 | tf_op jit(solution)/shard_map/ppermute | solution.py:400
  43.8 0.7 %copy.8 = f32[4,16,2,128]{3,2,1,0:T(2,128)} copy(f32[4,16,2,128]{3,0,2,1:T(4,128)S(1)} %bitcast.15) | data formatting | bytes 131072 | tf_op jit(solution)/shard_map/transpose | solution.py:408
  44.5 5.5 %collective-permute-done.10.high = bf16[4,256,128]{2,1,0:T(8,128)(2,1)S(1)} collective-permute-done((bf16[4,256,128]{2,1,0:T(8,128)(2,1)S(1)}, bf16[4,256,128]{2,1,0:T(8,128)(2,1)S(1)}, u32[]{:S(2)}, u32[]{:S(2)}) %collective-permute-start.10) | collective-permute-done | bytes 262176 | tf_op jit(solution)/shard_map/ppermute | solution.py:400
  49.9 2.7 %collective-permute-done.9.low = bf16[7,256,128]{2,1,0:T(8,128)(2,1)S(1)} collective-permute-done((bf16[7,256,128]{2,1,0:T(8,128)(2,1)S(1)}, bf16[7,256,128]{2,1,0:T(8,128)(2,1)S(1)}, u32[]{:S(2)}, u32[]{:S(2)}) %collective-permute-start.9) | collective-permute-done | bytes 458784 | tf_op jit(solution)/shard_map/ppermute | solution.py:399
  52.6 2.8 %shard_map.82 = f32[4,64,512]{2,1,0:T(8,128)} custom-call(f32[5,64,128]{2,1,0:T(8,128)S(1)} %get-tuple-element.14.coef, f32[4,256,128]{2,1,0:T(8,128)S(1)} %get-tuple-element.19.own, bf16[7,256,128]{2,1,0:T(8,128)(2,1)S(1)} %collective-permute-done.9.low, bf16[4,256,128]{2,1,0:T(8,128)(2,1)S(1)} %collective-permute-done.10.high), custom_call_target="tpu_custom_call" | custom-call | flops 1024 | bytes 1024 | tf_op jit(solution)/shard_map/pallas_call | solution.py:401
  (2 shorter events, 0.0 us)
Async XLA Ops:
  0.6 16.3 %collective-permute-start = (bf16[1024,128]{1,0:T(8,128)(2,1)}, bf16[1024,128]{1,0:T(8,128)(2,1)S(1)}, u32[]{:S(2)}, u32[]{:S(2)}) collective-permute-start(bf16[1024,128]{1,0:T(8,128)(2,1)} %bitcast.12), channel_id=1, source_target_pairs={{0,2},{1,3},{2,0},{3,1},{4,6},{5,7},{6,4},{7,5},{8,10},{9,11},{10,... | collective-permute-start | bytes 786440 | tf_op jit(solution)/shard_map/ppermute | solution.py:352
  4.7 13.0 %collective-permute-start.2 = (f32[4,64,512]{2,1,0:T(8,128)}, f32[4,64,512]{2,1,0:T(8,128)S(1)}, u32[]{:S(2)}, u32[]{:S(2)}) collective-permute-start(f32[4,64,512]{2,1,0:T(8,128)} %bitcast.10), channel_id=1, source_target_pairs={{0,28},{4,0},{8,4},{12,8},{16,12},{20,16},{24,20},{28,24},{1,29},{... | collective-permute-start | bytes 1572872 | tf_op jit(solution)/shard_map/ppermute | solution.py:335
  6.3 14.1 %collective-permute-start.4 = (bf16[1024,128]{1,0:T(8,128)(2,1)}, bf16[1024,128]{1,0:T(8,128)(2,1)S(1)}, u32[]{:S(2)}, u32[]{:S(2)}) collective-permute-start(bf16[1024,128]{1,0:T(8,128)(2,1)} %bitcast.13), channel_id=1, source_target_pairs={{0,1},{1,0},{2,3},{3,2},{4,5},{5,4},{6,7},{7,6},{8,9},{9,8},{10,11... | collective-permute-start | bytes 786440 | tf_op jit(solution)/shard_map/ppermute | solution.py:282
  9.0 8.8 %collective-permute-start.1 = (bf16[4,64,512]{2,1,0:T(8,128)(2,1)S(1)}, bf16[4,64,512]{2,1,0:T(8,128)(2,1)S(1)}, u32[]{:S(2)}, u32[]{:S(2)}) collective-permute-start(bf16[4,64,512]{2,1,0:T(8,128)(2,1)S(1)} %bitcast_convert_fusion), channel_id=1, source_target_pairs={{0,4},{4,8},{8,12},{12,16},{16,20},{20,24},{24,28},{28,0},{1,5},{5... | collective-permute-start | bytes 786440 | tf_op jit(solution)/shard_map/ppermute | solution.py:336
  9.7 1.0 %copy-start = (f32[1,4,64,512]{3,2,1,0:T(8,128)S(1)}, f32[1,4,64,512]{3,2,1,0:T(8,128)}, u32[]{:S(2)}) copy-start(f32[1,4,64,512]{3,2,1,0:T(8,128)} %param.6) | copy-start | bytes 1572868
  10.7 0.9 %copy-start.1 = (bf16[1,1024,128]{2,1,0:T(8,128)(2,1)S(1)}, bf16[1,1024,128]{2,1,0:T(8,128)(2,1)}, u32[]{:S(2)}) copy-start(bf16[1,1024,128]{2,1,0:T(8,128)(2,1)} %param.11) | copy-start | bytes 786436
  11.7 0.7 %copy-start.2 = (s32[1,4096]{1,0:T(1,128)S(1)}, s32[1,4096]{1,0:T(1,128)}, u32[]{:S(2)}) copy-start(s32[1,4096]{1,0:T(1,128)} %tile.1) | copy-start | bytes 49156
  12.4 0.7 %copy-start.3 = (f32[64]{0:T(128)S(1)}, f32[64]{0:T(128)}, u32[]{:S(2)}) copy-start(f32[64]{0:T(128)} %param.7) | copy-start | bytes 772
  13.1 0.7 %copy-start.4 = (f32[64]{0:T(128)S(1)}, f32[64]{0:T(128)}, u32[]{:S(2)}) copy-start(f32[64]{0:T(128)} %param.8) | copy-start | bytes 772
  17.0 7.9 %collective-permute-start.3 = (bf16[1024,128]{1,0:T(8,128)(2,1)S(1)}, bf16[1024,128]{1,0:T(8,128)(2,1)S(1)}, u32[]{:S(2)}, u32[]{:S(2)}) collective-permute-start(bf16[1024,128]{1,0:T(8,128)(2,1)S(1)} %collective-permute-done.refs_5_.refs_8_), channel_id=1, source_target_pairs={{0,1},{1,0},{2,3},{3,2},{4,5},{5,4},{6,7},{7,6},{8,9},{9,8},{10,11... | collective-permute-start | bytes 786440 | tf_op jit(solution)/shard_map/ppermute | solution.py:282
  26.9 1.3 %collective-permute-start.5 = (f32[16,8,128]{2,1,0:T(8,128)S(1)}, f32[16,8,128]{2,1,0:T(8,128)S(1)}, u32[]{:S(2)}, u32[]{:S(2)}) collective-permute-start(f32[16,8,128]{2,1,0:T(8,128)S(1)} %shard_map.80), channel_id=1, source_target_pairs={{0,4},{4,0},{8,12},{12,8},{16,20},{20,16},{24,28},{28,24},{1,5},{5... | collective-permute-start | bytes 196616 | tf_op jit(solution)/shard_map/ppermute | solution.py:317
  28.2 4.3 %collective-permute-start.6 = (f32[16,8,128]{2,1,0:T(8,128)S(1)}, f32[16,8,128]{2,1,0:T(8,128)S(1)}, u32[]{:S(2)}, u32[]{:S(2)}) collective-permute-start(f32[16,8,128]{2,1,0:T(8,128)S(1)} %add.3.refs_2_), channel_id=1, source_target_pairs={{0,8},{4,12},{8,0},{12,4},{16,24},{20,28},{24,16},{28,20},{1,9},{5... | collective-permute-start | bytes 196616 | tf_op jit(solution)/shard_map/ppermute | solution.py:317
  29.8 4.3 %collective-permute-start.7 = (f32[16,8,128]{2,1,0:T(8,128)S(1)}, f32[16,8,128]{2,1,0:T(8,128)S(1)}, u32[]{:S(2)}, u32[]{:S(2)}) collective-permute-start(f32[16,8,128]{2,1,0:T(8,128)S(1)} %add.3.refs_2_), channel_id=1, source_target_pairs={{0,16},{4,20},{8,24},{12,28},{16,0},{20,4},{24,8},{28,12},{1,17},{... | collective-permute-start | bytes 196616 | tf_op jit(solution)/shard_map/ppermute | solution.py:317
  31.3 5.2 %collective-permute-start.8 = (f32[16,8,128]{2,1,0:T(8,128)S(1)}, f32[16,8,128]{2,1,0:T(8,128)S(1)}, u32[]{:S(2)}, u32[]{:S(2)}) collective-permute-start(f32[16,8,128]{2,1,0:T(8,128)S(1)} %add.3.refs_2_), channel_id=1, source_target_pairs={{0,24},{4,28},{8,16},{12,20},{16,8},{20,12},{24,0},{28,4},{1,25},{... | collective-permute-start | bytes 196616 | tf_op jit(solution)/shard_map/ppermute | solution.py:317
  41.1 11.5 %collective-permute-start.9 = (bf16[7,256,128]{2,1,0:T(8,128)(2,1)S(1)}, bf16[7,256,128]{2,1,0:T(8,128)(2,1)S(1)}, u32[]{:S(2)}, u32[]{:S(2)}) collective-permute-start(bf16[7,256,128]{2,1,0:T(8,128)(2,1)S(1)} %get-tuple-element.20), channel_id=1, source_target_pairs={{0,4},{4,8},{8,12},{12,16},{16,20},{20,24},{24,28},{28,0},{1,5},{5... | collective-permute-start | bytes 1376264 | tf_op jit(solution)/shard_map/ppermute | solution.py:399
  41.2 8.8 %collective-permute-start.10 = (bf16[4,256,128]{2,1,0:T(8,128)(2,1)S(1)}, bf16[4,256,128]{2,1,0:T(8,128)(2,1)S(1)}, u32[]{:S(2)}, u32[]{:S(2)}) collective-permute-start(bf16[4,256,128]{2,1,0:T(8,128)(2,1)S(1)} %get-tuple-element.21), channel_id=1, source_target_pairs={{0,28},{4,0},{8,4},{12,8},{16,12},{20,16},{24,20},{28,24},{1,29},{... | collective-permute-start | bytes 786440 | tf_op jit(solution)/shard_map/ppermute | solution.py:400

commit v13 on v12

--- a/solution.py
+++ b/solution.py
@@ -202,7 +202,8 @@
             out[number] = sums
             return carry
 
-        lax.fori_loop(0, panel.shape[0] // GROUP, body, 0)
+        groups = panel.shape[0] // GROUP
+        lax.fori_loop(0, groups, body, 0, unroll=2 if groups % 2 == 0 else 1)
 
 
 def deposit_kernel(count, places, shard, source, start, *refs):
@@ -224,7 +225,7 @@
                 target[pl.ds(top, rows), pl.ds(left, TILE)] = found
 
     choose(0)
-    total[...] = tree_sum([part[...] for part in parts])
+    total[...] = tree_sum([part[...] for part in parts[::-1]])
     blocks = []
     for (chunk, offset), panel in zip(places, panels):
         for group in range(panel.shape[0] // GROUP):
@@ -313,8 +314,10 @@
         span = min(span, count // done)
         if span > 1:
             part = tree_sum(parts)
-            pairs = [[(i, i ^ (k * done)) for i in range(count)] for k in range(1, span)]
-            parts = [part] + [lax.ppermute(part, axis, pair) for pair in pairs]
+            came = {0: part}
+            for k in range(span - 1, 0, -1):
+                came[k] = lax.ppermute(part, axis, [(i, i ^ (k * done)) for i in range(count)])
+            parts = [came[k] for k in range(span)]
             done *= span
     return parts
 
@@ -395,7 +398,7 @@
         ),
         smem=1,
         inputs=2 + len(parts) + len(pieces),
-    )(source, start, *parts, *pieces)
+    )(source, start, *parts[::-1], *pieces)
     from_low = lax.ppermute(rightward, "state", shift_pairs(slabs, 1))
     from_high = lax.ppermute(leftward, "state", shift_pairs(slabs, -1))
     response = call(

time: 55.8 us -> 54.4 us (0.975)
  waiting for transfers between devices: 16.8 us -> 15.9 us
  Pallas kernels: 17.2 us -> 16.6 us
    ppermute x4, waiting for transfers between devices: 5.92 us -> 4.96 us  [summands(): lax.ppermute(part, axis, [(i, i ^ k * done) for i in range(count)])]
    pallas_call x2, Pallas kernels: 6.46 us -> 5.85 us  [project(): call(lambda *refs: project_kernel(layout(shards), shard, *refs), jax.Shap...]
  transfers between devices with their start and end apart: 11 -> 11, of which waited for: 7 -> 7; matrix products, arithmetic and copies ran while one was open for 3% -> 3% of each run, Pallas kernels for 14% -> 13%
where the time goes in v13:
time: 54.4 us; the launch traced here: 54 us
  Pallas kernels  16.6 us (31%)
  waiting for transfers between devices  15.9 us (29%)
  starting transfers between devices  14.4 us (26%)
  local copies, waits for them, and re-layouts  4.68 us (9%)
  between operations  1.36 us (2%)
  other arithmetic  1.09 us (2%)
    pallas_call x2, Pallas kernels, project(): call(lambda *refs: project_kernel(layout(shards), shard, *refs), jax.Shap...  5.85 us
    ppermute x1, waiting for transfers between devices, local(): from_high = lax.ppermute(leftward, 'state', shift_pairs(slabs, -1))  5.7 us
    ppermute x4, waiting for transfers between devices, summands(): lax.ppermute(part, axis, [(i, i ^ k * done) for i in range(count)])  4.96 us
    pallas_call x1, Pallas kernels, local(): call(lambda *refs: deposit_kernel(len(parts), layout(panels), shard, *ref...  4.64 us
    ppermute x1, starting transfers between devices, local(): lax.ppermute(actuator_panel[0], 'probe', [(i, i ^ half) for i in range(pr...  4.1 us
    unnamed x10, local copies, waits for them, and re-layouts  4.01 us
    ppermute x4, starting transfers between devices, summands(): lax.ppermute(part, axis, [(i, i ^ k * done) for i in range(count)])  3.62 us
    pallas_call x1, Pallas kernels, local(): call(forward_kernel, jax.ShapeDtypeStruct((cells, height, width), f32), v...  2.83 us
  transfers between devices with their start and end apart: 11, of which 7 were waited for; matrix products, arithmetic and copies ran while one was open for 3% of the time, Pallas kernels for 13%

profile of v13, /device:TPU:0, one launch (start us, length us, event | category | flops | bytes accessed | tf_op | source)
XLA Modules:
  0.0 54.0 jit_solution(11089650619132271848)
XLA Ops:
  0.6 4.1 %collective-permute-start = (bf16[1024,128]{1,0:T(8,128)(2,1)}, bf16[1024,128]{1,0:T(8,128)(2,1)S(1)}, u32[]{:S(2)}, u32[]{:S(2)}) collective-permute-start(bf16[1024,128]{1,0:T(8,128)(2,1)} %bitcast.12), channel_id=1, source_target_pairs={{0,2},{1,3},{2,0},{3,1},{4,6},{5,7},{6,4},{7,5},{8,10},{9,11},{10,... | collective-permute-start | bytes 786440 | tf_op jit(solution)/shard_map/ppermute | solution.py:355
  4.7 1.6 %collective-permute-start.2 = (f32[4,64,512]{2,1,0:T(8,128)}, f32[4,64,512]{2,1,0:T(8,128)S(1)}, u32[]{:S(2)}, u32[]{:S(2)}) collective-permute-start(f32[4,64,512]{2,1,0:T(8,128)} %bitcast.10), channel_id=1, source_target_pairs={{0,28},{4,0},{8,4},{12,8},{16,12},{20,16},{24,20},{28,24},{1,29},{... | collective-permute-start | bytes 1572872 | tf_op jit(solution)/shard_map/ppermute | solution.py:338
  6.3 1.6 %collective-permute-start.4 = (bf16[1024,128]{1,0:T(8,128)(2,1)}, bf16[1024,128]{1,0:T(8,128)(2,1)S(1)}, u32[]{:S(2)}, u32[]{:S(2)}) collective-permute-start(bf16[1024,128]{1,0:T(8,128)(2,1)} %bitcast.13), channel_id=1, source_target_pairs={{0,1},{1,0},{2,3},{3,2},{4,5},{5,4},{6,7},{7,6},{8,9},{9,8},{10,11... | collective-permute-start | bytes 786440 | tf_op jit(solution)/shard_map/ppermute | solution.py:283
  7.9 1.1 %bitcast_convert_fusion = bf16[4,64,512]{2,1,0:T(8,128)(2,1)S(1)} fusion(f32[1,4,64,512]{3,2,1,0:T(8,128)} %param.6), kind=kLoop, calls=%fused_computation.1 | loop fusion | flops 131072 | bytes 786432 | tf_op jit(solution)/shard_map/convert_element_type | solution.py:339
  9.0 0.1 collective-permute-start.1
  9.7 0.0 copy-start
  9.7 1.0 %copy-done = f32[1,4,64,512]{3,2,1,0:T(8,128)S(1)} copy-done((f32[1,4,64,512]{3,2,1,0:T(8,128)S(1)}, f32[1,4,64,512]{3,2,1,0:T(8,128)}, u32[]{:S(2)}) %copy-start) | copy-done | bytes 524312
  10.7 0.0 copy-start.1
  10.8 0.9 %copy-done.1 = bf16[1,1024,128]{2,1,0:T(8,128)(2,1)S(1)} copy-done((bf16[1,1024,128]{2,1,0:T(8,128)(2,1)S(1)}, bf16[1,1024,128]{2,1,0:T(8,128)(2,1)}, u32[]{:S(2)}) %copy-start.1) | copy-done | bytes 262168
  11.7 0.0 copy-start.2
  11.7 0.7 %copy-done.2 = s32[1,4096]{1,0:T(1,128)S(1)} copy-done((s32[1,4096]{1,0:T(1,128)S(1)}, s32[1,4096]{1,0:T(1,128)}, u32[]{:S(2)}) %copy-start.2) | copy-done | bytes 16408
  12.4 0.0 copy-start.3
  12.4 0.7 %copy-done.3 = f32[64]{0:T(128)S(1)} copy-done((f32[64]{0:T(128)S(1)}, f32[64]{0:T(128)}, u32[]{:S(2)}) %copy-start.3) | copy-done | bytes 280
  13.1 0.0 copy-start.4
  13.1 0.7 %copy-done.4 = f32[64]{0:T(128)S(1)} copy-done((f32[64]{0:T(128)S(1)}, f32[64]{0:T(128)}, u32[]{:S(2)}) %copy-start.4) | copy-done | bytes 280
  13.7 0.6 %shard_map.77 = (f32[4,4,64,128]{3,2,1,0:T(8,128)S(1)}, f32[5,64,128]{2,1,0:T(8,128)S(1)}, s32[1,4096]{1,0:T(1,128)S(1)}, bf16[1024,128]{1,0:T(8,128)(2,1)S(1)}) custom-call(s32[1]{0:T(128)S(6)} %copy.9.offset, f32[4,64,512]{2,1,0:T(8,128)S(1)} %bitcast.11, f32[1,64]{1,0:T(1,128)S(1)} %bitcast.16, f32[1,64]{1,0:T(1,128)S(1)} %bitcast.17, ...), custom_call_target="tpu_custom_call" | custom-call | flops 1024 | bytes 1024 | tf_op jit(solution)/shard_map/pallas_call | solution.py:341
  14.3 2.6 %collective-permute-done.refs_5_.refs_8_ = bf16[1024,128]{1,0:T(8,128)(2,1)S(1)} collective-permute-done((bf16[1024,128]{1,0:T(8,128)(2,1)}, bf16[1024,128]{1,0:T(8,128)(2,1)S(1)}, u32[]{:S(2)}, u32[]{:S(2)}) %collective-permute-start) | collective-permute-done | bytes 262176 | tf_op jit(solution)/shard_map/ppermute | solution.py:355
  17.0 0.8 %collective-permute-start.3 = (bf16[1024,128]{1,0:T(8,128)(2,1)S(1)}, bf16[1024,128]{1,0:T(8,128)(2,1)S(1)}, u32[]{:S(2)}, u32[]{:S(2)}) collective-permute-start(bf16[1024,128]{1,0:T(8,128)(2,1)S(1)} %collective-permute-done.refs_5_.refs_8_), channel_id=1, source_target_pairs={{0,1},{1,0},{2,3},{3,2},{4,5},{5,4},{6,7},{7,6},{8,9},{9,8},{10,11... | collective-permute-start | bytes 786440 | tf_op jit(solution)/shard_map/ppermute | solution.py:283
  17.7 0.0 collective-permute-done.1.low
  17.7 0.0 collective-permute-done.2.high
  17.7 2.6 %shard_map.78.refs_2_ = f32[4112,128]{1,0:T(8,128)S(1)} custom-call(s32[1]{0:T(128)S(6)} %copy.9.offset, f32[5,64,128]{2,1,0:T(8,128)S(1)} %get-tuple-element.14.coef, f32[4,4,64,128]{3,2,1,0:T(8,128)S(1)} %get-tuple-element.15.own, bf16[4,64,512]{2,1,0:T(8,128)(2,1)S(1)} %collective-permute-done.1.low, f32[4,64,512]{2,1,0:T(8,128)S(1)} %collective-permute-done.2.high), custom_call_target="tpu_custom_call" | custom-call | flops 1024 | bytes 1024 | tf_op jit(solution)/shard_map/pallas_call | solution.py:358
  20.4 0.0 collective-permute-done.4.refs_4_.refs_7_
  20.4 4.0 %shard_map.79.refs_4_ = f32[16,8,128]{2,1,0:T(8,128)S(1)} custom-call(s32[4]{0:T(128)S(1)} %iota_xor_fusion.refs_0_, s32[1,4096]{1,0:T(1,128)S(1)} %get-tuple-element.12.refs_1_, f32[4112,128]{1,0:T(8,128)S(1)} %shard_map.78.refs_2_, bf16[1024,128]{1,0:T(8,128)(2,1)S(1)} %get-tuple-element.17.refs_3_.refs_6_, ...), custom_call_target="tpu_custom_call" | custom-call | flops 1024 | bytes 1024 | tf_op jit(solution)/shard_map/pallas_call | solution.py:371
  24.4 0.0 collective-permute-done.3.refs_3_.refs_9_
  24.4 1.9 %shard_map.80 = f32[16,8,128]{2,1,0:T(8,128)S(1)} custom-call(s32[4]{0:T(128)S(1)} %iota_xor_fusion.refs_0_, s32[1,4096]{1,0:T(1,128)S(1)} %get-tuple-element.12.refs_1_, f32[4112,128]{1,0:T(8,128)S(1)} %shard_map.78.refs_2_, bf16[1024,128]{1,0:T(8,128)(2,1)S(1)} %collective-permute-done.3.refs_3_.refs_9_, f32[16,8,128]{2,1,0:T(8,128)S(1)} %shard_map.79.refs_4_), custom_call_target="tpu_custom_call" | custom-call | flops 1024 | bytes 1024 | tf_op jit(solution)/shard_map/pallas_call | solution.py:371
  26.3 0.1 collective-permute-start.5
  26.4 1.2 %collective-permute-done.5 = f32[16,8,128]{2,1,0:T(8,128)S(1)} collective-permute-done((f32[16,8,128]{2,1,0:T(8,128)S(1)}, f32[16,8,128]{2,1,0:T(8,128)S(1)}, u32[]{:S(2)}, u32[]{:S(2)}) %collective-permute-start.5) | collective-permute-done | bytes 65568 | tf_op jit(solution)/shard_map/ppermute | solution.py:319
  27.6 2.5 %collective-permute-start.6 = (f32[16,8,128]{2,1,0:T(8,128)S(1)}, f32[16,8,128]{2,1,0:T(8,128)S(1)}, u32[]{:S(2)}, u32[]{:S(2)}) collective-permute-start(f32[16,8,128]{2,1,0:T(8,128)S(1)} %add.3.refs_5_), channel_id=1, source_target_pairs={{0,24},{4,28},{8,16},{12,20},{16,8},{20,12},{24,0},{28,4},{1,25},{... | collective-permute-start | bytes 196616 | tf_op jit(solution)/shard_map/ppermute | solution.py:319
  30.1 0.5 collective-permute-start.7
  30.6 0.5 %collective-permute-start.8 = (f32[16,8,128]{2,1,0:T(8,128)S(1)}, f32[16,8,128]{2,1,0:T(8,128)S(1)}, u32[]{:S(2)}, u32[]{:S(2)}) collective-permute-start(f32[16,8,128]{2,1,0:T(8,128)S(1)} %add.3.refs_5_), channel_id=1, source_target_pairs={{0,8},{4,12},{8,0},{12,4},{16,24},{20,28},{24,16},{28,20},{1,9},{5... | collective-permute-start | bytes 196616 | tf_op jit(solution)/shard_map/ppermute | solution.py:319
  31.2 1.7 %collective-permute-done.6.refs_2_ = f32[16,8,128]{2,1,0:T(8,128)S(1)} collective-permute-done((f32[16,8,128]{2,1,0:T(8,128)S(1)}, f32[16,8,128]{2,1,0:T(8,128)S(1)}, u32[]{:S(2)}, u32[]{:S(2)}) %collective-permute-start.6) | collective-permute-done | bytes 65568 | tf_op jit(solution)/shard_map/ppermute | solution.py:319
  32.9 1.5 %collective-permute-done.7.refs_3_ = f32[16,8,128]{2,1,0:T(8,128)S(1)} collective-permute-done((f32[16,8,128]{2,1,0:T(8,128)S(1)}, f32[16,8,128]{2,1,0:T(8,128)S(1)}, u32[]{:S(2)}, u32[]{:S(2)}) %collective-permute-start.7) | collective-permute-done | bytes 65568 | tf_op jit(solution)/shard_map/ppermute | solution.py:319
  34.4 0.5 collective-permute-done.8.refs_4_
  34.9 4.6 %shard_map.81 = (f32[16,8,128]{2,1,0:T(8,128)S(1)}, f32[4,256,128]{2,1,0:T(8,128)S(1)}, bf16[7,256,128]{2,1,0:T(8,128)(2,1)S(1)}, bf16[4,256,128]{2,1,0:T(8,128)(2,1)S(1)}) custom-call(s32[4]{0:T(128)S(1)} %iota_xor_fusion.refs_0_, s32[1,4096]{1,0:T(1,128)S(1)} %get-tuple-element.12.refs_1_, f32[16,8,128]{2,1,0:T(8,128)S(1)} %collective-permute-done.6.refs_2_, ...), custom_call_target="tpu_custom_call" | custom-call | flops 1024 | bytes 1024 | tf_op jit(solution)/shard_map/pallas_call | solution.py:385
  39.5 0.1 collective-permute-start.9
  39.6 2.6 %collective-permute-start.10 = (bf16[4,256,128]{2,1,0:T(8,128)(2,1)S(1)}, bf16[4,256,128]{2,1,0:T(8,128)(2,1)S(1)}, u32[]{:S(2)}, u32[]{:S(2)}) collective-permute-start(bf16[4,256,128]{2,1,0:T(8,128)(2,1)S(1)} %get-tuple-element.21), channel_id=1, source_target_pairs={{0,28},{4,0},{8,4},{12,8},{16,12},{20,16},{24,20},{28,24},{1,29},{... | collective-permute-start | bytes 786440 | tf_op jit(solution)/shard_map/ppermute | solution.py:403
  42.2 0.7 %copy.8 = f32[4,16,2,128]{3,2,1,0:T(2,128)} copy(f32[4,16,2,128]{3,0,2,1:T(4,128)S(1)} %bitcast.15) | data formatting | bytes 131072 | tf_op jit(solution)/shard_map/transpose | solution.py:411
  42.9 5.7 %collective-permute-done.10.high = bf16[4,256,128]{2,1,0:T(8,128)(2,1)S(1)} collective-permute-done((bf16[4,256,128]{2,1,0:T(8,128)(2,1)S(1)}, bf16[4,256,128]{2,1,0:T(8,128)(2,1)S(1)}, u32[]{:S(2)}, u32[]{:S(2)}) %collective-permute-start.10) | collective-permute-done | bytes 262176 | tf_op jit(solution)/shard_map/ppermute | solution.py:403
  48.6 2.6 %collective-permute-done.9.low = bf16[7,256,128]{2,1,0:T(8,128)(2,1)S(1)} collective-permute-done((bf16[7,256,128]{2,1,0:T(8,128)(2,1)S(1)}, bf16[7,256,128]{2,1,0:T(8,128)(2,1)S(1)}, u32[]{:S(2)}, u32[]{:S(2)}) %collective-permute-start.9) | collective-permute-done | bytes 458784 | tf_op jit(solution)/shard_map/ppermute | solution.py:402
  51.2 2.8 %shard_map.82 = f32[4,64,512]{2,1,0:T(8,128)} custom-call(f32[5,64,128]{2,1,0:T(8,128)S(1)} %get-tuple-element.14.coef, f32[4,256,128]{2,1,0:T(8,128)S(1)} %get-tuple-element.19.own, bf16[7,256,128]{2,1,0:T(8,128)(2,1)S(1)} %collective-permute-done.9.low, bf16[4,256,128]{2,1,0:T(8,128)(2,1)S(1)} %collective-permute-done.10.high), custom_call_target="tpu_custom_call" | custom-call | flops 1024 | bytes 1024 | tf_op jit(solution)/shard_map/pallas_call | solution.py:404
  (2 shorter events, 0.0 us)
Async XLA Ops:
  0.6 16.3 %collective-permute-start = (bf16[1024,128]{1,0:T(8,128)(2,1)}, bf16[1024,128]{1,0:T(8,128)(2,1)S(1)}, u32[]{:S(2)}, u32[]{:S(2)}) collective-permute-start(bf16[1024,128]{1,0:T(8,128)(2,1)} %bitcast.12), channel_id=1, source_target_pairs={{0,2},{1,3},{2,0},{3,1},{4,6},{5,7},{6,4},{7,5},{8,10},{9,11},{10,... | collective-permute-start | bytes 786440 | tf_op jit(solution)/shard_map/ppermute | solution.py:355
  4.7 13.0 %collective-permute-start.2 = (f32[4,64,512]{2,1,0:T(8,128)}, f32[4,64,512]{2,1,0:T(8,128)S(1)}, u32[]{:S(2)}, u32[]{:S(2)}) collective-permute-start(f32[4,64,512]{2,1,0:T(8,128)} %bitcast.10), channel_id=1, source_target_pairs={{0,28},{4,0},{8,4},{12,8},{16,12},{20,16},{24,20},{28,24},{1,29},{... | collective-permute-start | bytes 1572872 | tf_op jit(solution)/shard_map/ppermute | solution.py:338
  6.3 14.1 %collective-permute-start.4 = (bf16[1024,128]{1,0:T(8,128)(2,1)}, bf16[1024,128]{1,0:T(8,128)(2,1)S(1)}, u32[]{:S(2)}, u32[]{:S(2)}) collective-permute-start(bf16[1024,128]{1,0:T(8,128)(2,1)} %bitcast.13), channel_id=1, source_target_pairs={{0,1},{1,0},{2,3},{3,2},{4,5},{5,4},{6,7},{7,6},{8,9},{9,8},{10,11... | collective-permute-start | bytes 786440 | tf_op jit(solution)/shard_map/ppermute | solution.py:283
  9.0 8.8 %collective-permute-start.1 = (bf16[4,64,512]{2,1,0:T(8,128)(2,1)S(1)}, bf16[4,64,512]{2,1,0:T(8,128)(2,1)S(1)}, u32[]{:S(2)}, u32[]{:S(2)}) collective-permute-start(bf16[4,64,512]{2,1,0:T(8,128)(2,1)S(1)} %bitcast_convert_fusion), channel_id=1, source_target_pairs={{0,4},{4,8},{8,12},{12,16},{16,20},{20,24},{24,28},{28,0},{1,5},{5... | collective-permute-start | bytes 786440 | tf_op jit(solution)/shard_map/ppermute | solution.py:339
  9.7 1.0 %copy-start = (f32[1,4,64,512]{3,2,1,0:T(8,128)S(1)}, f32[1,4,64,512]{3,2,1,0:T(8,128)}, u32[]{:S(2)}) copy-start(f32[1,4,64,512]{3,2,1,0:T(8,128)} %param.6) | copy-start | bytes 1572868
  10.7 0.9 %copy-start.1 = (bf16[1,1024,128]{2,1,0:T(8,128)(2,1)S(1)}, bf16[1,1024,128]{2,1,0:T(8,128)(2,1)}, u32[]{:S(2)}) copy-start(bf16[1,1024,128]{2,1,0:T(8,128)(2,1)} %param.11) | copy-start | bytes 786436
  11.7 0.7 %copy-start.2 = (s32[1,4096]{1,0:T(1,128)S(1)}, s32[1,4096]{1,0:T(1,128)}, u32[]{:S(2)}) copy-start(s32[1,4096]{1,0:T(1,128)} %tile.1) | copy-start | bytes 49156
  12.4 0.7 %copy-start.3 = (f32[64]{0:T(128)S(1)}, f32[64]{0:T(128)}, u32[]{:S(2)}) copy-start(f32[64]{0:T(128)} %param.7) | copy-start | bytes 772
  13.1 0.7 %copy-start.4 = (f32[64]{0:T(128)S(1)}, f32[64]{0:T(128)}, u32[]{:S(2)}) copy-start(f32[64]{0:T(128)} %param.8) | copy-start | bytes 772
  17.0 7.4 %collective-permute-start.3 = (bf16[1024,128]{1,0:T(8,128)(2,1)S(1)}, bf16[1024,128]{1,0:T(8,128)(2,1)S(1)}, u32[]{:S(2)}, u32[]{:S(2)}) collective-permute-start(bf16[1024,128]{1,0:T(8,128)(2,1)S(1)} %collective-permute-done.refs_5_.refs_8_), channel_id=1, source_target_pairs={{0,1},{1,0},{2,3},{3,2},{4,5},{5,4},{6,7},{7,6},{8,9},{9,8},{10,11... | collective-permute-start | bytes 786440 | tf_op jit(solution)/shard_map/ppermute | solution.py:283
  26.3 1.3 %collective-permute-start.5 = (f32[16,8,128]{2,1,0:T(8,128)S(1)}, f32[16,8,128]{2,1,0:T(8,128)S(1)}, u32[]{:S(2)}, u32[]{:S(2)}) collective-permute-start(f32[16,8,128]{2,1,0:T(8,128)S(1)} %shard_map.80), channel_id=1, source_target_pairs={{0,4},{4,0},{8,12},{12,8},{16,20},{20,16},{24,28},{28,24},{1,5},{5... | collective-permute-start | bytes 196616 | tf_op jit(solution)/shard_map/ppermute | solution.py:319
  27.6 5.3 %collective-permute-start.6 = (f32[16,8,128]{2,1,0:T(8,128)S(1)}, f32[16,8,128]{2,1,0:T(8,128)S(1)}, u32[]{:S(2)}, u32[]{:S(2)}) collective-permute-start(f32[16,8,128]{2,1,0:T(8,128)S(1)} %add.3.refs_5_), channel_id=1, source_target_pairs={{0,24},{4,28},{8,16},{12,20},{16,8},{20,12},{24,0},{28,4},{1,25},{... | collective-permute-start | bytes 196616 | tf_op jit(solution)/shard_map/ppermute | solution.py:319
  30.1 4.3 %collective-permute-start.7 = (f32[16,8,128]{2,1,0:T(8,128)S(1)}, f32[16,8,128]{2,1,0:T(8,128)S(1)}, u32[]{:S(2)}, u32[]{:S(2)}) collective-permute-start(f32[16,8,128]{2,1,0:T(8,128)S(1)} %add.3.refs_5_), channel_id=1, source_target_pairs={{0,16},{4,20},{8,24},{12,28},{16,0},{20,4},{24,8},{28,12},{1,17},{... | collective-permute-start | bytes 196616 | tf_op jit(solution)/shard_map/ppermute | solution.py:319
  30.6 4.3 %collective-permute-start.8 = (f32[16,8,128]{2,1,0:T(8,128)S(1)}, f32[16,8,128]{2,1,0:T(8,128)S(1)}, u32[]{:S(2)}, u32[]{:S(2)}) collective-permute-start(f32[16,8,128]{2,1,0:T(8,128)S(1)} %add.3.refs_5_), channel_id=1, source_target_pairs={{0,8},{4,12},{8,0},{12,4},{16,24},{20,28},{24,16},{28,20},{1,9},{5... | collective-permute-start | bytes 196616 | tf_op jit(solution)/shard_map/ppermute | solution.py:319
  39.5 11.7 %collective-permute-start.9 = (bf16[7,256,128]{2,1,0:T(8,128)(2,1)S(1)}, bf16[7,256,128]{2,1,0:T(8,128)(2,1)S(1)}, u32[]{:S(2)}, u32[]{:S(2)}) collective-permute-start(bf16[7,256,128]{2,1,0:T(8,128)(2,1)S(1)} %get-tuple-element.20), channel_id=1, source_target_pairs={{0,4},{4,8},{8,12},{12,16},{16,20},{20,24},{24,28},{28,0},{1,5},{5... | collective-permute-start | bytes 1376264 | tf_op jit(solution)/shard_map/ppermute | solution.py:402
  39.6 9.0 %collective-permute-start.10 = (bf16[4,256,128]{2,1,0:T(8,128)(2,1)S(1)}, bf16[4,256,128]{2,1,0:T(8,128)(2,1)S(1)}, u32[]{:S(2)}, u32[]{:S(2)}) collective-permute-start(bf16[4,256,128]{2,1,0:T(8,128)(2,1)S(1)} %get-tuple-element.21), channel_id=1, source_target_pairs={{0,28},{4,0},{8,4},{12,8},{16,12},{20,16},{24,20},{28,24},{1,29},{... | collective-permute-start | bytes 786440 | tf_op jit(solution)/shard_map/ppermute | solution.py:403

commit v14 on v13

--- a/solution.py
+++ b/solution.py
@@ -206,12 +206,20 @@
         lax.fori_loop(0, groups, body, 0, unroll=2 if groups % 2 == 0 else 1)
 
 
-def deposit_kernel(count, places, shard, source, start, *refs):
-    parts, panels = refs[:count], refs[count:-7]
+def deposit_kernel(order, places, shard, source, start, *refs):
+    parts, panels = refs[: len(order)], refs[len(order) : -7]
     total, field, rightward, leftward, scaled, *chosen = refs[-7:]
     cells, per_plane = field.shape[0], field.shape[1]
-    tile = start[...].astype(jnp.int16)
+    blocks = []
+    for (chunk, offset), panel in zip(places, panels):
+        for group in range(panel.shape[0] // GROUP):
+            number = source[chunk] * shard + offset + group
+            blocks += [(number, half, panel, group * GROUP + half * TILE) for half in range(2)]
     one, none = jnp.ones((), jnp.bfloat16), jnp.zeros((), jnp.bfloat16)
+    tiles = []
+    for number, half, _, _ in blocks:
+        where = pl.ds(pl.multiple_of(number * GROUP + half * TILE, TILE), TILE)
+        tiles.append(start[:, where].astype(jnp.int16))
 
     def choose(plane):
         target = chosen[plane % 2]
@@ -220,30 +228,11 @@
             first = (plane * per_plane + top) * STEPS
             by_row = lax.broadcasted_iota(jnp.int32, (rows, TILE), 0) * STEPS + first
             by_row = by_row.astype(jnp.int16)
-            for left in range(0, tile.shape[1], TILE):
-                found = jnp.where(tile[:, left : left + TILE] == by_row, one, none)
-                target[pl.ds(top, rows), pl.ds(left, TILE)] = found
-
-    choose(0)
-    total[...] = tree_sum([part[...] for part in parts[::-1]])
-    blocks = []
-    for (chunk, offset), panel in zip(places, panels):
-        for group in range(panel.shape[0] // GROUP):
-            number = source[chunk] * shard + offset + group
-            blocks += [(number, half, panel, group * GROUP + half * TILE) for half in range(2)]
-    last = [total[number, pl.ds(half * STEPS + STEPS - 1, 1), :] for number, half, _, _ in blocks]
-    drive = jnp.concatenate(last, axis=0).T
-    for place, (number, half, panel, row) in enumerate(blocks):
-        rows = panel[pl.ds(row, TILE), :].astype(jnp.float32)
-        head, tail = split(drive[:, place : place + 1] * rows)
-        where = pl.ds(pl.multiple_of(number * GROUP + half * TILE, TILE), TILE)
-        scaled[where, pl.ds(0, TILE)] = head
-        scaled[where, pl.ds(TILE, TILE)] = tail
-
-    for plane in range(cells):
-        if plane < cells - 1:
-            choose(plane + 1)
-        sums = jnp.dot(chosen[plane % 2][...], scaled[...], preferred_element_type=jnp.float32)
+            for place, tile in enumerate(tiles):
+                found = jnp.where(tile == by_row, one, none)
+                target[pl.ds(top, rows), pl.ds(place * TILE, TILE)] = found
+
+    def finish(plane, sums):
         value = sums[:, :TILE] + sums[:, TILE:]
         field[plane] = value
         head, tail = split(value)
@@ -251,6 +240,31 @@
         rightward[plane] = head
         if plane > 0:
             rightward[cells + plane - 1] = tail
+
+    choose(0)
+    summed = dict(zip(order, [part[...] for part in parts]))
+    total[...] = tree_sum([summed[k] for k in range(len(parts))])
+    last = [total[number, pl.ds(half * STEPS + STEPS - 1, 1), :] for number, half, _, _ in blocks]
+    drive = jnp.concatenate(last, axis=0).T
+    sums = jnp.zeros((per_plane, 2 * TILE), jnp.float32)
+    for place, (_, half, panel, row) in enumerate(blocks):
+        rows = panel[pl.ds(row, TILE), :].astype(jnp.float32)
+        head, tail = split(drive[:, place : place + 1] * rows)
+        scaled[pl.ds(place * TILE, TILE), pl.ds(0, TILE)] = head
+        scaled[pl.ds(place * TILE, TILE), pl.ds(TILE, TILE)] = tail
+        if half:
+            where = pl.ds((place - 1) * TILE, GROUP)
+            sums = sums + jnp.dot(
+                chosen[0][:, where], scaled[where, :], preferred_element_type=jnp.float32
+            )
+    choose(1)
+    finish(0, sums)
+    for plane in range(1, cells):
+        if plane < cells - 1:
+            choose(plane + 1)
+        finish(
+            plane, jnp.dot(chosen[plane % 2][...], scaled[...], preferred_element_type=jnp.float32)
+        )
 
 
 def call(kernel, out_shape, vmem, scratch=(), smem=0, inputs=0):
@@ -380,10 +394,11 @@
     before = project(panels[:-1])
     parts = summands(project(panels[-1:], before), "state")
     pieces = [piece for _, pieces in panels for piece in pieces]
+    order = [len(parts) - 1] + list(range(1, len(parts) - 1)) + [0] if len(parts) > 1 else [0]
     payload = jax.ShapeDtypeStruct((2 * cells - 1, height * columns, TILE), bf16)
     heads = jax.ShapeDtypeStruct((cells, height * columns, TILE), bf16)
     total, forced, rightward, leftward = call(
-        lambda *refs: deposit_kernel(len(parts), layout(panels), shard, *refs),
+        lambda *refs: deposit_kernel(order, layout(panels), shard, *refs),
         (
             jax.ShapeDtypeStruct(before.shape, f32),
             jax.ShapeDtypeStruct((cells, height * columns, TILE), f32),
@@ -398,7 +413,7 @@
         ),
         smem=1,
         inputs=2 + len(parts) + len(pieces),
-    )(source, start, *parts[::-1], *pieces)
+    )(source, start, *[parts[k] for k in order], *pieces)
     from_low = lax.ppermute(rightward, "state", shift_pairs(slabs, 1))
     from_high = lax.ppermute(leftward, "state", shift_pairs(slabs, -1))
     response = call(

time: 54.4 us -> 54.3 us (level)
  no operation moved by 1% of the time
where the time goes in v14:
time: 54.3 us; the launch traced here: 53.9 us
  Pallas kernels  16.5 us (30%)
  waiting for transfers between devices  16 us (29%)
  starting transfers between devices  14.4 us (27%)
  local copies, waits for them, and re-layouts  4.68 us (9%)
  between operations  1.36 us (3%)
  other arithmetic  1.09 us (2%)
    ppermute x1, waiting for transfers between devices, local(): from_high = lax.ppermute(leftward, 'state', shift_pairs(slabs, -1))  6.1 us
    pallas_call x2, Pallas kernels, project(): call(lambda *refs: project_kernel(layout(shards), shard, *refs), jax.Shap...  5.86 us
    ppermute x4, waiting for transfers between devices, summands(): lax.ppermute(part, axis, [(i, i ^ k * done) for i in range(count)])  4.98 us
    pallas_call x1, Pallas kernels, local(): call(lambda *refs: deposit_kernel(order, layout(panels), shard, *refs), (...  4.53 us
    ppermute x1, starting transfers between devices, local(): lax.ppermute(actuator_panel[0], 'probe', [(i, i ^ half) for i in range(pr...  4.1 us
    unnamed x10, local copies, waits for them, and re-layouts  4.01 us
    ppermute x4, starting transfers between devices, summands(): lax.ppermute(part, axis, [(i, i ^ k * done) for i in range(count)])  3.62 us
    pallas_call x1, Pallas kernels, local(): call(forward_kernel, jax.ShapeDtypeStruct((cells, height, width), f32), v...  2.83 us
  transfers between devices with their start and end apart: 11, of which 7 were waited for; matrix products, arithmetic and copies ran while one was open for 3% of the time, Pallas kernels for 13%

profile of v14, /device:TPU:0, one launch (start us, length us, event | category | flops | bytes accessed | tf_op | source)
XLA Modules:
  0.0 53.9 jit_solution(875675294484883105)
XLA Ops:
  0.6 4.1 %collective-permute-start = (bf16[1024,128]{1,0:T(8,128)(2,1)}, bf16[1024,128]{1,0:T(8,128)(2,1)S(1)}, u32[]{:S(2)}, u32[]{:S(2)}) collective-permute-start(bf16[1024,128]{1,0:T(8,128)(2,1)} %bitcast.12), channel_id=1, source_target_pairs={{0,2},{1,3},{2,0},{3,1},{4,6},{5,7},{6,4},{7,5},{8,10},{9,11},{10,... | collective-permute-start | bytes 786440 | tf_op jit(solution)/shard_map/ppermute | solution.py:369
  4.7 1.6 %collective-permute-start.2 = (f32[4,64,512]{2,1,0:T(8,128)}, f32[4,64,512]{2,1,0:T(8,128)S(1)}, u32[]{:S(2)}, u32[]{:S(2)}) collective-permute-start(f32[4,64,512]{2,1,0:T(8,128)} %bitcast.10), channel_id=1, source_target_pairs={{0,28},{4,0},{8,4},{12,8},{16,12},{20,16},{24,20},{28,24},{1,29},{... | collective-permute-start | bytes 1572872 | tf_op jit(solution)/shard_map/ppermute | solution.py:352
  6.3 1.6 %collective-permute-start.4 = (bf16[1024,128]{1,0:T(8,128)(2,1)}, bf16[1024,128]{1,0:T(8,128)(2,1)S(1)}, u32[]{:S(2)}, u32[]{:S(2)}) collective-permute-start(bf16[1024,128]{1,0:T(8,128)(2,1)} %bitcast.13), channel_id=1, source_target_pairs={{0,1},{1,0},{2,3},{3,2},{4,5},{5,4},{6,7},{7,6},{8,9},{9,8},{10,11... | collective-permute-start | bytes 786440 | tf_op jit(solution)/shard_map/ppermute | solution.py:297
  7.9 1.1 %bitcast_convert_fusion = bf16[4,64,512]{2,1,0:T(8,128)(2,1)S(1)} fusion(f32[1,4,64,512]{3,2,1,0:T(8,128)} %param.6), kind=kLoop, calls=%fused_computation.1 | loop fusion | flops 131072 | bytes 786432 | tf_op jit(solution)/shard_map/convert_element_type | solution.py:353
  9.0 0.1 collective-permute-start.1
  9.7 0.0 copy-start
  9.7 1.0 %copy-done = f32[1,4,64,512]{3,2,1,0:T(8,128)S(1)} copy-done((f32[1,4,64,512]{3,2,1,0:T(8,128)S(1)}, f32[1,4,64,512]{3,2,1,0:T(8,128)}, u32[]{:S(2)}) %copy-start) | copy-done | bytes 524312
  10.7 0.0 copy-start.1
  10.8 0.9 %copy-done.1 = bf16[1,1024,128]{2,1,0:T(8,128)(2,1)S(1)} copy-done((bf16[1,1024,128]{2,1,0:T(8,128)(2,1)S(1)}, bf16[1,1024,128]{2,1,0:T(8,128)(2,1)}, u32[]{:S(2)}) %copy-start.1) | copy-done | bytes 262168
  11.7 0.0 copy-start.2
  11.7 0.7 %copy-done.2 = s32[1,4096]{1,0:T(1,128)S(1)} copy-done((s32[1,4096]{1,0:T(1,128)S(1)}, s32[1,4096]{1,0:T(1,128)}, u32[]{:S(2)}) %copy-start.2) | copy-done | bytes 16408
  12.4 0.0 copy-start.3
  12.4 0.7 %copy-done.3 = f32[64]{0:T(128)S(1)} copy-done((f32[64]{0:T(128)S(1)}, f32[64]{0:T(128)}, u32[]{:S(2)}) %copy-start.3) | copy-done | bytes 280
  13.1 0.0 copy-start.4
  13.1 0.7 %copy-done.4 = f32[64]{0:T(128)S(1)} copy-done((f32[64]{0:T(128)S(1)}, f32[64]{0:T(128)}, u32[]{:S(2)}) %copy-start.4) | copy-done | bytes 280
  13.7 0.6 %shard_map.77 = (f32[4,4,64,128]{3,2,1,0:T(8,128)S(1)}, f32[5,64,128]{2,1,0:T(8,128)S(1)}, s32[1,4096]{1,0:T(1,128)S(1)}, bf16[1024,128]{1,0:T(8,128)(2,1)S(1)}) custom-call(s32[1]{0:T(128)S(6)} %copy.9.offset, f32[4,64,512]{2,1,0:T(8,128)S(1)} %bitcast.11, f32[1,64]{1,0:T(1,128)S(1)} %bitcast.16, f32[1,64]{1,0:T(1,128)S(1)} %bitcast.17, ...), custom_call_target="tpu_custom_call" | custom-call | flops 1024 | bytes 1024 | tf_op jit(solution)/shard_map/pallas_call | solution.py:355
  14.3 2.6 %collective-permute-done.refs_5_.refs_8_ = bf16[1024,128]{1,0:T(8,128)(2,1)S(1)} collective-permute-done((bf16[1024,128]{1,0:T(8,128)(2,1)}, bf16[1024,128]{1,0:T(8,128)(2,1)S(1)}, u32[]{:S(2)}, u32[]{:S(2)}) %collective-permute-start) | collective-permute-done | bytes 262176 | tf_op jit(solution)/shard_map/ppermute | solution.py:369
  17.0 0.8 %collective-permute-start.3 = (bf16[1024,128]{1,0:T(8,128)(2,1)S(1)}, bf16[1024,128]{1,0:T(8,128)(2,1)S(1)}, u32[]{:S(2)}, u32[]{:S(2)}) collective-permute-start(bf16[1024,128]{1,0:T(8,128)(2,1)S(1)} %collective-permute-done.refs_5_.refs_8_), channel_id=1, source_target_pairs={{0,1},{1,0},{2,3},{3,2},{4,5},{5,4},{6,7},{7,6},{8,9},{9,8},{10,11... | collective-permute-start | bytes 786440 | tf_op jit(solution)/shard_map/ppermute | solution.py:297
  17.7 0.0 collective-permute-done.1.low
  17.7 0.0 collective-permute-done.2.high
  17.7 2.6 %shard_map.78.refs_2_ = f32[4112,128]{1,0:T(8,128)S(1)} custom-call(s32[1]{0:T(128)S(6)} %copy.9.offset, f32[5,64,128]{2,1,0:T(8,128)S(1)} %get-tuple-element.14.coef, f32[4,4,64,128]{3,2,1,0:T(8,128)S(1)} %get-tuple-element.15.own, bf16[4,64,512]{2,1,0:T(8,128)(2,1)S(1)} %collective-permute-done.1.low, f32[4,64,512]{2,1,0:T(8,128)S(1)} %collective-permute-done.2.high), custom_call_target="tpu_custom_call" | custom-call | flops 1024 | bytes 1024 | tf_op jit(solution)/shard_map/pallas_call | solution.py:372
  20.4 0.0 collective-permute-done.4.refs_4_.refs_7_
  20.4 4.0 %shard_map.79.refs_4_ = f32[16,8,128]{2,1,0:T(8,128)S(1)} custom-call(s32[4]{0:T(128)S(1)} %iota_xor_fusion.refs_0_, s32[1,4096]{1,0:T(1,128)S(1)} %get-tuple-element.12.refs_1_, f32[4112,128]{1,0:T(8,128)S(1)} %shard_map.78.refs_2_, bf16[1024,128]{1,0:T(8,128)(2,1)S(1)} %get-tuple-element.17.refs_3_.refs_6_, ...), custom_call_target="tpu_custom_call" | custom-call | flops 1024 | bytes 1024 | tf_op jit(solution)/shard_map/pallas_call | solution.py:385
  24.4 0.0 collective-permute-done.3.refs_3_.refs_9_
  24.4 1.9 %shard_map.80 = f32[16,8,128]{2,1,0:T(8,128)S(1)} custom-call(s32[4]{0:T(128)S(1)} %iota_xor_fusion.refs_0_, s32[1,4096]{1,0:T(1,128)S(1)} %get-tuple-element.12.refs_1_, f32[4112,128]{1,0:T(8,128)S(1)} %shard_map.78.refs_2_, bf16[1024,128]{1,0:T(8,128)(2,1)S(1)} %collective-permute-done.3.refs_3_.refs_9_, f32[16,8,128]{2,1,0:T(8,128)S(1)} %shard_map.79.refs_4_), custom_call_target="tpu_custom_call" | custom-call | flops 1024 | bytes 1024 | tf_op jit(solution)/shard_map/pallas_call | solution.py:385
  26.3 0.1 collective-permute-start.5
  26.4 1.2 %collective-permute-done.5 = f32[16,8,128]{2,1,0:T(8,128)S(1)} collective-permute-done((f32[16,8,128]{2,1,0:T(8,128)S(1)}, f32[16,8,128]{2,1,0:T(8,128)S(1)}, u32[]{:S(2)}, u32[]{:S(2)}) %collective-permute-start.5) | collective-permute-done | bytes 65568 | tf_op jit(solution)/shard_map/ppermute | solution.py:333
  27.6 2.5 %collective-permute-start.6 = (f32[16,8,128]{2,1,0:T(8,128)S(1)}, f32[16,8,128]{2,1,0:T(8,128)S(1)}, u32[]{:S(2)}, u32[]{:S(2)}) collective-permute-start(f32[16,8,128]{2,1,0:T(8,128)S(1)} %add.3.refs_5_), channel_id=1, source_target_pairs={{0,24},{4,28},{8,16},{12,20},{16,8},{20,12},{24,0},{28,4},{1,25},{... | collective-permute-start | bytes 196616 | tf_op jit(solution)/shard_map/ppermute | solution.py:333
  30.1 0.5 collective-permute-start.7
  30.6 0.5 collective-permute-start.8
  31.2 2.1 %collective-permute-done.6.refs_2_ = f32[16,8,128]{2,1,0:T(8,128)S(1)} collective-permute-done((f32[16,8,128]{2,1,0:T(8,128)S(1)}, f32[16,8,128]{2,1,0:T(8,128)S(1)}, u32[]{:S(2)}, u32[]{:S(2)}) %collective-permute-start.6) | collective-permute-done | bytes 65568 | tf_op jit(solution)/shard_map/ppermute | solution.py:333
  33.2 1.2 %collective-permute-done.7.refs_3_ = f32[16,8,128]{2,1,0:T(8,128)S(1)} collective-permute-done((f32[16,8,128]{2,1,0:T(8,128)S(1)}, f32[16,8,128]{2,1,0:T(8,128)S(1)}, u32[]{:S(2)}, u32[]{:S(2)}) %collective-permute-start.7) | collective-permute-done | bytes 65568 | tf_op jit(solution)/shard_map/ppermute | solution.py:333
  34.4 0.5 collective-permute-done.8.refs_4_
  34.9 4.5 %shard_map.81 = (f32[16,8,128]{2,1,0:T(8,128)S(1)}, f32[4,256,128]{2,1,0:T(8,128)S(1)}, bf16[7,256,128]{2,1,0:T(8,128)(2,1)S(1)}, bf16[4,256,128]{2,1,0:T(8,128)(2,1)S(1)}) custom-call(s32[4]{0:T(128)S(1)} %iota_xor_fusion.refs_0_, s32[1,4096]{1,0:T(1,128)S(1)} %get-tuple-element.12.refs_1_, f32[16,8,128]{2,1,0:T(8,128)S(1)} %collective-permute-done.6.refs_2_, ...), custom_call_target="tpu_custom_call" | custom-call | flops 1024 | bytes 1024 | tf_op jit(solution)/shard_map/pallas_call | solution.py:400
  39.4 0.1 collective-permute-start.9
  39.5 2.6 %collective-permute-start.10 = (bf16[4,256,128]{2,1,0:T(8,128)(2,1)S(1)}, bf16[4,256,128]{2,1,0:T(8,128)(2,1)S(1)}, u32[]{:S(2)}, u32[]{:S(2)}) collective-permute-start(bf16[4,256,128]{2,1,0:T(8,128)(2,1)S(1)} %get-tuple-element.21), channel_id=1, source_target_pairs={{0,28},{4,0},{8,4},{12,8},{16,12},{20,16},{24,20},{28,24},{1,29},{... | collective-permute-start | bytes 786440 | tf_op jit(solution)/shard_map/ppermute | solution.py:418
  42.1 0.7 %copy.8 = f32[4,16,2,128]{3,2,1,0:T(2,128)} copy(f32[4,16,2,128]{3,0,2,1:T(4,128)S(1)} %bitcast.15) | data formatting | bytes 131072 | tf_op jit(solution)/shard_map/transpose | solution.py:426
  42.8 6.1 %collective-permute-done.10.high = bf16[4,256,128]{2,1,0:T(8,128)(2,1)S(1)} collective-permute-done((bf16[4,256,128]{2,1,0:T(8,128)(2,1)S(1)}, bf16[4,256,128]{2,1,0:T(8,128)(2,1)S(1)}, u32[]{:S(2)}, u32[]{:S(2)}) %collective-permute-start.10) | collective-permute-done | bytes 262176 | tf_op jit(solution)/shard_map/ppermute | solution.py:418
  48.9 2.2 %collective-permute-done.9.low = bf16[7,256,128]{2,1,0:T(8,128)(2,1)S(1)} collective-permute-done((bf16[7,256,128]{2,1,0:T(8,128)(2,1)S(1)}, bf16[7,256,128]{2,1,0:T(8,128)(2,1)S(1)}, u32[]{:S(2)}, u32[]{:S(2)}) %collective-permute-start.9) | collective-permute-done | bytes 458784 | tf_op jit(solution)/shard_map/ppermute | solution.py:417
  51.1 2.8 %shard_map.82 = f32[4,64,512]{2,1,0:T(8,128)} custom-call(f32[5,64,128]{2,1,0:T(8,128)S(1)} %get-tuple-element.14.coef, f32[4,256,128]{2,1,0:T(8,128)S(1)} %get-tuple-element.19.own, bf16[7,256,128]{2,1,0:T(8,128)(2,1)S(1)} %collective-permute-done.9.low, bf16[4,256,128]{2,1,0:T(8,128)(2,1)S(1)} %collective-permute-done.10.high), custom_call_target="tpu_custom_call" | custom-call | flops 1024 | bytes 1024 | tf_op jit(solution)/shard_map/pallas_call | solution.py:419
  (2 shorter events, 0.0 us)
Async XLA Ops:
  0.6 16.3 %collective-permute-start = (bf16[1024,128]{1,0:T(8,128)(2,1)}, bf16[1024,128]{1,0:T(8,128)(2,1)S(1)}, u32[]{:S(2)}, u32[]{:S(2)}) collective-permute-start(bf16[1024,128]{1,0:T(8,128)(2,1)} %bitcast.12), channel_id=1, source_target_pairs={{0,2},{1,3},{2,0},{3,1},{4,6},{5,7},{6,4},{7,5},{8,10},{9,11},{10,... | collective-permute-start | bytes 786440 | tf_op jit(solution)/shard_map/ppermute | solution.py:369
  4.7 13.0 %collective-permute-start.2 = (f32[4,64,512]{2,1,0:T(8,128)}, f32[4,64,512]{2,1,0:T(8,128)S(1)}, u32[]{:S(2)}, u32[]{:S(2)}) collective-permute-start(f32[4,64,512]{2,1,0:T(8,128)} %bitcast.10), channel_id=1, source_target_pairs={{0,28},{4,0},{8,4},{12,8},{16,12},{20,16},{24,20},{28,24},{1,29},{... | collective-permute-start | bytes 1572872 | tf_op jit(solution)/shard_map/ppermute | solution.py:352
  6.3 14.1 %collective-permute-start.4 = (bf16[1024,128]{1,0:T(8,128)(2,1)}, bf16[1024,128]{1,0:T(8,128)(2,1)S(1)}, u32[]{:S(2)}, u32[]{:S(2)}) collective-permute-start(bf16[1024,128]{1,0:T(8,128)(2,1)} %bitcast.13), channel_id=1, source_target_pairs={{0,1},{1,0},{2,3},{3,2},{4,5},{5,4},{6,7},{7,6},{8,9},{9,8},{10,11... | collective-permute-start | bytes 786440 | tf_op jit(solution)/shard_map/ppermute | solution.py:297
  9.0 8.8 %collective-permute-start.1 = (bf16[4,64,512]{2,1,0:T(8,128)(2,1)S(1)}, bf16[4,64,512]{2,1,0:T(8,128)(2,1)S(1)}, u32[]{:S(2)}, u32[]{:S(2)}) collective-permute-start(bf16[4,64,512]{2,1,0:T(8,128)(2,1)S(1)} %bitcast_convert_fusion), channel_id=1, source_target_pairs={{0,4},{4,8},{8,12},{12,16},{16,20},{20,24},{24,28},{28,0},{1,5},{5... | collective-permute-start | bytes 786440 | tf_op jit(solution)/shard_map/ppermute | solution.py:353
  9.7 1.0 %copy-start = (f32[1,4,64,512]{3,2,1,0:T(8,128)S(1)}, f32[1,4,64,512]{3,2,1,0:T(8,128)}, u32[]{:S(2)}) copy-start(f32[1,4,64,512]{3,2,1,0:T(8,128)} %param.6) | copy-start | bytes 1572868
  10.7 0.9 %copy-start.1 = (bf16[1,1024,128]{2,1,0:T(8,128)(2,1)S(1)}, bf16[1,1024,128]{2,1,0:T(8,128)(2,1)}, u32[]{:S(2)}) copy-start(bf16[1,1024,128]{2,1,0:T(8,128)(2,1)} %param.11) | copy-start | bytes 786436
  11.7 0.7 %copy-start.2 = (s32[1,4096]{1,0:T(1,128)S(1)}, s32[1,4096]{1,0:T(1,128)}, u32[]{:S(2)}) copy-start(s32[1,4096]{1,0:T(1,128)} %tile.1) | copy-start | bytes 49156
  12.4 0.7 %copy-start.3 = (f32[64]{0:T(128)S(1)}, f32[64]{0:T(128)}, u32[]{:S(2)}) copy-start(f32[64]{0:T(128)} %param.7) | copy-start | bytes 772
  13.1 0.7 %copy-start.4 = (f32[64]{0:T(128)S(1)}, f32[64]{0:T(128)}, u32[]{:S(2)}) copy-start(f32[64]{0:T(128)} %param.8) | copy-start | bytes 772
  17.0 7.4 %collective-permute-start.3 = (bf16[1024,128]{1,0:T(8,128)(2,1)S(1)}, bf16[1024,128]{1,0:T(8,128)(2,1)S(1)}, u32[]{:S(2)}, u32[]{:S(2)}) collective-permute-start(bf16[1024,128]{1,0:T(8,128)(2,1)S(1)} %collective-permute-done.refs_5_.refs_8_), channel_id=1, source_target_pairs={{0,1},{1,0},{2,3},{3,2},{4,5},{5,4},{6,7},{7,6},{8,9},{9,8},{10,11... | collective-permute-start | bytes 786440 | tf_op jit(solution)/shard_map/ppermute | solution.py:297
  26.3 1.3 %collective-permute-start.5 = (f32[16,8,128]{2,1,0:T(8,128)S(1)}, f32[16,8,128]{2,1,0:T(8,128)S(1)}, u32[]{:S(2)}, u32[]{:S(2)}) collective-permute-start(f32[16,8,128]{2,1,0:T(8,128)S(1)} %shard_map.80), channel_id=1, source_target_pairs={{0,4},{4,0},{8,12},{12,8},{16,20},{20,16},{24,28},{28,24},{1,5},{5... | collective-permute-start | bytes 196616 | tf_op jit(solution)/shard_map/ppermute | solution.py:333
  27.6 5.6 %collective-permute-start.6 = (f32[16,8,128]{2,1,0:T(8,128)S(1)}, f32[16,8,128]{2,1,0:T(8,128)S(1)}, u32[]{:S(2)}, u32[]{:S(2)}) collective-permute-start(f32[16,8,128]{2,1,0:T(8,128)S(1)} %add.3.refs_5_), channel_id=1, source_target_pairs={{0,24},{4,28},{8,16},{12,20},{16,8},{20,12},{24,0},{28,4},{1,25},{... | collective-permute-start | bytes 196616 | tf_op jit(solution)/shard_map/ppermute | solution.py:333
  30.1 4.3 %collective-permute-start.7 = (f32[16,8,128]{2,1,0:T(8,128)S(1)}, f32[16,8,128]{2,1,0:T(8,128)S(1)}, u32[]{:S(2)}, u32[]{:S(2)}) collective-permute-start(f32[16,8,128]{2,1,0:T(8,128)S(1)} %add.3.refs_5_), channel_id=1, source_target_pairs={{0,8},{4,12},{8,0},{12,4},{16,24},{20,28},{24,16},{28,20},{1,9},{5... | collective-permute-start | bytes 196616 | tf_op jit(solution)/shard_map/ppermute | solution.py:333
  30.6 4.3 %collective-permute-start.8 = (f32[16,8,128]{2,1,0:T(8,128)S(1)}, f32[16,8,128]{2,1,0:T(8,128)S(1)}, u32[]{:S(2)}, u32[]{:S(2)}) collective-permute-start(f32[16,8,128]{2,1,0:T(8,128)S(1)} %add.3.refs_5_), channel_id=1, source_target_pairs={{0,16},{4,20},{8,24},{12,28},{16,0},{20,4},{24,8},{28,12},{1,17},{... | collective-permute-start | bytes 196616 | tf_op jit(solution)/shard_map/ppermute | solution.py:333
  39.4 11.7 %collective-permute-start.9 = (bf16[7,256,128]{2,1,0:T(8,128)(2,1)S(1)}, bf16[7,256,128]{2,1,0:T(8,128)(2,1)S(1)}, u32[]{:S(2)}, u32[]{:S(2)}) collective-permute-start(bf16[7,256,128]{2,1,0:T(8,128)(2,1)S(1)} %get-tuple-element.20), channel_id=1, source_target_pairs={{0,4},{4,8},{8,12},{12,16},{16,20},{20,24},{24,28},{28,0},{1,5},{5... | collective-permute-start | bytes 1376264 | tf_op jit(solution)/shard_map/ppermute | solution.py:417
  39.5 9.4 %collective-permute-start.10 = (bf16[4,256,128]{2,1,0:T(8,128)(2,1)S(1)}, bf16[4,256,128]{2,1,0:T(8,128)(2,1)S(1)}, u32[]{:S(2)}, u32[]{:S(2)}) collective-permute-start(bf16[4,256,128]{2,1,0:T(8,128)(2,1)S(1)} %get-tuple-element.21), channel_id=1, source_target_pairs={{0,28},{4,0},{8,4},{12,8},{16,12},{20,16},{24,20},{28,24},{1,29},{... | collective-permute-start | bytes 786440 | tf_op jit(solution)/shard_map/ppermute | solution.py:418

commit v15 on v14

--- a/solution.py
+++ b/solution.py
@@ -203,7 +203,7 @@
             return carry
 
         groups = panel.shape[0] // GROUP
-        lax.fori_loop(0, groups, body, 0, unroll=2 if groups % 2 == 0 else 1)
+        lax.fori_loop(0, groups, body, 0, unroll=min(4, groups))
 
 
 def deposit_kernel(order, places, shard, source, start, *refs):
@@ -282,7 +282,7 @@
     )
 
 
-def gathered_panel(panel, axis, late, first):
+def gathered_panel(panel, axis, soon, late, first):
     count = lax.axis_size(axis)
     shards, mask = {0: [panel]}, count // 2
     while mask:
@@ -291,6 +291,8 @@
             pieces = shards[held]
             if held:
                 pieces = [tied(piece, late) for piece in pieces]
+            else:
+                pieces = [tied(piece, soon) for piece in pieces]
             if len(shards) == 1:
                 shards[mask] = [first]
                 continue
@@ -350,7 +352,8 @@
 
     source = lax.axis_index("probe") ^ jnp.arange(probes, dtype=jnp.int32)
     high = lax.ppermute(own, "state", shift_pairs(slabs, -1))
-    low = lax.ppermute(own.astype(bf16), "state", shift_pairs(slabs, 1))
+    rounded = own.astype(bf16)
+    low = lax.ppermute(rounded, "state", shift_pairs(slabs, 1))
 
     shifted, coef, start, panel = call(
         prelude_kernel,
@@ -378,7 +381,7 @@
         inputs=5,
     )(probe_offset, coef, shifted, low, high)
 
-    panels = list(enumerate([[panel]] + gathered_panel(actuator_panel[0], "probe", coef, far)))
+    panels = list(enumerate([[panel]] + gathered_panel(actuator_panel[0], "probe", rounded, coef, far)))
 
     def project(shards, *given):
         pieces = [piece for _, pieces in shards for piece in pieces]

time: 54.3 us -> 55.8 us (1.028)
  waiting for transfers between devices: 16 us -> 17.9 us
  Pallas kernels: 16.5 us -> 15.9 us
    ppermute x2, waiting for transfers between devices: 0.03 us -> 2.02 us  [gathered_panel(): shards[held | mask] = [lax.ppermute(piece, axis, pairs) for piece in pieces]]
  transfers between devices with their start and end apart: 11 -> 11, of which waited for: 7 -> 9; matrix products, arithmetic and copies ran while one was open for 3% -> 3% of each run, Pallas kernels for 13% -> 12%
where the time goes in v15:
time: 55.8 us; the launch traced here: 55.5 us
  waiting for transfers between devices  17.9 us (32%)
  Pallas kernels  15.9 us (28%)
  starting transfers between devices  14.5 us (26%)
  local copies, waits for them, and re-layouts  4.68 us (8%)
  between operations  1.36 us (2%)
  other arithmetic  1.12 us (2%)
    ppermute x1, waiting for transfers between devices, local(): from_high = lax.ppermute(leftward, 'state', shift_pairs(slabs, -1))  6.1 us
    pallas_call x2, Pallas kernels, project(): call(lambda *refs: project_kernel(layout(shards), shard, *refs), jax.Shap...  5.35 us
    ppermute x4, waiting for transfers between devices, summands(): lax.ppermute(part, axis, [(i, i ^ k * done) for i in range(count)])  5.05 us
    pallas_call x1, Pallas kernels, local(): call(lambda *refs: deposit_kernel(order, layout(panels), shard, *refs), (...  4.53 us
    ppermute x1, starting transfers between devices, local(): lax.ppermute(actuator_panel[0], 'probe', [(i, i ^ half) for i in range(pr...  4.1 us
    unnamed x10, local copies, waits for them, and re-layouts  4.01 us
    ppermute x4, starting transfers between devices, summands(): lax.ppermute(part, axis, [(i, i ^ k * done) for i in range(count)])  3.62 us
    pallas_call x1, Pallas kernels, local(): call(forward_kernel, jax.ShapeDtypeStruct((cells, height, width), f32), v...  2.83 us
  transfers between devices with their start and end apart: 11, of which 9 were waited for; matrix products, arithmetic and copies ran while one was open for 3% of the time, Pallas kernels for 12%

profile of v15, /device:TPU:0, one launch (start us, length us, event | category | flops | bytes accessed | tf_op | source)
XLA Modules:
  0.0 55.5 jit_solution(12005652425187043922)
XLA Ops:
  0.6 4.1 %collective-permute-start = (bf16[1024,128]{1,0:T(8,128)(2,1)}, bf16[1024,128]{1,0:T(8,128)(2,1)S(1)}, u32[]{:S(2)}, u32[]{:S(2)}) collective-permute-start(bf16[1024,128]{1,0:T(8,128)(2,1)} %bitcast.12), channel_id=1, source_target_pairs={{0,2},{1,3},{2,0},{3,1},{4,6},{5,7},{6,4},{7,5},{8,10},{9,11},{10,... | collective-permute-start | bytes 786440 | tf_op jit(solution)/shard_map/ppermute | solution.py:372
  4.7 1.6 %collective-permute-start.2 = (f32[4,64,512]{2,1,0:T(8,128)}, f32[4,64,512]{2,1,0:T(8,128)S(1)}, u32[]{:S(2)}, u32[]{:S(2)}) collective-permute-start(f32[4,64,512]{2,1,0:T(8,128)} %bitcast.10), channel_id=1, source_target_pairs={{0,28},{4,0},{8,4},{12,8},{16,12},{20,16},{24,20},{28,24},{1,29},{... | collective-permute-start | bytes 1572872 | tf_op jit(solution)/shard_map/ppermute | solution.py:354
  6.3 1.1 %bitcast_convert_fusion = bf16[4,64,512]{2,1,0:T(8,128)(2,1)S(1)} fusion(f32[1,4,64,512]{3,2,1,0:T(8,128)} %param.6), kind=kLoop, calls=%fused_computation.1 | loop fusion | flops 131072 | bytes 786432 | tf_op jit(solution)/shard_map/convert_element_type | solution.py:355
  7.4 0.1 collective-permute-start.1
  7.5 1.6 %collective-permute-start.4 = (bf16[1024,128]{1,0:T(8,128)(2,1)}, bf16[1024,128]{1,0:T(8,128)(2,1)S(1)}, u32[]{:S(2)}, u32[]{:S(2)}) collective-permute-start(bf16[1024,128]{1,0:T(8,128)(2,1)} %bitcast.13), channel_id=1, source_target_pairs={{0,1},{1,0},{2,3},{3,2},{4,5},{5,4},{6,7},{7,6},{8,9},{9,8},{10,11... | collective-permute-start | bytes 786440 | tf_op jit(solution)/shard_map/ppermute | solution.py:299
  9.8 0.0 copy-start
  9.8 1.0 %copy-done = f32[1,4,64,512]{3,2,1,0:T(8,128)S(1)} copy-done((f32[1,4,64,512]{3,2,1,0:T(8,128)S(1)}, f32[1,4,64,512]{3,2,1,0:T(8,128)}, u32[]{:S(2)}) %copy-start) | copy-done | bytes 524312
  10.9 0.0 copy-start.1
  10.9 0.9 %copy-done.1 = bf16[1,1024,128]{2,1,0:T(8,128)(2,1)S(1)} copy-done((bf16[1,1024,128]{2,1,0:T(8,128)(2,1)S(1)}, bf16[1,1024,128]{2,1,0:T(8,128)(2,1)}, u32[]{:S(2)}) %copy-start.1) | copy-done | bytes 262168
  11.8 0.0 copy-start.2
  11.8 0.7 %copy-done.2 = s32[1,4096]{1,0:T(1,128)S(1)} copy-done((s32[1,4096]{1,0:T(1,128)S(1)}, s32[1,4096]{1,0:T(1,128)}, u32[]{:S(2)}) %copy-start.2) | copy-done | bytes 16408
  12.5 0.0 copy-start.3
  12.5 0.7 %copy-done.3 = f32[64]{0:T(128)S(1)} copy-done((f32[64]{0:T(128)S(1)}, f32[64]{0:T(128)}, u32[]{:S(2)}) %copy-start.3) | copy-done | bytes 280
  13.2 0.0 copy-start.4
  13.2 0.7 %copy-done.4 = f32[64]{0:T(128)S(1)} copy-done((f32[64]{0:T(128)S(1)}, f32[64]{0:T(128)}, u32[]{:S(2)}) %copy-start.4) | copy-done | bytes 280
  13.8 0.6 %shard_map.77 = (f32[4,4,64,128]{3,2,1,0:T(8,128)S(1)}, f32[5,64,128]{2,1,0:T(8,128)S(1)}, s32[1,4096]{1,0:T(1,128)S(1)}, bf16[1024,128]{1,0:T(8,128)(2,1)S(1)}) custom-call(s32[1]{0:T(128)S(6)} %copy.9.offset, f32[4,64,512]{2,1,0:T(8,128)S(1)} %bitcast.11, f32[1,64]{1,0:T(1,128)S(1)} %bitcast.16, f32[1,64]{1,0:T(1,128)S(1)} %bitcast.17, ...), custom_call_target="tpu_custom_call" | custom-call | flops 1024 | bytes 1024 | tf_op jit(solution)/shard_map/pallas_call | solution.py:358
  14.4 2.5 %collective-permute-done.refs_5_.refs_8_ = bf16[1024,128]{1,0:T(8,128)(2,1)S(1)} collective-permute-done((bf16[1024,128]{1,0:T(8,128)(2,1)}, bf16[1024,128]{1,0:T(8,128)(2,1)S(1)}, u32[]{:S(2)}, u32[]{:S(2)}) %collective-permute-start) | collective-permute-done | bytes 262176 | tf_op jit(solution)/shard_map/ppermute | solution.py:372
  17.0 0.8 %collective-permute-start.3 = (bf16[1024,128]{1,0:T(8,128)(2,1)S(1)}, bf16[1024,128]{1,0:T(8,128)(2,1)S(1)}, u32[]{:S(2)}, u32[]{:S(2)}) collective-permute-start(bf16[1024,128]{1,0:T(8,128)(2,1)S(1)} %collective-permute-done.refs_5_.refs_8_), channel_id=1, source_target_pairs={{0,1},{1,0},{2,3},{3,2},{4,5},{5,4},{6,7},{7,6},{8,9},{9,8},{10,11... | collective-permute-start | bytes 786440 | tf_op jit(solution)/shard_map/ppermute | solution.py:299
  17.7 0.0 collective-permute-done.1.low
  17.7 0.0 collective-permute-done.2.high
  17.8 2.6 %shard_map.78.refs_2_ = f32[4112,128]{1,0:T(8,128)S(1)} custom-call(s32[1]{0:T(128)S(6)} %copy.9.offset, f32[5,64,128]{2,1,0:T(8,128)S(1)} %get-tuple-element.15.coef, f32[4,4,64,128]{3,2,1,0:T(8,128)S(1)} %get-tuple-element.16.own, bf16[4,64,512]{2,1,0:T(8,128)(2,1)S(1)} %collective-permute-done.1.low, f32[4,64,512]{2,1,0:T(8,128)S(1)} %collective-permute-done.2.high), custom_call_target="tpu_custom_call" | custom-call | flops 1024 | bytes 1024 | tf_op jit(solution)/shard_map/pallas_call | solution.py:375
  20.4 1.0 %collective-permute-done.4.refs_4_.refs_7_ = bf16[1024,128]{1,0:T(8,128)(2,1)S(1)} collective-permute-done((bf16[1024,128]{1,0:T(8,128)(2,1)}, bf16[1024,128]{1,0:T(8,128)(2,1)S(1)}, u32[]{:S(2)}, u32[]{:S(2)}) %collective-permute-start.4) | collective-permute-done | bytes 262176 | tf_op jit(solution)/shard_map/ppermute | solution.py:299
  21.4 3.6 %shard_map.79.refs_4_ = f32[16,8,128]{2,1,0:T(8,128)S(1)} custom-call(s32[4]{0:T(128)S(1)} %iota_xor_fusion.refs_0_, s32[1,4096]{1,0:T(1,128)S(1)} %get-tuple-element.13.refs_1_, f32[4112,128]{1,0:T(8,128)S(1)} %shard_map.78.refs_2_, bf16[1024,128]{1,0:T(8,128)(2,1)S(1)} %get-tuple-element.18.refs_3_.refs_6_, ...), custom_call_target="tpu_custom_call" | custom-call | flops 1024 | bytes 1024 | tf_op jit(solution)/shard_map/pallas_call | solution.py:388
  25.0 1.0 %collective-permute-done.3.refs_3_.refs_9_ = bf16[1024,128]{1,0:T(8,128)(2,1)S(1)} collective-permute-done((bf16[1024,128]{1,0:T(8,128)(2,1)S(1)}, bf16[1024,128]{1,0:T(8,128)(2,1)S(1)}, u32[]{:S(2)}, u32[]{:S(2)}) %collective-permute-start.3) | collective-permute-done | bytes 262176 | tf_op jit(solution)/shard_map/ppermute | solution.py:299
  26.0 1.8 %shard_map.80 = f32[16,8,128]{2,1,0:T(8,128)S(1)} custom-call(s32[4]{0:T(128)S(1)} %iota_xor_fusion.refs_0_, s32[1,4096]{1,0:T(1,128)S(1)} %get-tuple-element.13.refs_1_, f32[4112,128]{1,0:T(8,128)S(1)} %shard_map.78.refs_2_, bf16[1024,128]{1,0:T(8,128)(2,1)S(1)} %collective-permute-done.3.refs_3_.refs_9_, f32[16,8,128]{2,1,0:T(8,128)S(1)} %shard_map.79.refs_4_), custom_call_target="tpu_custom_call" | custom-call | flops 1024 | bytes 1024 | tf_op jit(solution)/shard_map/pallas_call | solution.py:388
  27.8 0.1 collective-permute-start.5
  27.8 1.2 %collective-permute-done.5 = f32[16,8,128]{2,1,0:T(8,128)S(1)} collective-permute-done((f32[16,8,128]{2,1,0:T(8,128)S(1)}, f32[16,8,128]{2,1,0:T(8,128)S(1)}, u32[]{:S(2)}, u32[]{:S(2)}) %collective-permute-start.5) | collective-permute-done | bytes 65568 | tf_op jit(solution)/shard_map/ppermute | solution.py:335
  29.1 2.4 %collective-permute-start.6 = (f32[16,8,128]{2,1,0:T(8,128)S(1)}, f32[16,8,128]{2,1,0:T(8,128)S(1)}, u32[]{:S(2)}, u32[]{:S(2)}) collective-permute-start(f32[16,8,128]{2,1,0:T(8,128)S(1)} %add.3.refs_5_), channel_id=1, source_target_pairs={{0,24},{4,28},{8,16},{12,20},{16,8},{20,12},{24,0},{28,4},{1,25},{... | collective-permute-start | bytes 196616 | tf_op jit(solution)/shard_map/ppermute | solution.py:335
  31.5 0.7 %collective-permute-start.7 = (f32[16,8,128]{2,1,0:T(8,128)S(1)}, f32[16,8,128]{2,1,0:T(8,128)S(1)}, u32[]{:S(2)}, u32[]{:S(2)}) collective-permute-start(f32[16,8,128]{2,1,0:T(8,128)S(1)} %add.3.refs_5_), channel_id=1, source_target_pairs={{0,8},{4,12},{8,0},{12,4},{16,24},{20,28},{24,16},{28,20},{1,9},{5... | collective-permute-start | bytes 196616 | tf_op jit(solution)/shard_map/ppermute | solution.py:335
  32.2 0.5 collective-permute-start.8
  32.7 2.1 %collective-permute-done.6.refs_2_ = f32[16,8,128]{2,1,0:T(8,128)S(1)} collective-permute-done((f32[16,8,128]{2,1,0:T(8,128)S(1)}, f32[16,8,128]{2,1,0:T(8,128)S(1)}, u32[]{:S(2)}, u32[]{:S(2)}) %collective-permute-start.6) | collective-permute-done | bytes 65568 | tf_op jit(solution)/shard_map/ppermute | solution.py:335
  34.7 1.1 %collective-permute-done.7.refs_3_ = f32[16,8,128]{2,1,0:T(8,128)S(1)} collective-permute-done((f32[16,8,128]{2,1,0:T(8,128)S(1)}, f32[16,8,128]{2,1,0:T(8,128)S(1)}, u32[]{:S(2)}, u32[]{:S(2)}) %collective-permute-start.7) | collective-permute-done | bytes 65568 | tf_op jit(solution)/shard_map/ppermute | solution.py:335
  35.8 0.6 %collective-permute-done.8.refs_4_ = f32[16,8,128]{2,1,0:T(8,128)S(1)} collective-permute-done((f32[16,8,128]{2,1,0:T(8,128)S(1)}, f32[16,8,128]{2,1,0:T(8,128)S(1)}, u32[]{:S(2)}, u32[]{:S(2)}) %collective-permute-start.8) | collective-permute-done | bytes 65568 | tf_op jit(solution)/shard_map/ppermute | solution.py:335
  36.5 4.5 %shard_map.81 = (f32[16,8,128]{2,1,0:T(8,128)S(1)}, f32[4,256,128]{2,1,0:T(8,128)S(1)}, bf16[7,256,128]{2,1,0:T(8,128)(2,1)S(1)}, bf16[4,256,128]{2,1,0:T(8,128)(2,1)S(1)}) custom-call(s32[4]{0:T(128)S(1)} %iota_xor_fusion.refs_0_, s32[1,4096]{1,0:T(1,128)S(1)} %get-tuple-element.13.refs_1_, f32[16,8,128]{2,1,0:T(8,128)S(1)} %collective-permute-done.6.refs_2_, ...), custom_call_target="tpu_custom_call" | custom-call | flops 1024 | bytes 1024 | tf_op jit(solution)/shard_map/pallas_call | solution.py:403
  41.0 0.1 collective-permute-start.9
  41.1 2.6 %collective-permute-start.10 = (bf16[4,256,128]{2,1,0:T(8,128)(2,1)S(1)}, bf16[4,256,128]{2,1,0:T(8,128)(2,1)S(1)}, u32[]{:S(2)}, u32[]{:S(2)}) collective-permute-start(bf16[4,256,128]{2,1,0:T(8,128)(2,1)S(1)} %get-tuple-element.23), channel_id=1, source_target_pairs={{0,28},{4,0},{8,4},{12,8},{16,12},{20,16},{24,20},{28,24},{1,29},{... | collective-permute-start | bytes 786440 | tf_op jit(solution)/shard_map/ppermute | solution.py:421
  43.7 0.7 %copy.8 = f32[4,16,2,128]{3,2,1,0:T(2,128)} copy(f32[4,16,2,128]{3,0,2,1:T(4,128)S(1)} %bitcast.15) | data formatting | bytes 131072 | tf_op jit(solution)/shard_map/transpose | solution.py:429
  44.4 6.1 %collective-permute-done.10.high = bf16[4,256,128]{2,1,0:T(8,128)(2,1)S(1)} collective-permute-done((bf16[4,256,128]{2,1,0:T(8,128)(2,1)S(1)}, bf16[4,256,128]{2,1,0:T(8,128)(2,1)S(1)}, u32[]{:S(2)}, u32[]{:S(2)}) %collective-permute-start.10) | collective-permute-done | bytes 262176 | tf_op jit(solution)/shard_map/ppermute | solution.py:421
  50.5 2.2 %collective-permute-done.9.low = bf16[7,256,128]{2,1,0:T(8,128)(2,1)S(1)} collective-permute-done((bf16[7,256,128]{2,1,0:T(8,128)(2,1)S(1)}, bf16[7,256,128]{2,1,0:T(8,128)(2,1)S(1)}, u32[]{:S(2)}, u32[]{:S(2)}) %collective-permute-start.9) | collective-permute-done | bytes 458784 | tf_op jit(solution)/shard_map/ppermute | solution.py:420
  52.7 2.8 %shard_map.82 = f32[4,64,512]{2,1,0:T(8,128)} custom-call(f32[5,64,128]{2,1,0:T(8,128)S(1)} %get-tuple-element.15.coef, f32[4,256,128]{2,1,0:T(8,128)S(1)} %get-tuple-element.21.own, bf16[7,256,128]{2,1,0:T(8,128)(2,1)S(1)} %collective-permute-done.9.low, bf16[4,256,128]{2,1,0:T(8,128)(2,1)S(1)} %collective-permute-done.10.high), custom_call_target="tpu_custom_call" | custom-call | flops 1024 | bytes 1024 | tf_op jit(solution)/shard_map/pallas_call | solution.py:422
  (2 shorter events, 0.0 us)
Async XLA Ops:
  0.6 16.3 %collective-permute-start = (bf16[1024,128]{1,0:T(8,128)(2,1)}, bf16[1024,128]{1,0:T(8,128)(2,1)S(1)}, u32[]{:S(2)}, u32[]{:S(2)}) collective-permute-start(bf16[1024,128]{1,0:T(8,128)(2,1)} %bitcast.12), channel_id=1, source_target_pairs={{0,2},{1,3},{2,0},{3,1},{4,6},{5,7},{6,4},{7,5},{8,10},{9,11},{10,... | collective-permute-start | bytes 786440 | tf_op jit(solution)/shard_map/ppermute | solution.py:372
  4.7 13.0 %collective-permute-start.2 = (f32[4,64,512]{2,1,0:T(8,128)}, f32[4,64,512]{2,1,0:T(8,128)S(1)}, u32[]{:S(2)}, u32[]{:S(2)}) collective-permute-start(f32[4,64,512]{2,1,0:T(8,128)} %bitcast.10), channel_id=1, source_target_pairs={{0,28},{4,0},{8,4},{12,8},{16,12},{20,16},{24,20},{28,24},{1,29},{... | collective-permute-start | bytes 1572872 | tf_op jit(solution)/shard_map/ppermute | solution.py:354
  7.4 10.3 %collective-permute-start.1 = (bf16[4,64,512]{2,1,0:T(8,128)(2,1)S(1)}, bf16[4,64,512]{2,1,0:T(8,128)(2,1)S(1)}, u32[]{:S(2)}, u32[]{:S(2)}) collective-permute-start(bf16[4,64,512]{2,1,0:T(8,128)(2,1)S(1)} %bitcast_convert_fusion), channel_id=1, source_target_pairs={{0,4},{4,8},{8,12},{12,16},{16,20},{20,24},{24,28},{28,0},{1,5},{5... | collective-permute-start | bytes 786440 | tf_op jit(solution)/shard_map/ppermute | solution.py:356
  7.5 13.9 %collective-permute-start.4 = (bf16[1024,128]{1,0:T(8,128)(2,1)}, bf16[1024,128]{1,0:T(8,128)(2,1)S(1)}, u32[]{:S(2)}, u32[]{:S(2)}) collective-permute-start(bf16[1024,128]{1,0:T(8,128)(2,1)} %bitcast.13), channel_id=1, source_target_pairs={{0,1},{1,0},{2,3},{3,2},{4,5},{5,4},{6,7},{7,6},{8,9},{9,8},{10,11... | collective-permute-start | bytes 786440 | tf_op jit(solution)/shard_map/ppermute | solution.py:299
  9.8 1.0 %copy-start = (f32[1,4,64,512]{3,2,1,0:T(8,128)S(1)}, f32[1,4,64,512]{3,2,1,0:T(8,128)}, u32[]{:S(2)}) copy-start(f32[1,4,64,512]{3,2,1,0:T(8,128)} %param.6) | copy-start | bytes 1572868
  10.9 0.9 %copy-start.1 = (bf16[1,1024,128]{2,1,0:T(8,128)(2,1)S(1)}, bf16[1,1024,128]{2,1,0:T(8,128)(2,1)}, u32[]{:S(2)}) copy-start(bf16[1,1024,128]{2,1,0:T(8,128)(2,1)} %param.11) | copy-start | bytes 786436
  11.8 0.7 %copy-start.2 = (s32[1,4096]{1,0:T(1,128)S(1)}, s32[1,4096]{1,0:T(1,128)}, u32[]{:S(2)}) copy-start(s32[1,4096]{1,0:T(1,128)} %tile.1) | copy-start | bytes 49156
  12.5 0.7 %copy-start.3 = (f32[64]{0:T(128)S(1)}, f32[64]{0:T(128)}, u32[]{:S(2)}) copy-start(f32[64]{0:T(128)} %param.7) | copy-start | bytes 772
  13.2 0.7 %copy-start.4 = (f32[64]{0:T(128)S(1)}, f32[64]{0:T(128)}, u32[]{:S(2)}) copy-start(f32[64]{0:T(128)} %param.8) | copy-start | bytes 772
  17.0 9.0 %collective-permute-start.3 = (bf16[1024,128]{1,0:T(8,128)(2,1)S(1)}, bf16[1024,128]{1,0:T(8,128)(2,1)S(1)}, u32[]{:S(2)}, u32[]{:S(2)}) collective-permute-start(bf16[1024,128]{1,0:T(8,128)(2,1)S(1)} %collective-permute-done.refs_5_.refs_8_), channel_id=1, source_target_pairs={{0,1},{1,0},{2,3},{3,2},{4,5},{5,4},{6,7},{7,6},{8,9},{9,8},{10,11... | collective-permute-start | bytes 786440 | tf_op jit(solution)/shard_map/ppermute | solution.py:299
  27.8 1.3 %collective-permute-start.5 = (f32[16,8,128]{2,1,0:T(8,128)S(1)}, f32[16,8,128]{2,1,0:T(8,128)S(1)}, u32[]{:S(2)}, u32[]{:S(2)}) collective-permute-start(f32[16,8,128]{2,1,0:T(8,128)S(1)} %shard_map.80), channel_id=1, source_target_pairs={{0,4},{4,0},{8,12},{12,8},{16,20},{20,16},{24,28},{28,24},{1,5},{5... | collective-permute-start | bytes 196616 | tf_op jit(solution)/shard_map/ppermute | solution.py:335
  29.1 5.6 %collective-permute-start.6 = (f32[16,8,128]{2,1,0:T(8,128)S(1)}, f32[16,8,128]{2,1,0:T(8,128)S(1)}, u32[]{:S(2)}, u32[]{:S(2)}) collective-permute-start(f32[16,8,128]{2,1,0:T(8,128)S(1)} %add.3.refs_5_), channel_id=1, source_target_pairs={{0,24},{4,28},{8,16},{12,20},{16,8},{20,12},{24,0},{28,4},{1,25},{... | collective-permute-start | bytes 196616 | tf_op jit(solution)/shard_map/ppermute | solution.py:335
  31.5 4.3 %collective-permute-start.7 = (f32[16,8,128]{2,1,0:T(8,128)S(1)}, f32[16,8,128]{2,1,0:T(8,128)S(1)}, u32[]{:S(2)}, u32[]{:S(2)}) collective-permute-start(f32[16,8,128]{2,1,0:T(8,128)S(1)} %add.3.refs_5_), channel_id=1, source_target_pairs={{0,8},{4,12},{8,0},{12,4},{16,24},{20,28},{24,16},{28,20},{1,9},{5... | collective-permute-start | bytes 196616 | tf_op jit(solution)/shard_map/ppermute | solution.py:335
  32.2 4.3 %collective-permute-start.8 = (f32[16,8,128]{2,1,0:T(8,128)S(1)}, f32[16,8,128]{2,1,0:T(8,128)S(1)}, u32[]{:S(2)}, u32[]{:S(2)}) collective-permute-start(f32[16,8,128]{2,1,0:T(8,128)S(1)} %add.3.refs_5_), channel_id=1, source_target_pairs={{0,16},{4,20},{8,24},{12,28},{16,0},{20,4},{24,8},{28,12},{1,17},{... | collective-permute-start | bytes 196616 | tf_op jit(solution)/shard_map/ppermute | solution.py:335
  41.0 11.7 %collective-permute-start.9 = (bf16[7,256,128]{2,1,0:T(8,128)(2,1)S(1)}, bf16[7,256,128]{2,1,0:T(8,128)(2,1)S(1)}, u32[]{:S(2)}, u32[]{:S(2)}) collective-permute-start(bf16[7,256,128]{2,1,0:T(8,128)(2,1)S(1)} %get-tuple-element.22), channel_id=1, source_target_pairs={{0,4},{4,8},{8,12},{12,16},{16,20},{20,24},{24,28},{28,0},{1,5},{5... | collective-permute-start | bytes 1376264 | tf_op jit(solution)/shard_map/ppermute | solution.py:420
  41.1 9.4 %collective-permute-start.10 = (bf16[4,256,128]{2,1,0:T(8,128)(2,1)S(1)}, bf16[4,256,128]{2,1,0:T(8,128)(2,1)S(1)}, u32[]{:S(2)}, u32[]{:S(2)}) collective-permute-start(bf16[4,256,128]{2,1,0:T(8,128)(2,1)S(1)} %get-tuple-element.23), channel_id=1, source_target_pairs={{0,28},{4,0},{8,4},{12,8},{16,12},{20,16},{24,20},{28,24},{1,29},{... | collective-permute-start | bytes 786440 | tf_op jit(solution)/shard_map/ppermute | solution.py:421

commit v16 on v14

--- a/solution.py
+++ b/solution.py
@@ -203,7 +203,7 @@
             return carry
 
         groups = panel.shape[0] // GROUP
-        lax.fori_loop(0, groups, body, 0, unroll=2 if groups % 2 == 0 else 1)
+        lax.fori_loop(0, groups, body, 0, unroll=min(4, groups))
 
 
 def deposit_kernel(order, places, shard, source, start, *refs):

time: 54.3 us -> 54 us (level)
  transfers between devices with their start and end apart: 11 -> 11, of which waited for: 7 -> 8; matrix products, arithmetic and copies ran while one was open for 3% -> 3% of each run, Pallas kernels for 13% -> 13%
where the time goes in v16:
time: 54 us; the launch traced here: 53.7 us
  waiting for transfers between devices  16.2 us (30%)
  Pallas kernels  16 us (30%)
  starting transfers between devices  14.4 us (27%)
  local copies, waits for them, and re-layouts  4.68 us (9%)
  between operations  1.36 us (3%)
  other arithmetic  1.09 us (2%)
    ppermute x1, waiting for transfers between devices, local(): from_high = lax.ppermute(leftward, 'state', shift_pairs(slabs, -1))  6.1 us
    pallas_call x2, Pallas kernels, project(): call(lambda *refs: project_kernel(layout(shards), shard, *refs), jax.Shap...  5.36 us
    ppermute x4, waiting for transfers between devices, summands(): lax.ppermute(part, axis, [(i, i ^ k * done) for i in range(count)])  4.82 us
    pallas_call x1, Pallas kernels, local(): call(lambda *refs: deposit_kernel(order, layout(panels), shard, *refs), (...  4.53 us
    ppermute x1, starting transfers between devices, local(): lax.ppermute(actuator_panel[0], 'probe', [(i, i ^ half) for i in range(pr...  4.1 us
    unnamed x10, local copies, waits for them, and re-layouts  4.01 us
    ppermute x4, starting transfers between devices, summands(): lax.ppermute(part, axis, [(i, i ^ k * done) for i in range(count)])  3.62 us
    pallas_call x1, Pallas kernels, local(): call(forward_kernel, jax.ShapeDtypeStruct((cells, height, width), f32), v...  2.83 us
  transfers between devices with their start and end apart: 11, of which 8 were waited for; matrix products, arithmetic and copies ran while one was open for 3% of the time, Pallas kernels for 13%

profile of v16, /device:TPU:0, one launch (start us, length us, event | category | flops | bytes accessed | tf_op | source)
XLA Modules:
  0.0 53.7 jit_solution(2050685028475760374)
XLA Ops:
  0.6 4.1 %collective-permute-start = (bf16[1024,128]{1,0:T(8,128)(2,1)}, bf16[1024,128]{1,0:T(8,128)(2,1)S(1)}, u32[]{:S(2)}, u32[]{:S(2)}) collective-permute-start(bf16[1024,128]{1,0:T(8,128)(2,1)} %bitcast.12), channel_id=1, source_target_pairs={{0,2},{1,3},{2,0},{3,1},{4,6},{5,7},{6,4},{7,5},{8,10},{9,11},{10,... | collective-permute-start | bytes 786440 | tf_op jit(solution)/shard_map/ppermute | solution.py:369
  4.7 1.6 %collective-permute-start.2 = (f32[4,64,512]{2,1,0:T(8,128)}, f32[4,64,512]{2,1,0:T(8,128)S(1)}, u32[]{:S(2)}, u32[]{:S(2)}) collective-permute-start(f32[4,64,512]{2,1,0:T(8,128)} %bitcast.10), channel_id=1, source_target_pairs={{0,28},{4,0},{8,4},{12,8},{16,12},{20,16},{24,20},{28,24},{1,29},{... | collective-permute-start | bytes 1572872 | tf_op jit(solution)/shard_map/ppermute | solution.py:352
  6.3 1.6 %collective-permute-start.4 = (bf16[1024,128]{1,0:T(8,128)(2,1)}, bf16[1024,128]{1,0:T(8,128)(2,1)S(1)}, u32[]{:S(2)}, u32[]{:S(2)}) collective-permute-start(bf16[1024,128]{1,0:T(8,128)(2,1)} %bitcast.13), channel_id=1, source_target_pairs={{0,1},{1,0},{2,3},{3,2},{4,5},{5,4},{6,7},{7,6},{8,9},{9,8},{10,11... | collective-permute-start | bytes 786440 | tf_op jit(solution)/shard_map/ppermute | solution.py:297
  7.9 1.1 %bitcast_convert_fusion = bf16[4,64,512]{2,1,0:T(8,128)(2,1)S(1)} fusion(f32[1,4,64,512]{3,2,1,0:T(8,128)} %param.6), kind=kLoop, calls=%fused_computation.1 | loop fusion | flops 131072 | bytes 786432 | tf_op jit(solution)/shard_map/convert_element_type | solution.py:353
  9.0 0.1 collective-permute-start.1
  9.7 0.0 copy-start
  9.7 1.0 %copy-done = f32[1,4,64,512]{3,2,1,0:T(8,128)S(1)} copy-done((f32[1,4,64,512]{3,2,1,0:T(8,128)S(1)}, f32[1,4,64,512]{3,2,1,0:T(8,128)}, u32[]{:S(2)}) %copy-start) | copy-done | bytes 524312
  10.7 0.0 copy-start.1
  10.8 0.9 %copy-done.1 = bf16[1,1024,128]{2,1,0:T(8,128)(2,1)S(1)} copy-done((bf16[1,1024,128]{2,1,0:T(8,128)(2,1)S(1)}, bf16[1,1024,128]{2,1,0:T(8,128)(2,1)}, u32[]{:S(2)}) %copy-start.1) | copy-done | bytes 262168
  11.7 0.0 copy-start.2
  11.7 0.7 %copy-done.2 = s32[1,4096]{1,0:T(1,128)S(1)} copy-done((s32[1,4096]{1,0:T(1,128)S(1)}, s32[1,4096]{1,0:T(1,128)}, u32[]{:S(2)}) %copy-start.2) | copy-done | bytes 16408
  12.4 0.0 copy-start.3
  12.4 0.7 %copy-done.3 = f32[64]{0:T(128)S(1)} copy-done((f32[64]{0:T(128)S(1)}, f32[64]{0:T(128)}, u32[]{:S(2)}) %copy-start.3) | copy-done | bytes 280
  13.1 0.0 copy-start.4
  13.1 0.7 %copy-done.4 = f32[64]{0:T(128)S(1)} copy-done((f32[64]{0:T(128)S(1)}, f32[64]{0:T(128)}, u32[]{:S(2)}) %copy-start.4) | copy-done | bytes 280
  13.7 0.6 %shard_map.77 = (f32[4,4,64,128]{3,2,1,0:T(8,128)S(1)}, f32[5,64,128]{2,1,0:T(8,128)S(1)}, s32[1,4096]{1,0:T(1,128)S(1)}, bf16[1024,128]{1,0:T(8,128)(2,1)S(1)}) custom-call(s32[1]{0:T(128)S(6)} %copy.9.offset, f32[4,64,512]{2,1,0:T(8,128)S(1)} %bitcast.11, f32[1,64]{1,0:T(1,128)S(1)} %bitcast.16, f32[1,64]{1,0:T(1,128)S(1)} %bitcast.17, ...), custom_call_target="tpu_custom_call" | custom-call | flops 1024 | bytes 1024 | tf_op jit(solution)/shard_map/pallas_call | solution.py:355
  14.3 2.6 %collective-permute-done.refs_5_.refs_8_ = bf16[1024,128]{1,0:T(8,128)(2,1)S(1)} collective-permute-done((bf16[1024,128]{1,0:T(8,128)(2,1)}, bf16[1024,128]{1,0:T(8,128)(2,1)S(1)}, u32[]{:S(2)}, u32[]{:S(2)}) %collective-permute-start) | collective-permute-done | bytes 262176 | tf_op jit(solution)/shard_map/ppermute | solution.py:369
  17.0 0.8 %collective-permute-start.3 = (bf16[1024,128]{1,0:T(8,128)(2,1)S(1)}, bf16[1024,128]{1,0:T(8,128)(2,1)S(1)}, u32[]{:S(2)}, u32[]{:S(2)}) collective-permute-start(bf16[1024,128]{1,0:T(8,128)(2,1)S(1)} %collective-permute-done.refs_5_.refs_8_), channel_id=1, source_target_pairs={{0,1},{1,0},{2,3},{3,2},{4,5},{5,4},{6,7},{7,6},{8,9},{9,8},{10,11... | collective-permute-start | bytes 786440 | tf_op jit(solution)/shard_map/ppermute | solution.py:297
  17.7 0.0 collective-permute-done.1.low
  17.7 0.0 collective-permute-done.2.high
  17.7 2.6 %shard_map.78.refs_2_ = f32[4112,128]{1,0:T(8,128)S(1)} custom-call(s32[1]{0:T(128)S(6)} %copy.9.offset, f32[5,64,128]{2,1,0:T(8,128)S(1)} %get-tuple-element.14.coef, f32[4,4,64,128]{3,2,1,0:T(8,128)S(1)} %get-tuple-element.15.own, bf16[4,64,512]{2,1,0:T(8,128)(2,1)S(1)} %collective-permute-done.1.low, f32[4,64,512]{2,1,0:T(8,128)S(1)} %collective-permute-done.2.high), custom_call_target="tpu_custom_call" | custom-call | flops 1024 | bytes 1024 | tf_op jit(solution)/shard_map/pallas_call | solution.py:372
  20.4 0.0 collective-permute-done.4.refs_4_.refs_7_
  20.4 3.6 %shard_map.79.refs_4_ = f32[16,8,128]{2,1,0:T(8,128)S(1)} custom-call(s32[4]{0:T(128)S(1)} %iota_xor_fusion.refs_0_, s32[1,4096]{1,0:T(1,128)S(1)} %get-tuple-element.12.refs_1_, f32[4112,128]{1,0:T(8,128)S(1)} %shard_map.78.refs_2_, bf16[1024,128]{1,0:T(8,128)(2,1)S(1)} %get-tuple-element.17.refs_3_.refs_6_, ...), custom_call_target="tpu_custom_call" | custom-call | flops 1024 | bytes 1024 | tf_op jit(solution)/shard_map/pallas_call | solution.py:385
  24.0 0.4 collective-permute-done.3.refs_3_.refs_9_
  24.4 1.8 %shard_map.80 = f32[16,8,128]{2,1,0:T(8,128)S(1)} custom-call(s32[4]{0:T(128)S(1)} %iota_xor_fusion.refs_0_, s32[1,4096]{1,0:T(1,128)S(1)} %get-tuple-element.12.refs_1_, f32[4112,128]{1,0:T(8,128)S(1)} %shard_map.78.refs_2_, bf16[1024,128]{1,0:T(8,128)(2,1)S(1)} %collective-permute-done.3.refs_3_.refs_9_, f32[16,8,128]{2,1,0:T(8,128)S(1)} %shard_map.79.refs_4_), custom_call_target="tpu_custom_call" | custom-call | flops 1024 | bytes 1024 | tf_op jit(solution)/shard_map/pallas_call | solution.py:385
  26.2 0.1 collective-permute-start.5
  26.2 1.2 %collective-permute-done.5 = f32[16,8,128]{2,1,0:T(8,128)S(1)} collective-permute-done((f32[16,8,128]{2,1,0:T(8,128)S(1)}, f32[16,8,128]{2,1,0:T(8,128)S(1)}, u32[]{:S(2)}, u32[]{:S(2)}) %collective-permute-start.5) | collective-permute-done | bytes 65568 | tf_op jit(solution)/shard_map/ppermute | solution.py:333
  27.5 2.3 %collective-permute-start.6 = (f32[16,8,128]{2,1,0:T(8,128)S(1)}, f32[16,8,128]{2,1,0:T(8,128)S(1)}, u32[]{:S(2)}, u32[]{:S(2)}) collective-permute-start(f32[16,8,128]{2,1,0:T(8,128)S(1)} %add.3.refs_5_), channel_id=1, source_target_pairs={{0,24},{4,28},{8,16},{12,20},{16,8},{20,12},{24,0},{28,4},{1,25},{... | collective-permute-start | bytes 196616 | tf_op jit(solution)/shard_map/ppermute | solution.py:333
  29.8 0.5 %collective-permute-start.7 = (f32[16,8,128]{2,1,0:T(8,128)S(1)}, f32[16,8,128]{2,1,0:T(8,128)S(1)}, u32[]{:S(2)}, u32[]{:S(2)}) collective-permute-start(f32[16,8,128]{2,1,0:T(8,128)S(1)} %add.3.refs_5_), channel_id=1, source_target_pairs={{0,8},{4,12},{8,0},{12,4},{16,24},{20,28},{24,16},{28,20},{1,9},{5... | collective-permute-start | bytes 196616 | tf_op jit(solution)/shard_map/ppermute | solution.py:333
  30.4 0.7 %collective-permute-start.8 = (f32[16,8,128]{2,1,0:T(8,128)S(1)}, f32[16,8,128]{2,1,0:T(8,128)S(1)}, u32[]{:S(2)}, u32[]{:S(2)}) collective-permute-start(f32[16,8,128]{2,1,0:T(8,128)S(1)} %add.3.refs_5_), channel_id=1, source_target_pairs={{0,16},{4,20},{8,24},{12,28},{16,0},{20,4},{24,8},{28,12},{1,17},{... | collective-permute-start | bytes 196616 | tf_op jit(solution)/shard_map/ppermute | solution.py:333
  31.1 2.2 %collective-permute-done.6.refs_2_ = f32[16,8,128]{2,1,0:T(8,128)S(1)} collective-permute-done((f32[16,8,128]{2,1,0:T(8,128)S(1)}, f32[16,8,128]{2,1,0:T(8,128)S(1)}, u32[]{:S(2)}, u32[]{:S(2)}) %collective-permute-start.6) | collective-permute-done | bytes 65568 | tf_op jit(solution)/shard_map/ppermute | solution.py:333
  33.2 0.9 %collective-permute-done.7.refs_3_ = f32[16,8,128]{2,1,0:T(8,128)S(1)} collective-permute-done((f32[16,8,128]{2,1,0:T(8,128)S(1)}, f32[16,8,128]{2,1,0:T(8,128)S(1)}, u32[]{:S(2)}, u32[]{:S(2)}) %collective-permute-start.7) | collective-permute-done | bytes 65568 | tf_op jit(solution)/shard_map/ppermute | solution.py:333
  34.1 0.5 %collective-permute-done.8.refs_4_ = f32[16,8,128]{2,1,0:T(8,128)S(1)} collective-permute-done((f32[16,8,128]{2,1,0:T(8,128)S(1)}, f32[16,8,128]{2,1,0:T(8,128)S(1)}, u32[]{:S(2)}, u32[]{:S(2)}) %collective-permute-start.8) | collective-permute-done | bytes 65568 | tf_op jit(solution)/shard_map/ppermute | solution.py:333
  34.6 4.5 %shard_map.81 = (f32[16,8,128]{2,1,0:T(8,128)S(1)}, f32[4,256,128]{2,1,0:T(8,128)S(1)}, bf16[7,256,128]{2,1,0:T(8,128)(2,1)S(1)}, bf16[4,256,128]{2,1,0:T(8,128)(2,1)S(1)}) custom-call(s32[4]{0:T(128)S(1)} %iota_xor_fusion.refs_0_, s32[1,4096]{1,0:T(1,128)S(1)} %get-tuple-element.12.refs_1_, f32[16,8,128]{2,1,0:T(8,128)S(1)} %collective-permute-done.6.refs_2_, ...), custom_call_target="tpu_custom_call" | custom-call | flops 1024 | bytes 1024 | tf_op jit(solution)/shard_map/pallas_call | solution.py:400
  39.2 0.1 collective-permute-start.9
  39.2 2.6 %collective-permute-start.10 = (bf16[4,256,128]{2,1,0:T(8,128)(2,1)S(1)}, bf16[4,256,128]{2,1,0:T(8,128)(2,1)S(1)}, u32[]{:S(2)}, u32[]{:S(2)}) collective-permute-start(bf16[4,256,128]{2,1,0:T(8,128)(2,1)S(1)} %get-tuple-element.21), channel_id=1, source_target_pairs={{0,28},{4,0},{8,4},{12,8},{16,12},{20,16},{24,20},{28,24},{1,29},{... | collective-permute-start | bytes 786440 | tf_op jit(solution)/shard_map/ppermute | solution.py:418
  41.9 0.7 %copy.8 = f32[4,16,2,128]{3,2,1,0:T(2,128)} copy(f32[4,16,2,128]{3,0,2,1:T(4,128)S(1)} %bitcast.15) | data formatting | bytes 131072 | tf_op jit(solution)/shard_map/transpose | solution.py:426
  42.5 6.1 %collective-permute-done.10.high = bf16[4,256,128]{2,1,0:T(8,128)(2,1)S(1)} collective-permute-done((bf16[4,256,128]{2,1,0:T(8,128)(2,1)S(1)}, bf16[4,256,128]{2,1,0:T(8,128)(2,1)S(1)}, u32[]{:S(2)}, u32[]{:S(2)}) %collective-permute-start.10) | collective-permute-done | bytes 262176 | tf_op jit(solution)/shard_map/ppermute | solution.py:418
  48.6 2.2 %collective-permute-done.9.low = bf16[7,256,128]{2,1,0:T(8,128)(2,1)S(1)} collective-permute-done((bf16[7,256,128]{2,1,0:T(8,128)(2,1)S(1)}, bf16[7,256,128]{2,1,0:T(8,128)(2,1)S(1)}, u32[]{:S(2)}, u32[]{:S(2)}) %collective-permute-start.9) | collective-permute-done | bytes 458784 | tf_op jit(solution)/shard_map/ppermute | solution.py:417
  50.8 2.8 %shard_map.82 = f32[4,64,512]{2,1,0:T(8,128)} custom-call(f32[5,64,128]{2,1,0:T(8,128)S(1)} %get-tuple-element.14.coef, f32[4,256,128]{2,1,0:T(8,128)S(1)} %get-tuple-element.19.own, bf16[7,256,128]{2,1,0:T(8,128)(2,1)S(1)} %collective-permute-done.9.low, bf16[4,256,128]{2,1,0:T(8,128)(2,1)S(1)} %collective-permute-done.10.high), custom_call_target="tpu_custom_call" | custom-call | flops 1024 | bytes 1024 | tf_op jit(solution)/shard_map/pallas_call | solution.py:419
  (2 shorter events, 0.0 us)
Async XLA Ops:
  0.6 16.3 %collective-permute-start = (bf16[1024,128]{1,0:T(8,128)(2,1)}, bf16[1024,128]{1,0:T(8,128)(2,1)S(1)}, u32[]{:S(2)}, u32[]{:S(2)}) collective-permute-start(bf16[1024,128]{1,0:T(8,128)(2,1)} %bitcast.12), channel_id=1, source_target_pairs={{0,2},{1,3},{2,0},{3,1},{4,6},{5,7},{6,4},{7,5},{8,10},{9,11},{10,... | collective-permute-start | bytes 786440 | tf_op jit(solution)/shard_map/ppermute | solution.py:369
  4.7 13.0 %collective-permute-start.2 = (f32[4,64,512]{2,1,0:T(8,128)}, f32[4,64,512]{2,1,0:T(8,128)S(1)}, u32[]{:S(2)}, u32[]{:S(2)}) collective-permute-start(f32[4,64,512]{2,1,0:T(8,128)} %bitcast.10), channel_id=1, source_target_pairs={{0,28},{4,0},{8,4},{12,8},{16,12},{20,16},{24,20},{28,24},{1,29},{... | collective-permute-start | bytes 1572872 | tf_op jit(solution)/shard_map/ppermute | solution.py:352
  6.3 14.1 %collective-permute-start.4 = (bf16[1024,128]{1,0:T(8,128)(2,1)}, bf16[1024,128]{1,0:T(8,128)(2,1)S(1)}, u32[]{:S(2)}, u32[]{:S(2)}) collective-permute-start(bf16[1024,128]{1,0:T(8,128)(2,1)} %bitcast.13), channel_id=1, source_target_pairs={{0,1},{1,0},{2,3},{3,2},{4,5},{5,4},{6,7},{7,6},{8,9},{9,8},{10,11... | collective-permute-start | bytes 786440 | tf_op jit(solution)/shard_map/ppermute | solution.py:297
  9.0 8.8 %collective-permute-start.1 = (bf16[4,64,512]{2,1,0:T(8,128)(2,1)S(1)}, bf16[4,64,512]{2,1,0:T(8,128)(2,1)S(1)}, u32[]{:S(2)}, u32[]{:S(2)}) collective-permute-start(bf16[4,64,512]{2,1,0:T(8,128)(2,1)S(1)} %bitcast_convert_fusion), channel_id=1, source_target_pairs={{0,4},{4,8},{8,12},{12,16},{16,20},{20,24},{24,28},{28,0},{1,5},{5... | collective-permute-start | bytes 786440 | tf_op jit(solution)/shard_map/ppermute | solution.py:353
  9.7 1.0 %copy-start = (f32[1,4,64,512]{3,2,1,0:T(8,128)S(1)}, f32[1,4,64,512]{3,2,1,0:T(8,128)}, u32[]{:S(2)}) copy-start(f32[1,4,64,512]{3,2,1,0:T(8,128)} %param.6) | copy-start | bytes 1572868
  10.7 0.9 %copy-start.1 = (bf16[1,1024,128]{2,1,0:T(8,128)(2,1)S(1)}, bf16[1,1024,128]{2,1,0:T(8,128)(2,1)}, u32[]{:S(2)}) copy-start(bf16[1,1024,128]{2,1,0:T(8,128)(2,1)} %param.11) | copy-start | bytes 786436
  11.7 0.7 %copy-start.2 = (s32[1,4096]{1,0:T(1,128)S(1)}, s32[1,4096]{1,0:T(1,128)}, u32[]{:S(2)}) copy-start(s32[1,4096]{1,0:T(1,128)} %tile.1) | copy-start | bytes 49156
  12.4 0.7 %copy-start.3 = (f32[64]{0:T(128)S(1)}, f32[64]{0:T(128)}, u32[]{:S(2)}) copy-start(f32[64]{0:T(128)} %param.7) | copy-start | bytes 772
  13.1 0.7 %copy-start.4 = (f32[64]{0:T(128)S(1)}, f32[64]{0:T(128)}, u32[]{:S(2)}) copy-start(f32[64]{0:T(128)} %param.8) | copy-start | bytes 772
  17.0 7.4 %collective-permute-start.3 = (bf16[1024,128]{1,0:T(8,128)(2,1)S(1)}, bf16[1024,128]{1,0:T(8,128)(2,1)S(1)}, u32[]{:S(2)}, u32[]{:S(2)}) collective-permute-start(bf16[1024,128]{1,0:T(8,128)(2,1)S(1)} %collective-permute-done.refs_5_.refs_8_), channel_id=1, source_target_pairs={{0,1},{1,0},{2,3},{3,2},{4,5},{5,4},{6,7},{7,6},{8,9},{9,8},{10,11... | collective-permute-start | bytes 786440 | tf_op jit(solution)/shard_map/ppermute | solution.py:297
  26.2 1.3 %collective-permute-start.5 = (f32[16,8,128]{2,1,0:T(8,128)S(1)}, f32[16,8,128]{2,1,0:T(8,128)S(1)}, u32[]{:S(2)}, u32[]{:S(2)}) collective-permute-start(f32[16,8,128]{2,1,0:T(8,128)S(1)} %shard_map.80), channel_id=1, source_target_pairs={{0,4},{4,0},{8,12},{12,8},{16,20},{20,16},{24,28},{28,24},{1,5},{5... | collective-permute-start | bytes 196616 | tf_op jit(solution)/shard_map/ppermute | solution.py:333
  27.5 5.7 %collective-permute-start.6 = (f32[16,8,128]{2,1,0:T(8,128)S(1)}, f32[16,8,128]{2,1,0:T(8,128)S(1)}, u32[]{:S(2)}, u32[]{:S(2)}) collective-permute-start(f32[16,8,128]{2,1,0:T(8,128)S(1)} %add.3.refs_5_), channel_id=1, source_target_pairs={{0,24},{4,28},{8,16},{12,20},{16,8},{20,12},{24,0},{28,4},{1,25},{... | collective-permute-start | bytes 196616 | tf_op jit(solution)/shard_map/ppermute | solution.py:333
  29.8 4.3 %collective-permute-start.7 = (f32[16,8,128]{2,1,0:T(8,128)S(1)}, f32[16,8,128]{2,1,0:T(8,128)S(1)}, u32[]{:S(2)}, u32[]{:S(2)}) collective-permute-start(f32[16,8,128]{2,1,0:T(8,128)S(1)} %add.3.refs_5_), channel_id=1, source_target_pairs={{0,8},{4,12},{8,0},{12,4},{16,24},{20,28},{24,16},{28,20},{1,9},{5... | collective-permute-start | bytes 196616 | tf_op jit(solution)/shard_map/ppermute | solution.py:333
  30.4 4.3 %collective-permute-start.8 = (f32[16,8,128]{2,1,0:T(8,128)S(1)}, f32[16,8,128]{2,1,0:T(8,128)S(1)}, u32[]{:S(2)}, u32[]{:S(2)}) collective-permute-start(f32[16,8,128]{2,1,0:T(8,128)S(1)} %add.3.refs_5_), channel_id=1, source_target_pairs={{0,16},{4,20},{8,24},{12,28},{16,0},{20,4},{24,8},{28,12},{1,17},{... | collective-permute-start | bytes 196616 | tf_op jit(solution)/shard_map/ppermute | solution.py:333
  39.2 11.7 %collective-permute-start.9 = (bf16[7,256,128]{2,1,0:T(8,128)(2,1)S(1)}, bf16[7,256,128]{2,1,0:T(8,128)(2,1)S(1)}, u32[]{:S(2)}, u32[]{:S(2)}) collective-permute-start(bf16[7,256,128]{2,1,0:T(8,128)(2,1)S(1)} %get-tuple-element.20), channel_id=1, source_target_pairs={{0,4},{4,8},{8,12},{12,16},{16,20},{20,24},{24,28},{28,0},{1,5},{5... | collective-permute-start | bytes 1376264 | tf_op jit(solution)/shard_map/ppermute | solution.py:417
  39.2 9.4 %collective-permute-start.10 = (bf16[4,256,128]{2,1,0:T(8,128)(2,1)S(1)}, bf16[4,256,128]{2,1,0:T(8,128)(2,1)S(1)}, u32[]{:S(2)}, u32[]{:S(2)}) collective-permute-start(bf16[4,256,128]{2,1,0:T(8,128)(2,1)S(1)} %get-tuple-element.21), channel_id=1, source_target_pairs={{0,28},{4,0},{8,4},{12,8},{16,12},{20,16},{24,20},{28,24},{1,29},{... | collective-permute-start | bytes 786440 | tf_op jit(solution)/shard_map/ppermute | solution.py:418
